TPU v7x, 256 devices: a whole 4x4x8 slice. The times are simulated.
256 devices in a mesh: cuts: 16 (over z, core), row: 16 (over y, x).
Axes of the slice: x: 4, y: 4, z: 8, core: 2. Of those that a mesh axis runs over, the one named last changes fastest.
Arguments:
- diagonal_blocks: bfloat16 [32, 2, 1024, 1024], P('cuts', None, 'row'), as said below
- diagonal_inverses: bfloat16 [32, 2, 1024, 1024], P('cuts', None, 'row'), as said below
- lower_blocks: bfloat16 [32, 2, 1024, 1024], P('cuts', None, 'row'), may hold values from -0.140625 to 0.140625
- upper_blocks: bfloat16 [32, 2, 1024, 1024], P('cuts', None, 'row'), may hold values from -0.140625 to 0.140625
- injection: bfloat16 [32, 2, 1024, 128], P('cuts', None, 'row'), may hold values from -6 to 6
- orbitals: int32 [32], replicated, may hold values from 512 to 1024, as said below
Outputs:
- reduced_diagonal: bfloat16 [16, 2, 1024, 1024], P('cuts', None, 'row')
- reduced_lower: bfloat16 [16, 2, 1024, 1024], P('cuts', None, 'row')
- reduced_upper: bfloat16 [16, 2, 1024, 1024], P('cuts', None, 'row')
- reduced_rhs: float32 [16, 2, 1024, 128], P('cuts', None, 'row')
- block_solutions: float32 [16, 2, 1024, 128], P('cuts', None, 'row')
Inputs may be any that keep to these rules, and one draw needn't show every extreme that they name: Active orbitals of each slice, at least half of 1024; block rows and columns at or beyond the count are inactive; some slice has all 1024. `diagonal_blocks`: diagonal blocks, a varying diagonal plus a dense part. `diagonal_inverses`: approximate inverses of the diagonal blocks.
All inputs are finite; a program needn't handle non-finite values.
Results may differ from a plain program's by a relative error of at most 0.014.
Values may be sent and summed in bfloat16 or wider, within the bound.
No kernel may reach another device: no remote copies, remote signals or barrier semaphores. Data moves between devices by JAX's collectives and lax.ppermute only.
A program may use at most 64 MiB of HBM per device.

v0:
```python
import functools

import jax
import jax.numpy as jnp
from jax import lax
from jax.experimental import pallas as pl
from jax.experimental.pallas import tpu as pltpu
from jax.sharding import PartitionSpec as P

REFINE = 2
BF = jnp.bfloat16
F32 = jnp.float32
VMEM = pl.BlockSpec(memory_space=pltpu.VMEM)
MIB = 24
SMEM = pl.BlockSpec(memory_space=pltpu.SMEM)


def call(kernel, out_shapes, flops, *args, scratch=(), hbm=0, mib=MIB, hbm_out=False):
    moved = sum(a.size * a.dtype.itemsize for a in args) + sum(
        s.size * s.dtype.itemsize for s in out_shapes
    )
    anywhere = pl.BlockSpec(memory_space=pl.ANY)
    return pl.pallas_call(
        kernel,
        out_shape=tuple(out_shapes),
        in_specs=[SMEM] + [anywhere] * hbm + [VMEM] * (len(args) - 1 - hbm),
        out_specs=tuple([anywhere if hbm_out else VMEM] * len(out_shapes)),
        scratch_shapes=list(scratch),
        compiler_params=pltpu.CompilerParams(vmem_limit_bytes=mib * 1024 * 1024),
        cost_estimate=pl.CostEstimate(flops=0, bytes_accessed=moved, transcendentals=0),
    )(*args)


def shape(dims, dtype=BF):
    return jax.ShapeDtypeStruct(dims, dtype)


def mod4(v):
    return lax.rem(v + 8, 4)


def at(chunk, size):
    return pl.ds(pl.multiple_of(chunk * size, size), size)


def lanes_of(rows):
    return lax.broadcasted_iota(jnp.int32, (rows, 128), 1)


def combine_small(real_rows, imag_rows):
    lane = lanes_of(real_rows.shape[0])
    turned = jnp.where(lane < 32, -pltpu.roll(imag_rows, 96, 1), pltpu.roll(imag_rows, 32, 1))
    return jnp.where(lane < 64, real_rows + turned, 0.0)


def packed(block):
    half = block.shape[0] // 2
    return jnp.where(lanes_of(half) < 64, block[:half], pltpu.roll(block[half:], 64, 1))


def halves(block):
    return block, pltpu.roll(block, 64, 1)


def masked(block, first_row, rows_on, chunk, cols_on):
    row = first_row + lax.broadcasted_iota(jnp.int32, (64, 256), 0)
    col = chunk * 256 + lax.broadcasted_iota(jnp.int32, (64, 256), 1)
    return jnp.where((row < rows_on) & (col < cols_on), block.astype(F32), 0.0).astype(BF)


def prepare_kernel(s_ref, d_hbm, g_hbm, a_hbm, c_hbm, b_hbm, piece0, piece1, piece2, piece3,
                   a_even, c_even, g0, g1, g2, g3, g_odd,
                   d_ref, a_ref, c_ref, b_ref, a_first, c_first, g_first, sems):
    y, x = s_ref[0], s_ref[1]
    first_row = (y * 4 + x) * 64
    before, own, odd, after = s_ref[2], s_ref[3], s_ref[4], s_ref[5]
    copies = [
        pltpu.make_async_copy(source, target, sems.at[index])
        for index, (source, target) in enumerate(
            (
                (c_hbm.at[1, 0], c_ref.at[0]),
                (c_hbm.at[1, 1], c_ref.at[1]),
                (b_hbm, b_ref),
                (a_hbm.at[1, 0], a_ref.at[0]),
                (a_hbm.at[1, 1], a_ref.at[1]),
                (d_hbm.at[0, 0], d_ref.at[0]),
                (d_hbm.at[0, 1], d_ref.at[1]),
                (a_hbm.at[0], a_first),
                (c_hbm.at[0], c_first),
                (g_hbm.at[0], g_first),
                (g_hbm.at[1], g_odd),
            )
        )
    ]
    for copy in copies:
        copy.start()
    pieces = (piece0, piece1, piece2, piece3)
    row_b = first_row + lax.broadcasted_iota(jnp.int32, (64, 128), 0)
    lane = lanes_of(64)
    copies[0].wait()
    copies[1].wait()
    for shift, piece in enumerate(pieces):
        chunk = mod4(x + shift)
        for part in range(2):
            piece[:, pl.ds(part * 256, 256)] = masked(
                c_ref[part, :, at(chunk, 256)], first_row, odd, chunk, after
            )
    copies[2].wait()
    blocks = [
        jnp.where(row_b < rows_on, b_ref[which, part].astype(F32), 0.0)
        for which, part, rows_on in ((1, 0, odd), (1, 1, odd), (0, 0, own), (0, 1, own))
    ]
    for shift, piece in enumerate(pieces):
        chunk = mod4(x + shift)
        tile = jnp.zeros((64, 128), F32)
        for place, block in enumerate(blocks):
            turned = pltpu.roll(block, mod4(place - chunk) * 32, 1)
            tile = jnp.where((lane >= place * 32) & (lane < place * 32 + 32), turned, tile)
        piece[:, pl.ds(512, 128)] = tile.astype(BF)
    copies[3].wait()
    copies[4].wait()
    for shift, piece in enumerate(pieces):
        chunk = mod4(x + shift)
        for part in range(2):
            piece[:, pl.ds(640 + part * 256, 256)] = masked(
                a_ref[part, :, at(chunk, 256)], first_row, odd, chunk, own
            )
    copies[5].wait()
    copies[6].wait()
    for shift, piece in enumerate(pieces):
        chunk = mod4(x + shift)
        for part in range(2):
            piece[:, pl.ds(1152 + part * 256, 256)] = d_ref[part, :, at(chunk, 256)]
    copies[7].wait()
    copies[8].wait()
    for chunk in range(4):
        cols = pl.ds(chunk * 256, 256)
        for part in range(2):
            a_even[part, :, cols] = masked(a_first[part, :, cols], first_row, own, chunk, before)
            c_even[part, :, cols] = masked(c_first[part, :, cols], first_row, own, chunk, odd)
    copies[9].wait()
    for shift, piece in enumerate((g0, g1, g2, g3)):
        for part in range(2):
            piece[part] = g_first[part, :, at(mod4(y + shift), 256)]
    copies[10].wait()


def assemble_kernel(s_ref, piece0, piece1, piece2, piece3, g0, g1, g2, g3,
                    panel, diagonal, g_columns):
    y, x = s_ref[0], s_ref[1]
    for shift, piece in enumerate((piece0, piece1, piece2, piece3)):
        rows = at(mod4(x - shift), 64)
        panel[rows, :] = piece[:, pl.ds(0, 1152)]
        diagonal[rows, :] = piece[:, pl.ds(1152, 512)]
    for shift, piece in enumerate((g0, g1, g2, g3)):
        g_columns[mod4(y - shift)] = piece[...]


def stack_rows(x, blocks, held):
    for shift, block in enumerate(blocks):
        held[at(mod4(x - shift), 128), :] = block[...].reshape(128, 1024)


def wide_dot(y, held, panels, start, width):
    total = None
    for place, panel in enumerate(panels):
        term = jnp.dot(
            held[:, at(mod4(y + place), 256)],
            panel[pl.ds(0, 256), pl.ds(start, width)],
            preferred_element_type=F32,
        )
        total = term if total is None else total + term
    parts = total.reshape(4, 2, 64, width)
    return parts[:, 0].reshape(256, width), parts[:, 1].reshape(256, width)


def wide_product(y, held, panels, start=0):
    real_rows, imag_rows = wide_dot(y, held, panels, start, 512)
    real = real_rows[:, :256] - imag_rows[:, 256:]
    imag = real_rows[:, 256:] + imag_rows[:, :256]
    return real, imag


def small_product(y, held, panels):
    return combine_small(*wide_dot(y, held, panels, 512, 128))


def put_pair(out, real, imag):
    out[pl.ds(0, 256), pl.ds(0, 256)] = real.astype(out.dtype)
    out[pl.ds(0, 256), pl.ds(256, 256)] = imag.astype(out.dtype)


def odd_kernel(s_ref, g0, g1, g2, g3, panel0, panel1, panel2, panel3, out, out_second, held):
    y, x = s_ref[0], s_ref[1]
    panels = (panel0, panel1, panel2, panel3)
    stack_rows(x, (g0, g1, g2, g3), held)
    put_pair(out, *wide_product(y, held, panels))
    out[:, pl.ds(512, 128)] = small_product(y, held, panels).astype(BF)
    put_pair(out_second, *wide_product(y, held, panels, 640))
    out_second[pl.ds(256, 16), :] = jnp.zeros((16, 512), BF)


def even_kernel(s_ref, a0, a1, a2, a3, c_ref, panel0, panel1, panel2, panel3, source,
                ship, ship_source, upper_new, source_part, a_rows, c_rows):
    y, x = s_ref[0], s_ref[1]
    panels = (panel0, panel1, panel2, panel3)
    stack_rows(x, (a0, a1, a2, a3), a_rows)
    c_rows[...] = c_ref[...].reshape(512, 1024)
    ship_source[...] = small_product(y, a_rows, panels).astype(BF)
    put_pair(ship, *wide_product(y, a_rows, panels))
    own = pltpu.roll(source[:, pl.ds(512, 128)].astype(F32), 64, 1)
    own = jnp.where(lanes_of(256) < 64, own, 0.0)
    source_part[...] = own - small_product(y, c_rows, panels)
    real, imag = wide_product(y, c_rows, panels)
    put_pair(upper_new, -real, -imag)


def diagonal_kernel(s_ref, c_rows, a_rows, panel0, panel1, panel2, panel3, diagonal, shipped,
                    out, lower):
    real, imag = wide_product(s_ref[0], c_rows, (panel0, panel1, panel2, panel3))
    real = diagonal[:, pl.ds(0, 256)].astype(F32) - real - shipped[:, pl.ds(0, 256)].astype(F32)
    imag = diagonal[:, pl.ds(256, 256)].astype(F32) - imag - shipped[:, pl.ds(256, 256)].astype(F32)
    put_pair(out, real, imag)
    real, imag = wide_product(s_ref[0], a_rows, (panel0, panel1, panel2, panel3))
    put_pair(lower, -real, -imag)


def pair_kernel(s_ref, lower, upper, out):
    out[:, pl.ds(0, 512)] = lower[...]
    out[:, pl.ds(512, 512)] = upper[...]


def block_product(block, right):
    real = jnp.dot(block[:, pl.ds(0, 256)], right, preferred_element_type=F32)
    imag = jnp.dot(block[:, pl.ds(256, 256)], right, preferred_element_type=F32)
    return real, imag


def put_partial(g_ref, right, own, send, whole):
    for index in range(4):
        total = jnp.dot(g_ref[index].reshape(512, 256), right, preferred_element_type=F32)
        parts = total.reshape(4, 2, 64, 128)
        value = combine_small(parts[:, 0].reshape(256, 128), parts[:, 1].reshape(256, 128))
        value = value.reshape(4, 64, 128)
        for group in range(4):
            whole[pl.ds(group * 256 + index * 64, 64), :] = value[group]
    total = packed(whole[...])
    own[...] = total
    send[...] = total.astype(BF)


def source_kernel(s_ref, g_ref, source_part, shipped, source_new, own, send, whole):
    source = (source_part[...] - shipped[...].astype(F32)).astype(BF)
    source_new[...] = source
    put_partial(g_ref, source, own, send, whole)


def summed(own, got):
    total = own[...]
    for other in got:
        total = total + other[...].astype(F32)
    return total


def turn_kernel(s_ref, own, got1, got2, got3, *refs, first):
    solved = None if first else refs[0]
    blocks, refs = refs[:4] if first else refs[1:5], refs[4:] if first else refs[5:]
    source, g_ref, out, own_new, send, vector, whole = refs
    x = s_ref[1]
    total = summed(own, (got1, got2, got3))
    if not first:
        total = solved[...].astype(F32) + total
    out[...] = total.astype(BF)
    unpack(out, vector)
    residue = (source[...].astype(F32) - blocks_product(x, blocks, vector)).astype(BF)
    put_partial(g_ref, residue, own_new, send, whole)


def last_kernel(s_ref, own, got1, got2, got3, solved, out):
    out[...] = (solved[...].astype(F32) + summed(own, (got1, got2, got3))).astype(BF)


def diagonal_rows_kernel(s_ref, block0, block1, block2, block3, rows_out):
    x = s_ref[1]
    rows = at(x, 64)
    for shift, block in enumerate((block0, block1, block2, block3)):
        cols = at(mod4(x - shift), 256)
        rows_out[0, :, cols] = block[rows, pl.ds(0, 256)]
        rows_out[1, :, cols] = block[rows, pl.ds(256, 256)]


def coupling_rows_kernel(s_ref, pair0, pair1, pair2, pair3, lower_out, upper_out):
    x = s_ref[1]
    rows = at(x, 64)
    for shift, pair in enumerate((pair0, pair1, pair2, pair3)):
        cols = at(mod4(x - shift), 256)
        lower_out[0, :, cols] = pair[rows, pl.ds(0, 256)]
        lower_out[1, :, cols] = pair[rows, pl.ds(256, 256)]
        upper_out[0, :, cols] = pair[rows, pl.ds(512, 256)]
        upper_out[1, :, cols] = pair[rows, pl.ds(768, 256)]


def unpack(solved, vector):
    low, high = halves(solved[...].astype(F32))
    vector[pl.ds(0, 512), :] = low.astype(BF)
    vector[pl.ds(512, 512), :] = high.astype(BF)


def blocks_product(x, blocks, vector):
    real_rows = imag_rows = None
    for shift, block in enumerate(blocks):
        real, imag = block_product(block, vector[at(mod4(x - shift), 256), :])
        real_rows = real if real_rows is None else real_rows + real
        imag_rows = imag if imag_rows is None else imag_rows + imag
    return combine_small(real_rows, imag_rows)


def couple_kernel(s_ref, pair0, pair1, pair2, pair3, source, solved, below, above,
                  out0, out1, out2, out3, held, vector):
    y, x = s_ref[0], s_ref[1]
    pairs = (pair0, pair1, pair2, pair3)
    unpack(below, vector)
    combined = source[...].astype(F32)
    combined = combined - blocks_product(x, [p.at[:, pl.ds(0, 512)] for p in pairs], vector)
    unpack(above, vector)
    combined = combined - blocks_product(x, [p.at[:, pl.ds(512, 512)] for p in pairs], vector)
    rows = pl.ds(pl.multiple_of(lax.rem(y, 2) * 256, 256), 256)
    moved = pltpu.roll(solved[rows, :].astype(F32), jnp.where(y < 2, 64, 0), 1)
    held[...] = jnp.where(lanes_of(256) < 64, combined, moved)
    for shift, out in enumerate((out0, out1, out2, out3)):
        out[...] = held[at(mod4(x + shift), 64), :]


def spread_kernel(s_ref, piece0, piece1, piece2, piece3, combined, solved):
    x = s_ref[1]
    lane = lanes_of(64)
    totals = [jnp.zeros((64, 128), F32) for _ in range(4)]
    for shift, piece in enumerate((piece0, piece1, piece2, piece3)):
        chunk = mod4(x - shift)
        value = piece[...]
        on = (lane >= chunk * 32) & (lane < chunk * 32 + 32)
        for place in range(4):
            turned = pltpu.roll(value, mod4(chunk - place) * 32, 1)
            totals[place] = jnp.where(on, turned, totals[place])
    combined[0] = totals[0]
    combined[1] = totals[1]
    solved[0] = totals[2]
    solved[1] = totals[3]


def moved_x(block, by):
    pairs = [(y * 4 + x, y * 4 + (x + by) % 4) for y in range(4) for x in range(4)]
    return lax.ppermute(block, "row", pairs)


def moved_y(block, by):
    pairs = [(y * 4 + x, ((y + by) % 4) * 4 + x) for y in range(4) for x in range(4)]
    return lax.ppermute(block, "row", pairs)


def gathered_y(block):
    return (block, moved_y(block, 3), moved_y(block, 2), moved_y(block, 1))


def gathered_x(block):
    groups = [[y * 4 + x for x in range(4)] for y in range(4)]
    return lax.all_gather(block, "row", axis_index_groups=groups)


def along_cuts(block, by):
    count = lax.axis_size("cuts")
    pairs = [(i, i + by) for i in range(count) if 0 <= i + by < count]
    return lax.ppermute(block, "cuts", pairs)


def body(diagonal_blocks, diagonal_inverses, lower_blocks, upper_blocks, injection, orbitals):
    cut = lax.axis_index("cuts")
    place = lax.axis_index("row")
    zero = jnp.zeros((1,), jnp.int32)
    window = lax.dynamic_slice_in_dim(jnp.concatenate([zero, orbitals, zero]), 2 * cut, 4)
    scalars = jnp.concatenate([jnp.stack([place // 4, place % 4]).astype(jnp.int32), window])
    turns = (1, 2, 3)
    after = lax.optimization_barrier
    wide_flops = 2 * 512 * 1024 * 512
    solve_flops = 2 * 2048 * 256 * 128

    *pieces, a_even, c_even, g0, g1, g2, g3, g_odd = call(
        prepare_kernel,
        [shape((64, 1664))] * 4 + [shape((2, 64, 1024))] * 2 + [shape((2, 64, 256))] * 4
        + [shape((2, 64, 1024))],
        0,
        scalars, diagonal_blocks, diagonal_inverses, lower_blocks, upper_blocks, injection,
        hbm=5, mib=52,
        scratch=[pltpu.VMEM((2, 64, 1024), BF)] * 3
        + [pltpu.VMEM((2, 2, 64, 128), BF)]
        + [pltpu.VMEM((2, 64, 1024), BF)] * 3
        + [pltpu.SemaphoreType.DMA((11,))],
    )
    pieces = [pieces[0]] + [moved_x(pieces[by], by) for by in turns]
    c_gathered = gathered_x(c_even)
    a_next = along_cuts(a_even, -1)
    g1, g2, g3 = [moved_y(piece, by) for by, piece in zip(turns, (g1, g2, g3))]
    a_next, g1, g2, g3, g_odd, *pieces = after((a_next, g1, g2, g3, g_odd, *pieces))
    panel, diagonal, g_columns = call(
        assemble_kernel,
        [shape((256, 1152)), shape((256, 512)), shape((4, 2, 64, 256))],
        0, scalars, *pieces, g0, g1, g2, g3,
    )
    g_columns = gathered_x(g_columns)
    panels = gathered_y(panel)
    g_blocks = [g_odd] + [moved_x(g_odd, by) for by in turns]
    a_blocks = [a_next] + [moved_x(a_next, by) for by in turns]
    first, second = call(
        odd_kernel, [shape((256, 640)), shape((272, 512))], wide_flops,
        scalars, *g_blocks, *panels, scratch=[pltpu.VMEM((512, 1024), BF)],
    )
    first, *a_blocks = after((first, *a_blocks))
    firsts = gathered_y(first)
    seconds = gathered_y(second)
    ship, ship_source, upper_new, source_part, a_rows, c_rows = call(
        even_kernel,
        [shape((256, 512)), shape((256, 128)), shape((256, 512)), shape((256, 128), F32),
         shape((512, 1024)),
         shape((512, 1024))],
        2 * wide_flops,
        scalars, *a_blocks, c_gathered, *firsts, panel,
    )
    shipped = along_cuts(ship, 1)
    shipped_source = along_cuts(ship_source, 1)
    diagonal_new, ship_lower = call(
        diagonal_kernel, [shape((256, 512))] * 2, 2 * wide_flops,
        scalars, c_rows, a_rows, *seconds, diagonal, shipped,
    )
    diagonals = [diagonal_new] + [moved_x(diagonal_new, by) for by in turns]
    packed_shapes = [shape((512, 128), F32), shape((512, 128))]
    whole = pltpu.VMEM((1024, 128), F32)
    vector = pltpu.VMEM((1024, 128), BF)
    source, own, send = call(
        source_kernel, [shape((256, 128))] + packed_shapes, solve_flops,
        scalars, g_columns, source_part, shipped_source, scratch=[whole],
    )
    got = gathered_y(send)[1:]
    ship_lower, *both = after((ship_lower, *diagonals, *got))
    diagonals, got = both[:4], both[4:]
    lower_new = along_cuts(ship_lower, 1)
    (pair,) = call(pair_kernel, [shape((256, 1024))], 0, scalars, lower_new, upper_new)
    pairs = [pair] + [moved_x(pair, by) for by in turns]
    solved = ()
    for turn in range(REFINE):
        *solved, own, send = call(
            functools.partial(turn_kernel, first=turn == 0),
            [shape((512, 128))] + packed_shapes, 2 * solve_flops,
            scalars, own, *got, *solved, *diagonals, source, g_columns,
            scratch=[vector, whole],
        )
        got = gathered_y(send)[1:]
    (solved,) = call(
        last_kernel, [shape((512, 128))], 0,
        scalars, own, *got, *solved,
    )
    below, above = along_cuts(solved, 1), along_cuts(solved, -1)
    (diagonal_rows,) = call(
        diagonal_rows_kernel, [shape((2, 64, 1024))], 0, scalars, *diagonals
    )
    lower_rows, upper_rows = call(
        coupling_rows_kernel, [shape((2, 64, 1024))] * 2, 0, scalars, *pairs
    )
    ends = call(
        couple_kernel, [shape((64, 128), F32)] * 4, solve_flops // 2,
        scalars, *pairs, source, solved, below, above,
        scratch=[pltpu.VMEM((256, 128), F32), vector],
    )
    ends = [ends[0]] + [moved_x(ends[by], by) for by in turns]
    combined, solved_rows = call(
        spread_kernel, [shape((2, 64, 128), F32)] * 2, 0, scalars, *ends
    )
    return (
        diagonal_rows[None],
        lower_rows[None],
        upper_rows[None],
        combined[None],
        solved_rows[None],
    )


def solution(mesh):
    split = P("cuts", None, "row", None)
    return jax.shard_map(
        body,
        mesh=mesh,
        in_specs=(split, split, split, split, split, P()),
        out_specs=(split,) * 5,
        check_vma=False,
    )
```

profile of v0, /device:TPU:97, one launch (start us, length us, event | category | flops | bytes accessed | tf_op | source)
XLA Modules:
  0.0 197.3 jit_solution(4503704936981913190)
XLA Ops:
  8.1 2.9 %shard_map.101 = (bf16[64,1664]{1,0:T(8,128)(2,1)S(1)}, bf16[64,1664]{1,0:T(8,128)(2,1)S(1)}, bf16[64,1664]{1,0:T(8,128)(2,1)S(1)}, bf16[64,1664]{1,0:T(8,128)(2...) custom-call(s32[6]{0:T(128)S(1)} %pad_add_fusion.1.s_ref, ...), custom_call_target="tpu_custom_call" | custom-call | bytes 4063256 | tf_op jit(solution)/shard_map/pallas_call | solution.py:23
  11.1 2.6 %collective-permute-start = (bf16[2,64,1024]{2,1,0:T(8,128)(2,1)S(1)}, bf16[2,64,1024]{2,1,0:T(8,128)(2,1)S(1)}, u32[]{:S(2)}, u32[]{:S(2)}) collective-permute-start(bf16[2,64,1024]{2,1,0:T(8,128)(2,1)S(1)} %get-tuple-element.68), channel_id=1, source_target_pairs={{16,0},{32,16},{48,32},{64,48},{80,64},{96,80},{112,96},{128,112},... | collective-permute-start | bytes 786440 | tf_op jit(solution)/shard_map/ppermute | solution.py:373
  15.0 2.5 %collective-permute-start.5 = (bf16[64,1664]{1,0:T(8,128)(2,1)S(1)}, bf16[64,1664]{1,0:T(8,128)(2,1)S(1)}, u32[]{:S(2)}, u32[]{:S(2)}) collective-permute-start(bf16[64,1664]{1,0:T(8,128)(2,1)S(1)} %get-tuple-element.75), channel_id=1, source_target_pairs={{0,2},{1,3},{2,0},{3,1},{4,6},{5,7},{6,4},{7,5},{8,10},{9,11},{10,... | collective-permute-start | bytes 638984 | tf_op jit(solution)/shard_map/ppermute | solution.py:353
  19.9 3.1 %collective-permute-done.1.g1 = bf16[2,64,256]{2,1,0:T(8,128)(2,1)S(1)} collective-permute-done((bf16[2,64,256]{2,1,0:T(8,128)(2,1)S(1)}, bf16[2,64,256]{2,1,0:T(8,128)(2,1)S(1)}, u32[]{:S(2)}, u32[]{:S(2)}) %collective-permute-start.1) | collective-permute-done | bytes 65568 | tf_op jit(solution)/shard_map/ppermute | solution.py:358
  23.0 1.9 collective-permute-start.2
  24.9 2.9 %collective-permute-done.2.g2 = bf16[2,64,256]{2,1,0:T(8,128)(2,1)S(1)} collective-permute-done((bf16[2,64,256]{2,1,0:T(8,128)(2,1)S(1)}, bf16[2,64,256]{2,1,0:T(8,128)(2,1)S(1)}, u32[]{:S(2)}, u32[]{:S(2)}) %collective-permute-start.2) | collective-permute-done | bytes 65568 | tf_op jit(solution)/shard_map/ppermute | solution.py:358
  33.5 3.1 %collective-permute-start.10 = (bf16[256,1152]{1,0:T(8,128)(2,1)S(1)}, bf16[256,1152]{1,0:T(8,128)(2,1)S(1)}, u32[]{:S(2)}, u32[]{:S(2)}) collective-permute-start(bf16[256,1152]{1,0:T(8,128)(2,1)S(1)} %get-tuple-element.86.panel0.source), channel_id=1, source_target_pairs={{0,12},{1,13},{2,14},{3,15},{4,0},{5,1},{6,2},{7,3},{8,4},{9,5},{1... | collective-permute-start | bytes 1769480 | tf_op jit(solution)/shard_map/ppermute | solution.py:358
  38.1 8.7 %collective-permute-done.7.g1 = bf16[2,64,1024]{2,1,0:T(8,128)(2,1)S(1)} collective-permute-done((bf16[2,64,1024]{2,1,0:T(8,128)(2,1)S(1)}, bf16[2,64,1024]{2,1,0:T(8,128)(2,1)S(1)}, u32[]{:S(2)}, u32[]{:S(2)}) %collective-permute-start.7) | collective-permute-done | bytes 262176 | tf_op jit(solution)/shard_map/ppermute | solution.py:353
  48.4 4.0 %collective-permute-done.9.g3 = bf16[2,64,1024]{2,1,0:T(8,128)(2,1)S(1)} collective-permute-done((bf16[2,64,1024]{2,1,0:T(8,128)(2,1)S(1)}, bf16[2,64,1024]{2,1,0:T(8,128)(2,1)S(1)}, u32[]{:S(2)}, u32[]{:S(2)}) %collective-permute-start.9) | collective-permute-done | bytes 262176 | tf_op jit(solution)/shard_map/ppermute | solution.py:353
  52.5 2.2 %collective-permute-start.15 = (bf16[2,64,1024]{2,1,0:T(8,128)(2,1)S(1)}, bf16[2,64,1024]{2,1,0:T(8,128)(2,1)S(1)}, u32[]{:S(2)}, u32[]{:S(2)}) collective-permute-start(bf16[2,64,1024]{2,1,0:T(8,128)(2,1)S(1)} %collective-permute-done.a0), channel_id=1, source_target_pairs={{0,3},{1,0},{2,1},{3,2},{4,7},{5,4},{6,5},{7,6},{8,11},{9,8},{10,9... | collective-permute-start | bytes 786440 | tf_op jit(solution)/shard_map/ppermute | solution.py:353
  54.6 10.8 %collective-permute-done.12.panel3 = bf16[256,1152]{1,0:T(8,128)(2,1)S(1)} collective-permute-done((bf16[256,1152]{1,0:T(8,128)(2,1)S(1)}, bf16[256,1152]{1,0:T(8,128)(2,1)S(1)}, u32[]{:S(2)}, u32[]{:S(2)}) %collective-permute-start.12) | collective-permute-done | bytes 589856 | tf_op jit(solution)/shard_map/ppermute | solution.py:358
  65.4 2.8 %shard_map.103 = (bf16[256,640]{1,0:T(8,128)(2,1)S(1)}, bf16[272,512]{1,0:T(8,128)(2,1)}) custom-call(s32[6]{0:T(128)S(1)} %pad_add_fusion.1.s_ref, bf16[2,64,1024]{2,1,0:T(8,128)(2,1)S(1)} %get-tuple-element.77.g0, bf16[2,64,1024]{2,1,0:T(8,128)(2,1)S(1)} %collective-permute-done.7.g1, bf16[2,64,1024]{2,1,0:T(8,128)(2,1)S(1)} %collective-permute-done.8.g2, ...), custom_call_target="tpu_custom_call" | custom-call | bytes 4014104 | tf_op jit(solution)/shard_map/pallas_call | solution.py:23
  69.7 5.3 %collective-permute-done.15.a3 = bf16[2,64,1024]{2,1,0:T(8,128)(2,1)S(1)} collective-permute-done((bf16[2,64,1024]{2,1,0:T(8,128)(2,1)S(1)}, bf16[2,64,1024]{2,1,0:T(8,128)(2,1)S(1)}, u32[]{:S(2)}, u32[]{:S(2)}) %collective-permute-start.15) | collective-permute-done | bytes 262176 | tf_op jit(solution)/shard_map/ppermute | solution.py:353
  77.2 2.4 %collective-permute-start.19 = (bf16[272,512]{1,0:T(8,128)(2,1)}, bf16[272,512]{1,0:T(8,128)(2,1)}, u32[]{:S(2)}, u32[]{:S(2)}) collective-permute-start(bf16[272,512]{1,0:T(8,128)(2,1)} %get-tuple-element.97.panel0), channel_id=1, source_target_pairs={{0,12},{1,13},{2,14},{3,15},{4,0},{5,1},{6,2},{7,3},{8,4},{9,5},{1... | collective-permute-start | bytes 835592 | tf_op jit(solution)/shard_map/ppermute | solution.py:358
  84.0 11.2 %collective-permute-done.18.panel3 = bf16[256,640]{1,0:T(8,128)(2,1)S(1)} collective-permute-done((bf16[256,640]{1,0:T(8,128)(2,1)S(1)}, bf16[256,640]{1,0:T(8,128)(2,1)S(1)}, u32[]{:S(2)}, u32[]{:S(2)}) %collective-permute-start.18) | collective-permute-done | bytes 327712 | tf_op jit(solution)/shard_map/ppermute | solution.py:358
  102.9 3.1 %shard_map.104 = (bf16[256,512]{1,0:T(8,128)(2,1)}, bf16[256,128]{1,0:T(8,128)(2,1)S(1)}, bf16[256,512]{1,0:T(8,128)(2,1)S(1)}, f32[256,128]{1,0:T(8,128)S(1)}, ...) custom-call(s32[6]{0:T(128)S(1)} %pad_add_fusion.1.s_ref, bf16[2,64,1024]{2,1,0:T(8,128)(2,1)S(1)} %copy-done.8, ...), custom_call_target="tpu_custom_call" | custom-call | bytes 6815768 | tf_op jit(solution)/shard_map/pallas_call | solution.py:23
  106.7 8.5 %collective-permute-start.22 = (bf16[256,512]{1,0:T(8,128)(2,1)}, bf16[256,512]{1,0:T(8,128)(2,1)S(1)}, u32[]{:S(2)}, u32[]{:S(2)}) collective-permute-start(bf16[256,512]{1,0:T(8,128)(2,1)} %get-tuple-element.99), channel_id=1, source_target_pairs={{0,16},{16,32},{32,48},{48,64},{64,80},{80,96},{96,112},{112,128},... | collective-permute-start | bytes 786440 | tf_op jit(solution)/shard_map/ppermute | solution.py:373
  117.2 2.3 %collective-permute-done.26.shipped = bf16[256,128]{1,0:T(8,128)(2,1)S(1)} collective-permute-done((bf16[256,128]{1,0:T(8,128)(2,1)S(1)}, bf16[256,128]{1,0:T(8,128)(2,1)S(1)}, u32[]{:S(2)}, u32[]{:S(2)}) %collective-permute-start.26) | collective-permute-done | bytes 65568 | tf_op jit(solution)/shard_map/ppermute | solution.py:373
  123.5 2.6 %shard_map.105 = (bf16[256,512]{1,0:T(8,128)(2,1)S(1)}, bf16[256,512]{1,0:T(8,128)(2,1)S(1)}) custom-call(s32[6]{0:T(128)S(1)} %pad_add_fusion.1.s_ref, bf16[512,1024]{1,0:T(8,128)(2,1)S(1)} %get-tuple-element.95.c_rows, bf16[512,1024]{1,0:T(8,128)(2,1)S(1)} %get-tuple-element.96.a_rows, bf16[272,512]{1,0:T(8,128)(2,1)} %get-tuple-element.97.panel0, ...), custom_call_target="tpu_custom_call" | custom-call | bytes 4259864 | tf_op jit(solution)/shard_map/pallas_call | solution.py:23
  126.3 2.6 %collective-permute-start.25 = (bf16[256,512]{1,0:T(8,128)(2,1)S(1)}, bf16[256,512]{1,0:T(8,128)(2,1)S(1)}, u32[]{:S(2)}, u32[]{:S(2)}) collective-permute-start(bf16[256,512]{1,0:T(8,128)(2,1)S(1)} %get-tuple-element.106.block0.refs_0_.refs_1_), channel_id=1, source_target_pairs={{0,3},{1,0},{2,1},{3,2},{4,7},{5,4},{6,5},{7,6},{8,11},{9,8},{10,9... | collective-permute-start | bytes 786440 | tf_op jit(solution)/shard_map/ppermute | solution.py:353
  129.5 5.4 %collective-permute-done.28.got2 = bf16[512,128]{1,0:T(8,128)(2,1)S(1)} collective-permute-done((bf16[512,128]{1,0:T(8,128)(2,1)S(1)}, bf16[512,128]{1,0:T(8,128)(2,1)S(1)}, u32[]{:S(2)}, u32[]{:S(2)}) %collective-permute-start.28) | collective-permute-done | bytes 131104 | tf_op jit(solution)/shard_map/ppermute | solution.py:358
  134.9 3.1 %collective-permute-done.29.got3 = bf16[512,128]{1,0:T(8,128)(2,1)S(1)} collective-permute-done((bf16[512,128]{1,0:T(8,128)(2,1)S(1)}, bf16[512,128]{1,0:T(8,128)(2,1)S(1)}, u32[]{:S(2)}, u32[]{:S(2)}) %collective-permute-start.29) | collective-permute-done | bytes 131104 | tf_op jit(solution)/shard_map/ppermute | solution.py:358
  138.0 2.9 %collective-permute-done.23.block1.refs_1_.refs_2_ = bf16[256,512]{1,0:T(8,128)(2,1)S(1)} collective-permute-done((bf16[256,512]{1,0:T(8,128)(2,1)S(1)}, bf16[256,512]{1,0:T(8,128)(2,1)S(1)}, u32[]{:S(2)}, u32[]{:S(2)}) %collective-permute-start.23) | collective-permute-done | bytes 262176 | tf_op jit(solution)/shard_map/ppermute | solution.py:353
  141.2 3.5 %collective-permute-start.30 = (bf16[256,512]{1,0:T(8,128)(2,1)S(1)}, bf16[256,512]{1,0:T(8,128)(2,1)S(1)}, u32[]{:S(2)}, u32[]{:S(2)}) collective-permute-start(bf16[256,512]{1,0:T(8,128)(2,1)S(1)} %get-tuple-element.110), channel_id=1, source_target_pairs={{0,16},{16,32},{32,48},{48,64},{64,80},{80,96},{96,112},{112,128},... | collective-permute-start | bytes 786440 | tf_op jit(solution)/shard_map/ppermute | solution.py:373
  149.0 3.2 %collective-permute-start.32 = (bf16[256,1024]{1,0:T(8,128)(2,1)S(1)}, bf16[256,1024]{1,0:T(8,128)(2,1)S(1)}, u32[]{:S(2)}, u32[]{:S(2)}) collective-permute-start(bf16[256,1024]{1,0:T(8,128)(2,1)S(1)} %shard_map.108.pair0), channel_id=1, source_target_pairs={{0,2},{1,3},{2,0},{3,1},{4,6},{5,7},{6,4},{7,5},{8,10},{9,11},{10,... | collective-permute-start | bytes 1572872 | tf_op jit(solution)/shard_map/ppermute | solution.py:353
  154.0 2.4 %collective-permute-done.36.got3 = bf16[512,128]{1,0:T(8,128)(2,1)S(1)} collective-permute-done((bf16[512,128]{1,0:T(8,128)(2,1)S(1)}, bf16[512,128]{1,0:T(8,128)(2,1)S(1)}, u32[]{:S(2)}, u32[]{:S(2)}) %collective-permute-start.36) | collective-permute-done | bytes 131104 | tf_op jit(solution)/shard_map/ppermute | solution.py:358
  160.0 3.0 %collective-permute-done.37.got1 = bf16[512,128]{1,0:T(8,128)(2,1)S(1)} collective-permute-done((bf16[512,128]{1,0:T(8,128)(2,1)S(1)}, bf16[512,128]{1,0:T(8,128)(2,1)S(1)}, u32[]{:S(2)}, u32[]{:S(2)}) %collective-permute-start.37) | collective-permute-done | bytes 131104 | tf_op jit(solution)/shard_map/ppermute | solution.py:358
  163.0 2.0 %collective-permute-done.38.got2 = bf16[512,128]{1,0:T(8,128)(2,1)S(1)} collective-permute-done((bf16[512,128]{1,0:T(8,128)(2,1)S(1)}, bf16[512,128]{1,0:T(8,128)(2,1)S(1)}, u32[]{:S(2)}, u32[]{:S(2)}) %collective-permute-start.38) | collective-permute-done | bytes 131104 | tf_op jit(solution)/shard_map/ppermute | solution.py:358
  165.0 3.3 %collective-permute-done.39.got3 = bf16[512,128]{1,0:T(8,128)(2,1)S(1)} collective-permute-done((bf16[512,128]{1,0:T(8,128)(2,1)S(1)}, bf16[512,128]{1,0:T(8,128)(2,1)S(1)}, u32[]{:S(2)}, u32[]{:S(2)}) %collective-permute-start.39) | collective-permute-done | bytes 131104 | tf_op jit(solution)/shard_map/ppermute | solution.py:358
  168.9 5.1 %collective-permute-start.40 = (bf16[512,128]{1,0:T(8,128)(2,1)S(1)}, bf16[512,128]{1,0:T(8,128)(2,1)S(1)}, u32[]{:S(2)}, u32[]{:S(2)}) collective-permute-start(bf16[512,128]{1,0:T(8,128)(2,1)S(1)} %shard_map.112.solved), channel_id=1, source_target_pairs={{0,16},{16,32},{32,48},{48,64},{64,80},{80,96},{96,112},{112,128},... | collective-permute-start | bytes 393224 | tf_op jit(solution)/shard_map/ppermute | solution.py:373
  176.0 5.6 %collective-permute-done.41.above = bf16[512,128]{1,0:T(8,128)(2,1)S(1)} collective-permute-done((bf16[512,128]{1,0:T(8,128)(2,1)S(1)}, bf16[512,128]{1,0:T(8,128)(2,1)S(1)}, u32[]{:S(2)}, u32[]{:S(2)}) %collective-permute-start.41) | collective-permute-done | bytes 131104 | tf_op jit(solution)/shard_map/ppermute | solution.py:373
  183.5 2.8 %collective-permute-start.43 = (f32[64,128]{1,0:T(8,128)S(1)}, f32[64,128]{1,0:T(8,128)S(1)}, u32[]{:S(2)}, u32[]{:S(2)}) collective-permute-start(f32[64,128]{1,0:T(8,128)S(1)} %get-tuple-element.127), channel_id=1, source_target_pairs={{0,2},{1,3},{2,0},{3,1},{4,6},{5,7},{6,4},{7,5},{8,10},{9,11},{10,... | collective-permute-start | bytes 98312 | tf_op jit(solution)/shard_map/ppermute | solution.py:353
  (121 shorter events, 55.2 us)
Async XLA Ops:
  7.2 88.7 %all-gather.5.cloned.1.call-start = ((), (), s32[]{:S(2)}) async-start(), calls=%async_computation | async-start | bytes 1310720 | tf_op jit(solution)/shard_map/all_gather | solution.py:367
  11.1 108.4 %all-gather.7.cloned.1.call-start = ((), (), s32[]{:S(2)}) async-start(), calls=%async_computation.1 | async-start | bytes 1310720 | tf_op jit(solution)/shard_map/all_gather | solution.py:367
  11.1 20.2 %collective-permute-start = (bf16[2,64,1024]{2,1,0:T(8,128)(2,1)S(1)}, bf16[2,64,1024]{2,1,0:T(8,128)(2,1)S(1)}, u32[]{:S(2)}, u32[]{:S(2)}) collective-permute-start(bf16[2,64,1024]{2,1,0:T(8,128)(2,1)S(1)} %get-tuple-element.68), channel_id=1, source_target_pairs={{16,0},{32,16},{48,32},{64,48},{80,64},{96,80},{112,96},{128,112},... | collective-permute-start | bytes 786440 | tf_op jit(solution)/shard_map/ppermute | solution.py:373
  13.7 17.6 %collective-permute-start.4 = (bf16[64,1664]{1,0:T(8,128)(2,1)S(1)}, bf16[64,1664]{1,0:T(8,128)(2,1)S(1)}, u32[]{:S(2)}, u32[]{:S(2)}) collective-permute-start(bf16[64,1664]{1,0:T(8,128)(2,1)S(1)} %get-tuple-element.74), channel_id=1, source_target_pairs={{0,1},{1,2},{2,3},{3,0},{4,5},{5,6},{6,7},{7,4},{8,9},{9,10},{10,1... | collective-permute-start | bytes 638984 | tf_op jit(solution)/shard_map/ppermute | solution.py:353
  15.0 16.3 %collective-permute-start.5 = (bf16[64,1664]{1,0:T(8,128)(2,1)S(1)}, bf16[64,1664]{1,0:T(8,128)(2,1)S(1)}, u32[]{:S(2)}, u32[]{:S(2)}) collective-permute-start(bf16[64,1664]{1,0:T(8,128)(2,1)S(1)} %get-tuple-element.75), channel_id=1, source_target_pairs={{0,2},{1,3},{2,0},{3,1},{4,6},{5,7},{6,4},{7,5},{8,10},{9,11},{10,... | collective-permute-start | bytes 638984 | tf_op jit(solution)/shard_map/ppermute | solution.py:353
  17.5 13.9 %collective-permute-start.6 = (bf16[64,1664]{1,0:T(8,128)(2,1)S(1)}, bf16[64,1664]{1,0:T(8,128)(2,1)S(1)}, u32[]{:S(2)}, u32[]{:S(2)}) collective-permute-start(bf16[64,1664]{1,0:T(8,128)(2,1)S(1)} %get-tuple-element.76), channel_id=1, source_target_pairs={{0,3},{1,0},{2,1},{3,2},{4,7},{5,4},{6,5},{7,6},{8,11},{9,8},{10,9... | collective-permute-start | bytes 638984 | tf_op jit(solution)/shard_map/ppermute | solution.py:353
  33.5 19.0 %collective-permute-start.10 = (bf16[256,1152]{1,0:T(8,128)(2,1)S(1)}, bf16[256,1152]{1,0:T(8,128)(2,1)S(1)}, u32[]{:S(2)}, u32[]{:S(2)}) collective-permute-start(bf16[256,1152]{1,0:T(8,128)(2,1)S(1)} %get-tuple-element.86.panel0.source), channel_id=1, source_target_pairs={{0,12},{1,13},{2,14},{3,15},{4,0},{5,1},{6,2},{7,3},{8,4},{9,5},{1... | collective-permute-start | bytes 1769480 | tf_op jit(solution)/shard_map/ppermute | solution.py:358
  36.6 10.3 %collective-permute-start.7 = (bf16[2,64,1024]{2,1,0:T(8,128)(2,1)S(1)}, bf16[2,64,1024]{2,1,0:T(8,128)(2,1)S(1)}, u32[]{:S(2)}, u32[]{:S(2)}) collective-permute-start(bf16[2,64,1024]{2,1,0:T(8,128)(2,1)S(1)} %get-tuple-element.77.g0), channel_id=1, source_target_pairs={{0,1},{1,2},{2,3},{3,0},{4,5},{5,6},{6,7},{7,4},{8,9},{9,10},{10,1... | collective-permute-start | bytes 786440 | tf_op jit(solution)/shard_map/ppermute | solution.py:353
  36.6 18.1 %collective-permute-start.11 = (bf16[256,1152]{1,0:T(8,128)(2,1)S(1)}, bf16[256,1152]{1,0:T(8,128)(2,1)S(1)}, u32[]{:S(2)}, u32[]{:S(2)}) collective-permute-start(bf16[256,1152]{1,0:T(8,128)(2,1)S(1)} %get-tuple-element.86.panel0.source), channel_id=1, source_target_pairs={{0,8},{1,9},{2,10},{3,11},{4,12},{5,13},{6,14},{7,15},{8,0},{9,1},... | collective-permute-start | bytes 1769480 | tf_op jit(solution)/shard_map/ppermute | solution.py:358
  36.6 28.8 %collective-permute-start.12 = (bf16[256,1152]{1,0:T(8,128)(2,1)S(1)}, bf16[256,1152]{1,0:T(8,128)(2,1)S(1)}, u32[]{:S(2)}, u32[]{:S(2)}) collective-permute-start(bf16[256,1152]{1,0:T(8,128)(2,1)S(1)} %get-tuple-element.86.panel0.source), channel_id=1, source_target_pairs={{0,4},{1,5},{2,6},{3,7},{4,8},{5,9},{6,10},{7,11},{8,12},{9,13},{1... | collective-permute-start | bytes 1769480 | tf_op jit(solution)/shard_map/ppermute | solution.py:358
  37.4 9.5 %collective-permute-start.8 = (bf16[2,64,1024]{2,1,0:T(8,128)(2,1)S(1)}, bf16[2,64,1024]{2,1,0:T(8,128)(2,1)S(1)}, u32[]{:S(2)}, u32[]{:S(2)}) collective-permute-start(bf16[2,64,1024]{2,1,0:T(8,128)(2,1)S(1)} %get-tuple-element.77.g0), channel_id=1, source_target_pairs={{0,2},{1,3},{2,0},{3,1},{4,6},{5,7},{6,4},{7,5},{8,10},{9,11},{10,... | collective-permute-start | bytes 786440 | tf_op jit(solution)/shard_map/ppermute | solution.py:353
  46.9 21.4 %collective-permute-start.13 = (bf16[2,64,1024]{2,1,0:T(8,128)(2,1)S(1)}, bf16[2,64,1024]{2,1,0:T(8,128)(2,1)S(1)}, u32[]{:S(2)}, u32[]{:S(2)}) collective-permute-start(bf16[2,64,1024]{2,1,0:T(8,128)(2,1)S(1)} %collective-permute-done.a0), channel_id=1, source_target_pairs={{0,1},{1,2},{2,3},{3,0},{4,5},{5,6},{6,7},{7,4},{8,9},{9,10},{10,1... | collective-permute-start | bytes 786440 | tf_op jit(solution)/shard_map/ppermute | solution.py:353
  52.4 16.6 %collective-permute-start.14 = (bf16[2,64,1024]{2,1,0:T(8,128)(2,1)S(1)}, bf16[2,64,1024]{2,1,0:T(8,128)(2,1)S(1)}, u32[]{:S(2)}, u32[]{:S(2)}) collective-permute-start(bf16[2,64,1024]{2,1,0:T(8,128)(2,1)S(1)} %collective-permute-done.a0), channel_id=1, source_target_pairs={{0,2},{1,3},{2,0},{3,1},{4,6},{5,7},{6,4},{7,5},{8,10},{9,11},{10,... | collective-permute-start | bytes 786440 | tf_op jit(solution)/shard_map/ppermute | solution.py:353
  52.5 22.5 %collective-permute-start.15 = (bf16[2,64,1024]{2,1,0:T(8,128)(2,1)S(1)}, bf16[2,64,1024]{2,1,0:T(8,128)(2,1)S(1)}, u32[]{:S(2)}, u32[]{:S(2)}) collective-permute-start(bf16[2,64,1024]{2,1,0:T(8,128)(2,1)S(1)} %collective-permute-done.a0), channel_id=1, source_target_pairs={{0,3},{1,0},{2,1},{3,2},{4,7},{5,4},{6,5},{7,6},{8,11},{9,8},{10,9... | collective-permute-start | bytes 786440 | tf_op jit(solution)/shard_map/ppermute | solution.py:353
  75.7 7.5 %collective-permute-start.17 = (bf16[256,640]{1,0:T(8,128)(2,1)S(1)}, bf16[256,640]{1,0:T(8,128)(2,1)S(1)}, u32[]{:S(2)}, u32[]{:S(2)}) collective-permute-start(bf16[256,640]{1,0:T(8,128)(2,1)S(1)} %get-tuple-element.94.panel0), channel_id=1, source_target_pairs={{0,8},{1,9},{2,10},{3,11},{4,12},{5,13},{6,14},{7,15},{8,0},{9,1},... | collective-permute-start | bytes 983048 | tf_op jit(solution)/shard_map/ppermute | solution.py:358
  75.7 19.4 %collective-permute-start.18 = (bf16[256,640]{1,0:T(8,128)(2,1)S(1)}, bf16[256,640]{1,0:T(8,128)(2,1)S(1)}, u32[]{:S(2)}, u32[]{:S(2)}) collective-permute-start(bf16[256,640]{1,0:T(8,128)(2,1)S(1)} %get-tuple-element.94.panel0), channel_id=1, source_target_pairs={{0,4},{1,5},{2,6},{3,7},{4,8},{5,9},{6,10},{7,11},{8,12},{9,13},{1... | collective-permute-start | bytes 983048 | tf_op jit(solution)/shard_map/ppermute | solution.py:358
  77.2 46.3 %collective-permute-start.19 = (bf16[272,512]{1,0:T(8,128)(2,1)}, bf16[272,512]{1,0:T(8,128)(2,1)}, u32[]{:S(2)}, u32[]{:S(2)}) collective-permute-start(bf16[272,512]{1,0:T(8,128)(2,1)} %get-tuple-element.97.panel0), channel_id=1, source_target_pairs={{0,12},{1,13},{2,14},{3,15},{4,0},{5,1},{6,2},{7,3},{8,4},{9,5},{1... | collective-permute-start | bytes 835592 | tf_op jit(solution)/shard_map/ppermute | solution.py:358
  79.6 43.9 %collective-permute-start.20 = (bf16[272,512]{1,0:T(8,128)(2,1)}, bf16[272,512]{1,0:T(8,128)(2,1)}, u32[]{:S(2)}, u32[]{:S(2)}) collective-permute-start(bf16[272,512]{1,0:T(8,128)(2,1)} %get-tuple-element.97.panel0), channel_id=1, source_target_pairs={{0,8},{1,9},{2,10},{3,11},{4,12},{5,13},{6,14},{7,15},{8,0},{9,1},... | collective-permute-start | bytes 835592 | tf_op jit(solution)/shard_map/ppermute | solution.py:358
  81.7 41.8 %collective-permute-start.21 = (bf16[272,512]{1,0:T(8,128)(2,1)}, bf16[272,512]{1,0:T(8,128)(2,1)}, u32[]{:S(2)}, u32[]{:S(2)}) collective-permute-start(bf16[272,512]{1,0:T(8,128)(2,1)} %get-tuple-element.97.panel0), channel_id=1, source_target_pairs={{0,4},{1,5},{2,6},{3,7},{4,8},{5,9},{6,10},{7,11},{8,12},{9,13},{1... | collective-permute-start | bytes 835592 | tf_op jit(solution)/shard_map/ppermute | solution.py:358
  106.7 16.8 %collective-permute-start.22 = (bf16[256,512]{1,0:T(8,128)(2,1)}, bf16[256,512]{1,0:T(8,128)(2,1)S(1)}, u32[]{:S(2)}, u32[]{:S(2)}) collective-permute-start(bf16[256,512]{1,0:T(8,128)(2,1)} %get-tuple-element.99), channel_id=1, source_target_pairs={{0,16},{16,32},{32,48},{48,64},{64,80},{80,96},{96,112},{112,128},... | collective-permute-start | bytes 786440 | tf_op jit(solution)/shard_map/ppermute | solution.py:373
  126.1 14.8 %collective-permute-start.23 = (bf16[256,512]{1,0:T(8,128)(2,1)S(1)}, bf16[256,512]{1,0:T(8,128)(2,1)S(1)}, u32[]{:S(2)}, u32[]{:S(2)}) collective-permute-start(bf16[256,512]{1,0:T(8,128)(2,1)S(1)} %get-tuple-element.106.block0.refs_0_.refs_1_), channel_id=1, source_target_pairs={{0,1},{1,2},{2,3},{3,0},{4,5},{5,6},{6,7},{7,4},{8,9},{9,10},{10,1... | collective-permute-start | bytes 786440 | tf_op jit(solution)/shard_map/ppermute | solution.py:353
  126.2 14.7 %collective-permute-start.24 = (bf16[256,512]{1,0:T(8,128)(2,1)S(1)}, bf16[256,512]{1,0:T(8,128)(2,1)S(1)}, u32[]{:S(2)}, u32[]{:S(2)}) collective-permute-start(bf16[256,512]{1,0:T(8,128)(2,1)S(1)} %get-tuple-element.106.block0.refs_0_.refs_1_), channel_id=1, source_target_pairs={{0,2},{1,3},{2,0},{3,1},{4,6},{5,7},{6,4},{7,5},{8,10},{9,11},{10,... | collective-permute-start | bytes 786440 | tf_op jit(solution)/shard_map/ppermute | solution.py:353
  126.3 14.9 %collective-permute-start.25 = (bf16[256,512]{1,0:T(8,128)(2,1)S(1)}, bf16[256,512]{1,0:T(8,128)(2,1)S(1)}, u32[]{:S(2)}, u32[]{:S(2)}) collective-permute-start(bf16[256,512]{1,0:T(8,128)(2,1)S(1)} %get-tuple-element.106.block0.refs_0_.refs_1_), channel_id=1, source_target_pairs={{0,3},{1,0},{2,1},{3,2},{4,7},{5,4},{6,5},{7,6},{8,11},{9,8},{10,9... | collective-permute-start | bytes 786440 | tf_op jit(solution)/shard_map/ppermute | solution.py:353
  128.9 9.1 %collective-permute-start.29 = (bf16[512,128]{1,0:T(8,128)(2,1)S(1)}, bf16[512,128]{1,0:T(8,128)(2,1)S(1)}, u32[]{:S(2)}, u32[]{:S(2)}) collective-permute-start(bf16[512,128]{1,0:T(8,128)(2,1)S(1)} %get-tuple-element.105), channel_id=1, source_target_pairs={{0,4},{1,5},{2,6},{3,7},{4,8},{5,9},{6,10},{7,11},{8,12},{9,13},{1... | collective-permute-start | bytes 393224 | tf_op jit(solution)/shard_map/ppermute | solution.py:358
  141.2 7.1 %collective-permute-start.30 = (bf16[256,512]{1,0:T(8,128)(2,1)S(1)}, bf16[256,512]{1,0:T(8,128)(2,1)S(1)}, u32[]{:S(2)}, u32[]{:S(2)}) collective-permute-start(bf16[256,512]{1,0:T(8,128)(2,1)S(1)} %get-tuple-element.110), channel_id=1, source_target_pairs={{0,16},{16,32},{32,48},{48,64},{64,80},{80,96},{96,112},{112,128},... | collective-permute-start | bytes 786440 | tf_op jit(solution)/shard_map/ppermute | solution.py:373
  146.6 7.4 %collective-permute-start.35 = (bf16[512,128]{1,0:T(8,128)(2,1)S(1)}, bf16[512,128]{1,0:T(8,128)(2,1)S(1)}, u32[]{:S(2)}, u32[]{:S(2)}) collective-permute-start(bf16[512,128]{1,0:T(8,128)(2,1)S(1)} %get-tuple-element.120), channel_id=1, source_target_pairs={{0,8},{1,9},{2,10},{3,11},{4,12},{5,13},{6,14},{7,15},{8,0},{9,1},... | collective-permute-start | bytes 393224 | tf_op jit(solution)/shard_map/ppermute | solution.py:358
  148.3 8.2 %collective-permute-start.36 = (bf16[512,128]{1,0:T(8,128)(2,1)S(1)}, bf16[512,128]{1,0:T(8,128)(2,1)S(1)}, u32[]{:S(2)}, u32[]{:S(2)}) collective-permute-start(bf16[512,128]{1,0:T(8,128)(2,1)S(1)} %get-tuple-element.120), channel_id=1, source_target_pairs={{0,4},{1,5},{2,6},{3,7},{4,8},{5,9},{6,10},{7,11},{8,12},{9,13},{1... | collective-permute-start | bytes 393224 | tf_op jit(solution)/shard_map/ppermute | solution.py:358
  148.9 32.7 %collective-permute-start.31 = (bf16[256,1024]{1,0:T(8,128)(2,1)S(1)}, bf16[256,1024]{1,0:T(8,128)(2,1)S(1)}, u32[]{:S(2)}, u32[]{:S(2)}) collective-permute-start(bf16[256,1024]{1,0:T(8,128)(2,1)S(1)} %shard_map.108.pair0), channel_id=1, source_target_pairs={{0,1},{1,2},{2,3},{3,0},{4,5},{5,6},{6,7},{7,4},{8,9},{9,10},{10,1... | collective-permute-start | bytes 1572872 | tf_op jit(solution)/shard_map/ppermute | solution.py:353
  149.0 32.6 %collective-permute-start.32 = (bf16[256,1024]{1,0:T(8,128)(2,1)S(1)}, bf16[256,1024]{1,0:T(8,128)(2,1)S(1)}, u32[]{:S(2)}, u32[]{:S(2)}) collective-permute-start(bf16[256,1024]{1,0:T(8,128)(2,1)S(1)} %shard_map.108.pair0), channel_id=1, source_target_pairs={{0,2},{1,3},{2,0},{3,1},{4,6},{5,7},{6,4},{7,5},{8,10},{9,11},{10,... | collective-permute-start | bytes 1572872 | tf_op jit(solution)/shard_map/ppermute | solution.py:353
  152.1 29.4 %collective-permute-start.33 = (bf16[256,1024]{1,0:T(8,128)(2,1)S(1)}, bf16[256,1024]{1,0:T(8,128)(2,1)S(1)}, u32[]{:S(2)}, u32[]{:S(2)}) collective-permute-start(bf16[256,1024]{1,0:T(8,128)(2,1)S(1)} %shard_map.108.pair0), channel_id=1, source_target_pairs={{0,3},{1,0},{2,1},{3,2},{4,7},{5,4},{6,5},{7,6},{8,11},{9,8},{10,9... | collective-permute-start | bytes 1572872 | tf_op jit(solution)/shard_map/ppermute | solution.py:353
  168.9 7.0 %collective-permute-start.40 = (bf16[512,128]{1,0:T(8,128)(2,1)S(1)}, bf16[512,128]{1,0:T(8,128)(2,1)S(1)}, u32[]{:S(2)}, u32[]{:S(2)}) collective-permute-start(bf16[512,128]{1,0:T(8,128)(2,1)S(1)} %shard_map.112.solved), channel_id=1, source_target_pairs={{0,16},{16,32},{32,48},{48,64},{64,80},{80,96},{96,112},{112,128},... | collective-permute-start | bytes 393224 | tf_op jit(solution)/shard_map/ppermute | solution.py:373
  174.0 7.5 %collective-permute-start.41 = (bf16[512,128]{1,0:T(8,128)(2,1)S(1)}, bf16[512,128]{1,0:T(8,128)(2,1)S(1)}, u32[]{:S(2)}, u32[]{:S(2)}) collective-permute-start(bf16[512,128]{1,0:T(8,128)(2,1)S(1)} %shard_map.112.solved), channel_id=1, source_target_pairs={{16,0},{32,16},{48,32},{64,48},{80,64},{96,80},{112,96},{128,112},... | collective-permute-start | bytes 393224 | tf_op jit(solution)/shard_map/ppermute | solution.py:373
  (35 other events, 139.9 us)
Sparse Core Ops, SparseCore 0:
  11.2 27.4 all-gather.4
  40.5 34.5 all-gather.6
where the time goes:
time: 198 us; the launch traced here: 197 us
  waiting for transfers between devices  80.7 us (41%)
  starting transfers between devices  63.9 us (32%)
  Pallas kernels  24.3 us (12%)
  between operations  14.3 us (7%)
  local copies, waits for them, and re-layouts  13.3 us (7%)
    ppermute x21, waiting for transfers between devices, moved_y(): return lax.ppermute(block, 'row', pairs)  51.4 us
    pallas_call x14, Pallas kernels, call(): pl.pallas_call(kernel, out_shape=tuple(out_shapes), in_specs=[SMEM] + [an...  24.3 us
    ppermute x6, starting transfers between devices, along_cuts(): return lax.ppermute(block, 'cuts', pairs)  23.5 us
    ppermute x18, waiting for transfers between devices, moved_x(): return lax.ppermute(block, 'row', pairs)  21.4 us
    ppermute x18, starting transfers between devices, moved_x(): return lax.ppermute(block, 'row', pairs)  20.5 us
    ppermute x21, starting transfers between devices, moved_y(): return lax.ppermute(block, 'row', pairs)  19.8 us
    unnamed x40, local copies, waits for them, and re-layouts  13.2 us
    ppermute x6, waiting for transfers between devices, along_cuts(): return lax.ppermute(block, 'cuts', pairs)  7.85 us
  transfers between devices with their start and end apart: 47, of which 21 were waited for; matrix products, arithmetic and copies ran while one was open for 0% of the time, Pallas kernels for 9%

commit v1 on v0

--- a/solution.py
+++ b/solution.py
@@ -19,7 +19,11 @@
     moved = sum(a.size * a.dtype.itemsize for a in args) + sum(
         s.size * s.dtype.itemsize for s in out_shapes
     )
-    anywhere = pl.BlockSpec(memory_space=pl.ANY)
+    anywhere = pl.BlockSpec(memory_space=pltpu.HBM)
+    args = [
+        pltpu.with_memory_space_constraint(a, pltpu.HBM) if 0 < index <= hbm else a
+        for index, a in enumerate(args)
+    ]
     return pl.pallas_call(
         kernel,
         out_shape=tuple(out_shapes),
@@ -216,17 +220,19 @@
 
 
 def diagonal_kernel(s_ref, c_rows, a_rows, panel0, panel1, panel2, panel3, diagonal, shipped,
-                    out, lower):
+                    out, lower_real, lower_imag):
     real, imag = wide_product(s_ref[0], c_rows, (panel0, panel1, panel2, panel3))
     real = diagonal[:, pl.ds(0, 256)].astype(F32) - real - shipped[:, pl.ds(0, 256)].astype(F32)
     imag = diagonal[:, pl.ds(256, 256)].astype(F32) - imag - shipped[:, pl.ds(256, 256)].astype(F32)
     put_pair(out, real, imag)
     real, imag = wide_product(s_ref[0], a_rows, (panel0, panel1, panel2, panel3))
-    put_pair(lower, -real, -imag)
-
-
-def pair_kernel(s_ref, lower, upper, out):
-    out[:, pl.ds(0, 512)] = lower[...]
+    lower_real[...] = (-real).astype(BF)
+    lower_imag[...] = (-imag).astype(BF)
+
+
+def pair_kernel(s_ref, lower_real, lower_imag, upper, out):
+    out[:, pl.ds(0, 256)] = lower_real[...]
+    out[:, pl.ds(256, 256)] = lower_imag[...]
     out[:, pl.ds(512, 512)] = upper[...]
 
 
@@ -390,7 +396,7 @@
         + [shape((2, 64, 1024))],
         0,
         scalars, diagonal_blocks, diagonal_inverses, lower_blocks, upper_blocks, injection,
-        hbm=5, mib=52,
+        hbm=5,
         scratch=[pltpu.VMEM((2, 64, 1024), BF)] * 3
         + [pltpu.VMEM((2, 2, 64, 128), BF)]
         + [pltpu.VMEM((2, 64, 1024), BF)] * 3
@@ -414,8 +420,9 @@
         odd_kernel, [shape((256, 640)), shape((272, 512))], wide_flops,
         scalars, *g_blocks, *panels, scratch=[pltpu.VMEM((512, 1024), BF)],
     )
-    first, *a_blocks = after((first, *a_blocks))
+    first, c_gathered = after((first, c_gathered))
     firsts = gathered_y(first)
+    second, g_columns, *a_blocks = after((second, g_columns, *a_blocks))
     seconds = gathered_y(second)
     ship, ship_source, upper_new, source_part, a_rows, c_rows = call(
         even_kernel,
@@ -427,8 +434,8 @@
     )
     shipped = along_cuts(ship, 1)
     shipped_source = along_cuts(ship_source, 1)
-    diagonal_new, ship_lower = call(
-        diagonal_kernel, [shape((256, 512))] * 2, 2 * wide_flops,
+    diagonal_new, *ship_lower = call(
+        diagonal_kernel, [shape((256, 512))] + [shape((256, 256))] * 2, 2 * wide_flops,
         scalars, c_rows, a_rows, *seconds, diagonal, shipped,
     )
     diagonals = [diagonal_new] + [moved_x(diagonal_new, by) for by in turns]
@@ -440,10 +447,8 @@
         scalars, g_columns, source_part, shipped_source, scratch=[whole],
     )
     got = gathered_y(send)[1:]
-    ship_lower, *both = after((ship_lower, *diagonals, *got))
-    diagonals, got = both[:4], both[4:]
-    lower_new = along_cuts(ship_lower, 1)
-    (pair,) = call(pair_kernel, [shape((256, 1024))], 0, scalars, lower_new, upper_new)
+    lower_new = [along_cuts(half, 1) for half in ship_lower]
+    (pair,) = call(pair_kernel, [shape((256, 1024))], 0, scalars, *lower_new, upper_new)
     pairs = [pair] + [moved_x(pair, by) for by in turns]
     solved = ()
     for turn in range(REFINE):

time: 198 us -> 178 us (0.90)
  waiting for transfers between devices: 80.7 us -> 69 us
  local copies, waits for them, and re-layouts: 13.3 us -> 1.95 us
  starting transfers between devices: 63.9 us -> 68.8 us
  Pallas kernels: 24.3 us -> 22.2 us
    ppermute x21, waiting for transfers between devices: 51.4 us -> 38.8 us  [moved_y(): return lax.ppermute(block, 'row', pairs)]
    unnamed x40 -> x6, local copies, waits for them, and re-layouts: 13.2 us -> 1.88 us
    ppermute x6 -> x7, starting transfers between devices: 23.5 us -> 28.3 us  [along_cuts(): return lax.ppermute(block, 'cuts', pairs)]
    pallas_call x14, Pallas kernels: 24.3 us -> 22.2 us  [call(): pl.pallas_call(kernel, out_shape=tuple(out_shapes), in_specs=[SMEM] + [an...]
    ppermute x6 -> x7, waiting for transfers between devices: 7.85 us -> 7.06 us  [along_cuts(): return lax.ppermute(block, 'cuts', pairs)]
  transfers between devices with their start and end apart: 47 -> 48, of which waited for: 21 -> 18; matrix products, arithmetic and copies ran while one was open for 0% -> 0% of each run, Pallas kernels for 9% -> 9%
where the time goes in v1:
time: 178 us; the launch traced here: 176 us
  waiting for transfers between devices  69 us (39%)
  starting transfers between devices  68.8 us (39%)
  Pallas kernels  22.2 us (12%)
  between operations  14.3 us (8%)
  local copies, waits for them, and re-layouts  1.95 us (1%)
    ppermute x21, waiting for transfers between devices, moved_y(): return lax.ppermute(block, 'row', pairs)  38.8 us
    ppermute x7, starting transfers between devices, along_cuts(): return lax.ppermute(block, 'cuts', pairs)  28.3 us
    ppermute x18, waiting for transfers between devices, moved_x(): return lax.ppermute(block, 'row', pairs)  23.1 us
    pallas_call x14, Pallas kernels, call(): pl.pallas_call(kernel, out_shape=tuple(out_shapes), in_specs=[SMEM] + [an...  22.2 us
    ppermute x21, starting transfers between devices, moved_y(): return lax.ppermute(block, 'row', pairs)  20.7 us
    ppermute x18, starting transfers between devices, moved_x(): return lax.ppermute(block, 'row', pairs)  19.7 us
    ppermute x7, waiting for transfers between devices, along_cuts(): return lax.ppermute(block, 'cuts', pairs)  7.06 us
  transfers between devices with their start and end apart: 48, of which 18 were waited for; matrix products, arithmetic and copies ran while one was open for 0% of the time, Pallas kernels for 9%

profile of v1, /device:TPU:97, one launch (start us, length us, event | category | flops | bytes accessed | tf_op | source)
XLA Modules:
  0.0 176.4 jit_solution(6809971065166872589)
XLA Ops:
  8.1 2.9 %shard_map.101 = (bf16[64,1664]{1,0:T(8,128)(2,1)S(1)}, bf16[64,1664]{1,0:T(8,128)(2,1)S(1)}, bf16[64,1664]{1,0:T(8,128)(2,1)S(1)}, bf16[64,1664]{1,0:T(8,128)(2...) custom-call(s32[6]{0:T(128)S(1)} %pad_add_fusion.1.s_ref, ...), custom_call_target="tpu_custom_call" | custom-call | bytes 4063256 | tf_op jit(solution)/shard_map/pallas_call | solution.py:27
  11.1 2.6 %collective-permute-start = (bf16[2,64,1024]{2,1,0:T(8,128)(2,1)S(1)}, bf16[2,64,1024]{2,1,0:T(8,128)(2,1)S(1)}, u32[]{:S(2)}, u32[]{:S(2)}) collective-permute-start(bf16[2,64,1024]{2,1,0:T(8,128)(2,1)S(1)} %get-tuple-element.64), channel_id=1, source_target_pairs={{16,0},{32,16},{48,32},{64,48},{80,64},{96,80},{112,96},{128,112},... | collective-permute-start | bytes 786440 | tf_op jit(solution)/shard_map/ppermute | solution.py:379
  15.0 2.5 %collective-permute-start.5 = (bf16[64,1664]{1,0:T(8,128)(2,1)S(1)}, bf16[64,1664]{1,0:T(8,128)(2,1)S(1)}, u32[]{:S(2)}, u32[]{:S(2)}) collective-permute-start(bf16[64,1664]{1,0:T(8,128)(2,1)S(1)} %get-tuple-element.71), channel_id=1, source_target_pairs={{0,2},{1,3},{2,0},{3,1},{4,6},{5,7},{6,4},{7,5},{8,10},{9,11},{10,... | collective-permute-start | bytes 638984 | tf_op jit(solution)/shard_map/ppermute | solution.py:359
  19.9 3.1 %collective-permute-done.1.g1 = bf16[2,64,256]{2,1,0:T(8,128)(2,1)S(1)} collective-permute-done((bf16[2,64,256]{2,1,0:T(8,128)(2,1)S(1)}, bf16[2,64,256]{2,1,0:T(8,128)(2,1)S(1)}, u32[]{:S(2)}, u32[]{:S(2)}) %collective-permute-start.1) | collective-permute-done | bytes 65568 | tf_op jit(solution)/shard_map/ppermute | solution.py:364
  23.0 1.9 %collective-permute-start.2 = (bf16[2,64,256]{2,1,0:T(8,128)(2,1)S(1)}, bf16[2,64,256]{2,1,0:T(8,128)(2,1)S(1)}, u32[]{:S(2)}, u32[]{:S(2)}) collective-permute-start(bf16[2,64,256]{2,1,0:T(8,128)(2,1)S(1)} %get-tuple-element.66), channel_id=1, source_target_pairs={{0,8},{1,9},{2,10},{3,11},{4,12},{5,13},{6,14},{7,15},{8,0},{9,1},... | collective-permute-start | bytes 196616 | tf_op jit(solution)/shard_map/ppermute | solution.py:364
  24.9 2.9 %collective-permute-done.2.g2 = bf16[2,64,256]{2,1,0:T(8,128)(2,1)S(1)} collective-permute-done((bf16[2,64,256]{2,1,0:T(8,128)(2,1)S(1)}, bf16[2,64,256]{2,1,0:T(8,128)(2,1)S(1)}, u32[]{:S(2)}, u32[]{:S(2)}) %collective-permute-start.2) | collective-permute-done | bytes 65568 | tf_op jit(solution)/shard_map/ppermute | solution.py:364
  27.8 1.8 %collective-permute-start.3 = (bf16[2,64,256]{2,1,0:T(8,128)(2,1)S(1)}, bf16[2,64,256]{2,1,0:T(8,128)(2,1)S(1)}, u32[]{:S(2)}, u32[]{:S(2)}) collective-permute-start(bf16[2,64,256]{2,1,0:T(8,128)(2,1)S(1)} %get-tuple-element.67), channel_id=1, source_target_pairs={{0,12},{1,13},{2,14},{3,15},{4,0},{5,1},{6,2},{7,3},{8,4},{9,5},{1... | collective-permute-start | bytes 196616 | tf_op jit(solution)/shard_map/ppermute | solution.py:364
  32.7 3.1 %collective-permute-start.10 = (bf16[256,1152]{1,0:T(8,128)(2,1)S(1)}, bf16[256,1152]{1,0:T(8,128)(2,1)S(1)}, u32[]{:S(2)}, u32[]{:S(2)}) collective-permute-start(bf16[256,1152]{1,0:T(8,128)(2,1)S(1)} %get-tuple-element.82.panel0.source), channel_id=1, source_target_pairs={{0,12},{1,13},{2,14},{3,15},{4,0},{5,1},{6,2},{7,3},{8,4},{9,5},{1... | collective-permute-start | bytes 1769480 | tf_op jit(solution)/shard_map/ppermute | solution.py:364
  37.4 9.4 %collective-permute-done.7.g1 = bf16[2,64,1024]{2,1,0:T(8,128)(2,1)S(1)} collective-permute-done((bf16[2,64,1024]{2,1,0:T(8,128)(2,1)S(1)}, bf16[2,64,1024]{2,1,0:T(8,128)(2,1)S(1)}, u32[]{:S(2)}, u32[]{:S(2)}) %collective-permute-start.7) | collective-permute-done | bytes 262176 | tf_op jit(solution)/shard_map/ppermute | solution.py:359
  48.3 4.0 %collective-permute-done.9.g3 = bf16[2,64,1024]{2,1,0:T(8,128)(2,1)S(1)} collective-permute-done((bf16[2,64,1024]{2,1,0:T(8,128)(2,1)S(1)}, bf16[2,64,1024]{2,1,0:T(8,128)(2,1)S(1)}, u32[]{:S(2)}, u32[]{:S(2)}) %collective-permute-start.9) | collective-permute-done | bytes 262176 | tf_op jit(solution)/shard_map/ppermute | solution.py:359
  52.3 12.4 %collective-permute-done.12.panel3 = bf16[256,1152]{1,0:T(8,128)(2,1)S(1)} collective-permute-done((bf16[256,1152]{1,0:T(8,128)(2,1)S(1)}, bf16[256,1152]{1,0:T(8,128)(2,1)S(1)}, u32[]{:S(2)}, u32[]{:S(2)}) %collective-permute-start.12) | collective-permute-done | bytes 589856 | tf_op jit(solution)/shard_map/ppermute | solution.py:364
  64.7 2.2 %shard_map.103 = (bf16[256,640]{1,0:T(8,128)(2,1)S(1)}, bf16[272,512]{1,0:T(8,128)(2,1)S(1)}) custom-call(s32[6]{0:T(128)S(1)} %pad_add_fusion.1.s_ref, bf16[2,64,1024]{2,1,0:T(8,128)(2,1)S(1)} %get-tuple-element.73.g0, bf16[2,64,1024]{2,1,0:T(8,128)(2,1)S(1)} %collective-permute-done.7.g1, bf16[2,64,1024]{2,1,0:T(8,128)(2,1)S(1)} %collective-permute-done.8.g2, ...), custom_call_target="tpu_custom_call" | custom-call | bytes 4014104 | tf_op jit(solution)/shard_map/pallas_call | solution.py:27
  68.7 1.9 %collective-permute-start.15 = (bf16[2,64,1024]{2,1,0:T(8,128)(2,1)S(1)}, bf16[2,64,1024]{2,1,0:T(8,128)(2,1)S(1)}, u32[]{:S(2)}, u32[]{:S(2)}) collective-permute-start(bf16[2,64,1024]{2,1,0:T(8,128)(2,1)S(1)} %collective-permute-done.a0), channel_id=1, source_target_pairs={{0,3},{1,0},{2,1},{3,2},{4,7},{5,4},{6,5},{7,6},{8,11},{9,8},{10,9... | collective-permute-start | bytes 786440 | tf_op jit(solution)/shard_map/ppermute | solution.py:359
  70.6 6.1 %collective-permute-done.14.a2 = bf16[2,64,1024]{2,1,0:T(8,128)(2,1)S(1)} collective-permute-done((bf16[2,64,1024]{2,1,0:T(8,128)(2,1)S(1)}, bf16[2,64,1024]{2,1,0:T(8,128)(2,1)S(1)}, u32[]{:S(2)}, u32[]{:S(2)}) %collective-permute-start.14) | collective-permute-done | bytes 262176 | tf_op jit(solution)/shard_map/ppermute | solution.py:359
  76.8 3.5 %collective-permute-done.15.a3 = bf16[2,64,1024]{2,1,0:T(8,128)(2,1)S(1)} collective-permute-done((bf16[2,64,1024]{2,1,0:T(8,128)(2,1)S(1)}, bf16[2,64,1024]{2,1,0:T(8,128)(2,1)S(1)}, u32[]{:S(2)}, u32[]{:S(2)}) %collective-permute-start.15) | collective-permute-done | bytes 262176 | tf_op jit(solution)/shard_map/ppermute | solution.py:359
  80.2 2.2 %collective-permute-start.19 = (bf16[272,512]{1,0:T(8,128)(2,1)S(1)}, bf16[272,512]{1,0:T(8,128)(2,1)S(1)}, u32[]{:S(2)}, u32[]{:S(2)}) collective-permute-start(bf16[272,512]{1,0:T(8,128)(2,1)S(1)} %get-tuple-element.96.panel0), channel_id=1, source_target_pairs={{0,12},{1,13},{2,14},{3,15},{4,0},{5,1},{6,2},{7,3},{8,4},{9,5},{1... | collective-permute-start | bytes 835592 | tf_op jit(solution)/shard_map/ppermute | solution.py:364
  86.7 2.4 %shard_map.104 = (bf16[256,512]{1,0:T(8,128)(2,1)S(1)}, bf16[256,128]{1,0:T(8,128)(2,1)S(1)}, bf16[256,512]{1,0:T(8,128)(2,1)S(1)}, f32[256,128]{1,0:T(8,128)S(1...) custom-call(s32[6]{0:T(128)S(1)} %pad_add_fusion.1.s_ref, ...), custom_call_target="tpu_custom_call" | custom-call | bytes 6815768 | tf_op jit(solution)/shard_map/pallas_call | solution.py:27
  89.1 6.3 %collective-permute-start.22 = (bf16[256,512]{1,0:T(8,128)(2,1)S(1)}, bf16[256,512]{1,0:T(8,128)(2,1)S(1)}, u32[]{:S(2)}, u32[]{:S(2)}) collective-permute-start(bf16[256,512]{1,0:T(8,128)(2,1)S(1)} %get-tuple-element.98), channel_id=1, source_target_pairs={{0,16},{16,32},{32,48},{48,64},{64,80},{80,96},{96,112},{112,128},... | collective-permute-start | bytes 786440 | tf_op jit(solution)/shard_map/ppermute | solution.py:379
  95.5 1.9 %collective-permute-start.31 = (bf16[256,128]{1,0:T(8,128)(2,1)S(1)}, bf16[256,128]{1,0:T(8,128)(2,1)S(1)}, u32[]{:S(2)}, u32[]{:S(2)}) collective-permute-start(bf16[256,128]{1,0:T(8,128)(2,1)S(1)} %get-tuple-element.107), channel_id=1, source_target_pairs={{0,16},{16,32},{32,48},{48,64},{64,80},{80,96},{96,112},{112,128},... | collective-permute-start | bytes 196616 | tf_op jit(solution)/shard_map/ppermute | solution.py:379
  97.4 2.1 %collective-permute-done.31.shipped = bf16[256,128]{1,0:T(8,128)(2,1)S(1)} collective-permute-done((bf16[256,128]{1,0:T(8,128)(2,1)S(1)}, bf16[256,128]{1,0:T(8,128)(2,1)S(1)}, u32[]{:S(2)}, u32[]{:S(2)}) %collective-permute-start.31) | collective-permute-done | bytes 65568 | tf_op jit(solution)/shard_map/ppermute | solution.py:379
  104.1 2.3 %collective-permute-start.23 = (bf16[256,512]{1,0:T(8,128)(2,1)S(1)}, bf16[256,512]{1,0:T(8,128)(2,1)S(1)}, u32[]{:S(2)}, u32[]{:S(2)}) collective-permute-start(bf16[256,512]{1,0:T(8,128)(2,1)S(1)} %get-tuple-element.99.block0.refs_0_.refs_1_), channel_id=1, source_target_pairs={{0,1},{1,2},{2,3},{3,0},{4,5},{5,6},{6,7},{7,4},{8,9},{9,10},{10,1... | collective-permute-start | bytes 786440 | tf_op jit(solution)/shard_map/ppermute | solution.py:359
  109.9 4.9 %collective-permute-done.33.got2 = bf16[512,128]{1,0:T(8,128)(2,1)S(1)} collective-permute-done((bf16[512,128]{1,0:T(8,128)(2,1)S(1)}, bf16[512,128]{1,0:T(8,128)(2,1)S(1)}, u32[]{:S(2)}, u32[]{:S(2)}) %collective-permute-start.33) | collective-permute-done | bytes 131104 | tf_op jit(solution)/shard_map/ppermute | solution.py:364
  114.8 7.6 %collective-permute-start.26 = (bf16[256,256]{1,0:T(8,128)(2,1)S(1)}, bf16[256,256]{1,0:T(8,128)(2,1)S(1)}, u32[]{:S(2)}, u32[]{:S(2)}) collective-permute-start(bf16[256,256]{1,0:T(8,128)(2,1)S(1)} %get-tuple-element.100), channel_id=1, source_target_pairs={{0,16},{16,32},{32,48},{48,64},{64,80},{80,96},{96,112},{112,128},... | collective-permute-start | bytes 393224 | tf_op jit(solution)/shard_map/ppermute | solution.py:379
  122.4 2.1 %collective-permute-start.27 = (bf16[256,256]{1,0:T(8,128)(2,1)S(1)}, bf16[256,256]{1,0:T(8,128)(2,1)S(1)}, u32[]{:S(2)}, u32[]{:S(2)}) collective-permute-start(bf16[256,256]{1,0:T(8,128)(2,1)S(1)} %get-tuple-element.101), channel_id=1, source_target_pairs={{0,16},{16,32},{32,48},{48,64},{64,80},{80,96},{96,112},{112,128},... | collective-permute-start | bytes 393224 | tf_op jit(solution)/shard_map/ppermute | solution.py:379
  124.6 1.8 %shard_map.110 = (bf16[512,128]{1,0:T(8,128)(2,1)S(1)}, f32[512,128]{1,0:T(8,128)S(1)}, bf16[512,128]{1,0:T(8,128)(2,1)S(1)}) custom-call(s32[6]{0:T(128)S(1)} %pad_add_fusion.1.s_ref, f32[512,128]{1,0:T(8,128)S(1)} %get-tuple-element.109.own, bf16[512,128]{1,0:T(8,128)(2,1)S(1)} %collective-permute-done.32.got1, ...), custom_call_target="tpu_custom_call" | custom-call | bytes 3342360 | tf_op jit(solution)/shard_map/pallas_call | solution.py:27
  132.6 3.3 %collective-permute-done.37.got3 = bf16[512,128]{1,0:T(8,128)(2,1)S(1)} collective-permute-done((bf16[512,128]{1,0:T(8,128)(2,1)S(1)}, bf16[512,128]{1,0:T(8,128)(2,1)S(1)}, u32[]{:S(2)}, u32[]{:S(2)}) %collective-permute-start.37) | collective-permute-done | bytes 131104 | tf_op jit(solution)/shard_map/ppermute | solution.py:364
  135.9 1.8 %shard_map.111 = (bf16[512,128]{1,0:T(8,128)(2,1)S(1)}, f32[512,128]{1,0:T(8,128)S(1)}, bf16[512,128]{1,0:T(8,128)(2,1)S(1)}) custom-call(s32[6]{0:T(128)S(1)} %pad_add_fusion.1.s_ref, f32[512,128]{1,0:T(8,128)S(1)} %get-tuple-element.111.own, bf16[512,128]{1,0:T(8,128)(2,1)S(1)} %collective-permute-done.35.got1, ...), custom_call_target="tpu_custom_call" | custom-call | bytes 3473432 | tf_op jit(solution)/shard_map/pallas_call | solution.py:27
  139.7 2.3 %collective-permute-done.38.got1 = bf16[512,128]{1,0:T(8,128)(2,1)S(1)} collective-permute-done((bf16[512,128]{1,0:T(8,128)(2,1)S(1)}, bf16[512,128]{1,0:T(8,128)(2,1)S(1)}, u32[]{:S(2)}, u32[]{:S(2)}) %collective-permute-start.38) | collective-permute-done | bytes 131104 | tf_op jit(solution)/shard_map/ppermute | solution.py:364
  143.4 3.9 %collective-permute-done.40.got3 = bf16[512,128]{1,0:T(8,128)(2,1)S(1)} collective-permute-done((bf16[512,128]{1,0:T(8,128)(2,1)S(1)}, bf16[512,128]{1,0:T(8,128)(2,1)S(1)}, u32[]{:S(2)}, u32[]{:S(2)}) %collective-permute-start.40) | collective-permute-done | bytes 131104 | tf_op jit(solution)/shard_map/ppermute | solution.py:364
  148.0 5.2 %collective-permute-start.41 = (bf16[512,128]{1,0:T(8,128)(2,1)S(1)}, bf16[512,128]{1,0:T(8,128)(2,1)S(1)}, u32[]{:S(2)}, u32[]{:S(2)}) collective-permute-start(bf16[512,128]{1,0:T(8,128)(2,1)S(1)} %shard_map.112.solved), channel_id=1, source_target_pairs={{0,16},{16,32},{32,48},{48,64},{64,80},{80,96},{96,112},{112,128},... | collective-permute-start | bytes 393224 | tf_op jit(solution)/shard_map/ppermute | solution.py:379
  153.2 2.5 %collective-permute-start.42 = (bf16[512,128]{1,0:T(8,128)(2,1)S(1)}, bf16[512,128]{1,0:T(8,128)(2,1)S(1)}, u32[]{:S(2)}, u32[]{:S(2)}) collective-permute-start(bf16[512,128]{1,0:T(8,128)(2,1)S(1)} %shard_map.112.solved), channel_id=1, source_target_pairs={{16,0},{32,16},{48,32},{64,48},{80,64},{96,80},{112,96},{128,112},... | collective-permute-start | bytes 393224 | tf_op jit(solution)/shard_map/ppermute | solution.py:379
  155.7 5.0 %collective-permute-done.42.above = bf16[512,128]{1,0:T(8,128)(2,1)S(1)} collective-permute-done((bf16[512,128]{1,0:T(8,128)(2,1)S(1)}, bf16[512,128]{1,0:T(8,128)(2,1)S(1)}, u32[]{:S(2)}, u32[]{:S(2)}) %collective-permute-start.42) | collective-permute-done | bytes 131104 | tf_op jit(solution)/shard_map/ppermute | solution.py:379
  (89 shorter events, 44.0 us)
Async XLA Ops:
  7.2 59.8 %all-gather.7.cloned.1.call-start = ((), (), s32[]{:S(2)}) async-start(), calls=%async_computation.1 | async-start | bytes 1310720 | tf_op jit(solution)/shard_map/all_gather | solution.py:373
  11.1 69.2 %all-gather.5.cloned.1.call-start = ((), (), s32[]{:S(2)}) async-start(), calls=%async_computation | async-start | bytes 1310720 | tf_op jit(solution)/shard_map/all_gather | solution.py:373
  11.1 20.2 %collective-permute-start = (bf16[2,64,1024]{2,1,0:T(8,128)(2,1)S(1)}, bf16[2,64,1024]{2,1,0:T(8,128)(2,1)S(1)}, u32[]{:S(2)}, u32[]{:S(2)}) collective-permute-start(bf16[2,64,1024]{2,1,0:T(8,128)(2,1)S(1)} %get-tuple-element.64), channel_id=1, source_target_pairs={{16,0},{32,16},{48,32},{64,48},{80,64},{96,80},{112,96},{128,112},... | collective-permute-start | bytes 786440 | tf_op jit(solution)/shard_map/ppermute | solution.py:379
  13.7 17.6 %collective-permute-start.4 = (bf16[64,1664]{1,0:T(8,128)(2,1)S(1)}, bf16[64,1664]{1,0:T(8,128)(2,1)S(1)}, u32[]{:S(2)}, u32[]{:S(2)}) collective-permute-start(bf16[64,1664]{1,0:T(8,128)(2,1)S(1)} %get-tuple-element.70), channel_id=1, source_target_pairs={{0,1},{1,2},{2,3},{3,0},{4,5},{5,6},{6,7},{7,4},{8,9},{9,10},{10,1... | collective-permute-start | bytes 638984 | tf_op jit(solution)/shard_map/ppermute | solution.py:359
  15.0 16.3 %collective-permute-start.5 = (bf16[64,1664]{1,0:T(8,128)(2,1)S(1)}, bf16[64,1664]{1,0:T(8,128)(2,1)S(1)}, u32[]{:S(2)}, u32[]{:S(2)}) collective-permute-start(bf16[64,1664]{1,0:T(8,128)(2,1)S(1)} %get-tuple-element.71), channel_id=1, source_target_pairs={{0,2},{1,3},{2,0},{3,1},{4,6},{5,7},{6,4},{7,5},{8,10},{9,11},{10,... | collective-permute-start | bytes 638984 | tf_op jit(solution)/shard_map/ppermute | solution.py:359
  17.5 13.9 %collective-permute-start.6 = (bf16[64,1664]{1,0:T(8,128)(2,1)S(1)}, bf16[64,1664]{1,0:T(8,128)(2,1)S(1)}, u32[]{:S(2)}, u32[]{:S(2)}) collective-permute-start(bf16[64,1664]{1,0:T(8,128)(2,1)S(1)} %get-tuple-element.72), channel_id=1, source_target_pairs={{0,3},{1,0},{2,1},{3,2},{4,7},{5,4},{6,5},{7,6},{8,11},{9,8},{10,9... | collective-permute-start | bytes 638984 | tf_op jit(solution)/shard_map/ppermute | solution.py:359
  32.7 19.6 %collective-permute-start.10 = (bf16[256,1152]{1,0:T(8,128)(2,1)S(1)}, bf16[256,1152]{1,0:T(8,128)(2,1)S(1)}, u32[]{:S(2)}, u32[]{:S(2)}) collective-permute-start(bf16[256,1152]{1,0:T(8,128)(2,1)S(1)} %get-tuple-element.82.panel0.source), channel_id=1, source_target_pairs={{0,12},{1,13},{2,14},{3,15},{4,0},{5,1},{6,2},{7,3},{8,4},{9,5},{1... | collective-permute-start | bytes 1769480 | tf_op jit(solution)/shard_map/ppermute | solution.py:364
  35.9 16.5 %collective-permute-start.11 = (bf16[256,1152]{1,0:T(8,128)(2,1)S(1)}, bf16[256,1152]{1,0:T(8,128)(2,1)S(1)}, u32[]{:S(2)}, u32[]{:S(2)}) collective-permute-start(bf16[256,1152]{1,0:T(8,128)(2,1)S(1)} %get-tuple-element.82.panel0.source), channel_id=1, source_target_pairs={{0,8},{1,9},{2,10},{3,11},{4,12},{5,13},{6,14},{7,15},{8,0},{9,1},... | collective-permute-start | bytes 1769480 | tf_op jit(solution)/shard_map/ppermute | solution.py:364
  35.9 28.8 %collective-permute-start.12 = (bf16[256,1152]{1,0:T(8,128)(2,1)S(1)}, bf16[256,1152]{1,0:T(8,128)(2,1)S(1)}, u32[]{:S(2)}, u32[]{:S(2)}) collective-permute-start(bf16[256,1152]{1,0:T(8,128)(2,1)S(1)} %get-tuple-element.82.panel0.source), channel_id=1, source_target_pairs={{0,4},{1,5},{2,6},{3,7},{4,8},{5,9},{6,10},{7,11},{8,12},{9,13},{1... | collective-permute-start | bytes 1769480 | tf_op jit(solution)/shard_map/ppermute | solution.py:364
  36.5 10.3 %collective-permute-start.7 = (bf16[2,64,1024]{2,1,0:T(8,128)(2,1)S(1)}, bf16[2,64,1024]{2,1,0:T(8,128)(2,1)S(1)}, u32[]{:S(2)}, u32[]{:S(2)}) collective-permute-start(bf16[2,64,1024]{2,1,0:T(8,128)(2,1)S(1)} %get-tuple-element.73.g0), channel_id=1, source_target_pairs={{0,1},{1,2},{2,3},{3,0},{4,5},{5,6},{6,7},{7,4},{8,9},{9,10},{10,1... | collective-permute-start | bytes 786440 | tf_op jit(solution)/shard_map/ppermute | solution.py:359
  36.5 10.3 %collective-permute-start.8 = (bf16[2,64,1024]{2,1,0:T(8,128)(2,1)S(1)}, bf16[2,64,1024]{2,1,0:T(8,128)(2,1)S(1)}, u32[]{:S(2)}, u32[]{:S(2)}) collective-permute-start(bf16[2,64,1024]{2,1,0:T(8,128)(2,1)S(1)} %get-tuple-element.73.g0), channel_id=1, source_target_pairs={{0,2},{1,3},{2,0},{3,1},{4,6},{5,7},{6,4},{7,5},{8,10},{9,11},{10,... | collective-permute-start | bytes 786440 | tf_op jit(solution)/shard_map/ppermute | solution.py:359
  46.8 21.9 %collective-permute-start.13 = (bf16[2,64,1024]{2,1,0:T(8,128)(2,1)S(1)}, bf16[2,64,1024]{2,1,0:T(8,128)(2,1)S(1)}, u32[]{:S(2)}, u32[]{:S(2)}) collective-permute-start(bf16[2,64,1024]{2,1,0:T(8,128)(2,1)S(1)} %collective-permute-done.a0), channel_id=1, source_target_pairs={{0,1},{1,2},{2,3},{3,0},{4,5},{5,6},{6,7},{7,4},{8,9},{9,10},{10,1... | collective-permute-start | bytes 786440 | tf_op jit(solution)/shard_map/ppermute | solution.py:359
  66.9 16.4 %collective-permute-start.16 = (bf16[256,640]{1,0:T(8,128)(2,1)S(1)}, bf16[256,640]{1,0:T(8,128)(2,1)S(1)}, u32[]{:S(2)}, u32[]{:S(2)}) collective-permute-start(bf16[256,640]{1,0:T(8,128)(2,1)S(1)} %get-tuple-element.93.panel0), channel_id=1, source_target_pairs={{0,12},{1,13},{2,14},{3,15},{4,0},{5,1},{6,2},{7,3},{8,4},{9,5},{1... | collective-permute-start | bytes 983048 | tf_op jit(solution)/shard_map/ppermute | solution.py:364
  67.2 17.0 %collective-permute-start.17 = (bf16[256,640]{1,0:T(8,128)(2,1)S(1)}, bf16[256,640]{1,0:T(8,128)(2,1)S(1)}, u32[]{:S(2)}, u32[]{:S(2)}) collective-permute-start(bf16[256,640]{1,0:T(8,128)(2,1)S(1)} %get-tuple-element.93.panel0), channel_id=1, source_target_pairs={{0,8},{1,9},{2,10},{3,11},{4,12},{5,13},{6,14},{7,15},{8,0},{9,1},... | collective-permute-start | bytes 983048 | tf_op jit(solution)/shard_map/ppermute | solution.py:364
  68.0 17.5 %collective-permute-start.18 = (bf16[256,640]{1,0:T(8,128)(2,1)S(1)}, bf16[256,640]{1,0:T(8,128)(2,1)S(1)}, u32[]{:S(2)}, u32[]{:S(2)}) collective-permute-start(bf16[256,640]{1,0:T(8,128)(2,1)S(1)} %get-tuple-element.93.panel0), channel_id=1, source_target_pairs={{0,4},{1,5},{2,6},{3,7},{4,8},{5,9},{6,10},{7,11},{8,12},{9,13},{1... | collective-permute-start | bytes 983048 | tf_op jit(solution)/shard_map/ppermute | solution.py:364
  68.7 8.0 %collective-permute-start.14 = (bf16[2,64,1024]{2,1,0:T(8,128)(2,1)S(1)}, bf16[2,64,1024]{2,1,0:T(8,128)(2,1)S(1)}, u32[]{:S(2)}, u32[]{:S(2)}) collective-permute-start(bf16[2,64,1024]{2,1,0:T(8,128)(2,1)S(1)} %collective-permute-done.a0), channel_id=1, source_target_pairs={{0,2},{1,3},{2,0},{3,1},{4,6},{5,7},{6,4},{7,5},{8,10},{9,11},{10,... | collective-permute-start | bytes 786440 | tf_op jit(solution)/shard_map/ppermute | solution.py:359
  68.7 11.5 %collective-permute-start.15 = (bf16[2,64,1024]{2,1,0:T(8,128)(2,1)S(1)}, bf16[2,64,1024]{2,1,0:T(8,128)(2,1)S(1)}, u32[]{:S(2)}, u32[]{:S(2)}) collective-permute-start(bf16[2,64,1024]{2,1,0:T(8,128)(2,1)S(1)} %collective-permute-done.a0), channel_id=1, source_target_pairs={{0,3},{1,0},{2,1},{3,2},{4,7},{5,4},{6,5},{7,6},{8,11},{9,8},{10,9... | collective-permute-start | bytes 786440 | tf_op jit(solution)/shard_map/ppermute | solution.py:359
  80.2 22.1 %collective-permute-start.19 = (bf16[272,512]{1,0:T(8,128)(2,1)S(1)}, bf16[272,512]{1,0:T(8,128)(2,1)S(1)}, u32[]{:S(2)}, u32[]{:S(2)}) collective-permute-start(bf16[272,512]{1,0:T(8,128)(2,1)S(1)} %get-tuple-element.96.panel0), channel_id=1, source_target_pairs={{0,12},{1,13},{2,14},{3,15},{4,0},{5,1},{6,2},{7,3},{8,4},{9,5},{1... | collective-permute-start | bytes 835592 | tf_op jit(solution)/shard_map/ppermute | solution.py:364
  82.5 19.9 %collective-permute-start.20 = (bf16[272,512]{1,0:T(8,128)(2,1)S(1)}, bf16[272,512]{1,0:T(8,128)(2,1)S(1)}, u32[]{:S(2)}, u32[]{:S(2)}) collective-permute-start(bf16[272,512]{1,0:T(8,128)(2,1)S(1)} %get-tuple-element.96.panel0), channel_id=1, source_target_pairs={{0,8},{1,9},{2,10},{3,11},{4,12},{5,13},{6,14},{7,15},{8,0},{9,1},... | collective-permute-start | bytes 835592 | tf_op jit(solution)/shard_map/ppermute | solution.py:364
  83.3 19.0 %collective-permute-start.21 = (bf16[272,512]{1,0:T(8,128)(2,1)S(1)}, bf16[272,512]{1,0:T(8,128)(2,1)S(1)}, u32[]{:S(2)}, u32[]{:S(2)}) collective-permute-start(bf16[272,512]{1,0:T(8,128)(2,1)S(1)} %get-tuple-element.96.panel0), channel_id=1, source_target_pairs={{0,4},{1,5},{2,6},{3,7},{4,8},{5,9},{6,10},{7,11},{8,12},{9,13},{1... | collective-permute-start | bytes 835592 | tf_op jit(solution)/shard_map/ppermute | solution.py:364
  89.1 13.2 %collective-permute-start.22 = (bf16[256,512]{1,0:T(8,128)(2,1)S(1)}, bf16[256,512]{1,0:T(8,128)(2,1)S(1)}, u32[]{:S(2)}, u32[]{:S(2)}) collective-permute-start(bf16[256,512]{1,0:T(8,128)(2,1)S(1)} %get-tuple-element.98), channel_id=1, source_target_pairs={{0,16},{16,32},{32,48},{48,64},{64,80},{80,96},{96,112},{112,128},... | collective-permute-start | bytes 786440 | tf_op jit(solution)/shard_map/ppermute | solution.py:379
  100.6 9.3 %collective-permute-start.32 = (bf16[512,128]{1,0:T(8,128)(2,1)S(1)}, bf16[512,128]{1,0:T(8,128)(2,1)S(1)}, u32[]{:S(2)}, u32[]{:S(2)}) collective-permute-start(bf16[512,128]{1,0:T(8,128)(2,1)S(1)} %get-tuple-element.110), channel_id=1, source_target_pairs={{0,12},{1,13},{2,14},{3,15},{4,0},{5,1},{6,2},{7,3},{8,4},{9,5},{1... | collective-permute-start | bytes 393224 | tf_op jit(solution)/shard_map/ppermute | solution.py:364
  104.1 20.4 %collective-permute-start.23 = (bf16[256,512]{1,0:T(8,128)(2,1)S(1)}, bf16[256,512]{1,0:T(8,128)(2,1)S(1)}, u32[]{:S(2)}, u32[]{:S(2)}) collective-permute-start(bf16[256,512]{1,0:T(8,128)(2,1)S(1)} %get-tuple-element.99.block0.refs_0_.refs_1_), channel_id=1, source_target_pairs={{0,1},{1,2},{2,3},{3,0},{4,5},{5,6},{6,7},{7,4},{8,9},{9,10},{10,1... | collective-permute-start | bytes 786440 | tf_op jit(solution)/shard_map/ppermute | solution.py:359
  106.4 18.2 %collective-permute-start.24 = (bf16[256,512]{1,0:T(8,128)(2,1)S(1)}, bf16[256,512]{1,0:T(8,128)(2,1)S(1)}, u32[]{:S(2)}, u32[]{:S(2)}) collective-permute-start(bf16[256,512]{1,0:T(8,128)(2,1)S(1)} %get-tuple-element.99.block0.refs_0_.refs_1_), channel_id=1, source_target_pairs={{0,2},{1,3},{2,0},{3,1},{4,6},{5,7},{6,4},{7,5},{8,10},{9,11},{10,... | collective-permute-start | bytes 786440 | tf_op jit(solution)/shard_map/ppermute | solution.py:359
  107.8 16.8 %collective-permute-start.25 = (bf16[256,512]{1,0:T(8,128)(2,1)S(1)}, bf16[256,512]{1,0:T(8,128)(2,1)S(1)}, u32[]{:S(2)}, u32[]{:S(2)}) collective-permute-start(bf16[256,512]{1,0:T(8,128)(2,1)S(1)} %get-tuple-element.99.block0.refs_0_.refs_1_), channel_id=1, source_target_pairs={{0,3},{1,0},{2,1},{3,2},{4,7},{5,4},{6,5},{7,6},{8,11},{9,8},{10,9... | collective-permute-start | bytes 786440 | tf_op jit(solution)/shard_map/ppermute | solution.py:359
  109.9 12.5 %collective-permute-start.34 = (bf16[512,128]{1,0:T(8,128)(2,1)S(1)}, bf16[512,128]{1,0:T(8,128)(2,1)S(1)}, u32[]{:S(2)}, u32[]{:S(2)}) collective-permute-start(bf16[512,128]{1,0:T(8,128)(2,1)S(1)} %get-tuple-element.110), channel_id=1, source_target_pairs={{0,4},{1,5},{2,6},{3,7},{4,8},{5,9},{6,10},{7,11},{8,12},{9,13},{1... | collective-permute-start | bytes 393224 | tf_op jit(solution)/shard_map/ppermute | solution.py:364
  114.8 13.3 %collective-permute-start.26 = (bf16[256,256]{1,0:T(8,128)(2,1)S(1)}, bf16[256,256]{1,0:T(8,128)(2,1)S(1)}, u32[]{:S(2)}, u32[]{:S(2)}) collective-permute-start(bf16[256,256]{1,0:T(8,128)(2,1)S(1)} %get-tuple-element.100), channel_id=1, source_target_pairs={{0,16},{16,32},{32,48},{48,64},{64,80},{80,96},{96,112},{112,128},... | collective-permute-start | bytes 393224 | tf_op jit(solution)/shard_map/ppermute | solution.py:379
  128.0 7.9 %collective-permute-start.37 = (bf16[512,128]{1,0:T(8,128)(2,1)S(1)}, bf16[512,128]{1,0:T(8,128)(2,1)S(1)}, u32[]{:S(2)}, u32[]{:S(2)}) collective-permute-start(bf16[512,128]{1,0:T(8,128)(2,1)S(1)} %get-tuple-element.112), channel_id=1, source_target_pairs={{0,4},{1,5},{2,6},{3,7},{4,8},{5,9},{6,10},{7,11},{8,12},{9,13},{1... | collective-permute-start | bytes 393224 | tf_op jit(solution)/shard_map/ppermute | solution.py:364
  128.7 32.0 %collective-permute-start.28 = (bf16[256,1024]{1,0:T(8,128)(2,1)S(1)}, bf16[256,1024]{1,0:T(8,128)(2,1)S(1)}, u32[]{:S(2)}, u32[]{:S(2)}) collective-permute-start(bf16[256,1024]{1,0:T(8,128)(2,1)S(1)} %shard_map.107.pair0), channel_id=1, source_target_pairs={{0,1},{1,2},{2,3},{3,0},{4,5},{5,6},{6,7},{7,4},{8,9},{9,10},{10,1... | collective-permute-start | bytes 1572872 | tf_op jit(solution)/shard_map/ppermute | solution.py:359
  128.9 31.9 %collective-permute-start.29 = (bf16[256,1024]{1,0:T(8,128)(2,1)S(1)}, bf16[256,1024]{1,0:T(8,128)(2,1)S(1)}, u32[]{:S(2)}, u32[]{:S(2)}) collective-permute-start(bf16[256,1024]{1,0:T(8,128)(2,1)S(1)} %shard_map.107.pair0), channel_id=1, source_target_pairs={{0,2},{1,3},{2,0},{3,1},{4,6},{5,7},{6,4},{7,5},{8,10},{9,11},{10,... | collective-permute-start | bytes 1572872 | tf_op jit(solution)/shard_map/ppermute | solution.py:359
  131.0 29.7 %collective-permute-start.30 = (bf16[256,1024]{1,0:T(8,128)(2,1)S(1)}, bf16[256,1024]{1,0:T(8,128)(2,1)S(1)}, u32[]{:S(2)}, u32[]{:S(2)}) collective-permute-start(bf16[256,1024]{1,0:T(8,128)(2,1)S(1)} %shard_map.107.pair0), channel_id=1, source_target_pairs={{0,3},{1,0},{2,1},{3,2},{4,7},{5,4},{6,5},{7,6},{8,11},{9,8},{10,9... | collective-permute-start | bytes 1572872 | tf_op jit(solution)/shard_map/ppermute | solution.py:359
  148.0 7.8 %collective-permute-start.41 = (bf16[512,128]{1,0:T(8,128)(2,1)S(1)}, bf16[512,128]{1,0:T(8,128)(2,1)S(1)}, u32[]{:S(2)}, u32[]{:S(2)}) collective-permute-start(bf16[512,128]{1,0:T(8,128)(2,1)S(1)} %shard_map.112.solved), channel_id=1, source_target_pairs={{0,16},{16,32},{32,48},{48,64},{64,80},{80,96},{96,112},{112,128},... | collective-permute-start | bytes 393224 | tf_op jit(solution)/shard_map/ppermute | solution.py:379
  (19 other events, 103.8 us)
Sparse Core Ops, SparseCore 0:
  11.2 27.4 all-gather.6
  41.1 27.6 all-gather.4

commit v2 on v1

--- a/solution.py
+++ b/solution.py
@@ -149,13 +149,15 @@
     copies[10].wait()
 
 
-def assemble_kernel(s_ref, piece0, piece1, piece2, piece3, g0, g1, g2, g3,
-                    panel, diagonal, g_columns):
+def assemble_kernel(s_ref, piece0, piece1, piece2, piece3, c_even, a_next, g0, g1, g2, g3,
+                    panel, diagonal, couplings, g_columns):
     y, x = s_ref[0], s_ref[1]
     for shift, piece in enumerate((piece0, piece1, piece2, piece3)):
         rows = at(mod4(x - shift), 64)
         panel[rows, :] = piece[:, pl.ds(0, 1152)]
         diagonal[rows, :] = piece[:, pl.ds(1152, 512)]
+    couplings[0] = c_even[...]
+    couplings[1] = a_next[...]
     for shift, piece in enumerate((g0, g1, g2, g3)):
         g_columns[mod4(y - shift)] = piece[...]
 
@@ -194,23 +196,28 @@
     out[pl.ds(0, 256), pl.ds(256, 256)] = imag.astype(out.dtype)
 
 
-def odd_kernel(s_ref, g0, g1, g2, g3, panel0, panel1, panel2, panel3, out, out_second, held):
+def odd_kernel(s_ref, g_ref, panel0, panel1, panel2, panel3, out, out_second, held):
     y, x = s_ref[0], s_ref[1]
     panels = (panel0, panel1, panel2, panel3)
-    stack_rows(x, (g0, g1, g2, g3), held)
+    held[...] = g_ref[...].reshape(512, 1024)
     put_pair(out, *wide_product(y, held, panels))
     out[:, pl.ds(512, 128)] = small_product(y, held, panels).astype(BF)
     put_pair(out_second, *wide_product(y, held, panels, 640))
-    out_second[pl.ds(256, 16), :] = jnp.zeros((16, 512), BF)
-
-
-def even_kernel(s_ref, a0, a1, a2, a3, c_ref, panel0, panel1, panel2, panel3, source,
-                ship, ship_source, upper_new, source_part, a_rows, c_rows):
+    out_second[pl.ds(256, 48), :] = jnp.zeros((48, 512), BF)
+
+
+def even_kernel(s_ref, ca0, ca1, ca2, ca3, panel0, panel1, panel2, panel3, source,
+                ship, upper_new, source_part, a_rows, c_rows):
     y, x = s_ref[0], s_ref[1]
     panels = (panel0, panel1, panel2, panel3)
-    stack_rows(x, (a0, a1, a2, a3), a_rows)
-    c_rows[...] = c_ref[...].reshape(512, 1024)
-    ship_source[...] = small_product(y, a_rows, panels).astype(BF)
+    stack_rows(x, [block.at[1] for block in (ca0, ca1, ca2, ca3)], a_rows)
+    stack_rows(x, [block.at[0] for block in (ca0, ca1, ca2, ca3)], c_rows)
+    value = small_product(y, a_rows, panels)
+    lane = lanes_of(32)
+    for index in range(4):
+        low, high = value[index * 64 : index * 64 + 32], value[index * 64 + 32 : index * 64 + 64]
+        tile = jnp.where(lane < 64, low, pltpu.roll(high, 64, 1))
+        ship[pl.ds(256, 32), pl.ds(index * 128, 128)] = tile.astype(BF)
     put_pair(ship, *wide_product(y, a_rows, panels))
     own = pltpu.roll(source[:, pl.ds(512, 128)].astype(F32), 64, 1)
     own = jnp.where(lanes_of(256) < 64, own, 0.0)
@@ -222,8 +229,8 @@
 def diagonal_kernel(s_ref, c_rows, a_rows, panel0, panel1, panel2, panel3, diagonal, shipped,
                     out, lower_real, lower_imag):
     real, imag = wide_product(s_ref[0], c_rows, (panel0, panel1, panel2, panel3))
-    real = diagonal[:, pl.ds(0, 256)].astype(F32) - real - shipped[:, pl.ds(0, 256)].astype(F32)
-    imag = diagonal[:, pl.ds(256, 256)].astype(F32) - imag - shipped[:, pl.ds(256, 256)].astype(F32)
+    real = diagonal[:, pl.ds(0, 256)].astype(F32) - real - shipped[pl.ds(0, 256), pl.ds(0, 256)].astype(F32)
+    imag = diagonal[:, pl.ds(256, 256)].astype(F32) - imag - shipped[pl.ds(0, 256), pl.ds(256, 256)].astype(F32)
     put_pair(out, real, imag)
     real, imag = wide_product(s_ref[0], a_rows, (panel0, panel1, panel2, panel3))
     lower_real[...] = (-real).astype(BF)
@@ -256,8 +263,14 @@
 
 
 def source_kernel(s_ref, g_ref, source_part, shipped, source_new, own, send, whole):
-    source = (source_part[...] - shipped[...].astype(F32)).astype(BF)
-    source_new[...] = source
+    lane = lanes_of(32)
+    for index in range(4):
+        tile = shipped[pl.ds(256, 32), pl.ds(index * 128, 128)].astype(F32)
+        for half, moved in enumerate(halves(tile)):
+            rows = pl.ds(index * 64 + half * 32, 32)
+            value = source_part[rows, :] - jnp.where(lane < 64, moved, 0.0)
+            source_new[rows, :] = value.astype(BF)
+    source = source_new[...]
     put_partial(g_ref, source, own, send, whole)
 
 
@@ -403,37 +416,34 @@
         + [pltpu.SemaphoreType.DMA((11,))],
     )
     pieces = [pieces[0]] + [moved_x(pieces[by], by) for by in turns]
-    c_gathered = gathered_x(c_even)
+    g_rows = gathered_x(g_odd)
     a_next = along_cuts(a_even, -1)
     g1, g2, g3 = [moved_y(piece, by) for by, piece in zip(turns, (g1, g2, g3))]
-    a_next, g1, g2, g3, g_odd, *pieces = after((a_next, g1, g2, g3, g_odd, *pieces))
-    panel, diagonal, g_columns = call(
+    a_next, g1, g2, g3, *pieces = after((a_next, g1, g2, g3, *pieces))
+    panel, diagonal, couplings, g_columns = call(
         assemble_kernel,
-        [shape((256, 1152)), shape((256, 512)), shape((4, 2, 64, 256))],
-        0, scalars, *pieces, g0, g1, g2, g3,
+        [shape((256, 1152)), shape((256, 512)), shape((2, 2, 64, 1024)), shape((4, 2, 64, 256))],
+        0, scalars, *pieces, c_even, a_next, g0, g1, g2, g3,
     )
     g_columns = gathered_x(g_columns)
     panels = gathered_y(panel)
-    g_blocks = [g_odd] + [moved_x(g_odd, by) for by in turns]
-    a_blocks = [a_next] + [moved_x(a_next, by) for by in turns]
+    ca_blocks = [couplings] + [moved_x(couplings, by) for by in turns]
     first, second = call(
-        odd_kernel, [shape((256, 640)), shape((272, 512))], wide_flops,
-        scalars, *g_blocks, *panels, scratch=[pltpu.VMEM((512, 1024), BF)],
-    )
-    first, c_gathered = after((first, c_gathered))
+        odd_kernel, [shape((256, 640)), shape((304, 512))], wide_flops,
+        scalars, g_rows, *panels, scratch=[pltpu.VMEM((512, 1024), BF)],
+    )
     firsts = gathered_y(first)
-    second, g_columns, *a_blocks = after((second, g_columns, *a_blocks))
+    second, g_columns, *ca_blocks = after((second, g_columns, *ca_blocks))
     seconds = gathered_y(second)
-    ship, ship_source, upper_new, source_part, a_rows, c_rows = call(
+    ship, upper_new, source_part, a_rows, c_rows = call(
         even_kernel,
-        [shape((256, 512)), shape((256, 128)), shape((256, 512)), shape((256, 128), F32),
+        [shape((288, 512)), shape((256, 512)), shape((256, 128), F32),
          shape((512, 1024)),
          shape((512, 1024))],
         2 * wide_flops,
-        scalars, *a_blocks, c_gathered, *firsts, panel,
+        scalars, *ca_blocks, *firsts, panel,
     )
     shipped = along_cuts(ship, 1)
-    shipped_source = along_cuts(ship_source, 1)
     diagonal_new, *ship_lower = call(
         diagonal_kernel, [shape((256, 512))] + [shape((256, 256))] * 2, 2 * wide_flops,
         scalars, c_rows, a_rows, *seconds, diagonal, shipped,
@@ -444,7 +454,7 @@
     vector = pltpu.VMEM((1024, 128), BF)
     source, own, send = call(
         source_kernel, [shape((256, 128))] + packed_shapes, solve_flops,
-        scalars, g_columns, source_part, shipped_source, scratch=[whole],
+        scalars, g_columns, source_part, shipped, scratch=[whole],
     )
     got = gathered_y(send)[1:]
     lower_new = [along_cuts(half, 1) for half in ship_lower]

time: 178 us -> 179 us (level)
  starting transfers between devices: 68.8 us -> 62.8 us
  waiting for transfers between devices: 69 us -> 73.1 us
    ppermute x21, waiting for transfers between devices: 38.8 us -> 64.3 us  [moved_y(): return lax.ppermute(block, 'row', pairs)]
    ppermute x18 -> x15, waiting for transfers between devices: 23.1 us -> 0.04 us  [moved_x(): return lax.ppermute(block, 'row', pairs)]
    ppermute x7 -> x6, starting transfers between devices: 28.3 us -> 24.5 us  [along_cuts(): return lax.ppermute(block, 'cuts', pairs)]
    ppermute x18 -> x15, starting transfers between devices: 19.7 us -> 17.1 us  [moved_x(): return lax.ppermute(block, 'row', pairs)]
    ppermute x7 -> x6, waiting for transfers between devices: 7.06 us -> 8.17 us  [along_cuts(): return lax.ppermute(block, 'cuts', pairs)]
  transfers between devices with their start and end apart: 48 -> 44, of which waited for: 18 -> 17; matrix products, arithmetic and copies ran while one was open for 0% -> 0% of each run, Pallas kernels for 9% -> 10%
where the time goes in v2:
time: 179 us; the launch traced here: 177 us
  waiting for transfers between devices  73.1 us (41%)
  starting transfers between devices  62.8 us (35%)
  Pallas kernels  23.8 us (13%)
  between operations  14.3 us (8%)
  local copies, waits for them, and re-layouts  3.38 us (2%)
    ppermute x21, waiting for transfers between devices, moved_y(): return lax.ppermute(block, 'row', pairs)  64.3 us
    ppermute x6, starting transfers between devices, along_cuts(): return lax.ppermute(block, 'cuts', pairs)  24.5 us
    pallas_call x14, Pallas kernels, call(): pl.pallas_call(kernel, out_shape=tuple(out_shapes), in_specs=[SMEM] + [an...  23.8 us
    ppermute x21, starting transfers between devices, moved_y(): return lax.ppermute(block, 'row', pairs)  21.1 us
    ppermute x15, starting transfers between devices, moved_x(): return lax.ppermute(block, 'row', pairs)  17.1 us
    ppermute x6, waiting for transfers between devices, along_cuts(): return lax.ppermute(block, 'cuts', pairs)  8.17 us
  transfers between devices with their start and end apart: 44, of which 17 were waited for; matrix products, arithmetic and copies ran while one was open for 0% of the time, Pallas kernels for 10%

profile of v2, /device:TPU:97, one launch (start us, length us, event | category | flops | bytes accessed | tf_op | source)
XLA Modules:
  0.0 177.5 jit_solution(2891585810821569758)
XLA Ops:
  8.1 2.9 %shard_map.101 = (bf16[64,1664]{1,0:T(8,128)(2,1)S(1)}, bf16[64,1664]{1,0:T(8,128)(2,1)S(1)}, bf16[64,1664]{1,0:T(8,128)(2,1)S(1)}, bf16[64,1664]{1,0:T(8,128)(2...) custom-call(s32[6]{0:T(128)S(1)} %pad_add_fusion.1.s_ref, ...), custom_call_target="tpu_custom_call" | custom-call | bytes 4063256 | tf_op jit(solution)/shard_map/pallas_call | solution.py:27
  11.1 2.6 %collective-permute-start = (bf16[2,64,1024]{2,1,0:T(8,128)(2,1)S(1)}, bf16[2,64,1024]{2,1,0:T(8,128)(2,1)S(1)}, u32[]{:S(2)}, u32[]{:S(2)}) collective-permute-start(bf16[2,64,1024]{2,1,0:T(8,128)(2,1)S(1)} %get-tuple-element.62), channel_id=1, source_target_pairs={{16,0},{32,16},{48,32},{64,48},{80,64},{96,80},{112,96},{128,112},... | collective-permute-start | bytes 786440 | tf_op jit(solution)/shard_map/ppermute | solution.py:392
  15.0 2.5 %collective-permute-start.5 = (bf16[64,1664]{1,0:T(8,128)(2,1)S(1)}, bf16[64,1664]{1,0:T(8,128)(2,1)S(1)}, u32[]{:S(2)}, u32[]{:S(2)}) collective-permute-start(bf16[64,1664]{1,0:T(8,128)(2,1)S(1)} %get-tuple-element.68), channel_id=1, source_target_pairs={{0,2},{1,3},{2,0},{3,1},{4,6},{5,7},{6,4},{7,5},{8,10},{9,11},{10,... | collective-permute-start | bytes 638984 | tf_op jit(solution)/shard_map/ppermute | solution.py:372
  19.9 3.1 %collective-permute-done.1.g1 = bf16[2,64,256]{2,1,0:T(8,128)(2,1)S(1)} collective-permute-done((bf16[2,64,256]{2,1,0:T(8,128)(2,1)S(1)}, bf16[2,64,256]{2,1,0:T(8,128)(2,1)S(1)}, u32[]{:S(2)}, u32[]{:S(2)}) %collective-permute-start.1) | collective-permute-done | bytes 65568 | tf_op jit(solution)/shard_map/ppermute | solution.py:377
  23.0 1.9 %collective-permute-start.2 = (bf16[2,64,256]{2,1,0:T(8,128)(2,1)S(1)}, bf16[2,64,256]{2,1,0:T(8,128)(2,1)S(1)}, u32[]{:S(2)}, u32[]{:S(2)}) collective-permute-start(bf16[2,64,256]{2,1,0:T(8,128)(2,1)S(1)} %get-tuple-element.64), channel_id=1, source_target_pairs={{0,8},{1,9},{2,10},{3,11},{4,12},{5,13},{6,14},{7,15},{8,0},{9,1},... | collective-permute-start | bytes 196616 | tf_op jit(solution)/shard_map/ppermute | solution.py:377
  24.9 2.9 %collective-permute-done.2.g2 = bf16[2,64,256]{2,1,0:T(8,128)(2,1)S(1)} collective-permute-done((bf16[2,64,256]{2,1,0:T(8,128)(2,1)S(1)}, bf16[2,64,256]{2,1,0:T(8,128)(2,1)S(1)}, u32[]{:S(2)}, u32[]{:S(2)}) %collective-permute-start.2) | collective-permute-done | bytes 65568 | tf_op jit(solution)/shard_map/ppermute | solution.py:377
  27.8 1.8 %collective-permute-start.3 = (bf16[2,64,256]{2,1,0:T(8,128)(2,1)S(1)}, bf16[2,64,256]{2,1,0:T(8,128)(2,1)S(1)}, u32[]{:S(2)}, u32[]{:S(2)}) collective-permute-start(bf16[2,64,256]{2,1,0:T(8,128)(2,1)S(1)} %get-tuple-element.65), channel_id=1, source_target_pairs={{0,12},{1,13},{2,14},{3,15},{4,0},{5,1},{6,2},{7,3},{8,4},{9,5},{1... | collective-permute-start | bytes 196616 | tf_op jit(solution)/shard_map/ppermute | solution.py:377
  33.5 3.1 %collective-permute-start.7 = (bf16[256,1152]{1,0:T(8,128)(2,1)S(1)}, bf16[256,1152]{1,0:T(8,128)(2,1)S(1)}, u32[]{:S(2)}, u32[]{:S(2)}) collective-permute-start(bf16[256,1152]{1,0:T(8,128)(2,1)S(1)} %get-tuple-element.80.panel0.source), channel_id=1, source_target_pairs={{0,12},{1,13},{2,14},{3,15},{4,0},{5,1},{6,2},{7,3},{8,4},{9,5},{1... | collective-permute-start | bytes 1769480 | tf_op jit(solution)/shard_map/ppermute | solution.py:377
  38.2 9.4 %collective-permute-done.7.panel1 = bf16[256,1152]{1,0:T(8,128)(2,1)S(1)} collective-permute-done((bf16[256,1152]{1,0:T(8,128)(2,1)S(1)}, bf16[256,1152]{1,0:T(8,128)(2,1)S(1)}, u32[]{:S(2)}, u32[]{:S(2)}) %collective-permute-start.7) | collective-permute-done | bytes 589856 | tf_op jit(solution)/shard_map/ppermute | solution.py:377
  49.4 16.0 %collective-permute-done.9.panel3 = bf16[256,1152]{1,0:T(8,128)(2,1)S(1)} collective-permute-done((bf16[256,1152]{1,0:T(8,128)(2,1)S(1)}, bf16[256,1152]{1,0:T(8,128)(2,1)S(1)}, u32[]{:S(2)}, u32[]{:S(2)}) %collective-permute-start.9) | collective-permute-done | bytes 589856 | tf_op jit(solution)/shard_map/ppermute | solution.py:377
  66.7 3.0 %shard_map.103 = (bf16[256,640]{1,0:T(8,128)(2,1)}, bf16[304,512]{1,0:T(8,128)(2,1)S(1)}) custom-call(s32[6]{0:T(128)S(1)} %pad_add_fusion.1.s_ref, bf16[4,2,64,1024]{3,2,1,0:T(8,128)(2,1)S(1)} %bitcast.12, bf16[256,1152]{1,0:T(8,128)(2,1)S(1)} %get-tuple-element.80.panel0.source, bf16[256,1152]{1,0:T(8,128)(2,1)S(1)} %collective-permute-done.7.panel1, ...), custom_call_target="tpu_custom_call" | custom-call | bytes 4046872 | tf_op jit(solution)/shard_map/pallas_call | solution.py:27
  72.3 2.0 %collective-permute-start.16 = (bf16[304,512]{1,0:T(8,128)(2,1)}, bf16[304,512]{1,0:T(8,128)(2,1)S(1)}, u32[]{:S(2)}, u32[]{:S(2)}) collective-permute-start(bf16[304,512]{1,0:T(8,128)(2,1)} %copy-done.2), channel_id=1, source_target_pairs={{0,12},{1,13},{2,14},{3,15},{4,0},{5,1},{6,2},{7,3},{8,4},{9,5},{1... | collective-permute-start | bytes 933896 | tf_op jit(solution)/shard_map/ppermute | solution.py:377
  76.2 2.9 %collective-permute-done.13.panel1 = bf16[256,640]{1,0:T(8,128)(2,1)S(1)} collective-permute-done((bf16[256,640]{1,0:T(8,128)(2,1)}, bf16[256,640]{1,0:T(8,128)(2,1)S(1)}, u32[]{:S(2)}, u32[]{:S(2)}) %collective-permute-start.13) | collective-permute-done | bytes 327712 | tf_op jit(solution)/shard_map/ppermute | solution.py:377
  79.7 11.1 %collective-permute-done.15.panel3 = bf16[256,640]{1,0:T(8,128)(2,1)S(1)} collective-permute-done((bf16[256,640]{1,0:T(8,128)(2,1)}, bf16[256,640]{1,0:T(8,128)(2,1)S(1)}, u32[]{:S(2)}, u32[]{:S(2)}) %collective-permute-start.15) | collective-permute-done | bytes 327712 | tf_op jit(solution)/shard_map/ppermute | solution.py:377
  90.7 3.2 %shard_map.104 = (bf16[288,512]{1,0:T(8,128)(2,1)S(1)}, bf16[256,512]{1,0:T(8,128)(2,1)S(1)}, f32[256,128]{1,0:T(8,128)S(1)}, bf16[512,1024]{1,0:T(8,128)(2,1)S(1)}, bf16[512,1024]{1,0:T(8,128)(2,1)S(1)}) custom-call(s32[6]{0:T(128)S(1)} %pad_add_fusion.1.s_ref, bf16[2,2,64,1024]{3,2,1,0:T(8,128)(2,1)S(1)} %get-tuple-element.84.ca0, ...), custom_call_target="tpu_custom_call" | custom-call | bytes 6783000 | tf_op jit(solution)/shard_map/pallas_call | solution.py:27
  93.9 5.4 %collective-permute-start.19 = (bf16[288,512]{1,0:T(8,128)(2,1)S(1)}, bf16[288,512]{1,0:T(8,128)(2,1)S(1)}, u32[]{:S(2)}, u32[]{:S(2)}) collective-permute-start(bf16[288,512]{1,0:T(8,128)(2,1)S(1)} %get-tuple-element.93), channel_id=1, source_target_pairs={{0,16},{16,32},{32,48},{48,64},{64,80},{80,96},{96,112},{112,128},... | collective-permute-start | bytes 884744 | tf_op jit(solution)/shard_map/ppermute | solution.py:392
  99.4 3.6 %collective-permute-done.19.shipped = bf16[288,512]{1,0:T(8,128)(2,1)S(1)} collective-permute-done((bf16[288,512]{1,0:T(8,128)(2,1)S(1)}, bf16[288,512]{1,0:T(8,128)(2,1)S(1)}, u32[]{:S(2)}, u32[]{:S(2)}) %collective-permute-start.19) | collective-permute-done | bytes 294944 | tf_op jit(solution)/shard_map/ppermute | solution.py:392
  107.6 2.4 %collective-permute-start.22 = (bf16[256,512]{1,0:T(8,128)(2,1)S(1)}, bf16[256,512]{1,0:T(8,128)(2,1)S(1)}, u32[]{:S(2)}, u32[]{:S(2)}) collective-permute-start(bf16[256,512]{1,0:T(8,128)(2,1)S(1)} %get-tuple-element.94.block0.refs_0_.refs_1_), channel_id=1, source_target_pairs={{0,3},{1,0},{2,1},{3,2},{4,7},{5,4},{6,5},{7,6},{8,11},{9,8},{10,9... | collective-permute-start | bytes 786440 | tf_op jit(solution)/shard_map/ppermute | solution.py:372
  111.9 4.1 %collective-permute-done.29.got2 = bf16[512,128]{1,0:T(8,128)(2,1)S(1)} collective-permute-done((bf16[512,128]{1,0:T(8,128)(2,1)S(1)}, bf16[512,128]{1,0:T(8,128)(2,1)S(1)}, u32[]{:S(2)}, u32[]{:S(2)}) %collective-permute-start.29) | collective-permute-done | bytes 131104 | tf_op jit(solution)/shard_map/ppermute | solution.py:377
  116.0 7.0 %collective-permute-start.23 = (bf16[256,256]{1,0:T(8,128)(2,1)S(1)}, bf16[256,256]{1,0:T(8,128)(2,1)S(1)}, u32[]{:S(2)}, u32[]{:S(2)}) collective-permute-start(bf16[256,256]{1,0:T(8,128)(2,1)S(1)} %get-tuple-element.95), channel_id=1, source_target_pairs={{0,16},{16,32},{32,48},{48,64},{64,80},{80,96},{96,112},{112,128},... | collective-permute-start | bytes 393224 | tf_op jit(solution)/shard_map/ppermute | solution.py:392
  123.0 1.9 %collective-permute-start.24 = (bf16[256,256]{1,0:T(8,128)(2,1)S(1)}, bf16[256,256]{1,0:T(8,128)(2,1)S(1)}, u32[]{:S(2)}, u32[]{:S(2)}) collective-permute-start(bf16[256,256]{1,0:T(8,128)(2,1)S(1)} %get-tuple-element.96), channel_id=1, source_target_pairs={{0,16},{16,32},{32,48},{48,64},{64,80},{80,96},{96,112},{112,128},... | collective-permute-start | bytes 393224 | tf_op jit(solution)/shard_map/ppermute | solution.py:392
  130.2 2.2 %collective-permute-start.26 = (bf16[256,1024]{1,0:T(8,128)(2,1)S(1)}, bf16[256,1024]{1,0:T(8,128)(2,1)S(1)}, u32[]{:S(2)}, u32[]{:S(2)}) collective-permute-start(bf16[256,1024]{1,0:T(8,128)(2,1)S(1)} %shard_map.107.pair0), channel_id=1, source_target_pairs={{0,2},{1,3},{2,0},{3,1},{4,6},{5,7},{6,4},{7,5},{8,10},{9,11},{10,... | collective-permute-start | bytes 1572872 | tf_op jit(solution)/shard_map/ppermute | solution.py:372
  132.4 2.0 %collective-permute-start.27 = (bf16[256,1024]{1,0:T(8,128)(2,1)S(1)}, bf16[256,1024]{1,0:T(8,128)(2,1)S(1)}, u32[]{:S(2)}, u32[]{:S(2)}) collective-permute-start(bf16[256,1024]{1,0:T(8,128)(2,1)S(1)} %shard_map.107.pair0), channel_id=1, source_target_pairs={{0,3},{1,0},{2,1},{3,2},{4,7},{5,4},{6,5},{7,6},{8,11},{9,8},{10,9... | collective-permute-start | bytes 1572872 | tf_op jit(solution)/shard_map/ppermute | solution.py:372
  134.3 3.0 %collective-permute-done.33.got3 = bf16[512,128]{1,0:T(8,128)(2,1)S(1)} collective-permute-done((bf16[512,128]{1,0:T(8,128)(2,1)S(1)}, bf16[512,128]{1,0:T(8,128)(2,1)S(1)}, u32[]{:S(2)}, u32[]{:S(2)}) %collective-permute-start.33) | collective-permute-done | bytes 131104 | tf_op jit(solution)/shard_map/ppermute | solution.py:377
  137.3 1.8 %shard_map.111 = (bf16[512,128]{1,0:T(8,128)(2,1)S(1)}, f32[512,128]{1,0:T(8,128)S(1)}, bf16[512,128]{1,0:T(8,128)(2,1)S(1)}) custom-call(s32[6]{0:T(128)S(1)} %pad_add_fusion.1.s_ref, f32[512,128]{1,0:T(8,128)S(1)} %get-tuple-element.105.own, bf16[512,128]{1,0:T(8,128)(2,1)S(1)} %collective-permute-done.31.got1, ...), custom_call_target="tpu_custom_call" | custom-call | bytes 3473432 | tf_op jit(solution)/shard_map/pallas_call | solution.py:27
  139.3 1.9 %collective-permute-start.35 = (bf16[512,128]{1,0:T(8,128)(2,1)S(1)}, bf16[512,128]{1,0:T(8,128)(2,1)S(1)}, u32[]{:S(2)}, u32[]{:S(2)}) collective-permute-start(bf16[512,128]{1,0:T(8,128)(2,1)S(1)} %get-tuple-element.109), channel_id=1, source_target_pairs={{0,8},{1,9},{2,10},{3,11},{4,12},{5,13},{6,14},{7,15},{8,0},{9,1},... | collective-permute-start | bytes 393224 | tf_op jit(solution)/shard_map/ppermute | solution.py:377
  141.1 2.2 %collective-permute-done.34.got1 = bf16[512,128]{1,0:T(8,128)(2,1)S(1)} collective-permute-done((bf16[512,128]{1,0:T(8,128)(2,1)S(1)}, bf16[512,128]{1,0:T(8,128)(2,1)S(1)}, u32[]{:S(2)}, u32[]{:S(2)}) %collective-permute-start.34) | collective-permute-done | bytes 131104 | tf_op jit(solution)/shard_map/ppermute | solution.py:377
  144.7 4.3 %collective-permute-done.36.got3 = bf16[512,128]{1,0:T(8,128)(2,1)S(1)} collective-permute-done((bf16[512,128]{1,0:T(8,128)(2,1)S(1)}, bf16[512,128]{1,0:T(8,128)(2,1)S(1)}, u32[]{:S(2)}, u32[]{:S(2)}) %collective-permute-start.36) | collective-permute-done | bytes 131104 | tf_op jit(solution)/shard_map/ppermute | solution.py:377
  149.6 4.6 %collective-permute-start.37 = (bf16[512,128]{1,0:T(8,128)(2,1)S(1)}, bf16[512,128]{1,0:T(8,128)(2,1)S(1)}, u32[]{:S(2)}, u32[]{:S(2)}) collective-permute-start(bf16[512,128]{1,0:T(8,128)(2,1)S(1)} %shard_map.112.solved), channel_id=1, source_target_pairs={{0,16},{16,32},{32,48},{48,64},{64,80},{80,96},{96,112},{112,128},... | collective-permute-start | bytes 393224 | tf_op jit(solution)/shard_map/ppermute | solution.py:392
  154.2 3.0 %collective-permute-start.38 = (bf16[512,128]{1,0:T(8,128)(2,1)S(1)}, bf16[512,128]{1,0:T(8,128)(2,1)S(1)}, u32[]{:S(2)}, u32[]{:S(2)}) collective-permute-start(bf16[512,128]{1,0:T(8,128)(2,1)S(1)} %shard_map.112.solved), channel_id=1, source_target_pairs={{16,0},{32,16},{48,32},{64,48},{80,64},{96,80},{112,96},{128,112},... | collective-permute-start | bytes 393224 | tf_op jit(solution)/shard_map/ppermute | solution.py:392
  157.2 4.5 %collective-permute-done.38.above = bf16[512,128]{1,0:T(8,128)(2,1)S(1)} collective-permute-done((bf16[512,128]{1,0:T(8,128)(2,1)S(1)}, bf16[512,128]{1,0:T(8,128)(2,1)S(1)}, u32[]{:S(2)}, u32[]{:S(2)}) %collective-permute-start.38) | collective-permute-done | bytes 131104 | tf_op jit(solution)/shard_map/ppermute | solution.py:392
  163.3 1.8 %collective-permute-start.40 = (f32[64,128]{1,0:T(8,128)S(1)}, f32[64,128]{1,0:T(8,128)S(1)}, u32[]{:S(2)}, u32[]{:S(2)}) collective-permute-start(f32[64,128]{1,0:T(8,128)S(1)} %get-tuple-element.113), channel_id=1, source_target_pairs={{0,2},{1,3},{2,0},{3,1},{4,6},{5,7},{6,4},{7,5},{8,10},{9,11},{10,... | collective-permute-start | bytes 98312 | tf_op jit(solution)/shard_map/ppermute | solution.py:372
  (89 shorter events, 38.9 us)
Async XLA Ops:
  7.2 58.3 %all-gather.5.cloned.1.call-start = ((), (), s32[]{:S(2)}) async-start(), calls=%async_computation | async-start | bytes 1310720 | tf_op jit(solution)/shard_map/all_gather | solution.py:386
  11.1 61.3 %all-gather.7.cloned.1.call-start = ((), (), s32[]{:S(2)}) async-start(), calls=%async_computation.1 | async-start | bytes 1310720 | tf_op jit(solution)/shard_map/all_gather | solution.py:386
  11.1 20.2 %collective-permute-start = (bf16[2,64,1024]{2,1,0:T(8,128)(2,1)S(1)}, bf16[2,64,1024]{2,1,0:T(8,128)(2,1)S(1)}, u32[]{:S(2)}, u32[]{:S(2)}) collective-permute-start(bf16[2,64,1024]{2,1,0:T(8,128)(2,1)S(1)} %get-tuple-element.62), channel_id=1, source_target_pairs={{16,0},{32,16},{48,32},{64,48},{80,64},{96,80},{112,96},{128,112},... | collective-permute-start | bytes 786440 | tf_op jit(solution)/shard_map/ppermute | solution.py:392
  13.7 17.6 %collective-permute-start.4 = (bf16[64,1664]{1,0:T(8,128)(2,1)S(1)}, bf16[64,1664]{1,0:T(8,128)(2,1)S(1)}, u32[]{:S(2)}, u32[]{:S(2)}) collective-permute-start(bf16[64,1664]{1,0:T(8,128)(2,1)S(1)} %get-tuple-element.67), channel_id=1, source_target_pairs={{0,1},{1,2},{2,3},{3,0},{4,5},{5,6},{6,7},{7,4},{8,9},{9,10},{10,1... | collective-permute-start | bytes 638984 | tf_op jit(solution)/shard_map/ppermute | solution.py:372
  15.0 16.3 %collective-permute-start.5 = (bf16[64,1664]{1,0:T(8,128)(2,1)S(1)}, bf16[64,1664]{1,0:T(8,128)(2,1)S(1)}, u32[]{:S(2)}, u32[]{:S(2)}) collective-permute-start(bf16[64,1664]{1,0:T(8,128)(2,1)S(1)} %get-tuple-element.68), channel_id=1, source_target_pairs={{0,2},{1,3},{2,0},{3,1},{4,6},{5,7},{6,4},{7,5},{8,10},{9,11},{10,... | collective-permute-start | bytes 638984 | tf_op jit(solution)/shard_map/ppermute | solution.py:372
  17.5 13.9 %collective-permute-start.6 = (bf16[64,1664]{1,0:T(8,128)(2,1)S(1)}, bf16[64,1664]{1,0:T(8,128)(2,1)S(1)}, u32[]{:S(2)}, u32[]{:S(2)}) collective-permute-start(bf16[64,1664]{1,0:T(8,128)(2,1)S(1)} %get-tuple-element.69), channel_id=1, source_target_pairs={{0,3},{1,0},{2,1},{3,2},{4,7},{5,4},{6,5},{7,6},{8,11},{9,8},{10,9... | collective-permute-start | bytes 638984 | tf_op jit(solution)/shard_map/ppermute | solution.py:372
  33.5 14.1 %collective-permute-start.7 = (bf16[256,1152]{1,0:T(8,128)(2,1)S(1)}, bf16[256,1152]{1,0:T(8,128)(2,1)S(1)}, u32[]{:S(2)}, u32[]{:S(2)}) collective-permute-start(bf16[256,1152]{1,0:T(8,128)(2,1)S(1)} %get-tuple-element.80.panel0.source), channel_id=1, source_target_pairs={{0,12},{1,13},{2,14},{3,15},{4,0},{5,1},{6,2},{7,3},{8,4},{9,5},{1... | collective-permute-start | bytes 1769480 | tf_op jit(solution)/shard_map/ppermute | solution.py:377
  36.6 12.8 %collective-permute-start.8 = (bf16[256,1152]{1,0:T(8,128)(2,1)S(1)}, bf16[256,1152]{1,0:T(8,128)(2,1)S(1)}, u32[]{:S(2)}, u32[]{:S(2)}) collective-permute-start(bf16[256,1152]{1,0:T(8,128)(2,1)S(1)} %get-tuple-element.80.panel0.source), channel_id=1, source_target_pairs={{0,8},{1,9},{2,10},{3,11},{4,12},{5,13},{6,14},{7,15},{8,0},{9,1},... | collective-permute-start | bytes 1769480 | tf_op jit(solution)/shard_map/ppermute | solution.py:377
  36.6 28.8 %collective-permute-start.9 = (bf16[256,1152]{1,0:T(8,128)(2,1)S(1)}, bf16[256,1152]{1,0:T(8,128)(2,1)S(1)}, u32[]{:S(2)}, u32[]{:S(2)}) collective-permute-start(bf16[256,1152]{1,0:T(8,128)(2,1)S(1)} %get-tuple-element.80.panel0.source), channel_id=1, source_target_pairs={{0,4},{1,5},{2,6},{3,7},{4,8},{5,9},{6,10},{7,11},{8,12},{9,13},{1... | collective-permute-start | bytes 1769480 | tf_op jit(solution)/shard_map/ppermute | solution.py:377
  37.3 33.7 %collective-permute-start.10 = (bf16[2,2,64,1024]{3,2,1,0:T(8,128)(2,1)S(1)}, bf16[2,2,64,1024]{3,2,1,0:T(8,128)(2,1)S(1)}, u32[]{:S(2)}, u32[]{:S(2)}) collective-permute-start(bf16[2,2,64,1024]{3,2,1,0:T(8,128)(2,1)S(1)} %get-tuple-element.84.ca0), channel_id=1, source_target_pairs={{0,1},{1,2},{2,3},{3,0},{4,5},{5,6},{6,7},{7,4},{8,9},{9,10},{10,1... | collective-permute-start | bytes 1572872 | tf_op jit(solution)/shard_map/ppermute | solution.py:372
  37.3 34.6 %collective-permute-start.11 = (bf16[2,2,64,1024]{3,2,1,0:T(8,128)(2,1)S(1)}, bf16[2,2,64,1024]{3,2,1,0:T(8,128)(2,1)}, u32[]{:S(2)}, u32[]{:S(2)}) collective-permute-start(bf16[2,2,64,1024]{3,2,1,0:T(8,128)(2,1)S(1)} %get-tuple-element.84.ca0), channel_id=1, source_target_pairs={{0,2},{1,3},{2,0},{3,1},{4,6},{5,7},{6,4},{7,5},{8,10},{9,11},{10,... | collective-permute-start | bytes 1572872 | tf_op jit(solution)/shard_map/ppermute | solution.py:372
  47.6 24.3 %collective-permute-start.12 = (bf16[2,2,64,1024]{3,2,1,0:T(8,128)(2,1)S(1)}, bf16[2,2,64,1024]{3,2,1,0:T(8,128)(2,1)}, u32[]{:S(2)}, u32[]{:S(2)}) collective-permute-start(bf16[2,2,64,1024]{3,2,1,0:T(8,128)(2,1)S(1)} %get-tuple-element.84.ca0), channel_id=1, source_target_pairs={{0,3},{1,0},{2,1},{3,2},{4,7},{5,4},{6,5},{7,6},{8,11},{9,8},{10,9... | collective-permute-start | bytes 1572872 | tf_op jit(solution)/shard_map/ppermute | solution.py:372
  70.4 8.7 %collective-permute-start.13 = (bf16[256,640]{1,0:T(8,128)(2,1)}, bf16[256,640]{1,0:T(8,128)(2,1)S(1)}, u32[]{:S(2)}, u32[]{:S(2)}) collective-permute-start(bf16[256,640]{1,0:T(8,128)(2,1)} %get-tuple-element.88.panel0), channel_id=1, source_target_pairs={{0,12},{1,13},{2,14},{3,15},{4,0},{5,1},{6,2},{7,3},{8,4},{9,5},{1... | collective-permute-start | bytes 983048 | tf_op jit(solution)/shard_map/ppermute | solution.py:377
  70.4 9.3 %collective-permute-start.14 = (bf16[256,640]{1,0:T(8,128)(2,1)}, bf16[256,640]{1,0:T(8,128)(2,1)S(1)}, u32[]{:S(2)}, u32[]{:S(2)}) collective-permute-start(bf16[256,640]{1,0:T(8,128)(2,1)} %get-tuple-element.88.panel0), channel_id=1, source_target_pairs={{0,8},{1,9},{2,10},{3,11},{4,12},{5,13},{6,14},{7,15},{8,0},{9,1},... | collective-permute-start | bytes 983048 | tf_op jit(solution)/shard_map/ppermute | solution.py:377
  71.0 19.7 %collective-permute-start.15 = (bf16[256,640]{1,0:T(8,128)(2,1)}, bf16[256,640]{1,0:T(8,128)(2,1)S(1)}, u32[]{:S(2)}, u32[]{:S(2)}) collective-permute-start(bf16[256,640]{1,0:T(8,128)(2,1)} %get-tuple-element.88.panel0), channel_id=1, source_target_pairs={{0,4},{1,5},{2,6},{3,7},{4,8},{5,9},{6,10},{7,11},{8,12},{9,13},{1... | collective-permute-start | bytes 983048 | tf_op jit(solution)/shard_map/ppermute | solution.py:377
  72.3 32.2 %collective-permute-start.16 = (bf16[304,512]{1,0:T(8,128)(2,1)}, bf16[304,512]{1,0:T(8,128)(2,1)S(1)}, u32[]{:S(2)}, u32[]{:S(2)}) collective-permute-start(bf16[304,512]{1,0:T(8,128)(2,1)} %copy-done.2), channel_id=1, source_target_pairs={{0,12},{1,13},{2,14},{3,15},{4,0},{5,1},{6,2},{7,3},{8,4},{9,5},{1... | collective-permute-start | bytes 933896 | tf_op jit(solution)/shard_map/ppermute | solution.py:377
  74.4 30.2 %collective-permute-start.17 = (bf16[304,512]{1,0:T(8,128)(2,1)}, bf16[304,512]{1,0:T(8,128)(2,1)S(1)}, u32[]{:S(2)}, u32[]{:S(2)}) collective-permute-start(bf16[304,512]{1,0:T(8,128)(2,1)} %copy-done.2), channel_id=1, source_target_pairs={{0,8},{1,9},{2,10},{3,11},{4,12},{5,13},{6,14},{7,15},{8,0},{9,1},... | collective-permute-start | bytes 933896 | tf_op jit(solution)/shard_map/ppermute | solution.py:377
  79.0 25.5 %collective-permute-start.18 = (bf16[304,512]{1,0:T(8,128)(2,1)}, bf16[304,512]{1,0:T(8,128)(2,1)S(1)}, u32[]{:S(2)}, u32[]{:S(2)}) collective-permute-start(bf16[304,512]{1,0:T(8,128)(2,1)} %copy-done.2), channel_id=1, source_target_pairs={{0,4},{1,5},{2,6},{3,7},{4,8},{5,9},{6,10},{7,11},{8,12},{9,13},{1... | collective-permute-start | bytes 933896 | tf_op jit(solution)/shard_map/ppermute | solution.py:377
  93.9 9.1 %collective-permute-start.19 = (bf16[288,512]{1,0:T(8,128)(2,1)S(1)}, bf16[288,512]{1,0:T(8,128)(2,1)S(1)}, u32[]{:S(2)}, u32[]{:S(2)}) collective-permute-start(bf16[288,512]{1,0:T(8,128)(2,1)S(1)} %get-tuple-element.93), channel_id=1, source_target_pairs={{0,16},{16,32},{32,48},{48,64},{64,80},{80,96},{96,112},{112,128},... | collective-permute-start | bytes 884744 | tf_op jit(solution)/shard_map/ppermute | solution.py:392
  104.3 6.8 %collective-permute-start.28 = (bf16[512,128]{1,0:T(8,128)(2,1)S(1)}, bf16[512,128]{1,0:T(8,128)(2,1)S(1)}, u32[]{:S(2)}, u32[]{:S(2)}) collective-permute-start(bf16[512,128]{1,0:T(8,128)(2,1)S(1)} %get-tuple-element.104), channel_id=1, source_target_pairs={{0,12},{1,13},{2,14},{3,15},{4,0},{5,1},{6,2},{7,3},{8,4},{9,5},{1... | collective-permute-start | bytes 393224 | tf_op jit(solution)/shard_map/ppermute | solution.py:377
  106.4 18.6 %collective-permute-start.20 = (bf16[256,512]{1,0:T(8,128)(2,1)S(1)}, bf16[256,512]{1,0:T(8,128)(2,1)S(1)}, u32[]{:S(2)}, u32[]{:S(2)}) collective-permute-start(bf16[256,512]{1,0:T(8,128)(2,1)S(1)} %get-tuple-element.94.block0.refs_0_.refs_1_), channel_id=1, source_target_pairs={{0,1},{1,2},{2,3},{3,0},{4,5},{5,6},{6,7},{7,4},{8,9},{9,10},{10,1... | collective-permute-start | bytes 786440 | tf_op jit(solution)/shard_map/ppermute | solution.py:372
  107.5 17.4 %collective-permute-start.21 = (bf16[256,512]{1,0:T(8,128)(2,1)S(1)}, bf16[256,512]{1,0:T(8,128)(2,1)S(1)}, u32[]{:S(2)}, u32[]{:S(2)}) collective-permute-start(bf16[256,512]{1,0:T(8,128)(2,1)S(1)} %get-tuple-element.94.block0.refs_0_.refs_1_), channel_id=1, source_target_pairs={{0,2},{1,3},{2,0},{3,1},{4,6},{5,7},{6,4},{7,5},{8,10},{9,11},{10,... | collective-permute-start | bytes 786440 | tf_op jit(solution)/shard_map/ppermute | solution.py:372
  107.6 17.4 %collective-permute-start.22 = (bf16[256,512]{1,0:T(8,128)(2,1)S(1)}, bf16[256,512]{1,0:T(8,128)(2,1)S(1)}, u32[]{:S(2)}, u32[]{:S(2)}) collective-permute-start(bf16[256,512]{1,0:T(8,128)(2,1)S(1)} %get-tuple-element.94.block0.refs_0_.refs_1_), channel_id=1, source_target_pairs={{0,3},{1,0},{2,1},{3,2},{4,7},{5,4},{6,5},{7,6},{8,11},{9,8},{10,9... | collective-permute-start | bytes 786440 | tf_op jit(solution)/shard_map/ppermute | solution.py:372
  111.1 12.0 %collective-permute-start.30 = (bf16[512,128]{1,0:T(8,128)(2,1)S(1)}, bf16[512,128]{1,0:T(8,128)(2,1)S(1)}, u32[]{:S(2)}, u32[]{:S(2)}) collective-permute-start(bf16[512,128]{1,0:T(8,128)(2,1)S(1)} %get-tuple-element.104), channel_id=1, source_target_pairs={{0,4},{1,5},{2,6},{3,7},{4,8},{5,9},{6,10},{7,11},{8,12},{9,13},{1... | collective-permute-start | bytes 393224 | tf_op jit(solution)/shard_map/ppermute | solution.py:377
  116.0 13.4 %collective-permute-start.23 = (bf16[256,256]{1,0:T(8,128)(2,1)S(1)}, bf16[256,256]{1,0:T(8,128)(2,1)S(1)}, u32[]{:S(2)}, u32[]{:S(2)}) collective-permute-start(bf16[256,256]{1,0:T(8,128)(2,1)S(1)} %get-tuple-element.95), channel_id=1, source_target_pairs={{0,16},{16,32},{32,48},{48,64},{64,80},{80,96},{96,112},{112,128},... | collective-permute-start | bytes 393224 | tf_op jit(solution)/shard_map/ppermute | solution.py:392
  123.0 6.4 %collective-permute-start.24 = (bf16[256,256]{1,0:T(8,128)(2,1)S(1)}, bf16[256,256]{1,0:T(8,128)(2,1)S(1)}, u32[]{:S(2)}, u32[]{:S(2)}) collective-permute-start(bf16[256,256]{1,0:T(8,128)(2,1)S(1)} %get-tuple-element.96), channel_id=1, source_target_pairs={{0,16},{16,32},{32,48},{48,64},{64,80},{80,96},{96,112},{112,128},... | collective-permute-start | bytes 393224 | tf_op jit(solution)/shard_map/ppermute | solution.py:392
  129.4 7.9 %collective-permute-start.33 = (bf16[512,128]{1,0:T(8,128)(2,1)S(1)}, bf16[512,128]{1,0:T(8,128)(2,1)S(1)}, u32[]{:S(2)}, u32[]{:S(2)}) collective-permute-start(bf16[512,128]{1,0:T(8,128)(2,1)S(1)} %get-tuple-element.106), channel_id=1, source_target_pairs={{0,4},{1,5},{2,6},{3,7},{4,8},{5,9},{6,10},{7,11},{8,12},{9,13},{1... | collective-permute-start | bytes 393224 | tf_op jit(solution)/shard_map/ppermute | solution.py:377
  130.0 31.7 %collective-permute-start.25 = (bf16[256,1024]{1,0:T(8,128)(2,1)S(1)}, bf16[256,1024]{1,0:T(8,128)(2,1)S(1)}, u32[]{:S(2)}, u32[]{:S(2)}) collective-permute-start(bf16[256,1024]{1,0:T(8,128)(2,1)S(1)} %shard_map.107.pair0), channel_id=1, source_target_pairs={{0,1},{1,2},{2,3},{3,0},{4,5},{5,6},{6,7},{7,4},{8,9},{9,10},{10,1... | collective-permute-start | bytes 1572872 | tf_op jit(solution)/shard_map/ppermute | solution.py:372
  130.2 31.6 %collective-permute-start.26 = (bf16[256,1024]{1,0:T(8,128)(2,1)S(1)}, bf16[256,1024]{1,0:T(8,128)(2,1)S(1)}, u32[]{:S(2)}, u32[]{:S(2)}) collective-permute-start(bf16[256,1024]{1,0:T(8,128)(2,1)S(1)} %shard_map.107.pair0), channel_id=1, source_target_pairs={{0,2},{1,3},{2,0},{3,1},{4,6},{5,7},{6,4},{7,5},{8,10},{9,11},{10,... | collective-permute-start | bytes 1572872 | tf_op jit(solution)/shard_map/ppermute | solution.py:372
  132.4 29.4 %collective-permute-start.27 = (bf16[256,1024]{1,0:T(8,128)(2,1)S(1)}, bf16[256,1024]{1,0:T(8,128)(2,1)S(1)}, u32[]{:S(2)}, u32[]{:S(2)}) collective-permute-start(bf16[256,1024]{1,0:T(8,128)(2,1)S(1)} %shard_map.107.pair0), channel_id=1, source_target_pairs={{0,3},{1,0},{2,1},{3,2},{4,7},{5,4},{6,5},{7,6},{8,11},{9,8},{10,9... | collective-permute-start | bytes 1572872 | tf_op jit(solution)/shard_map/ppermute | solution.py:372
  149.6 7.6 %collective-permute-start.37 = (bf16[512,128]{1,0:T(8,128)(2,1)S(1)}, bf16[512,128]{1,0:T(8,128)(2,1)S(1)}, u32[]{:S(2)}, u32[]{:S(2)}) collective-permute-start(bf16[512,128]{1,0:T(8,128)(2,1)S(1)} %shard_map.112.solved), channel_id=1, source_target_pairs={{0,16},{16,32},{32,48},{48,64},{64,80},{80,96},{96,112},{112,128},... | collective-permute-start | bytes 393224 | tf_op jit(solution)/shard_map/ppermute | solution.py:392
  154.2 7.5 %collective-permute-start.38 = (bf16[512,128]{1,0:T(8,128)(2,1)S(1)}, bf16[512,128]{1,0:T(8,128)(2,1)S(1)}, u32[]{:S(2)}, u32[]{:S(2)}) collective-permute-start(bf16[512,128]{1,0:T(8,128)(2,1)S(1)} %shard_map.112.solved), channel_id=1, source_target_pairs={{16,0},{32,16},{48,32},{64,48},{80,64},{96,80},{112,96},{128,112},... | collective-permute-start | bytes 393224 | tf_op jit(solution)/shard_map/ppermute | solution.py:392
  (19 other events, 98.9 us)
Sparse Core Ops, SparseCore 0:
  11.2 27.4 all-gather.4
  41.1 31.2 all-gather.6

commit v3 on v2

--- a/solution.py
+++ b/solution.py
@@ -73,7 +73,7 @@
 
 
 def prepare_kernel(s_ref, d_hbm, g_hbm, a_hbm, c_hbm, b_hbm, piece0, piece1, piece2, piece3,
-                   a_even, c_even, g0, g1, g2, g3, g_odd,
+                   a_even, c_even, g_pieces, g_odd,
                    d_ref, a_ref, c_ref, b_ref, a_first, c_first, g_first, sems):
     y, x = s_ref[0], s_ref[1]
     first_row = (y * 4 + x) * 64
@@ -143,14 +143,14 @@
             a_even[part, :, cols] = masked(a_first[part, :, cols], first_row, own, chunk, before)
             c_even[part, :, cols] = masked(c_first[part, :, cols], first_row, own, chunk, odd)
     copies[9].wait()
-    for shift, piece in enumerate((g0, g1, g2, g3)):
+    for chunk in range(4):
         for part in range(2):
-            piece[part] = g_first[part, :, at(mod4(y + shift), 256)]
+            g_pieces[chunk, part] = g_first[part, :, pl.ds(chunk * 256, 256)]
     copies[10].wait()
 
 
-def assemble_kernel(s_ref, piece0, piece1, piece2, piece3, c_even, a_next, g0, g1, g2, g3,
-                    panel, diagonal, couplings, g_columns):
+def assemble_kernel(s_ref, piece0, piece1, piece2, piece3, c_even, a_next,
+                    panel, diagonal, couplings):
     y, x = s_ref[0], s_ref[1]
     for shift, piece in enumerate((piece0, piece1, piece2, piece3)):
         rows = at(mod4(x - shift), 64)
@@ -158,8 +158,6 @@
         diagonal[rows, :] = piece[:, pl.ds(1152, 512)]
     couplings[0] = c_even[...]
     couplings[1] = a_next[...]
-    for shift, piece in enumerate((g0, g1, g2, g3)):
-        g_columns[mod4(y - shift)] = piece[...]
 
 
 def stack_rows(x, blocks, held):
@@ -227,19 +225,17 @@
 
 
 def diagonal_kernel(s_ref, c_rows, a_rows, panel0, panel1, panel2, panel3, diagonal, shipped,
-                    out, lower_real, lower_imag):
+                    out, lower):
     real, imag = wide_product(s_ref[0], c_rows, (panel0, panel1, panel2, panel3))
     real = diagonal[:, pl.ds(0, 256)].astype(F32) - real - shipped[pl.ds(0, 256), pl.ds(0, 256)].astype(F32)
     imag = diagonal[:, pl.ds(256, 256)].astype(F32) - imag - shipped[pl.ds(0, 256), pl.ds(256, 256)].astype(F32)
     put_pair(out, real, imag)
     real, imag = wide_product(s_ref[0], a_rows, (panel0, panel1, panel2, panel3))
-    lower_real[...] = (-real).astype(BF)
-    lower_imag[...] = (-imag).astype(BF)
-
-
-def pair_kernel(s_ref, lower_real, lower_imag, upper, out):
-    out[:, pl.ds(0, 256)] = lower_real[...]
-    out[:, pl.ds(256, 256)] = lower_imag[...]
+    put_pair(lower, -real, -imag)
+
+
+def pair_kernel(s_ref, lower, upper, out):
+    out[:, pl.ds(0, 512)] = lower[...]
     out[:, pl.ds(512, 512)] = upper[...]
 
 
@@ -403,9 +399,9 @@
     wide_flops = 2 * 512 * 1024 * 512
     solve_flops = 2 * 2048 * 256 * 128
 
-    *pieces, a_even, c_even, g0, g1, g2, g3, g_odd = call(
+    *pieces, a_even, c_even, g_pieces, g_odd = call(
         prepare_kernel,
-        [shape((64, 1664))] * 4 + [shape((2, 64, 1024))] * 2 + [shape((2, 64, 256))] * 4
+        [shape((64, 1664))] * 4 + [shape((2, 64, 1024))] * 2 + [shape((4, 2, 64, 256))]
         + [shape((2, 64, 1024))],
         0,
         scalars, diagonal_blocks, diagonal_inverses, lower_blocks, upper_blocks, injection,
@@ -418,12 +414,15 @@
     pieces = [pieces[0]] + [moved_x(pieces[by], by) for by in turns]
     g_rows = gathered_x(g_odd)
     a_next = along_cuts(a_even, -1)
-    g1, g2, g3 = [moved_y(piece, by) for by, piece in zip(turns, (g1, g2, g3))]
-    a_next, g1, g2, g3, *pieces = after((a_next, g1, g2, g3, *pieces))
-    panel, diagonal, couplings, g_columns = call(
+    groups = [[y * 4 + x for y in range(4)] for x in range(4)]
+    g_columns = lax.all_to_all(
+        g_pieces, "row", 0, 0, axis_index_groups=groups, tiled=True
+    )
+    a_next, g_columns, *pieces = after((a_next, g_columns, *pieces))
+    panel, diagonal, couplings = call(
         assemble_kernel,
-        [shape((256, 1152)), shape((256, 512)), shape((2, 2, 64, 1024)), shape((4, 2, 64, 256))],
-        0, scalars, *pieces, c_even, a_next, g0, g1, g2, g3,
+        [shape((256, 1152)), shape((256, 512)), shape((2, 2, 64, 1024))],
+        0, scalars, *pieces, c_even, a_next,
     )
     g_columns = gathered_x(g_columns)
     panels = gathered_y(panel)
@@ -444,8 +443,8 @@
         scalars, *ca_blocks, *firsts, panel,
     )
     shipped = along_cuts(ship, 1)
-    diagonal_new, *ship_lower = call(
-        diagonal_kernel, [shape((256, 512))] + [shape((256, 256))] * 2, 2 * wide_flops,
+    diagonal_new, ship_lower = call(
+        diagonal_kernel, [shape((256, 512))] * 2, 2 * wide_flops,
         scalars, c_rows, a_rows, *seconds, diagonal, shipped,
     )
     diagonals = [diagonal_new] + [moved_x(diagonal_new, by) for by in turns]
@@ -457,8 +456,8 @@
         scalars, g_columns, source_part, shipped, scratch=[whole],
     )
     got = gathered_y(send)[1:]
-    lower_new = [along_cuts(half, 1) for half in ship_lower]
-    (pair,) = call(pair_kernel, [shape((256, 1024))], 0, scalars, *lower_new, upper_new)
+    lower_new = along_cuts(ship_lower, 1)
+    (pair,) = call(pair_kernel, [shape((256, 1024))], 0, scalars, lower_new, upper_new)
     pairs = [pair] + [moved_x(pair, by) for by in turns]
     solved = ()
     for turn in range(REFINE):

time: 179 us -> 179 us (level)
  waiting for transfers between devices: 73.1 us -> 60.9 us
  blocking collectives: 0 us -> 9.62 us
  starting transfers between devices: 62.8 us -> 67 us
    ppermute x21 -> x18, waiting for transfers between devices: 64.3 us -> 45.1 us  [moved_y(): return lax.ppermute(block, 'row', pairs)]
    all_to_all x0 -> x1, blocking collectives: none -> 9.62 us  [body(): lax.all_to_all(g_pieces, 'row', 0, 0, axis_index_groups=groups, tiled=True)]
    ppermute x15, starting transfers between devices: 17.1 us -> 20.8 us  [moved_x(): return lax.ppermute(block, 'row', pairs)]
    ppermute x15, waiting for transfers between devices: 0.04 us -> 3.34 us  [moved_x(): return lax.ppermute(block, 'row', pairs)]
    all_gather x2, waiting for transfers between devices: 0.47 us -> 3.28 us  [gathered_x(): return lax.all_gather(block, 'row', axis_index_groups=groups)]
    ppermute x6 -> x5, starting transfers between devices: 24.5 us -> 26.9 us  [along_cuts(): return lax.ppermute(block, 'cuts', pairs)]
    ppermute x21 -> x18, starting transfers between devices: 21.1 us -> 19.3 us  [moved_y(): return lax.ppermute(block, 'row', pairs)]
    ppermute x6 -> x5, waiting for transfers between devices: 8.17 us -> 9.21 us  [along_cuts(): return lax.ppermute(block, 'cuts', pairs)]
  transfers between devices with their start and end apart: 44 -> 40, of which waited for: 17 -> 15; matrix products, arithmetic and copies ran while one was open for 0% -> 0% of each run, Pallas kernels for 10% -> 10%
where the time goes in v3:
time: 179 us
  starting transfers between devices  67 us (37%)
  waiting for transfers between devices  60.9 us (34%)
  Pallas kernels  23.1 us (13%)
  between operations  14.3 us (8%)
  blocking collectives  9.62 us (5%)
  local copies, waits for them, and re-layouts  3.37 us (2%)
    ppermute x18, waiting for transfers between devices, moved_y(): return lax.ppermute(block, 'row', pairs)  45.1 us
    ppermute x5, starting transfers between devices, along_cuts(): return lax.ppermute(block, 'cuts', pairs)  26.9 us
    pallas_call x14, Pallas kernels, call(): pl.pallas_call(kernel, out_shape=tuple(out_shapes), in_specs=[SMEM] + [an...  23.1 us
    ppermute x15, starting transfers between devices, moved_x(): return lax.ppermute(block, 'row', pairs)  20.8 us
    ppermute x18, starting transfers between devices, moved_y(): return lax.ppermute(block, 'row', pairs)  19.3 us
    all_to_all x1, blocking collectives, body(): lax.all_to_all(g_pieces, 'row', 0, 0, axis_index_groups=groups, tiled=True)  9.62 us
    ppermute x5, waiting for transfers between devices, along_cuts(): return lax.ppermute(block, 'cuts', pairs)  9.21 us
  transfers between devices with their start and end apart: 40, of which 15 were waited for; matrix products, arithmetic and copies ran while one was open for 0% of the time, Pallas kernels for 10%

profile of v3, /device:TPU:97, one launch (start us, length us, event | category | flops | bytes accessed | tf_op | source)
XLA Modules:
  0.0 178.5 jit_solution(10107298332593065061)
XLA Ops:
  8.1 2.9 %shard_map.101 = (bf16[64,1664]{1,0:T(8,128)(2,1)S(1)}, bf16[64,1664]{1,0:T(8,128)(2,1)S(1)}, bf16[64,1664]{1,0:T(8,128)(2,1)S(1)}, bf16[64,1664]{1,0:T(8,128)(2...) custom-call(s32[6]{0:T(128)S(1)} %pad_add_fusion.1.s_ref, ...), custom_call_target="tpu_custom_call" | custom-call | bytes 4063256 | tf_op jit(solution)/shard_map/pallas_call | solution.py:27
  11.1 2.6 %collective-permute-start = (bf16[2,64,1024]{2,1,0:T(8,128)(2,1)S(1)}, bf16[2,64,1024]{2,1,0:T(8,128)(2,1)S(1)}, u32[]{:S(2)}, u32[]{:S(2)}) collective-permute-start(bf16[2,64,1024]{2,1,0:T(8,128)(2,1)S(1)} %get-tuple-element.55), channel_id=1, source_target_pairs={{16,0},{32,16},{48,32},{64,48},{80,64},{96,80},{112,96},{128,112},... | collective-permute-start | bytes 786440 | tf_op jit(solution)/shard_map/ppermute | solution.py:388
  15.0 2.5 %collective-permute-start.2 = (bf16[64,1664]{1,0:T(8,128)(2,1)S(1)}, bf16[64,1664]{1,0:T(8,128)(2,1)S(1)}, u32[]{:S(2)}, u32[]{:S(2)}) collective-permute-start(bf16[64,1664]{1,0:T(8,128)(2,1)S(1)} %get-tuple-element.59), channel_id=1, source_target_pairs={{0,2},{1,3},{2,0},{3,1},{4,6},{5,7},{6,4},{7,5},{8,10},{9,11},{10,... | collective-permute-start | bytes 638984 | tf_op jit(solution)/shard_map/ppermute | solution.py:368
  18.6 9.6 %all_to_all.5 = bf16[4,2,64,256]{3,2,1,0:T(8,128)(2,1)} all-to-all(bf16[4,2,64,256]{3,2,1,0:T(8,128)(2,1)S(1)} %get-tuple-element.56), channel_id=1, replica_groups={{0,4,8,12},{1,5,9,13},{2,6,10,14},{3,7,11,15},{16,20,24,28},{17,21,25,2..., dimensions={0} | all-to-all | bytes 524288 | tf_op jit(solution)/shard_map/all_to_all | solution.py:418
  29.6 2.0 %collective-permute-start.4 = (bf16[256,1152]{1,0:T(8,128)(2,1)S(1)}, bf16[256,1152]{1,0:T(8,128)(2,1)S(1)}, u32[]{:S(2)}, u32[]{:S(2)}) collective-permute-start(bf16[256,1152]{1,0:T(8,128)(2,1)S(1)} %get-tuple-element.67.panel0.source), channel_id=1, source_target_pairs={{0,12},{1,13},{2,14},{3,15},{4,0},{5,1},{6,2},{7,3},{8,4},{9,5},{1... | collective-permute-start | bytes 1769480 | tf_op jit(solution)/shard_map/ppermute | solution.py:373
  33.3 2.8 %collective-permute-start.8 = (bf16[2,2,64,1024]{3,2,1,0:T(8,128)(2,1)S(1)}, bf16[2,2,64,1024]{3,2,1,0:T(8,128)(2,1)}, u32[]{:S(2)}, u32[]{:S(2)}) collective-permute-start(bf16[2,2,64,1024]{3,2,1,0:T(8,128)(2,1)S(1)} %get-tuple-element.71.ca0), channel_id=1, source_target_pairs={{0,2},{1,3},{2,0},{3,1},{4,6},{5,7},{6,4},{7,5},{8,10},{9,11},{10,... | collective-permute-start | bytes 1572872 | tf_op jit(solution)/shard_map/ppermute | solution.py:368
  36.1 8.5 %collective-permute-done.4.panel1 = bf16[256,1152]{1,0:T(8,128)(2,1)S(1)} collective-permute-done((bf16[256,1152]{1,0:T(8,128)(2,1)S(1)}, bf16[256,1152]{1,0:T(8,128)(2,1)S(1)}, u32[]{:S(2)}, u32[]{:S(2)}) %collective-permute-start.4) | collective-permute-done | bytes 589856 | tf_op jit(solution)/shard_map/ppermute | solution.py:373
  44.6 1.9 %collective-permute-start.9 = (bf16[2,2,64,1024]{3,2,1,0:T(8,128)(2,1)S(1)}, bf16[2,2,64,1024]{3,2,1,0:T(8,128)(2,1)}, u32[]{:S(2)}, u32[]{:S(2)}) collective-permute-start(bf16[2,2,64,1024]{3,2,1,0:T(8,128)(2,1)S(1)} %get-tuple-element.71.ca0), channel_id=1, source_target_pairs={{0,3},{1,0},{2,1},{3,2},{4,7},{5,4},{6,5},{7,6},{8,11},{9,8},{10,9... | collective-permute-start | bytes 1572872 | tf_op jit(solution)/shard_map/ppermute | solution.py:368
  46.6 14.4 %collective-permute-done.6.panel3 = bf16[256,1152]{1,0:T(8,128)(2,1)S(1)} collective-permute-done((bf16[256,1152]{1,0:T(8,128)(2,1)S(1)}, bf16[256,1152]{1,0:T(8,128)(2,1)S(1)}, u32[]{:S(2)}, u32[]{:S(2)}) %collective-permute-start.6) | collective-permute-done | bytes 589856 | tf_op jit(solution)/shard_map/ppermute | solution.py:373
  62.3 3.0 %shard_map.103 = (bf16[256,640]{1,0:T(8,128)(2,1)}, bf16[304,512]{1,0:T(8,128)(2,1)S(1)}) custom-call(s32[6]{0:T(128)S(1)} %pad_add_fusion.1.s_ref, bf16[4,2,64,1024]{3,2,1,0:T(8,128)(2,1)S(1)} %bitcast.12, bf16[256,1152]{1,0:T(8,128)(2,1)S(1)} %get-tuple-element.67.panel0.source, bf16[256,1152]{1,0:T(8,128)(2,1)S(1)} %collective-permute-done.4.panel1, ...), custom_call_target="tpu_custom_call" | custom-call | bytes 4046872 | tf_op jit(solution)/shard_map/pallas_call | solution.py:27
  67.4 3.3 %all-gather.7.cloned.1.call-done = bf16[16,2,64,256]{3,2,1,0:T(8,128)(2,1)} async-done(((bf16[4,2,64,256]{3,2,1,0:T(8,128)(2,1)}), bf16[16,2,64,256]{3,2,1,0:T(8,128)(2,1)}) %all-gather.7.cloned.1.call-update) | async-done | bytes 1048592 | tf_op jit(solution)/shard_map/all_gather | solution.py:382
  70.7 6.5 %collective-permute-start.13 = (bf16[304,512]{1,0:T(8,128)(2,1)}, bf16[304,512]{1,0:T(8,128)(2,1)S(1)}, u32[]{:S(2)}, u32[]{:S(2)}) collective-permute-start(bf16[304,512]{1,0:T(8,128)(2,1)} %copy-done.2), channel_id=1, source_target_pairs={{0,12},{1,13},{2,14},{3,15},{4,0},{5,1},{6,2},{7,3},{8,4},{9,5},{1... | collective-permute-start | bytes 933896 | tf_op jit(solution)/shard_map/ppermute | solution.py:373
  77.8 9.9 %collective-permute-done.12.panel3 = bf16[256,640]{1,0:T(8,128)(2,1)S(1)} collective-permute-done((bf16[256,640]{1,0:T(8,128)(2,1)}, bf16[256,640]{1,0:T(8,128)(2,1)S(1)}, u32[]{:S(2)}, u32[]{:S(2)}) %collective-permute-start.12) | collective-permute-done | bytes 327712 | tf_op jit(solution)/shard_map/ppermute | solution.py:373
  87.7 3.2 %shard_map.104 = (bf16[288,512]{1,0:T(8,128)(2,1)S(1)}, bf16[256,512]{1,0:T(8,128)(2,1)S(1)}, f32[256,128]{1,0:T(8,128)S(1)}, bf16[512,1024]{1,0:T(8,128)(2,1)S(1)}, bf16[512,1024]{1,0:T(8,128)(2,1)S(1)}) custom-call(s32[6]{0:T(128)S(1)} %pad_add_fusion.1.s_ref, bf16[2,2,64,1024]{3,2,1,0:T(8,128)(2,1)S(1)} %get-tuple-element.71.ca0, ...), custom_call_target="tpu_custom_call" | custom-call | bytes 6783000 | tf_op jit(solution)/shard_map/pallas_call | solution.py:27
  90.9 7.7 %collective-permute-start.16 = (bf16[288,512]{1,0:T(8,128)(2,1)S(1)}, bf16[288,512]{1,0:T(8,128)(2,1)S(1)}, u32[]{:S(2)}, u32[]{:S(2)}) collective-permute-start(bf16[288,512]{1,0:T(8,128)(2,1)S(1)} %get-tuple-element.80), channel_id=1, source_target_pairs={{0,16},{16,32},{32,48},{48,64},{64,80},{80,96},{96,112},{112,128},... | collective-permute-start | bytes 884744 | tf_op jit(solution)/shard_map/ppermute | solution.py:388
  98.6 3.6 %collective-permute-done.16.shipped = bf16[288,512]{1,0:T(8,128)(2,1)S(1)} collective-permute-done((bf16[288,512]{1,0:T(8,128)(2,1)S(1)}, bf16[288,512]{1,0:T(8,128)(2,1)S(1)}, u32[]{:S(2)}, u32[]{:S(2)}) %collective-permute-start.16) | collective-permute-done | bytes 294944 | tf_op jit(solution)/shard_map/ppermute | solution.py:388
  103.7 1.8 %shard_map.105 = (bf16[256,512]{1,0:T(8,128)(2,1)S(1)}, bf16[256,512]{1,0:T(8,128)(2,1)S(1)}) custom-call(s32[6]{0:T(128)S(1)} %pad_add_fusion.1.s_ref, bf16[512,1024]{1,0:T(8,128)(2,1)S(1)} %get-tuple-element.76.c_rows, bf16[512,1024]{1,0:T(8,128)(2,1)S(1)} %get-tuple-element.77.a_rows, bf16[304,512]{1,0:T(8,128)(2,1)S(1)} %copy-done.3, ...), custom_call_target="tpu_custom_call" | custom-call | bytes 4423704 | tf_op jit(solution)/shard_map/pallas_call | solution.py:27
  105.7 2.6 %collective-permute-start.19 = (bf16[256,512]{1,0:T(8,128)(2,1)S(1)}, bf16[256,512]{1,0:T(8,128)(2,1)S(1)}, u32[]{:S(2)}, u32[]{:S(2)}) collective-permute-start(bf16[256,512]{1,0:T(8,128)(2,1)S(1)} %get-tuple-element.81.block0.refs_0_.refs_1_), channel_id=1, source_target_pairs={{0,3},{1,0},{2,1},{3,2},{4,7},{5,4},{6,5},{7,6},{8,11},{9,8},{10,9... | collective-permute-start | bytes 786440 | tf_op jit(solution)/shard_map/ppermute | solution.py:368
  109.7 6.7 %collective-permute-start.20 = (bf16[256,512]{1,0:T(8,128)(2,1)S(1)}, bf16[256,512]{1,0:T(8,128)(2,1)S(1)}, u32[]{:S(2)}, u32[]{:S(2)}) collective-permute-start(bf16[256,512]{1,0:T(8,128)(2,1)S(1)} %get-tuple-element.82), channel_id=1, source_target_pairs={{0,16},{16,32},{32,48},{48,64},{64,80},{80,96},{96,112},{112,128},... | collective-permute-start | bytes 786440 | tf_op jit(solution)/shard_map/ppermute | solution.py:388
  116.4 2.4 %collective-permute-done.17.block1.refs_1_.refs_2_ = bf16[256,512]{1,0:T(8,128)(2,1)S(1)} collective-permute-done((bf16[256,512]{1,0:T(8,128)(2,1)S(1)}, bf16[256,512]{1,0:T(8,128)(2,1)S(1)}, u32[]{:S(2)}, u32[]{:S(2)}) %collective-permute-start.17) | collective-permute-done | bytes 262176 | tf_op jit(solution)/shard_map/ppermute | solution.py:368
  119.7 1.8 %shard_map.110 = (bf16[512,128]{1,0:T(8,128)(2,1)S(1)}, f32[512,128]{1,0:T(8,128)S(1)}, bf16[512,128]{1,0:T(8,128)(2,1)S(1)}) custom-call(s32[6]{0:T(128)S(1)} %pad_add_fusion.1.s_ref, f32[512,128]{1,0:T(8,128)S(1)} %get-tuple-element.89.own, bf16[512,128]{1,0:T(8,128)(2,1)S(1)} %collective-permute-done.24.got1, ...), custom_call_target="tpu_custom_call" | custom-call | bytes 3342360 | tf_op jit(solution)/shard_map/pallas_call | solution.py:27
  121.5 3.9 %collective-permute-start.27 = (bf16[512,128]{1,0:T(8,128)(2,1)S(1)}, bf16[512,128]{1,0:T(8,128)(2,1)S(1)}, u32[]{:S(2)}, u32[]{:S(2)}) collective-permute-start(bf16[512,128]{1,0:T(8,128)(2,1)S(1)} %get-tuple-element.92), channel_id=1, source_target_pairs={{0,12},{1,13},{2,14},{3,15},{4,0},{5,1},{6,2},{7,3},{8,4},{9,5},{1... | collective-permute-start | bytes 393224 | tf_op jit(solution)/shard_map/ppermute | solution.py:373
  126.8 3.2 %collective-permute-start.22 = (bf16[256,1024]{1,0:T(8,128)(2,1)S(1)}, bf16[256,1024]{1,0:T(8,128)(2,1)S(1)}, u32[]{:S(2)}, u32[]{:S(2)}) collective-permute-start(bf16[256,1024]{1,0:T(8,128)(2,1)S(1)} %shard_map.107.pair0), channel_id=1, source_target_pairs={{0,2},{1,3},{2,0},{3,1},{4,6},{5,7},{6,4},{7,5},{8,10},{9,11},{10,... | collective-permute-start | bytes 1572872 | tf_op jit(solution)/shard_map/ppermute | solution.py:368
  133.1 1.7 collective-permute-done.29.got3
  134.8 1.8 %shard_map.111 = (bf16[512,128]{1,0:T(8,128)(2,1)S(1)}, f32[512,128]{1,0:T(8,128)S(1)}, bf16[512,128]{1,0:T(8,128)(2,1)S(1)}) custom-call(s32[6]{0:T(128)S(1)} %pad_add_fusion.1.s_ref, f32[512,128]{1,0:T(8,128)S(1)} %get-tuple-element.91.own, bf16[512,128]{1,0:T(8,128)(2,1)S(1)} %collective-permute-done.27.got1, ...), custom_call_target="tpu_custom_call" | custom-call | bytes 3473432 | tf_op jit(solution)/shard_map/pallas_call | solution.py:27
  136.6 1.8 %collective-permute-start.30 = (bf16[512,128]{1,0:T(8,128)(2,1)S(1)}, bf16[512,128]{1,0:T(8,128)(2,1)S(1)}, u32[]{:S(2)}, u32[]{:S(2)}) collective-permute-start(bf16[512,128]{1,0:T(8,128)(2,1)S(1)} %get-tuple-element.95), channel_id=1, source_target_pairs={{0,12},{1,13},{2,14},{3,15},{4,0},{5,1},{6,2},{7,3},{8,4},{9,5},{1... | collective-permute-start | bytes 393224 | tf_op jit(solution)/shard_map/ppermute | solution.py:373
  138.4 2.8 %collective-permute-done.30.got1 = bf16[512,128]{1,0:T(8,128)(2,1)S(1)} collective-permute-done((bf16[512,128]{1,0:T(8,128)(2,1)S(1)}, bf16[512,128]{1,0:T(8,128)(2,1)S(1)}, u32[]{:S(2)}, u32[]{:S(2)}) %collective-permute-start.30) | collective-permute-done | bytes 131104 | tf_op jit(solution)/shard_map/ppermute | solution.py:373
  141.3 2.8 %collective-permute-done.31.got2 = bf16[512,128]{1,0:T(8,128)(2,1)S(1)} collective-permute-done((bf16[512,128]{1,0:T(8,128)(2,1)S(1)}, bf16[512,128]{1,0:T(8,128)(2,1)S(1)}, u32[]{:S(2)}, u32[]{:S(2)}) %collective-permute-start.31) | collective-permute-done | bytes 131104 | tf_op jit(solution)/shard_map/ppermute | solution.py:373
  144.1 3.3 %collective-permute-done.32.got3 = bf16[512,128]{1,0:T(8,128)(2,1)S(1)} collective-permute-done((bf16[512,128]{1,0:T(8,128)(2,1)S(1)}, bf16[512,128]{1,0:T(8,128)(2,1)S(1)}, u32[]{:S(2)}, u32[]{:S(2)}) %collective-permute-start.32) | collective-permute-done | bytes 131104 | tf_op jit(solution)/shard_map/ppermute | solution.py:373
  148.0 7.9 %collective-permute-start.33 = (bf16[512,128]{1,0:T(8,128)(2,1)S(1)}, bf16[512,128]{1,0:T(8,128)(2,1)S(1)}, u32[]{:S(2)}, u32[]{:S(2)}) collective-permute-start(bf16[512,128]{1,0:T(8,128)(2,1)S(1)} %shard_map.112.solved), channel_id=1, source_target_pairs={{0,16},{16,32},{32,48},{48,64},{64,80},{80,96},{96,112},{112,128},... | collective-permute-start | bytes 393224 | tf_op jit(solution)/shard_map/ppermute | solution.py:388
  155.9 1.9 %collective-permute-start.34 = (bf16[512,128]{1,0:T(8,128)(2,1)S(1)}, bf16[512,128]{1,0:T(8,128)(2,1)S(1)}, u32[]{:S(2)}, u32[]{:S(2)}) collective-permute-start(bf16[512,128]{1,0:T(8,128)(2,1)S(1)} %shard_map.112.solved), channel_id=1, source_target_pairs={{16,0},{32,16},{48,32},{64,48},{80,64},{96,80},{112,96},{128,112},... | collective-permute-start | bytes 393224 | tf_op jit(solution)/shard_map/ppermute | solution.py:388
  157.8 5.6 %collective-permute-done.34.above = bf16[512,128]{1,0:T(8,128)(2,1)S(1)} collective-permute-done((bf16[512,128]{1,0:T(8,128)(2,1)S(1)}, bf16[512,128]{1,0:T(8,128)(2,1)S(1)}, u32[]{:S(2)}, u32[]{:S(2)}) %collective-permute-start.34) | collective-permute-done | bytes 131104 | tf_op jit(solution)/shard_map/ppermute | solution.py:388
  (82 shorter events, 27.8 us)
Async XLA Ops:
  7.2 53.9 %all-gather.5.cloned.1.call-start = ((), (), s32[]{:S(2)}) async-start(), calls=%async_computation.1 | async-start | bytes 1310720 | tf_op jit(solution)/shard_map/all_gather | solution.py:382
  11.1 59.7 %all-gather.7.cloned.1.call-start = ((), (), s32[]{:S(2)}) async-start(), calls=%async_computation.2 | async-start | bytes 1310720 | tf_op jit(solution)/shard_map/all_gather | solution.py:382
  11.1 17.1 %collective-permute-start = (bf16[2,64,1024]{2,1,0:T(8,128)(2,1)S(1)}, bf16[2,64,1024]{2,1,0:T(8,128)(2,1)S(1)}, u32[]{:S(2)}, u32[]{:S(2)}) collective-permute-start(bf16[2,64,1024]{2,1,0:T(8,128)(2,1)S(1)} %get-tuple-element.55), channel_id=1, source_target_pairs={{16,0},{32,16},{48,32},{64,48},{80,64},{96,80},{112,96},{128,112},... | collective-permute-start | bytes 786440 | tf_op jit(solution)/shard_map/ppermute | solution.py:388
  13.7 14.5 %collective-permute-start.1 = (bf16[64,1664]{1,0:T(8,128)(2,1)S(1)}, bf16[64,1664]{1,0:T(8,128)(2,1)S(1)}, u32[]{:S(2)}, u32[]{:S(2)}) collective-permute-start(bf16[64,1664]{1,0:T(8,128)(2,1)S(1)} %get-tuple-element.58), channel_id=1, source_target_pairs={{0,1},{1,2},{2,3},{3,0},{4,5},{5,6},{6,7},{7,4},{8,9},{9,10},{10,1... | collective-permute-start | bytes 638984 | tf_op jit(solution)/shard_map/ppermute | solution.py:368
  15.0 13.2 %collective-permute-start.2 = (bf16[64,1664]{1,0:T(8,128)(2,1)S(1)}, bf16[64,1664]{1,0:T(8,128)(2,1)S(1)}, u32[]{:S(2)}, u32[]{:S(2)}) collective-permute-start(bf16[64,1664]{1,0:T(8,128)(2,1)S(1)} %get-tuple-element.59), channel_id=1, source_target_pairs={{0,2},{1,3},{2,0},{3,1},{4,6},{5,7},{6,4},{7,5},{8,10},{9,11},{10,... | collective-permute-start | bytes 638984 | tf_op jit(solution)/shard_map/ppermute | solution.py:368
  17.4 10.8 %collective-permute-start.3 = (bf16[64,1664]{1,0:T(8,128)(2,1)S(1)}, bf16[64,1664]{1,0:T(8,128)(2,1)S(1)}, u32[]{:S(2)}, u32[]{:S(2)}) collective-permute-start(bf16[64,1664]{1,0:T(8,128)(2,1)S(1)} %get-tuple-element.60), channel_id=1, source_target_pairs={{0,3},{1,0},{2,1},{3,2},{4,7},{5,4},{6,5},{7,6},{8,11},{9,8},{10,9... | collective-permute-start | bytes 638984 | tf_op jit(solution)/shard_map/ppermute | solution.py:368
  29.6 15.0 %collective-permute-start.4 = (bf16[256,1152]{1,0:T(8,128)(2,1)S(1)}, bf16[256,1152]{1,0:T(8,128)(2,1)S(1)}, u32[]{:S(2)}, u32[]{:S(2)}) collective-permute-start(bf16[256,1152]{1,0:T(8,128)(2,1)S(1)} %get-tuple-element.67.panel0.source), channel_id=1, source_target_pairs={{0,12},{1,13},{2,14},{3,15},{4,0},{5,1},{6,2},{7,3},{8,4},{9,5},{1... | collective-permute-start | bytes 1769480 | tf_op jit(solution)/shard_map/ppermute | solution.py:373
  31.6 15.0 %collective-permute-start.5 = (bf16[256,1152]{1,0:T(8,128)(2,1)S(1)}, bf16[256,1152]{1,0:T(8,128)(2,1)S(1)}, u32[]{:S(2)}, u32[]{:S(2)}) collective-permute-start(bf16[256,1152]{1,0:T(8,128)(2,1)S(1)} %get-tuple-element.67.panel0.source), channel_id=1, source_target_pairs={{0,8},{1,9},{2,10},{3,11},{4,12},{5,13},{6,14},{7,15},{8,0},{9,1},... | collective-permute-start | bytes 1769480 | tf_op jit(solution)/shard_map/ppermute | solution.py:373
  31.9 29.2 %collective-permute-start.6 = (bf16[256,1152]{1,0:T(8,128)(2,1)S(1)}, bf16[256,1152]{1,0:T(8,128)(2,1)S(1)}, u32[]{:S(2)}, u32[]{:S(2)}) collective-permute-start(bf16[256,1152]{1,0:T(8,128)(2,1)S(1)} %get-tuple-element.67.panel0.source), channel_id=1, source_target_pairs={{0,4},{1,5},{2,6},{3,7},{4,8},{5,9},{6,10},{7,11},{8,12},{9,13},{1... | collective-permute-start | bytes 1769480 | tf_op jit(solution)/shard_map/ppermute | solution.py:373
  32.6 34.2 %collective-permute-start.7 = (bf16[2,2,64,1024]{3,2,1,0:T(8,128)(2,1)S(1)}, bf16[2,2,64,1024]{3,2,1,0:T(8,128)(2,1)S(1)}, u32[]{:S(2)}, u32[]{:S(2)}) collective-permute-start(bf16[2,2,64,1024]{3,2,1,0:T(8,128)(2,1)S(1)} %get-tuple-element.71.ca0), channel_id=1, source_target_pairs={{0,1},{1,2},{2,3},{3,0},{4,5},{5,6},{6,7},{7,4},{8,9},{9,10},{10,1... | collective-permute-start | bytes 1572872 | tf_op jit(solution)/shard_map/ppermute | solution.py:368
  33.3 34.2 %collective-permute-start.8 = (bf16[2,2,64,1024]{3,2,1,0:T(8,128)(2,1)S(1)}, bf16[2,2,64,1024]{3,2,1,0:T(8,128)(2,1)}, u32[]{:S(2)}, u32[]{:S(2)}) collective-permute-start(bf16[2,2,64,1024]{3,2,1,0:T(8,128)(2,1)S(1)} %get-tuple-element.71.ca0), channel_id=1, source_target_pairs={{0,2},{1,3},{2,0},{3,1},{4,6},{5,7},{6,4},{7,5},{8,10},{9,11},{10,... | collective-permute-start | bytes 1572872 | tf_op jit(solution)/shard_map/ppermute | solution.py:368
  44.6 22.8 %collective-permute-start.9 = (bf16[2,2,64,1024]{3,2,1,0:T(8,128)(2,1)S(1)}, bf16[2,2,64,1024]{3,2,1,0:T(8,128)(2,1)}, u32[]{:S(2)}, u32[]{:S(2)}) collective-permute-start(bf16[2,2,64,1024]{3,2,1,0:T(8,128)(2,1)S(1)} %get-tuple-element.71.ca0), channel_id=1, source_target_pairs={{0,3},{1,0},{2,1},{3,2},{4,7},{5,4},{6,5},{7,6},{8,11},{9,8},{10,9... | collective-permute-start | bytes 1572872 | tf_op jit(solution)/shard_map/ppermute | solution.py:368
  66.0 11.2 %collective-permute-start.10 = (bf16[256,640]{1,0:T(8,128)(2,1)}, bf16[256,640]{1,0:T(8,128)(2,1)S(1)}, u32[]{:S(2)}, u32[]{:S(2)}) collective-permute-start(bf16[256,640]{1,0:T(8,128)(2,1)} %get-tuple-element.75.panel0), channel_id=1, source_target_pairs={{0,12},{1,13},{2,14},{3,15},{4,0},{5,1},{6,2},{7,3},{8,4},{9,5},{1... | collective-permute-start | bytes 983048 | tf_op jit(solution)/shard_map/ppermute | solution.py:373
  66.8 11.0 %collective-permute-start.11 = (bf16[256,640]{1,0:T(8,128)(2,1)}, bf16[256,640]{1,0:T(8,128)(2,1)S(1)}, u32[]{:S(2)}, u32[]{:S(2)}) collective-permute-start(bf16[256,640]{1,0:T(8,128)(2,1)} %get-tuple-element.75.panel0), channel_id=1, source_target_pairs={{0,8},{1,9},{2,10},{3,11},{4,12},{5,13},{6,14},{7,15},{8,0},{9,1},... | collective-permute-start | bytes 983048 | tf_op jit(solution)/shard_map/ppermute | solution.py:373
  66.8 20.9 %collective-permute-start.12 = (bf16[256,640]{1,0:T(8,128)(2,1)}, bf16[256,640]{1,0:T(8,128)(2,1)S(1)}, u32[]{:S(2)}, u32[]{:S(2)}) collective-permute-start(bf16[256,640]{1,0:T(8,128)(2,1)} %get-tuple-element.75.panel0), channel_id=1, source_target_pairs={{0,4},{1,5},{2,6},{3,7},{4,8},{5,9},{6,10},{7,11},{8,12},{9,13},{1... | collective-permute-start | bytes 983048 | tf_op jit(solution)/shard_map/ppermute | solution.py:373
  70.7 33.0 %collective-permute-start.13 = (bf16[304,512]{1,0:T(8,128)(2,1)}, bf16[304,512]{1,0:T(8,128)(2,1)S(1)}, u32[]{:S(2)}, u32[]{:S(2)}) collective-permute-start(bf16[304,512]{1,0:T(8,128)(2,1)} %copy-done.2), channel_id=1, source_target_pairs={{0,12},{1,13},{2,14},{3,15},{4,0},{5,1},{6,2},{7,3},{8,4},{9,5},{1... | collective-permute-start | bytes 933896 | tf_op jit(solution)/shard_map/ppermute | solution.py:373
  77.2 26.5 %collective-permute-start.14 = (bf16[304,512]{1,0:T(8,128)(2,1)}, bf16[304,512]{1,0:T(8,128)(2,1)S(1)}, u32[]{:S(2)}, u32[]{:S(2)}) collective-permute-start(bf16[304,512]{1,0:T(8,128)(2,1)} %copy-done.2), channel_id=1, source_target_pairs={{0,8},{1,9},{2,10},{3,11},{4,12},{5,13},{6,14},{7,15},{8,0},{9,1},... | collective-permute-start | bytes 933896 | tf_op jit(solution)/shard_map/ppermute | solution.py:373
  77.2 26.5 %collective-permute-start.15 = (bf16[304,512]{1,0:T(8,128)(2,1)}, bf16[304,512]{1,0:T(8,128)(2,1)S(1)}, u32[]{:S(2)}, u32[]{:S(2)}) collective-permute-start(bf16[304,512]{1,0:T(8,128)(2,1)} %copy-done.2), channel_id=1, source_target_pairs={{0,4},{1,5},{2,6},{3,7},{4,8},{5,9},{6,10},{7,11},{8,12},{9,13},{1... | collective-permute-start | bytes 933896 | tf_op jit(solution)/shard_map/ppermute | solution.py:373
  90.9 11.4 %collective-permute-start.16 = (bf16[288,512]{1,0:T(8,128)(2,1)S(1)}, bf16[288,512]{1,0:T(8,128)(2,1)S(1)}, u32[]{:S(2)}, u32[]{:S(2)}) collective-permute-start(bf16[288,512]{1,0:T(8,128)(2,1)S(1)} %get-tuple-element.80), channel_id=1, source_target_pairs={{0,16},{16,32},{32,48},{48,64},{64,80},{80,96},{96,112},{112,128},... | collective-permute-start | bytes 884744 | tf_op jit(solution)/shard_map/ppermute | solution.py:388
  105.5 13.2 %collective-permute-start.17 = (bf16[256,512]{1,0:T(8,128)(2,1)S(1)}, bf16[256,512]{1,0:T(8,128)(2,1)S(1)}, u32[]{:S(2)}, u32[]{:S(2)}) collective-permute-start(bf16[256,512]{1,0:T(8,128)(2,1)S(1)} %get-tuple-element.81.block0.refs_0_.refs_1_), channel_id=1, source_target_pairs={{0,1},{1,2},{2,3},{3,0},{4,5},{5,6},{6,7},{7,4},{8,9},{9,10},{10,1... | collective-permute-start | bytes 786440 | tf_op jit(solution)/shard_map/ppermute | solution.py:368
  105.6 13.2 %collective-permute-start.18 = (bf16[256,512]{1,0:T(8,128)(2,1)S(1)}, bf16[256,512]{1,0:T(8,128)(2,1)S(1)}, u32[]{:S(2)}, u32[]{:S(2)}) collective-permute-start(bf16[256,512]{1,0:T(8,128)(2,1)S(1)} %get-tuple-element.81.block0.refs_0_.refs_1_), channel_id=1, source_target_pairs={{0,2},{1,3},{2,0},{3,1},{4,6},{5,7},{6,4},{7,5},{8,10},{9,11},{10,... | collective-permute-start | bytes 786440 | tf_op jit(solution)/shard_map/ppermute | solution.py:368
  105.7 14.0 %collective-permute-start.19 = (bf16[256,512]{1,0:T(8,128)(2,1)S(1)}, bf16[256,512]{1,0:T(8,128)(2,1)S(1)}, u32[]{:S(2)}, u32[]{:S(2)}) collective-permute-start(bf16[256,512]{1,0:T(8,128)(2,1)S(1)} %get-tuple-element.81.block0.refs_0_.refs_1_), channel_id=1, source_target_pairs={{0,3},{1,0},{2,1},{3,2},{4,7},{5,4},{6,5},{7,6},{8,11},{9,8},{10,9... | collective-permute-start | bytes 786440 | tf_op jit(solution)/shard_map/ppermute | solution.py:368
  108.4 8.0 %collective-permute-start.26 = (bf16[512,128]{1,0:T(8,128)(2,1)S(1)}, bf16[512,128]{1,0:T(8,128)(2,1)S(1)}, u32[]{:S(2)}, u32[]{:S(2)}) collective-permute-start(bf16[512,128]{1,0:T(8,128)(2,1)S(1)} %get-tuple-element.90), channel_id=1, source_target_pairs={{0,4},{1,5},{2,6},{3,7},{4,8},{5,9},{6,10},{7,11},{8,12},{9,13},{1... | collective-permute-start | bytes 393224 | tf_op jit(solution)/shard_map/ppermute | solution.py:373
  109.7 16.4 %collective-permute-start.20 = (bf16[256,512]{1,0:T(8,128)(2,1)S(1)}, bf16[256,512]{1,0:T(8,128)(2,1)S(1)}, u32[]{:S(2)}, u32[]{:S(2)}) collective-permute-start(bf16[256,512]{1,0:T(8,128)(2,1)S(1)} %get-tuple-element.82), channel_id=1, source_target_pairs={{0,16},{16,32},{32,48},{48,64},{64,80},{80,96},{96,112},{112,128},... | collective-permute-start | bytes 786440 | tf_op jit(solution)/shard_map/ppermute | solution.py:388
  121.5 10.0 %collective-permute-start.27 = (bf16[512,128]{1,0:T(8,128)(2,1)S(1)}, bf16[512,128]{1,0:T(8,128)(2,1)S(1)}, u32[]{:S(2)}, u32[]{:S(2)}) collective-permute-start(bf16[512,128]{1,0:T(8,128)(2,1)S(1)} %get-tuple-element.92), channel_id=1, source_target_pairs={{0,12},{1,13},{2,14},{3,15},{4,0},{5,1},{6,2},{7,3},{8,4},{9,5},{1... | collective-permute-start | bytes 393224 | tf_op jit(solution)/shard_map/ppermute | solution.py:373
  125.4 7.7 %collective-permute-start.28 = (bf16[512,128]{1,0:T(8,128)(2,1)S(1)}, bf16[512,128]{1,0:T(8,128)(2,1)S(1)}, u32[]{:S(2)}, u32[]{:S(2)}) collective-permute-start(bf16[512,128]{1,0:T(8,128)(2,1)S(1)} %get-tuple-element.92), channel_id=1, source_target_pairs={{0,8},{1,9},{2,10},{3,11},{4,12},{5,13},{6,14},{7,15},{8,0},{9,1},... | collective-permute-start | bytes 393224 | tf_op jit(solution)/shard_map/ppermute | solution.py:373
  125.4 9.4 %collective-permute-start.29 = (bf16[512,128]{1,0:T(8,128)(2,1)S(1)}, bf16[512,128]{1,0:T(8,128)(2,1)S(1)}, u32[]{:S(2)}, u32[]{:S(2)}) collective-permute-start(bf16[512,128]{1,0:T(8,128)(2,1)S(1)} %get-tuple-element.92), channel_id=1, source_target_pairs={{0,4},{1,5},{2,6},{3,7},{4,8},{5,9},{6,10},{7,11},{8,12},{9,13},{1... | collective-permute-start | bytes 393224 | tf_op jit(solution)/shard_map/ppermute | solution.py:373
  126.7 36.7 %collective-permute-start.21 = (bf16[256,1024]{1,0:T(8,128)(2,1)S(1)}, bf16[256,1024]{1,0:T(8,128)(2,1)S(1)}, u32[]{:S(2)}, u32[]{:S(2)}) collective-permute-start(bf16[256,1024]{1,0:T(8,128)(2,1)S(1)} %shard_map.107.pair0), channel_id=1, source_target_pairs={{0,1},{1,2},{2,3},{3,0},{4,5},{5,6},{6,7},{7,4},{8,9},{9,10},{10,1... | collective-permute-start | bytes 1572872 | tf_op jit(solution)/shard_map/ppermute | solution.py:368
  126.8 36.6 %collective-permute-start.22 = (bf16[256,1024]{1,0:T(8,128)(2,1)S(1)}, bf16[256,1024]{1,0:T(8,128)(2,1)S(1)}, u32[]{:S(2)}, u32[]{:S(2)}) collective-permute-start(bf16[256,1024]{1,0:T(8,128)(2,1)S(1)} %shard_map.107.pair0), channel_id=1, source_target_pairs={{0,2},{1,3},{2,0},{3,1},{4,6},{5,7},{6,4},{7,5},{8,10},{9,11},{10,... | collective-permute-start | bytes 1572872 | tf_op jit(solution)/shard_map/ppermute | solution.py:368
  131.4 31.9 %collective-permute-start.23 = (bf16[256,1024]{1,0:T(8,128)(2,1)S(1)}, bf16[256,1024]{1,0:T(8,128)(2,1)S(1)}, u32[]{:S(2)}, u32[]{:S(2)}) collective-permute-start(bf16[256,1024]{1,0:T(8,128)(2,1)S(1)} %shard_map.107.pair0), channel_id=1, source_target_pairs={{0,3},{1,0},{2,1},{3,2},{4,7},{5,4},{6,5},{7,6},{8,11},{9,8},{10,9... | collective-permute-start | bytes 1572872 | tf_op jit(solution)/shard_map/ppermute | solution.py:368
  148.0 9.8 %collective-permute-start.33 = (bf16[512,128]{1,0:T(8,128)(2,1)S(1)}, bf16[512,128]{1,0:T(8,128)(2,1)S(1)}, u32[]{:S(2)}, u32[]{:S(2)}) collective-permute-start(bf16[512,128]{1,0:T(8,128)(2,1)S(1)} %shard_map.112.solved), channel_id=1, source_target_pairs={{0,16},{16,32},{32,48},{48,64},{64,80},{80,96},{96,112},{112,128},... | collective-permute-start | bytes 393224 | tf_op jit(solution)/shard_map/ppermute | solution.py:388
  155.9 7.5 %collective-permute-start.34 = (bf16[512,128]{1,0:T(8,128)(2,1)S(1)}, bf16[512,128]{1,0:T(8,128)(2,1)S(1)}, u32[]{:S(2)}, u32[]{:S(2)}) collective-permute-start(bf16[512,128]{1,0:T(8,128)(2,1)S(1)} %shard_map.112.solved), channel_id=1, source_target_pairs={{16,0},{32,16},{48,32},{64,48},{80,64},{96,80},{112,96},{128,112},... | collective-permute-start | bytes 393224 | tf_op jit(solution)/shard_map/ppermute | solution.py:388
  (15 other events, 79.4 us)
Sparse Core Ops, SparseCore 0:
  11.2 28.1 all-gather.4
  41.2 29.4 all-gather.6

commit v4 on v3

--- a/solution.py
+++ b/solution.py
@@ -194,8 +194,10 @@
     out[pl.ds(0, 256), pl.ds(256, 256)] = imag.astype(out.dtype)
 
 
-def odd_kernel(s_ref, g_ref, panel0, panel1, panel2, panel3, out, out_second, held):
+def odd_kernel(s_ref, g_ref, panel0, panel1, panel3, low, high, out, out_second, held, panel2):
     y, x = s_ref[0], s_ref[1]
+    panel2[pl.ds(0, 128), :] = low[...]
+    panel2[pl.ds(128, 128), :] = high[...]
     panels = (panel0, panel1, panel2, panel3)
     held[...] = g_ref[...].reshape(512, 1024)
     put_pair(out, *wide_product(y, held, panels))
@@ -377,6 +379,18 @@
     return (block, moved_y(block, 3), moved_y(block, 2), moved_y(block, 1))
 
 
+def split_kernel(s_ref, block, other, low, high):
+    low[...] = block[pl.ds(0, 128), :]
+    high[...] = other[pl.ds(128, 128), :]
+
+
+def ring_gathered_y(scalars, block):
+    above, below = moved_y(block, 3), moved_y(block, 1)
+    half = shape((128, block.shape[1]))
+    low, high = call(split_kernel, [half, half], 0, scalars, below, above)
+    return block, above, below, moved_y(low, 1), moved_y(high, 3)
+
+
 def gathered_x(block):
     groups = [[y * 4 + x for x in range(4)] for y in range(4)]
     return lax.all_gather(block, "row", axis_index_groups=groups)
@@ -425,11 +439,12 @@
         0, scalars, *pieces, c_even, a_next,
     )
     g_columns = gathered_x(g_columns)
-    panels = gathered_y(panel)
+    panels = ring_gathered_y(scalars, panel)
     ca_blocks = [couplings] + [moved_x(couplings, by) for by in turns]
     first, second = call(
         odd_kernel, [shape((256, 640)), shape((304, 512))], wide_flops,
-        scalars, g_rows, *panels, scratch=[pltpu.VMEM((512, 1024), BF)],
+        scalars, g_rows, *panels,
+        scratch=[pltpu.VMEM((512, 1024), BF), pltpu.VMEM((256, 1152), BF)],
     )
     firsts = gathered_y(first)
     second, g_columns, *ca_blocks = after((second, g_columns, *ca_blocks))

time: 179 us -> 176 us (0.983)
  waiting for transfers between devices: 60.9 us -> 55.6 us
  local copies, waits for them, and re-layouts: 3.37 us -> 6.09 us
    ppermute x18 -> x19, waiting for transfers between devices: 45.1 us -> 23.2 us  [moved_y(): return lax.ppermute(block, 'row', pairs)]
    ppermute x15, waiting for transfers between devices: 3.34 us -> 23.1 us  [moved_x(): return lax.ppermute(block, 'row', pairs)]
    all_gather x2, waiting for transfers between devices: 3.28 us -> 0.01 us  [gathered_x(): return lax.all_gather(block, 'row', axis_index_groups=groups)]
    unnamed x14 -> x22, local copies, waits for them, and re-layouts: 3.3 us -> 6.01 us
    ppermute x18 -> x19, starting transfers between devices: 19.3 us -> 17.7 us  [moved_y(): return lax.ppermute(block, 'row', pairs)]
    pallas_call x14 -> x15, Pallas kernels: 23.1 us -> 23.5 us  [call(): pl.pallas_call(kernel, out_shape=tuple(out_shapes), in_specs=[SMEM] + [an...]
  transfers between devices with their start and end apart: 40 -> 41, of which waited for: 15 -> 12; matrix products, arithmetic and copies ran while one was open for 0% -> 0% of each run, Pallas kernels for 10% -> 10%
where the time goes in v4:
time: 176 us
  starting transfers between devices  66.8 us (38%)
  waiting for transfers between devices  55.6 us (32%)
  Pallas kernels  23.5 us (13%)
  between operations  14.3 us (8%)
  blocking collectives  9.62 us (5%)
  local copies, waits for them, and re-layouts  6.09 us (3%)
    ppermute x5, starting transfers between devices, along_cuts(): return lax.ppermute(block, 'cuts', pairs)  27.1 us
    pallas_call x15, Pallas kernels, call(): pl.pallas_call(kernel, out_shape=tuple(out_shapes), in_specs=[SMEM] + [an...  23.5 us
    ppermute x19, waiting for transfers between devices, moved_y(): return lax.ppermute(block, 'row', pairs)  23.2 us
    ppermute x15, waiting for transfers between devices, moved_x(): return lax.ppermute(block, 'row', pairs)  23.1 us
    ppermute x15, starting transfers between devices, moved_x(): return lax.ppermute(block, 'row', pairs)  21.8 us
    ppermute x19, starting transfers between devices, moved_y(): return lax.ppermute(block, 'row', pairs)  17.7 us
    all_to_all x1, blocking collectives, body(): lax.all_to_all(g_pieces, 'row', 0, 0, axis_index_groups=groups, tiled=True)  9.62 us
    ppermute x5, waiting for transfers between devices, along_cuts(): return lax.ppermute(block, 'cuts', pairs)  9.21 us
  transfers between devices with their start and end apart: 41, of which 12 were waited for; matrix products, arithmetic and copies ran while one was open for 0% of the time, Pallas kernels for 10%

profile of v4, /device:TPU:97, one launch (start us, length us, event | category | flops | bytes accessed | tf_op | source)
XLA Modules:
  0.0 176.0 jit_solution(11833674183125878169)
XLA Ops:
  8.1 2.9 %shard_map.101 = (bf16[64,1664]{1,0:T(8,128)(2,1)S(1)}, bf16[64,1664]{1,0:T(8,128)(2,1)S(1)}, bf16[64,1664]{1,0:T(8,128)(2,1)S(1)}, bf16[64,1664]{1,0:T(8,128)(2...) custom-call(s32[6]{0:T(128)S(1)} %pad_add_fusion.1.s_ref, ...), custom_call_target="tpu_custom_call" | custom-call | bytes 4063256 | tf_op jit(solution)/shard_map/pallas_call | solution.py:27
  11.1 2.6 %collective-permute-start = (bf16[2,64,1024]{2,1,0:T(8,128)(2,1)S(1)}, bf16[2,64,1024]{2,1,0:T(8,128)(2,1)S(1)}, u32[]{:S(2)}, u32[]{:S(2)}) collective-permute-start(bf16[2,64,1024]{2,1,0:T(8,128)(2,1)S(1)} %get-tuple-element.57), channel_id=1, source_target_pairs={{16,0},{32,16},{48,32},{64,48},{80,64},{96,80},{112,96},{128,112},... | collective-permute-start | bytes 786440 | tf_op jit(solution)/shard_map/ppermute | solution.py:402
  15.0 2.5 %collective-permute-start.2 = (bf16[64,1664]{1,0:T(8,128)(2,1)S(1)}, bf16[64,1664]{1,0:T(8,128)(2,1)S(1)}, u32[]{:S(2)}, u32[]{:S(2)}) collective-permute-start(bf16[64,1664]{1,0:T(8,128)(2,1)S(1)} %get-tuple-element.61), channel_id=1, source_target_pairs={{0,2},{1,3},{2,0},{3,1},{4,6},{5,7},{6,4},{7,5},{8,10},{9,11},{10,... | collective-permute-start | bytes 638984 | tf_op jit(solution)/shard_map/ppermute | solution.py:370
  18.6 9.6 %all_to_all.5 = bf16[4,2,64,256]{3,2,1,0:T(8,128)(2,1)} all-to-all(bf16[4,2,64,256]{3,2,1,0:T(8,128)(2,1)S(1)} %get-tuple-element.58), channel_id=1, replica_groups={{0,4,8,12},{1,5,9,13},{2,6,10,14},{3,7,11,15},{16,20,24,28},{17,21,25,2..., dimensions={0} | all-to-all | bytes 524288 | tf_op jit(solution)/shard_map/all_to_all | solution.py:432
  28.9 2.1 %collective-permute-start.4 = (bf16[256,1152]{1,0:T(8,128)(2,1)S(1)}, bf16[256,1152]{1,0:T(8,128)(2,1)S(1)}, u32[]{:S(2)}, u32[]{:S(2)}) collective-permute-start(bf16[256,1152]{1,0:T(8,128)(2,1)S(1)} %get-tuple-element.69.panel0.source), channel_id=1, source_target_pairs={{0,12},{1,13},{2,14},{3,15},{4,0},{5,1},{6,2},{7,3},{8,4},{9,5},{1... | collective-permute-start | bytes 1769480 | tf_op jit(solution)/shard_map/ppermute | solution.py:375
  31.0 2.2 %collective-permute-start.10 = (bf16[2,2,64,1024]{3,2,1,0:T(8,128)(2,1)S(1)}, bf16[2,2,64,1024]{3,2,1,0:T(8,128)(2,1)S(1)}, u32[]{:S(2)}, u32[]{:S(2)}) collective-permute-start(bf16[2,2,64,1024]{3,2,1,0:T(8,128)(2,1)S(1)} %get-tuple-element.75.ca0), channel_id=1, source_target_pairs={{0,3},{1,0},{2,1},{3,2},{4,7},{5,4},{6,5},{7,6},{8,11},{9,8},{10,9... | collective-permute-start | bytes 1572872 | tf_op jit(solution)/shard_map/ppermute | solution.py:370
  33.3 9.2 %collective-permute-done.4.other.panel1 = bf16[256,1152]{1,0:T(8,128)(2,1)S(1)} collective-permute-done((bf16[256,1152]{1,0:T(8,128)(2,1)S(1)}, bf16[256,1152]{1,0:T(8,128)(2,1)S(1)}, u32[]{:S(2)}, u32[]{:S(2)}) %collective-permute-start.4) | collective-permute-done | bytes 589856 | tf_op jit(solution)/shard_map/ppermute | solution.py:375
  42.5 3.1 %collective-permute-done.5.block.panel3 = bf16[256,1152]{1,0:T(8,128)(2,1)S(1)} collective-permute-done((bf16[256,1152]{1,0:T(8,128)(2,1)S(1)}, bf16[256,1152]{1,0:T(8,128)(2,1)S(1)}, u32[]{:S(2)}, u32[]{:S(2)}) %collective-permute-start.5) | collective-permute-done | bytes 589856 | tf_op jit(solution)/shard_map/ppermute | solution.py:375
  46.3 2.7 %collective-permute-start.7 = (bf16[128,1152]{1,0:T(8,128)(2,1)S(1)}, bf16[128,1152]{1,0:T(8,128)(2,1)S(1)}, u32[]{:S(2)}, u32[]{:S(2)}) collective-permute-start(bf16[128,1152]{1,0:T(8,128)(2,1)S(1)} %get-tuple-element.71), channel_id=1, source_target_pairs={{0,12},{1,13},{2,14},{3,15},{4,0},{5,1},{6,2},{7,3},{8,4},{9,5},{1... | collective-permute-start | bytes 884744 | tf_op jit(solution)/shard_map/ppermute | solution.py:375
  49.7 3.1 %collective-permute-start.9 = (bf16[2,2,64,1024]{3,2,1,0:T(8,128)(2,1)S(1)}, bf16[2,2,64,1024]{3,2,1,0:T(8,128)(2,1)}, u32[]{:S(2)}, u32[]{:S(2)}) collective-permute-start(bf16[2,2,64,1024]{3,2,1,0:T(8,128)(2,1)S(1)} %get-tuple-element.75.ca0), channel_id=1, source_target_pairs={{0,2},{1,3},{2,0},{3,1},{4,6},{5,7},{6,4},{7,5},{8,10},{9,11},{10,... | collective-permute-start | bytes 1572872 | tf_op jit(solution)/shard_map/ppermute | solution.py:370
  58.3 2.9 %shard_map.104 = (bf16[256,640]{1,0:T(8,128)(2,1)}, bf16[304,512]{1,0:T(8,128)(2,1)S(1)}) custom-call(s32[6]{0:T(128)S(1)} %pad_add_fusion.1.s_ref, bf16[4,2,64,1024]{3,2,1,0:T(8,128)(2,1)S(1)} %bitcast.12, bf16[256,1152]{1,0:T(8,128)(2,1)S(1)} %get-tuple-element.69.panel0.source, bf16[256,1152]{1,0:T(8,128)(2,1)S(1)} %collective-permute-done.4.other.panel1, ...), custom_call_target="tpu_custom_call" | custom-call | bytes 4046872 | tf_op jit(solution)/shard_map/pallas_call | solution.py:27
  64.2 17.8 %collective-permute-done.9.ca2 = bf16[2,2,64,1024]{3,2,1,0:T(8,128)(2,1)} collective-permute-done((bf16[2,2,64,1024]{3,2,1,0:T(8,128)(2,1)S(1)}, bf16[2,2,64,1024]{3,2,1,0:T(8,128)(2,1)}, u32[]{:S(2)}, u32[]{:S(2)}) %collective-permute-start.9) | collective-permute-done | bytes 524320 | tf_op jit(solution)/shard_map/ppermute | solution.py:370
  83.5 3.0 %shard_map.105 = (bf16[288,512]{1,0:T(8,128)(2,1)S(1)}, bf16[256,512]{1,0:T(8,128)(2,1)S(1)}, f32[256,128]{1,0:T(8,128)S(1)}, bf16[512,1024]{1,0:T(8,128)(2,1)S(1)}, bf16[512,1024]{1,0:T(8,128)(2,1)S(1)}) custom-call(s32[6]{0:T(128)S(1)} %pad_add_fusion.1.s_ref, bf16[2,2,64,1024]{3,2,1,0:T(8,128)(2,1)S(1)} %get-tuple-element.75.ca0, ...), custom_call_target="tpu_custom_call" | custom-call | bytes 6783000 | tf_op jit(solution)/shard_map/pallas_call | solution.py:27
  86.5 9.4 %collective-permute-start.17 = (bf16[288,512]{1,0:T(8,128)(2,1)S(1)}, bf16[288,512]{1,0:T(8,128)(2,1)S(1)}, u32[]{:S(2)}, u32[]{:S(2)}) collective-permute-start(bf16[288,512]{1,0:T(8,128)(2,1)S(1)} %get-tuple-element.84), channel_id=1, source_target_pairs={{0,16},{16,32},{32,48},{48,64},{64,80},{80,96},{96,112},{112,128},... | collective-permute-start | bytes 884744 | tf_op jit(solution)/shard_map/ppermute | solution.py:402
  95.9 3.6 %collective-permute-done.17.shipped = bf16[288,512]{1,0:T(8,128)(2,1)S(1)} collective-permute-done((bf16[288,512]{1,0:T(8,128)(2,1)S(1)}, bf16[288,512]{1,0:T(8,128)(2,1)S(1)}, u32[]{:S(2)}, u32[]{:S(2)}) %collective-permute-start.17) | collective-permute-done | bytes 294944 | tf_op jit(solution)/shard_map/ppermute | solution.py:402
  100.8 2.5 %collective-permute-start.25 = (bf16[512,128]{1,0:T(8,128)(2,1)S(1)}, bf16[512,128]{1,0:T(8,128)(2,1)S(1)}, u32[]{:S(2)}, u32[]{:S(2)}) collective-permute-start(bf16[512,128]{1,0:T(8,128)(2,1)S(1)} %get-tuple-element.94), channel_id=1, source_target_pairs={{0,12},{1,13},{2,14},{3,15},{4,0},{5,1},{6,2},{7,3},{8,4},{9,5},{1... | collective-permute-start | bytes 393224 | tf_op jit(solution)/shard_map/ppermute | solution.py:375
  104.9 1.8 %shard_map.106 = (bf16[256,512]{1,0:T(8,128)(2,1)S(1)}, bf16[256,512]{1,0:T(8,128)(2,1)S(1)}) custom-call(s32[6]{0:T(128)S(1)} %pad_add_fusion.1.s_ref, bf16[512,1024]{1,0:T(8,128)(2,1)S(1)} %get-tuple-element.80.c_rows, bf16[512,1024]{1,0:T(8,128)(2,1)S(1)} %get-tuple-element.81.a_rows, bf16[304,512]{1,0:T(8,128)(2,1)S(1)} %copy-done.3, ...), custom_call_target="tpu_custom_call" | custom-call | bytes 4423704 | tf_op jit(solution)/shard_map/pallas_call | solution.py:27
  110.2 7.0 %collective-permute-start.21 = (bf16[256,512]{1,0:T(8,128)(2,1)S(1)}, bf16[256,512]{1,0:T(8,128)(2,1)S(1)}, u32[]{:S(2)}, u32[]{:S(2)}) collective-permute-start(bf16[256,512]{1,0:T(8,128)(2,1)S(1)} %get-tuple-element.86), channel_id=1, source_target_pairs={{0,16},{16,32},{32,48},{48,64},{64,80},{80,96},{96,112},{112,128},... | collective-permute-start | bytes 786440 | tf_op jit(solution)/shard_map/ppermute | solution.py:402
  117.2 4.2 %collective-permute-done.18.block1.refs_1_.refs_2_ = bf16[256,512]{1,0:T(8,128)(2,1)S(1)} collective-permute-done((bf16[256,512]{1,0:T(8,128)(2,1)S(1)}, bf16[256,512]{1,0:T(8,128)(2,1)S(1)}, u32[]{:S(2)}, u32[]{:S(2)}) %collective-permute-start.18) | collective-permute-done | bytes 262176 | tf_op jit(solution)/shard_map/ppermute | solution.py:370
  122.5 1.8 %shard_map.111 = (bf16[512,128]{1,0:T(8,128)(2,1)S(1)}, f32[512,128]{1,0:T(8,128)S(1)}, bf16[512,128]{1,0:T(8,128)(2,1)S(1)}) custom-call(s32[6]{0:T(128)S(1)} %pad_add_fusion.1.s_ref, f32[512,128]{1,0:T(8,128)S(1)} %get-tuple-element.93.own, bf16[512,128]{1,0:T(8,128)(2,1)S(1)} %collective-permute-done.25.got1, ...), custom_call_target="tpu_custom_call" | custom-call | bytes 3342360 | tf_op jit(solution)/shard_map/pallas_call | solution.py:27
  124.4 2.2 %collective-permute-start.29 = (bf16[512,128]{1,0:T(8,128)(2,1)S(1)}, bf16[512,128]{1,0:T(8,128)(2,1)S(1)}, u32[]{:S(2)}, u32[]{:S(2)}) collective-permute-start(bf16[512,128]{1,0:T(8,128)(2,1)S(1)} %get-tuple-element.96), channel_id=1, source_target_pairs={{0,8},{1,9},{2,10},{3,11},{4,12},{5,13},{6,14},{7,15},{8,0},{9,1},... | collective-permute-start | bytes 393224 | tf_op jit(solution)/shard_map/ppermute | solution.py:375
  127.7 3.4 %collective-permute-start.23 = (bf16[256,1024]{1,0:T(8,128)(2,1)S(1)}, bf16[256,1024]{1,0:T(8,128)(2,1)S(1)}, u32[]{:S(2)}, u32[]{:S(2)}) collective-permute-start(bf16[256,1024]{1,0:T(8,128)(2,1)S(1)} %shard_map.108.pair0), channel_id=1, source_target_pairs={{0,2},{1,3},{2,0},{3,1},{4,6},{5,7},{6,4},{7,5},{8,10},{9,11},{10,... | collective-permute-start | bytes 1572872 | tf_op jit(solution)/shard_map/ppermute | solution.py:370
  131.1 2.3 %collective-permute-done.30.got3 = bf16[512,128]{1,0:T(8,128)(2,1)S(1)} collective-permute-done((bf16[512,128]{1,0:T(8,128)(2,1)S(1)}, bf16[512,128]{1,0:T(8,128)(2,1)S(1)}, u32[]{:S(2)}, u32[]{:S(2)}) %collective-permute-start.30) | collective-permute-done | bytes 131104 | tf_op jit(solution)/shard_map/ppermute | solution.py:375
  133.4 1.8 %shard_map.112 = (bf16[512,128]{1,0:T(8,128)(2,1)S(1)}, f32[512,128]{1,0:T(8,128)S(1)}, bf16[512,128]{1,0:T(8,128)(2,1)S(1)}) custom-call(s32[6]{0:T(128)S(1)} %pad_add_fusion.1.s_ref, f32[512,128]{1,0:T(8,128)S(1)} %get-tuple-element.95.own, bf16[512,128]{1,0:T(8,128)(2,1)S(1)} %collective-permute-done.28.got1, ...), custom_call_target="tpu_custom_call" | custom-call | bytes 3473432 | tf_op jit(solution)/shard_map/pallas_call | solution.py:27
  137.2 2.2 %collective-permute-done.31.got1 = bf16[512,128]{1,0:T(8,128)(2,1)S(1)} collective-permute-done((bf16[512,128]{1,0:T(8,128)(2,1)S(1)}, bf16[512,128]{1,0:T(8,128)(2,1)S(1)}, u32[]{:S(2)}, u32[]{:S(2)}) %collective-permute-start.31) | collective-permute-done | bytes 131104 | tf_op jit(solution)/shard_map/ppermute | solution.py:375
  139.6 1.9 %collective-permute-done.32.got2 = bf16[512,128]{1,0:T(8,128)(2,1)S(1)} collective-permute-done((bf16[512,128]{1,0:T(8,128)(2,1)S(1)}, bf16[512,128]{1,0:T(8,128)(2,1)S(1)}, u32[]{:S(2)}, u32[]{:S(2)}) %collective-permute-start.32) | collective-permute-done | bytes 131104 | tf_op jit(solution)/shard_map/ppermute | solution.py:375
  141.5 3.5 %collective-permute-done.33.got3 = bf16[512,128]{1,0:T(8,128)(2,1)S(1)} collective-permute-done((bf16[512,128]{1,0:T(8,128)(2,1)S(1)}, bf16[512,128]{1,0:T(8,128)(2,1)S(1)}, u32[]{:S(2)}, u32[]{:S(2)}) %collective-permute-start.33) | collective-permute-done | bytes 131104 | tf_op jit(solution)/shard_map/ppermute | solution.py:375
  145.6 6.2 %collective-permute-start.34 = (bf16[512,128]{1,0:T(8,128)(2,1)S(1)}, bf16[512,128]{1,0:T(8,128)(2,1)S(1)}, u32[]{:S(2)}, u32[]{:S(2)}) collective-permute-start(bf16[512,128]{1,0:T(8,128)(2,1)S(1)} %shard_map.113.solved), channel_id=1, source_target_pairs={{0,16},{16,32},{32,48},{48,64},{64,80},{80,96},{96,112},{112,128},... | collective-permute-start | bytes 393224 | tf_op jit(solution)/shard_map/ppermute | solution.py:402
  151.8 1.9 %collective-permute-start.35 = (bf16[512,128]{1,0:T(8,128)(2,1)S(1)}, bf16[512,128]{1,0:T(8,128)(2,1)S(1)}, u32[]{:S(2)}, u32[]{:S(2)}) collective-permute-start(bf16[512,128]{1,0:T(8,128)(2,1)S(1)} %shard_map.113.solved), channel_id=1, source_target_pairs={{16,0},{32,16},{48,32},{64,48},{80,64},{96,80},{112,96},{128,112},... | collective-permute-start | bytes 393224 | tf_op jit(solution)/shard_map/ppermute | solution.py:402
  153.8 5.6 %collective-permute-done.35.above = bf16[512,128]{1,0:T(8,128)(2,1)S(1)} collective-permute-done((bf16[512,128]{1,0:T(8,128)(2,1)S(1)}, bf16[512,128]{1,0:T(8,128)(2,1)S(1)}, u32[]{:S(2)}, u32[]{:S(2)}) %collective-permute-start.35) | collective-permute-done | bytes 131104 | tf_op jit(solution)/shard_map/ppermute | solution.py:402
  160.8 1.8 %collective-permute-start.36 = (f32[64,128]{1,0:T(8,128)S(1)}, f32[64,128]{1,0:T(8,128)S(1)}, u32[]{:S(2)}, u32[]{:S(2)}) collective-permute-start(f32[64,128]{1,0:T(8,128)S(1)} %get-tuple-element.102), channel_id=1, source_target_pairs={{0,1},{1,2},{2,3},{3,0},{4,5},{5,6},{6,7},{7,4},{8,9},{9,10},{10,1... | collective-permute-start | bytes 98312 | tf_op jit(solution)/shard_map/ppermute | solution.py:370
  163.2 1.9 %collective-permute-start.38 = (f32[64,128]{1,0:T(8,128)S(1)}, f32[64,128]{1,0:T(8,128)S(1)}, u32[]{:S(2)}, u32[]{:S(2)}) collective-permute-start(f32[64,128]{1,0:T(8,128)S(1)} %get-tuple-element.104), channel_id=1, source_target_pairs={{0,3},{1,0},{2,1},{3,2},{4,7},{5,4},{6,5},{7,6},{8,11},{9,8},{10,9... | collective-permute-start | bytes 98312 | tf_op jit(solution)/shard_map/ppermute | solution.py:370
  (93 shorter events, 32.9 us)
Async XLA Ops:
  7.2 47.9 %all-gather.5.cloned.1.call-start = ((), (), s32[]{:S(2)}) async-start(), calls=%async_computation.1 | async-start | bytes 1310720 | tf_op jit(solution)/shard_map/all_gather | solution.py:396
  11.1 70.9 %all-gather.7.cloned.1.call-start = ((), (), s32[]{:S(2)}) async-start(), calls=%async_computation.2 | async-start | bytes 1310720 | tf_op jit(solution)/shard_map/all_gather | solution.py:396
  11.1 17.1 %collective-permute-start = (bf16[2,64,1024]{2,1,0:T(8,128)(2,1)S(1)}, bf16[2,64,1024]{2,1,0:T(8,128)(2,1)S(1)}, u32[]{:S(2)}, u32[]{:S(2)}) collective-permute-start(bf16[2,64,1024]{2,1,0:T(8,128)(2,1)S(1)} %get-tuple-element.57), channel_id=1, source_target_pairs={{16,0},{32,16},{48,32},{64,48},{80,64},{96,80},{112,96},{128,112},... | collective-permute-start | bytes 786440 | tf_op jit(solution)/shard_map/ppermute | solution.py:402
  13.7 14.5 %collective-permute-start.1 = (bf16[64,1664]{1,0:T(8,128)(2,1)S(1)}, bf16[64,1664]{1,0:T(8,128)(2,1)S(1)}, u32[]{:S(2)}, u32[]{:S(2)}) collective-permute-start(bf16[64,1664]{1,0:T(8,128)(2,1)S(1)} %get-tuple-element.60), channel_id=1, source_target_pairs={{0,1},{1,2},{2,3},{3,0},{4,5},{5,6},{6,7},{7,4},{8,9},{9,10},{10,1... | collective-permute-start | bytes 638984 | tf_op jit(solution)/shard_map/ppermute | solution.py:370
  15.0 13.2 %collective-permute-start.2 = (bf16[64,1664]{1,0:T(8,128)(2,1)S(1)}, bf16[64,1664]{1,0:T(8,128)(2,1)S(1)}, u32[]{:S(2)}, u32[]{:S(2)}) collective-permute-start(bf16[64,1664]{1,0:T(8,128)(2,1)S(1)} %get-tuple-element.61), channel_id=1, source_target_pairs={{0,2},{1,3},{2,0},{3,1},{4,6},{5,7},{6,4},{7,5},{8,10},{9,11},{10,... | collective-permute-start | bytes 638984 | tf_op jit(solution)/shard_map/ppermute | solution.py:370
  17.4 10.8 %collective-permute-start.3 = (bf16[64,1664]{1,0:T(8,128)(2,1)S(1)}, bf16[64,1664]{1,0:T(8,128)(2,1)S(1)}, u32[]{:S(2)}, u32[]{:S(2)}) collective-permute-start(bf16[64,1664]{1,0:T(8,128)(2,1)S(1)} %get-tuple-element.62), channel_id=1, source_target_pairs={{0,3},{1,0},{2,1},{3,2},{4,7},{5,4},{6,5},{7,6},{8,11},{9,8},{10,9... | collective-permute-start | bytes 638984 | tf_op jit(solution)/shard_map/ppermute | solution.py:370
  28.9 13.6 %collective-permute-start.4 = (bf16[256,1152]{1,0:T(8,128)(2,1)S(1)}, bf16[256,1152]{1,0:T(8,128)(2,1)S(1)}, u32[]{:S(2)}, u32[]{:S(2)}) collective-permute-start(bf16[256,1152]{1,0:T(8,128)(2,1)S(1)} %get-tuple-element.69.panel0.source), channel_id=1, source_target_pairs={{0,12},{1,13},{2,14},{3,15},{4,0},{5,1},{6,2},{7,3},{8,4},{9,5},{1... | collective-permute-start | bytes 1769480 | tf_op jit(solution)/shard_map/ppermute | solution.py:375
  31.0 14.6 %collective-permute-start.5 = (bf16[256,1152]{1,0:T(8,128)(2,1)S(1)}, bf16[256,1152]{1,0:T(8,128)(2,1)S(1)}, u32[]{:S(2)}, u32[]{:S(2)}) collective-permute-start(bf16[256,1152]{1,0:T(8,128)(2,1)S(1)} %get-tuple-element.69.panel0.source), channel_id=1, source_target_pairs={{0,4},{1,5},{2,6},{3,7},{4,8},{5,9},{6,10},{7,11},{8,12},{9,13},{1... | collective-permute-start | bytes 1769480 | tf_op jit(solution)/shard_map/ppermute | solution.py:375
  31.0 32.6 %collective-permute-start.10 = (bf16[2,2,64,1024]{3,2,1,0:T(8,128)(2,1)S(1)}, bf16[2,2,64,1024]{3,2,1,0:T(8,128)(2,1)S(1)}, u32[]{:S(2)}, u32[]{:S(2)}) collective-permute-start(bf16[2,2,64,1024]{3,2,1,0:T(8,128)(2,1)S(1)} %get-tuple-element.75.ca0), channel_id=1, source_target_pairs={{0,3},{1,0},{2,1},{3,2},{4,7},{5,4},{6,5},{7,6},{8,11},{9,8},{10,9... | collective-permute-start | bytes 1572872 | tf_op jit(solution)/shard_map/ppermute | solution.py:370
  46.2 7.5 %collective-permute-start.6 = (bf16[128,1152]{1,0:T(8,128)(2,1)S(1)}, bf16[128,1152]{1,0:T(8,128)(2,1)S(1)}, u32[]{:S(2)}, u32[]{:S(2)}) collective-permute-start(bf16[128,1152]{1,0:T(8,128)(2,1)S(1)} %get-tuple-element.70), channel_id=1, source_target_pairs={{0,4},{1,5},{2,6},{3,7},{4,8},{5,9},{6,10},{7,11},{8,12},{9,13},{1... | collective-permute-start | bytes 884744 | tf_op jit(solution)/shard_map/ppermute | solution.py:375
  46.3 8.1 %collective-permute-start.7 = (bf16[128,1152]{1,0:T(8,128)(2,1)S(1)}, bf16[128,1152]{1,0:T(8,128)(2,1)S(1)}, u32[]{:S(2)}, u32[]{:S(2)}) collective-permute-start(bf16[128,1152]{1,0:T(8,128)(2,1)S(1)} %get-tuple-element.71), channel_id=1, source_target_pairs={{0,12},{1,13},{2,14},{3,15},{4,0},{5,1},{6,2},{7,3},{8,4},{9,5},{1... | collective-permute-start | bytes 884744 | tf_op jit(solution)/shard_map/ppermute | solution.py:375
  49.0 15.2 %collective-permute-start.8 = (bf16[2,2,64,1024]{3,2,1,0:T(8,128)(2,1)S(1)}, bf16[2,2,64,1024]{3,2,1,0:T(8,128)(2,1)S(1)}, u32[]{:S(2)}, u32[]{:S(2)}) collective-permute-start(bf16[2,2,64,1024]{3,2,1,0:T(8,128)(2,1)S(1)} %get-tuple-element.75.ca0), channel_id=1, source_target_pairs={{0,1},{1,2},{2,3},{3,0},{4,5},{5,6},{6,7},{7,4},{8,9},{9,10},{10,1... | collective-permute-start | bytes 1572872 | tf_op jit(solution)/shard_map/ppermute | solution.py:370
  49.7 32.2 %collective-permute-start.9 = (bf16[2,2,64,1024]{3,2,1,0:T(8,128)(2,1)S(1)}, bf16[2,2,64,1024]{3,2,1,0:T(8,128)(2,1)}, u32[]{:S(2)}, u32[]{:S(2)}) collective-permute-start(bf16[2,2,64,1024]{3,2,1,0:T(8,128)(2,1)S(1)} %get-tuple-element.75.ca0), channel_id=1, source_target_pairs={{0,2},{1,3},{2,0},{3,1},{4,6},{5,7},{6,4},{7,5},{8,10},{9,11},{10,... | collective-permute-start | bytes 1572872 | tf_op jit(solution)/shard_map/ppermute | solution.py:370
  62.0 21.0 %collective-permute-start.11 = (bf16[256,640]{1,0:T(8,128)(2,1)}, bf16[256,640]{1,0:T(8,128)(2,1)S(1)}, u32[]{:S(2)}, u32[]{:S(2)}) collective-permute-start(bf16[256,640]{1,0:T(8,128)(2,1)} %get-tuple-element.79.panel0), channel_id=1, source_target_pairs={{0,12},{1,13},{2,14},{3,15},{4,0},{5,1},{6,2},{7,3},{8,4},{9,5},{1... | collective-permute-start | bytes 983048 | tf_op jit(solution)/shard_map/ppermute | solution.py:375
  63.6 19.8 %collective-permute-start.12 = (bf16[256,640]{1,0:T(8,128)(2,1)}, bf16[256,640]{1,0:T(8,128)(2,1)S(1)}, u32[]{:S(2)}, u32[]{:S(2)}) collective-permute-start(bf16[256,640]{1,0:T(8,128)(2,1)} %get-tuple-element.79.panel0), channel_id=1, source_target_pairs={{0,8},{1,9},{2,10},{3,11},{4,12},{5,13},{6,14},{7,15},{8,0},{9,1},... | collective-permute-start | bytes 983048 | tf_op jit(solution)/shard_map/ppermute | solution.py:375
  63.6 19.8 %collective-permute-start.13 = (bf16[256,640]{1,0:T(8,128)(2,1)}, bf16[256,640]{1,0:T(8,128)(2,1)S(1)}, u32[]{:S(2)}, u32[]{:S(2)}) collective-permute-start(bf16[256,640]{1,0:T(8,128)(2,1)} %get-tuple-element.79.panel0), channel_id=1, source_target_pairs={{0,4},{1,5},{2,6},{3,7},{4,8},{5,9},{6,10},{7,11},{8,12},{9,13},{1... | collective-permute-start | bytes 983048 | tf_op jit(solution)/shard_map/ppermute | solution.py:375
  82.0 22.8 %collective-permute-start.14 = (bf16[304,512]{1,0:T(8,128)(2,1)}, bf16[304,512]{1,0:T(8,128)(2,1)S(1)}, u32[]{:S(2)}, u32[]{:S(2)}) collective-permute-start(bf16[304,512]{1,0:T(8,128)(2,1)} %copy-done.2), channel_id=1, source_target_pairs={{0,12},{1,13},{2,14},{3,15},{4,0},{5,1},{6,2},{7,3},{8,4},{9,5},{1... | collective-permute-start | bytes 933896 | tf_op jit(solution)/shard_map/ppermute | solution.py:375
  82.3 22.6 %collective-permute-start.15 = (bf16[304,512]{1,0:T(8,128)(2,1)}, bf16[304,512]{1,0:T(8,128)(2,1)S(1)}, u32[]{:S(2)}, u32[]{:S(2)}) collective-permute-start(bf16[304,512]{1,0:T(8,128)(2,1)} %copy-done.2), channel_id=1, source_target_pairs={{0,8},{1,9},{2,10},{3,11},{4,12},{5,13},{6,14},{7,15},{8,0},{9,1},... | collective-permute-start | bytes 933896 | tf_op jit(solution)/shard_map/ppermute | solution.py:375
  83.0 21.9 %collective-permute-start.16 = (bf16[304,512]{1,0:T(8,128)(2,1)}, bf16[304,512]{1,0:T(8,128)(2,1)S(1)}, u32[]{:S(2)}, u32[]{:S(2)}) collective-permute-start(bf16[304,512]{1,0:T(8,128)(2,1)} %copy-done.2), channel_id=1, source_target_pairs={{0,4},{1,5},{2,6},{3,7},{4,8},{5,9},{6,10},{7,11},{8,12},{9,13},{1... | collective-permute-start | bytes 933896 | tf_op jit(solution)/shard_map/ppermute | solution.py:375
  86.5 13.0 %collective-permute-start.17 = (bf16[288,512]{1,0:T(8,128)(2,1)S(1)}, bf16[288,512]{1,0:T(8,128)(2,1)S(1)}, u32[]{:S(2)}, u32[]{:S(2)}) collective-permute-start(bf16[288,512]{1,0:T(8,128)(2,1)S(1)} %get-tuple-element.84), channel_id=1, source_target_pairs={{0,16},{16,32},{32,48},{48,64},{64,80},{80,96},{96,112},{112,128},... | collective-permute-start | bytes 884744 | tf_op jit(solution)/shard_map/ppermute | solution.py:402
  100.8 8.6 %collective-permute-start.25 = (bf16[512,128]{1,0:T(8,128)(2,1)S(1)}, bf16[512,128]{1,0:T(8,128)(2,1)S(1)}, u32[]{:S(2)}, u32[]{:S(2)}) collective-permute-start(bf16[512,128]{1,0:T(8,128)(2,1)S(1)} %get-tuple-element.94), channel_id=1, source_target_pairs={{0,12},{1,13},{2,14},{3,15},{4,0},{5,1},{6,2},{7,3},{8,4},{9,5},{1... | collective-permute-start | bytes 393224 | tf_op jit(solution)/shard_map/ppermute | solution.py:375
  106.7 14.7 %collective-permute-start.18 = (bf16[256,512]{1,0:T(8,128)(2,1)S(1)}, bf16[256,512]{1,0:T(8,128)(2,1)S(1)}, u32[]{:S(2)}, u32[]{:S(2)}) collective-permute-start(bf16[256,512]{1,0:T(8,128)(2,1)S(1)} %get-tuple-element.85.block0.refs_0_.refs_1_), channel_id=1, source_target_pairs={{0,1},{1,2},{2,3},{3,0},{4,5},{5,6},{6,7},{7,4},{8,9},{9,10},{10,1... | collective-permute-start | bytes 786440 | tf_op jit(solution)/shard_map/ppermute | solution.py:370
  106.8 14.6 %collective-permute-start.19 = (bf16[256,512]{1,0:T(8,128)(2,1)S(1)}, bf16[256,512]{1,0:T(8,128)(2,1)S(1)}, u32[]{:S(2)}, u32[]{:S(2)}) collective-permute-start(bf16[256,512]{1,0:T(8,128)(2,1)S(1)} %get-tuple-element.85.block0.refs_0_.refs_1_), channel_id=1, source_target_pairs={{0,2},{1,3},{2,0},{3,1},{4,6},{5,7},{6,4},{7,5},{8,10},{9,11},{10,... | collective-permute-start | bytes 786440 | tf_op jit(solution)/shard_map/ppermute | solution.py:370
  108.3 14.2 %collective-permute-start.20 = (bf16[256,512]{1,0:T(8,128)(2,1)S(1)}, bf16[256,512]{1,0:T(8,128)(2,1)S(1)}, u32[]{:S(2)}, u32[]{:S(2)}) collective-permute-start(bf16[256,512]{1,0:T(8,128)(2,1)S(1)} %get-tuple-element.85.block0.refs_0_.refs_1_), channel_id=1, source_target_pairs={{0,3},{1,0},{2,1},{3,2},{4,7},{5,4},{6,5},{7,6},{8,11},{9,8},{10,9... | collective-permute-start | bytes 786440 | tf_op jit(solution)/shard_map/ppermute | solution.py:370
  109.4 7.8 %collective-permute-start.27 = (bf16[512,128]{1,0:T(8,128)(2,1)S(1)}, bf16[512,128]{1,0:T(8,128)(2,1)S(1)}, u32[]{:S(2)}, u32[]{:S(2)}) collective-permute-start(bf16[512,128]{1,0:T(8,128)(2,1)S(1)} %get-tuple-element.94), channel_id=1, source_target_pairs={{0,4},{1,5},{2,6},{3,7},{4,8},{5,9},{6,10},{7,11},{8,12},{9,13},{1... | collective-permute-start | bytes 393224 | tf_op jit(solution)/shard_map/ppermute | solution.py:375
  110.2 16.4 %collective-permute-start.21 = (bf16[256,512]{1,0:T(8,128)(2,1)S(1)}, bf16[256,512]{1,0:T(8,128)(2,1)S(1)}, u32[]{:S(2)}, u32[]{:S(2)}) collective-permute-start(bf16[256,512]{1,0:T(8,128)(2,1)S(1)} %get-tuple-element.86), channel_id=1, source_target_pairs={{0,16},{16,32},{32,48},{48,64},{64,80},{80,96},{96,112},{112,128},... | collective-permute-start | bytes 786440 | tf_op jit(solution)/shard_map/ppermute | solution.py:402
  127.2 32.1 %collective-permute-start.22 = (bf16[256,1024]{1,0:T(8,128)(2,1)S(1)}, bf16[256,1024]{1,0:T(8,128)(2,1)S(1)}, u32[]{:S(2)}, u32[]{:S(2)}) collective-permute-start(bf16[256,1024]{1,0:T(8,128)(2,1)S(1)} %shard_map.108.pair0), channel_id=1, source_target_pairs={{0,1},{1,2},{2,3},{3,0},{4,5},{5,6},{6,7},{7,4},{8,9},{9,10},{10,1... | collective-permute-start | bytes 1572872 | tf_op jit(solution)/shard_map/ppermute | solution.py:370
  127.7 31.6 %collective-permute-start.23 = (bf16[256,1024]{1,0:T(8,128)(2,1)S(1)}, bf16[256,1024]{1,0:T(8,128)(2,1)S(1)}, u32[]{:S(2)}, u32[]{:S(2)}) collective-permute-start(bf16[256,1024]{1,0:T(8,128)(2,1)S(1)} %shard_map.108.pair0), channel_id=1, source_target_pairs={{0,2},{1,3},{2,0},{3,1},{4,6},{5,7},{6,4},{7,5},{8,10},{9,11},{10,... | collective-permute-start | bytes 1572872 | tf_op jit(solution)/shard_map/ppermute | solution.py:370
  131.1 28.2 %collective-permute-start.24 = (bf16[256,1024]{1,0:T(8,128)(2,1)S(1)}, bf16[256,1024]{1,0:T(8,128)(2,1)S(1)}, u32[]{:S(2)}, u32[]{:S(2)}) collective-permute-start(bf16[256,1024]{1,0:T(8,128)(2,1)S(1)} %shard_map.108.pair0), channel_id=1, source_target_pairs={{0,3},{1,0},{2,1},{3,2},{4,7},{5,4},{6,5},{7,6},{8,11},{9,8},{10,9... | collective-permute-start | bytes 1572872 | tf_op jit(solution)/shard_map/ppermute | solution.py:370
  145.6 8.2 %collective-permute-start.34 = (bf16[512,128]{1,0:T(8,128)(2,1)S(1)}, bf16[512,128]{1,0:T(8,128)(2,1)S(1)}, u32[]{:S(2)}, u32[]{:S(2)}) collective-permute-start(bf16[512,128]{1,0:T(8,128)(2,1)S(1)} %shard_map.113.solved), channel_id=1, source_target_pairs={{0,16},{16,32},{32,48},{48,64},{64,80},{80,96},{96,112},{112,128},... | collective-permute-start | bytes 393224 | tf_op jit(solution)/shard_map/ppermute | solution.py:402
  151.8 7.5 %collective-permute-start.35 = (bf16[512,128]{1,0:T(8,128)(2,1)S(1)}, bf16[512,128]{1,0:T(8,128)(2,1)S(1)}, u32[]{:S(2)}, u32[]{:S(2)}) collective-permute-start(bf16[512,128]{1,0:T(8,128)(2,1)S(1)} %shard_map.113.solved), channel_id=1, source_target_pairs={{16,0},{32,16},{48,32},{64,48},{80,64},{96,80},{112,96},{128,112},... | collective-permute-start | bytes 393224 | tf_op jit(solution)/shard_map/ppermute | solution.py:402
  160.8 7.0 %collective-permute-start.36 = (f32[64,128]{1,0:T(8,128)S(1)}, f32[64,128]{1,0:T(8,128)S(1)}, u32[]{:S(2)}, u32[]{:S(2)}) collective-permute-start(f32[64,128]{1,0:T(8,128)S(1)} %get-tuple-element.102), channel_id=1, source_target_pairs={{0,1},{1,2},{2,3},{3,0},{4,5},{5,6},{6,7},{7,4},{8,9},{9,10},{10,1... | collective-permute-start | bytes 98312 | tf_op jit(solution)/shard_map/ppermute | solution.py:370
  (20 other events, 103.4 us)
Sparse Core Ops, SparseCore 0:
  11.2 29.0 all-gather.4
  42.1 33.7 all-gather.6

commit v5 on v4

--- a/solution.py
+++ b/solution.py
@@ -11,7 +11,7 @@
 BF = jnp.bfloat16
 F32 = jnp.float32
 VMEM = pl.BlockSpec(memory_space=pltpu.VMEM)
-MIB = 24
+MIB = 12
 SMEM = pl.BlockSpec(memory_space=pltpu.SMEM)
 
 
@@ -384,11 +384,13 @@
     high[...] = other[pl.ds(128, 128), :]
 
 
-def ring_gathered_y(scalars, block):
-    above, below = moved_y(block, 3), moved_y(block, 1)
+def ring_gathered_y(scalars, block, beside):
+    above, below, *beside = lax.optimization_barrier(
+        (moved_y(block, 3), moved_y(block, 1), *beside)
+    )
     half = shape((128, block.shape[1]))
     low, high = call(split_kernel, [half, half], 0, scalars, below, above)
-    return block, above, below, moved_y(low, 1), moved_y(high, 3)
+    return (block, above, below, moved_y(low, 1), moved_y(high, 3)), beside
 
 
 def gathered_x(block):
@@ -439,8 +441,10 @@
         0, scalars, *pieces, c_even, a_next,
     )
     g_columns = gathered_x(g_columns)
-    panels = ring_gathered_y(scalars, panel)
-    ca_blocks = [couplings] + [moved_x(couplings, by) for by in turns]
+    near = (g_rows, moved_x(couplings, 1), moved_x(couplings, 3))
+    panels, near = ring_gathered_y(scalars, panel, near)
+    g_rows = near[0]
+    ca_blocks = [couplings, near[1], moved_x(couplings, 2), near[2]]
     first, second = call(
         odd_kernel, [shape((256, 640)), shape((304, 512))], wide_flops,
         scalars, g_rows, *panels,
@@ -494,6 +498,9 @@
     lower_rows, upper_rows = call(
         coupling_rows_kernel, [shape((2, 64, 1024))] * 2, 0, scalars, *pairs
     )
+    below, diagonal_rows, lower_rows, upper_rows = after(
+        (below, diagonal_rows, lower_rows, upper_rows)
+    )
     ends = call(
         couple_kernel, [shape((64, 128), F32)] * 4, solve_flops // 2,
         scalars, *pairs, source, solved, below, above,

time: 176 us -> 174 us (0.989)
  starting transfers between devices: 66.8 us -> 71.3 us
  waiting for transfers between devices: 55.6 us -> 51.1 us
  local copies, waits for them, and re-layouts: 6.09 us -> 3.99 us
    ppermute x19, waiting for transfers between devices: 23.2 us -> 18 us  [moved_y(): return lax.ppermute(block, 'row', pairs)]
    all_gather x2, waiting for transfers between devices: 0.01 us -> 5 us  [gathered_x(): return lax.all_gather(block, 'row', axis_index_groups=groups)]
    ppermute x19, starting transfers between devices: 17.7 us -> 22.1 us  [moved_y(): return lax.ppermute(block, 'row', pairs)]
    ppermute x15, starting transfers between devices: 21.8 us -> 25.9 us  [moved_x(): return lax.ppermute(block, 'row', pairs)]
    ppermute x5, starting transfers between devices: 27.1 us -> 23.3 us  [along_cuts(): return lax.ppermute(block, 'cuts', pairs)]
    ppermute x5, waiting for transfers between devices: 9.21 us -> 6.54 us  [along_cuts(): return lax.ppermute(block, 'cuts', pairs)]
    unnamed x22 -> x18, local copies, waits for them, and re-layouts: 6.01 us -> 3.92 us
  transfers between devices with their start and end apart: 41 -> 41, of which waited for: 12 -> 14; matrix products, arithmetic and copies ran while one was open for 0% -> 0% of each run, Pallas kernels for 10% -> 10%
where the time goes in v5:
time: 174 us
  starting transfers between devices  71.3 us (41%)
  waiting for transfers between devices  51.1 us (29%)
  Pallas kernels  23.3 us (13%)
  between operations  14.3 us (8%)
  blocking collectives  9.62 us (6%)
  local copies, waits for them, and re-layouts  3.99 us (2%)
    ppermute x15, starting transfers between devices, moved_x(): return lax.ppermute(block, 'row', pairs)  25.9 us
    pallas_call x15, Pallas kernels, call(): pl.pallas_call(kernel, out_shape=tuple(out_shapes), in_specs=[SMEM] + [an...  23.3 us
    ppermute x5, starting transfers between devices, along_cuts(): return lax.ppermute(block, 'cuts', pairs)  23.3 us
    ppermute x19, starting transfers between devices, moved_y(): return lax.ppermute(block, 'row', pairs)  22.1 us
    ppermute x15, waiting for transfers between devices, moved_x(): return lax.ppermute(block, 'row', pairs)  21.6 us
    ppermute x19, waiting for transfers between devices, moved_y(): return lax.ppermute(block, 'row', pairs)  18 us
    all_to_all x1, blocking collectives, body(): lax.all_to_all(g_pieces, 'row', 0, 0, axis_index_groups=groups, tiled=True)  9.62 us
    ppermute x5, waiting for transfers between devices, along_cuts(): return lax.ppermute(block, 'cuts', pairs)  6.54 us
  transfers between devices with their start and end apart: 41, of which 14 were waited for; matrix products, arithmetic and copies ran while one was open for 0% of the time, Pallas kernels for 10%

profile of v5, /device:TPU:97, one launch (start us, length us, event | category | flops | bytes accessed | tf_op | source)
XLA Modules:
  0.0 173.8 jit_solution(12633371647296757430)
XLA Ops:
  8.1 2.9 %shard_map.101 = (bf16[64,1664]{1,0:T(8,128)(2,1)S(1)}, bf16[64,1664]{1,0:T(8,128)(2,1)S(1)}, bf16[64,1664]{1,0:T(8,128)(2,1)S(1)}, bf16[64,1664]{1,0:T(8,128)(2...) custom-call(s32[6]{0:T(128)S(1)} %pad_add_fusion.1.s_ref, ...), custom_call_target="tpu_custom_call" | custom-call | bytes 4063256 | tf_op jit(solution)/shard_map/pallas_call | solution.py:27
  11.1 2.6 %collective-permute-start = (bf16[2,64,1024]{2,1,0:T(8,128)(2,1)S(1)}, bf16[2,64,1024]{2,1,0:T(8,128)(2,1)S(1)}, u32[]{:S(2)}, u32[]{:S(2)}) collective-permute-start(bf16[2,64,1024]{2,1,0:T(8,128)(2,1)S(1)} %get-tuple-element.65), channel_id=1, source_target_pairs={{16,0},{32,16},{48,32},{64,48},{80,64},{96,80},{112,96},{128,112},... | collective-permute-start | bytes 786440 | tf_op jit(solution)/shard_map/ppermute | solution.py:404
  15.0 2.5 %collective-permute-start.2 = (bf16[64,1664]{1,0:T(8,128)(2,1)S(1)}, bf16[64,1664]{1,0:T(8,128)(2,1)S(1)}, u32[]{:S(2)}, u32[]{:S(2)}) collective-permute-start(bf16[64,1664]{1,0:T(8,128)(2,1)S(1)} %get-tuple-element.69), channel_id=1, source_target_pairs={{0,2},{1,3},{2,0},{3,1},{4,6},{5,7},{6,4},{7,5},{8,10},{9,11},{10,... | collective-permute-start | bytes 638984 | tf_op jit(solution)/shard_map/ppermute | solution.py:370
  18.6 9.6 %all_to_all.5 = bf16[4,2,64,256]{3,2,1,0:T(8,128)(2,1)} all-to-all(bf16[4,2,64,256]{3,2,1,0:T(8,128)(2,1)S(1)} %get-tuple-element.66), channel_id=1, replica_groups={{0,4,8,12},{1,5,9,13},{2,6,10,14},{3,7,11,15},{16,20,24,28},{17,21,25,2..., dimensions={0} | all-to-all | bytes 524288 | tf_op jit(solution)/shard_map/all_to_all | solution.py:434
  29.6 2.0 %collective-permute-start.4 = (bf16[256,1152]{1,0:T(8,128)(2,1)S(1)}, bf16[256,1152]{1,0:T(8,128)(2,1)S(1)}, u32[]{:S(2)}, u32[]{:S(2)}) collective-permute-start(bf16[256,1152]{1,0:T(8,128)(2,1)S(1)} %get-tuple-element.77.panel0.source), channel_id=1, source_target_pairs={{0,12},{1,13},{2,14},{3,15},{4,0},{5,1},{6,2},{7,3},{8,4},{9,5},{1... | collective-permute-start | bytes 1769480 | tf_op jit(solution)/shard_map/ppermute | solution.py:375
  32.3 2.0 %collective-permute-start.7 = (bf16[2,2,64,1024]{3,2,1,0:T(8,128)(2,1)S(1)}, bf16[2,2,64,1024]{3,2,1,0:T(8,128)(2,1)S(1)}, u32[]{:S(2)}, u32[]{:S(2)}) collective-permute-start(bf16[2,2,64,1024]{3,2,1,0:T(8,128)(2,1)S(1)} %get-tuple-element.90.ca0), channel_id=1, source_target_pairs={{0,3},{1,0},{2,1},{3,2},{4,7},{5,4},{6,5},{7,6},{8,11},{9,8},{10,9... | collective-permute-start | bytes 1572872 | tf_op jit(solution)/shard_map/ppermute | solution.py:370
  34.3 13.8 %collective-permute-done.6.ca1 = bf16[2,2,64,1024]{3,2,1,0:T(8,128)(2,1)S(1)} collective-permute-done((bf16[2,2,64,1024]{3,2,1,0:T(8,128)(2,1)S(1)}, bf16[2,2,64,1024]{3,2,1,0:T(8,128)(2,1)S(1)}, u32[]{:S(2)}, u32[]{:S(2)}) %collective-permute-start.6) | collective-permute-done | bytes 524320 | tf_op jit(solution)/shard_map/ppermute | solution.py:370
  51.5 2.6 %collective-permute-start.10 = (bf16[2,2,64,1024]{3,2,1,0:T(8,128)(2,1)S(1)}, bf16[2,2,64,1024]{3,2,1,0:T(8,128)(2,1)S(1)}, u32[]{:S(2)}, u32[]{:S(2)}) collective-permute-start(bf16[2,2,64,1024]{3,2,1,0:T(8,128)(2,1)S(1)} %get-tuple-element.90.ca0), channel_id=1, source_target_pairs={{0,2},{1,3},{2,0},{3,1},{4,6},{5,7},{6,4},{7,5},{8,10},{9,11},{10,... | collective-permute-start | bytes 1572872 | tf_op jit(solution)/shard_map/ppermute | solution.py:370
  54.1 2.9 %collective-permute-done.8.low = bf16[128,1152]{1,0:T(8,128)(2,1)S(1)} collective-permute-done((bf16[128,1152]{1,0:T(8,128)(2,1)S(1)}, bf16[128,1152]{1,0:T(8,128)(2,1)S(1)}, u32[]{:S(2)}, u32[]{:S(2)}) %collective-permute-start.8) | collective-permute-done | bytes 294944 | tf_op jit(solution)/shard_map/ppermute | solution.py:375
  57.0 2.9 %shard_map.104 = (bf16[256,640]{1,0:T(8,128)(2,1)}, bf16[304,512]{1,0:T(8,128)(2,1)S(1)}) custom-call(s32[6]{0:T(128)S(1)} %pad_add_fusion.1.s_ref, bf16[4,2,64,1024]{3,2,1,0:T(8,128)(2,1)S(1)} %bitcast.12, bf16[256,1152]{1,0:T(8,128)(2,1)S(1)} %get-tuple-element.77.panel0.source, bf16[256,1152]{1,0:T(8,128)(2,1)S(1)} %collective-permute-done.4.other.panel1, ...), custom_call_target="tpu_custom_call" | custom-call | bytes 4046872 | tf_op jit(solution)/shard_map/pallas_call | solution.py:27
  60.7 2.4 %collective-permute-start.11 = (bf16[256,640]{1,0:T(8,128)(2,1)}, bf16[256,640]{1,0:T(8,128)(2,1)S(1)}, u32[]{:S(2)}, u32[]{:S(2)}) collective-permute-start(bf16[256,640]{1,0:T(8,128)(2,1)} %get-tuple-element.94.panel0), channel_id=1, source_target_pairs={{0,12},{1,13},{2,14},{3,15},{4,0},{5,1},{6,2},{7,3},{8,4},{9,5},{1... | collective-permute-start | bytes 983048 | tf_op jit(solution)/shard_map/ppermute | solution.py:375
  64.2 5.6 %collective-permute-done.10.ca2 = bf16[2,2,64,1024]{3,2,1,0:T(8,128)(2,1)S(1)} collective-permute-done((bf16[2,2,64,1024]{3,2,1,0:T(8,128)(2,1)S(1)}, bf16[2,2,64,1024]{3,2,1,0:T(8,128)(2,1)S(1)}, u32[]{:S(2)}, u32[]{:S(2)}) %collective-permute-start.10) | collective-permute-done | bytes 524320 | tf_op jit(solution)/shard_map/ppermute | solution.py:370
  70.6 5.0 %all-gather.7.cloned.1.call-done = bf16[16,2,64,256]{3,2,1,0:T(8,128)(2,1)} async-done(((bf16[4,2,64,256]{3,2,1,0:T(8,128)(2,1)}), bf16[16,2,64,256]{3,2,1,0:T(8,128)(2,1)}) %all-gather.7.cloned.1.call-update) | async-done | bytes 1048592 | tf_op jit(solution)/shard_map/all_gather | solution.py:398
  78.5 2.7 %collective-permute-done.13.panel3 = bf16[256,640]{1,0:T(8,128)(2,1)S(1)} collective-permute-done((bf16[256,640]{1,0:T(8,128)(2,1)}, bf16[256,640]{1,0:T(8,128)(2,1)S(1)}, u32[]{:S(2)}, u32[]{:S(2)}) %collective-permute-start.13) | collective-permute-done | bytes 327712 | tf_op jit(solution)/shard_map/ppermute | solution.py:375
  82.3 2.9 %shard_map.105 = (bf16[288,512]{1,0:T(8,128)(2,1)S(1)}, bf16[256,512]{1,0:T(8,128)(2,1)S(1)}, f32[256,128]{1,0:T(8,128)S(1)}, bf16[512,1024]{1,0:T(8,128)(2,1)S(1)}, bf16[512,1024]{1,0:T(8,128)(2,1)S(1)}) custom-call(s32[6]{0:T(128)S(1)} %pad_add_fusion.1.s_ref, bf16[2,2,64,1024]{3,2,1,0:T(8,128)(2,1)S(1)} %get-tuple-element.90.ca0, ...), custom_call_target="tpu_custom_call" | custom-call | bytes 6783000 | tf_op jit(solution)/shard_map/pallas_call | solution.py:27
  85.2 5.3 %collective-permute-start.14 = (bf16[288,512]{1,0:T(8,128)(2,1)S(1)}, bf16[288,512]{1,0:T(8,128)(2,1)S(1)}, u32[]{:S(2)}, u32[]{:S(2)}) collective-permute-start(bf16[288,512]{1,0:T(8,128)(2,1)S(1)} %get-tuple-element.96), channel_id=1, source_target_pairs={{0,16},{16,32},{32,48},{48,64},{64,80},{80,96},{96,112},{112,128},... | collective-permute-start | bytes 884744 | tf_op jit(solution)/shard_map/ppermute | solution.py:404
  90.4 3.6 %collective-permute-done.14.shipped = bf16[288,512]{1,0:T(8,128)(2,1)S(1)} collective-permute-done((bf16[288,512]{1,0:T(8,128)(2,1)S(1)}, bf16[288,512]{1,0:T(8,128)(2,1)S(1)}, u32[]{:S(2)}, u32[]{:S(2)}) %collective-permute-start.14) | collective-permute-done | bytes 294944 | tf_op jit(solution)/shard_map/ppermute | solution.py:404
  97.4 1.8 %shard_map.107 = (bf16[256,512]{1,0:T(8,128)(2,1)S(1)}, bf16[256,512]{1,0:T(8,128)(2,1)S(1)}) custom-call(s32[6]{0:T(128)S(1)} %pad_add_fusion.1.s_ref, bf16[512,1024]{1,0:T(8,128)(2,1)S(1)} %get-tuple-element.99.c_rows, bf16[512,1024]{1,0:T(8,128)(2,1)S(1)} %get-tuple-element.100.a_rows, bf16[304,512]{1,0:T(8,128)(2,1)S(1)} %copy-done.5, ...), custom_call_target="tpu_custom_call" | custom-call | bytes 4423704 | tf_op jit(solution)/shard_map/pallas_call | solution.py:27
  99.2 5.9 %collective-permute-start.21 = (bf16[256,512]{1,0:T(8,128)(2,1)S(1)}, bf16[256,512]{1,0:T(8,128)(2,1)S(1)}, u32[]{:S(2)}, u32[]{:S(2)}) collective-permute-start(bf16[256,512]{1,0:T(8,128)(2,1)S(1)} %get-tuple-element.103.refs_0_.refs_1_.block0), channel_id=1, source_target_pairs={{0,1},{1,2},{2,3},{3,0},{4,5},{5,6},{6,7},{7,4},{8,9},{9,10},{10,1... | collective-permute-start | bytes 786440 | tf_op jit(solution)/shard_map/ppermute | solution.py:370
  105.1 1.8 %collective-permute-start.22 = (bf16[256,512]{1,0:T(8,128)(2,1)S(1)}, bf16[256,512]{1,0:T(8,128)(2,1)S(1)}, u32[]{:S(2)}, u32[]{:S(2)}) collective-permute-start(bf16[256,512]{1,0:T(8,128)(2,1)S(1)} %get-tuple-element.103.refs_0_.refs_1_.block0), channel_id=1, source_target_pairs={{0,2},{1,3},{2,0},{3,1},{4,6},{5,7},{6,4},{7,5},{8,10},{9,11},{10,... | collective-permute-start | bytes 786440 | tf_op jit(solution)/shard_map/ppermute | solution.py:370
  106.8 2.0 %collective-permute-start.23 = (bf16[256,512]{1,0:T(8,128)(2,1)S(1)}, bf16[256,512]{1,0:T(8,128)(2,1)S(1)}, u32[]{:S(2)}, u32[]{:S(2)}) collective-permute-start(bf16[256,512]{1,0:T(8,128)(2,1)S(1)} %get-tuple-element.103.refs_0_.refs_1_.block0), channel_id=1, source_target_pairs={{0,3},{1,0},{2,1},{3,2},{4,7},{5,4},{6,5},{7,6},{8,11},{9,8},{10,9... | collective-permute-start | bytes 786440 | tf_op jit(solution)/shard_map/ppermute | solution.py:370
  109.9 7.0 %collective-permute-start.31 = (bf16[256,512]{1,0:T(8,128)(2,1)S(1)}, bf16[256,512]{1,0:T(8,128)(2,1)S(1)}, u32[]{:S(2)}, u32[]{:S(2)}) collective-permute-start(bf16[256,512]{1,0:T(8,128)(2,1)S(1)} %get-tuple-element.111), channel_id=1, source_target_pairs={{0,16},{16,32},{32,48},{48,64},{64,80},{80,96},{96,112},{112,128},... | collective-permute-start | bytes 786440 | tf_op jit(solution)/shard_map/ppermute | solution.py:404
  117.0 1.8 %shard_map.108 = (bf16[512,128]{1,0:T(8,128)(2,1)S(1)}, f32[512,128]{1,0:T(8,128)S(1)}, bf16[512,128]{1,0:T(8,128)(2,1)S(1)}) custom-call(s32[6]{0:T(128)S(1)} %pad_add_fusion.1.s_ref, f32[512,128]{1,0:T(8,128)S(1)} %get-tuple-element.97.own, bf16[512,128]{1,0:T(8,128)(2,1)S(1)} %collective-permute-done.15.got1, ...), custom_call_target="tpu_custom_call" | custom-call | bytes 3342360 | tf_op jit(solution)/shard_map/pallas_call | solution.py:27
  118.8 2.5 %collective-permute-start.24 = (bf16[512,128]{1,0:T(8,128)(2,1)S(1)}, bf16[512,128]{1,0:T(8,128)(2,1)S(1)}, u32[]{:S(2)}, u32[]{:S(2)}) collective-permute-start(bf16[512,128]{1,0:T(8,128)(2,1)S(1)} %get-tuple-element.106), channel_id=1, source_target_pairs={{0,12},{1,13},{2,14},{3,15},{4,0},{5,1},{6,2},{7,3},{8,4},{9,5},{1... | collective-permute-start | bytes 393224 | tf_op jit(solution)/shard_map/ppermute | solution.py:375
  125.4 2.0 %collective-permute-start.34 = (bf16[256,1024]{1,0:T(8,128)(2,1)S(1)}, bf16[256,1024]{1,0:T(8,128)(2,1)S(1)}, u32[]{:S(2)}, u32[]{:S(2)}) collective-permute-start(bf16[256,1024]{1,0:T(8,128)(2,1)S(1)} %shard_map.112.pair0), channel_id=1, source_target_pairs={{0,3},{1,0},{2,1},{3,2},{4,7},{5,4},{6,5},{7,6},{8,11},{9,8},{10,9... | collective-permute-start | bytes 1572872 | tf_op jit(solution)/shard_map/ppermute | solution.py:370
  128.3 1.8 %shard_map.109 = (bf16[512,128]{1,0:T(8,128)(2,1)S(1)}, f32[512,128]{1,0:T(8,128)S(1)}, bf16[512,128]{1,0:T(8,128)(2,1)S(1)}) custom-call(s32[6]{0:T(128)S(1)} %pad_add_fusion.1.s_ref, f32[512,128]{1,0:T(8,128)S(1)} %get-tuple-element.105.own, bf16[512,128]{1,0:T(8,128)(2,1)S(1)} %collective-permute-done.24.got1, ...), custom_call_target="tpu_custom_call" | custom-call | bytes 3473432 | tf_op jit(solution)/shard_map/pallas_call | solution.py:27
  130.1 2.8 %collective-permute-start.27 = (bf16[512,128]{1,0:T(8,128)(2,1)S(1)}, bf16[512,128]{1,0:T(8,128)(2,1)S(1)}, u32[]{:S(2)}, u32[]{:S(2)}) collective-permute-start(bf16[512,128]{1,0:T(8,128)(2,1)S(1)} %get-tuple-element.109), channel_id=1, source_target_pairs={{0,12},{1,13},{2,14},{3,15},{4,0},{5,1},{6,2},{7,3},{8,4},{9,5},{1... | collective-permute-start | bytes 393224 | tf_op jit(solution)/shard_map/ppermute | solution.py:375
  133.1 4.7 %collective-permute-done.27.got1 = bf16[512,128]{1,0:T(8,128)(2,1)S(1)} collective-permute-done((bf16[512,128]{1,0:T(8,128)(2,1)S(1)}, bf16[512,128]{1,0:T(8,128)(2,1)S(1)}, u32[]{:S(2)}, u32[]{:S(2)}) %collective-permute-start.27) | collective-permute-done | bytes 131104 | tf_op jit(solution)/shard_map/ppermute | solution.py:375
  139.0 5.6 %collective-permute-done.29.got3 = bf16[512,128]{1,0:T(8,128)(2,1)S(1)} collective-permute-done((bf16[512,128]{1,0:T(8,128)(2,1)S(1)}, bf16[512,128]{1,0:T(8,128)(2,1)S(1)}, u32[]{:S(2)}, u32[]{:S(2)}) %collective-permute-start.29) | collective-permute-done | bytes 131104 | tf_op jit(solution)/shard_map/ppermute | solution.py:375
  145.1 6.5 %collective-permute-start.30 = (bf16[512,128]{1,0:T(8,128)(2,1)S(1)}, bf16[512,128]{1,0:T(8,128)(2,1)S(1)}, u32[]{:S(2)}, u32[]{:S(2)}) collective-permute-start(bf16[512,128]{1,0:T(8,128)(2,1)S(1)} %shard_map.110.solved), channel_id=1, source_target_pairs={{0,16},{16,32},{32,48},{48,64},{64,80},{80,96},{96,112},{112,128},... | collective-permute-start | bytes 393224 | tf_op jit(solution)/shard_map/ppermute | solution.py:404
  151.7 1.9 %collective-permute-start.35 = (bf16[512,128]{1,0:T(8,128)(2,1)S(1)}, bf16[512,128]{1,0:T(8,128)(2,1)S(1)}, u32[]{:S(2)}, u32[]{:S(2)}) collective-permute-start(bf16[512,128]{1,0:T(8,128)(2,1)S(1)} %shard_map.110.solved), channel_id=1, source_target_pairs={{16,0},{32,16},{48,32},{64,48},{80,64},{96,80},{112,96},{128,112},... | collective-permute-start | bytes 393224 | tf_op jit(solution)/shard_map/ppermute | solution.py:404
  156.3 2.9 %collective-permute-done.35.above = bf16[512,128]{1,0:T(8,128)(2,1)S(1)} collective-permute-done((bf16[512,128]{1,0:T(8,128)(2,1)S(1)}, bf16[512,128]{1,0:T(8,128)(2,1)S(1)}, u32[]{:S(2)}, u32[]{:S(2)}) %collective-permute-start.35) | collective-permute-done | bytes 131104 | tf_op jit(solution)/shard_map/ppermute | solution.py:404
  (89 shorter events, 37.4 us)
Async XLA Ops:
  7.2 41.0 %all-gather.5.cloned.1.call-start = ((), (), s32[]{:S(2)}) async-start(), calls=%async_computation.1 | async-start | bytes 1310720 | tf_op jit(solution)/shard_map/all_gather | solution.py:398
  11.1 64.5 %all-gather.7.cloned.1.call-start = ((), (), s32[]{:S(2)}) async-start(), calls=%async_computation.2 | async-start | bytes 1310720 | tf_op jit(solution)/shard_map/all_gather | solution.py:398
  11.1 17.1 %collective-permute-start = (bf16[2,64,1024]{2,1,0:T(8,128)(2,1)S(1)}, bf16[2,64,1024]{2,1,0:T(8,128)(2,1)S(1)}, u32[]{:S(2)}, u32[]{:S(2)}) collective-permute-start(bf16[2,64,1024]{2,1,0:T(8,128)(2,1)S(1)} %get-tuple-element.65), channel_id=1, source_target_pairs={{16,0},{32,16},{48,32},{64,48},{80,64},{96,80},{112,96},{128,112},... | collective-permute-start | bytes 786440 | tf_op jit(solution)/shard_map/ppermute | solution.py:404
  13.7 14.5 %collective-permute-start.1 = (bf16[64,1664]{1,0:T(8,128)(2,1)S(1)}, bf16[64,1664]{1,0:T(8,128)(2,1)S(1)}, u32[]{:S(2)}, u32[]{:S(2)}) collective-permute-start(bf16[64,1664]{1,0:T(8,128)(2,1)S(1)} %get-tuple-element.68), channel_id=1, source_target_pairs={{0,1},{1,2},{2,3},{3,0},{4,5},{5,6},{6,7},{7,4},{8,9},{9,10},{10,1... | collective-permute-start | bytes 638984 | tf_op jit(solution)/shard_map/ppermute | solution.py:370
  15.0 13.2 %collective-permute-start.2 = (bf16[64,1664]{1,0:T(8,128)(2,1)S(1)}, bf16[64,1664]{1,0:T(8,128)(2,1)S(1)}, u32[]{:S(2)}, u32[]{:S(2)}) collective-permute-start(bf16[64,1664]{1,0:T(8,128)(2,1)S(1)} %get-tuple-element.69), channel_id=1, source_target_pairs={{0,2},{1,3},{2,0},{3,1},{4,6},{5,7},{6,4},{7,5},{8,10},{9,11},{10,... | collective-permute-start | bytes 638984 | tf_op jit(solution)/shard_map/ppermute | solution.py:370
  17.4 10.8 %collective-permute-start.3 = (bf16[64,1664]{1,0:T(8,128)(2,1)S(1)}, bf16[64,1664]{1,0:T(8,128)(2,1)S(1)}, u32[]{:S(2)}, u32[]{:S(2)}) collective-permute-start(bf16[64,1664]{1,0:T(8,128)(2,1)S(1)} %get-tuple-element.70), channel_id=1, source_target_pairs={{0,3},{1,0},{2,1},{3,2},{4,7},{5,4},{6,5},{7,6},{8,11},{9,8},{10,9... | collective-permute-start | bytes 638984 | tf_op jit(solution)/shard_map/ppermute | solution.py:370
  29.6 18.5 %collective-permute-start.4 = (bf16[256,1152]{1,0:T(8,128)(2,1)S(1)}, bf16[256,1152]{1,0:T(8,128)(2,1)S(1)}, u32[]{:S(2)}, u32[]{:S(2)}) collective-permute-start(bf16[256,1152]{1,0:T(8,128)(2,1)S(1)} %get-tuple-element.77.panel0.source), channel_id=1, source_target_pairs={{0,12},{1,13},{2,14},{3,15},{4,0},{5,1},{6,2},{7,3},{8,4},{9,5},{1... | collective-permute-start | bytes 1769480 | tf_op jit(solution)/shard_map/ppermute | solution.py:375
  31.6 16.5 %collective-permute-start.5 = (bf16[256,1152]{1,0:T(8,128)(2,1)S(1)}, bf16[256,1152]{1,0:T(8,128)(2,1)S(1)}, u32[]{:S(2)}, u32[]{:S(2)}) collective-permute-start(bf16[256,1152]{1,0:T(8,128)(2,1)S(1)} %get-tuple-element.77.panel0.source), channel_id=1, source_target_pairs={{0,4},{1,5},{2,6},{3,7},{4,8},{5,9},{6,10},{7,11},{8,12},{9,13},{1... | collective-permute-start | bytes 1769480 | tf_op jit(solution)/shard_map/ppermute | solution.py:375
  31.6 16.5 %collective-permute-start.6 = (bf16[2,2,64,1024]{3,2,1,0:T(8,128)(2,1)S(1)}, bf16[2,2,64,1024]{3,2,1,0:T(8,128)(2,1)S(1)}, u32[]{:S(2)}, u32[]{:S(2)}) collective-permute-start(bf16[2,2,64,1024]{3,2,1,0:T(8,128)(2,1)S(1)} %get-tuple-element.90.ca0), channel_id=1, source_target_pairs={{0,1},{1,2},{2,3},{3,0},{4,5},{5,6},{6,7},{7,4},{8,9},{9,10},{10,1... | collective-permute-start | bytes 1572872 | tf_op jit(solution)/shard_map/ppermute | solution.py:370
  32.3 15.8 %collective-permute-start.7 = (bf16[2,2,64,1024]{3,2,1,0:T(8,128)(2,1)S(1)}, bf16[2,2,64,1024]{3,2,1,0:T(8,128)(2,1)S(1)}, u32[]{:S(2)}, u32[]{:S(2)}) collective-permute-start(bf16[2,2,64,1024]{3,2,1,0:T(8,128)(2,1)S(1)} %get-tuple-element.90.ca0), channel_id=1, source_target_pairs={{0,3},{1,0},{2,1},{3,2},{4,7},{5,4},{6,5},{7,6},{8,11},{9,8},{10,9... | collective-permute-start | bytes 1572872 | tf_op jit(solution)/shard_map/ppermute | solution.py:370
  48.8 8.3 %collective-permute-start.8 = (bf16[128,1152]{1,0:T(8,128)(2,1)S(1)}, bf16[128,1152]{1,0:T(8,128)(2,1)S(1)}, u32[]{:S(2)}, u32[]{:S(2)}) collective-permute-start(bf16[128,1152]{1,0:T(8,128)(2,1)S(1)} %get-tuple-element.83), channel_id=1, source_target_pairs={{0,4},{1,5},{2,6},{3,7},{4,8},{5,9},{6,10},{7,11},{8,12},{9,13},{1... | collective-permute-start | bytes 884744 | tf_op jit(solution)/shard_map/ppermute | solution.py:375
  51.5 18.3 %collective-permute-start.10 = (bf16[2,2,64,1024]{3,2,1,0:T(8,128)(2,1)S(1)}, bf16[2,2,64,1024]{3,2,1,0:T(8,128)(2,1)S(1)}, u32[]{:S(2)}, u32[]{:S(2)}) collective-permute-start(bf16[2,2,64,1024]{3,2,1,0:T(8,128)(2,1)S(1)} %get-tuple-element.90.ca0), channel_id=1, source_target_pairs={{0,2},{1,3},{2,0},{3,1},{4,6},{5,7},{6,4},{7,5},{8,10},{9,11},{10,... | collective-permute-start | bytes 1572872 | tf_op jit(solution)/shard_map/ppermute | solution.py:370
  60.7 16.9 %collective-permute-start.11 = (bf16[256,640]{1,0:T(8,128)(2,1)}, bf16[256,640]{1,0:T(8,128)(2,1)S(1)}, u32[]{:S(2)}, u32[]{:S(2)}) collective-permute-start(bf16[256,640]{1,0:T(8,128)(2,1)} %get-tuple-element.94.panel0), channel_id=1, source_target_pairs={{0,12},{1,13},{2,14},{3,15},{4,0},{5,1},{6,2},{7,3},{8,4},{9,5},{1... | collective-permute-start | bytes 983048 | tf_op jit(solution)/shard_map/ppermute | solution.py:375
  63.1 15.4 %collective-permute-start.12 = (bf16[256,640]{1,0:T(8,128)(2,1)}, bf16[256,640]{1,0:T(8,128)(2,1)S(1)}, u32[]{:S(2)}, u32[]{:S(2)}) collective-permute-start(bf16[256,640]{1,0:T(8,128)(2,1)} %get-tuple-element.94.panel0), channel_id=1, source_target_pairs={{0,8},{1,9},{2,10},{3,11},{4,12},{5,13},{6,14},{7,15},{8,0},{9,1},... | collective-permute-start | bytes 983048 | tf_op jit(solution)/shard_map/ppermute | solution.py:375
  64.2 17.0 %collective-permute-start.13 = (bf16[256,640]{1,0:T(8,128)(2,1)}, bf16[256,640]{1,0:T(8,128)(2,1)S(1)}, u32[]{:S(2)}, u32[]{:S(2)}) collective-permute-start(bf16[256,640]{1,0:T(8,128)(2,1)} %get-tuple-element.94.panel0), channel_id=1, source_target_pairs={{0,4},{1,5},{2,6},{3,7},{4,8},{5,9},{6,10},{7,11},{8,12},{9,13},{1... | collective-permute-start | bytes 983048 | tf_op jit(solution)/shard_map/ppermute | solution.py:375
  75.6 21.8 %collective-permute-start.18 = (bf16[304,512]{1,0:T(8,128)(2,1)}, bf16[304,512]{1,0:T(8,128)(2,1)S(1)}, u32[]{:S(2)}, u32[]{:S(2)}) collective-permute-start(bf16[304,512]{1,0:T(8,128)(2,1)} %copy-done.4), channel_id=1, source_target_pairs={{0,12},{1,13},{2,14},{3,15},{4,0},{5,1},{6,2},{7,3},{8,4},{9,5},{1... | collective-permute-start | bytes 933896 | tf_op jit(solution)/shard_map/ppermute | solution.py:375
  77.0 20.4 %collective-permute-start.19 = (bf16[304,512]{1,0:T(8,128)(2,1)}, bf16[304,512]{1,0:T(8,128)(2,1)S(1)}, u32[]{:S(2)}, u32[]{:S(2)}) collective-permute-start(bf16[304,512]{1,0:T(8,128)(2,1)} %copy-done.4), channel_id=1, source_target_pairs={{0,8},{1,9},{2,10},{3,11},{4,12},{5,13},{6,14},{7,15},{8,0},{9,1},... | collective-permute-start | bytes 933896 | tf_op jit(solution)/shard_map/ppermute | solution.py:375
  77.6 19.8 %collective-permute-start.20 = (bf16[304,512]{1,0:T(8,128)(2,1)}, bf16[304,512]{1,0:T(8,128)(2,1)S(1)}, u32[]{:S(2)}, u32[]{:S(2)}) collective-permute-start(bf16[304,512]{1,0:T(8,128)(2,1)} %copy-done.4), channel_id=1, source_target_pairs={{0,4},{1,5},{2,6},{3,7},{4,8},{5,9},{6,10},{7,11},{8,12},{9,13},{1... | collective-permute-start | bytes 933896 | tf_op jit(solution)/shard_map/ppermute | solution.py:375
  85.2 8.9 %collective-permute-start.14 = (bf16[288,512]{1,0:T(8,128)(2,1)S(1)}, bf16[288,512]{1,0:T(8,128)(2,1)S(1)}, u32[]{:S(2)}, u32[]{:S(2)}) collective-permute-start(bf16[288,512]{1,0:T(8,128)(2,1)S(1)} %get-tuple-element.96), channel_id=1, source_target_pairs={{0,16},{16,32},{32,48},{48,64},{64,80},{80,96},{96,112},{112,128},... | collective-permute-start | bytes 884744 | tf_op jit(solution)/shard_map/ppermute | solution.py:404
  95.3 13.5 %collective-permute-start.15 = (bf16[512,128]{1,0:T(8,128)(2,1)S(1)}, bf16[512,128]{1,0:T(8,128)(2,1)S(1)}, u32[]{:S(2)}, u32[]{:S(2)}) collective-permute-start(bf16[512,128]{1,0:T(8,128)(2,1)S(1)} %get-tuple-element.98), channel_id=1, source_target_pairs={{0,12},{1,13},{2,14},{3,15},{4,0},{5,1},{6,2},{7,3},{8,4},{9,5},{1... | collective-permute-start | bytes 393224 | tf_op jit(solution)/shard_map/ppermute | solution.py:375
  95.7 14.2 %collective-permute-start.16 = (bf16[512,128]{1,0:T(8,128)(2,1)S(1)}, bf16[512,128]{1,0:T(8,128)(2,1)S(1)}, u32[]{:S(2)}, u32[]{:S(2)}) collective-permute-start(bf16[512,128]{1,0:T(8,128)(2,1)S(1)} %get-tuple-element.98), channel_id=1, source_target_pairs={{0,8},{1,9},{2,10},{3,11},{4,12},{5,13},{6,14},{7,15},{8,0},{9,1},... | collective-permute-start | bytes 393224 | tf_op jit(solution)/shard_map/ppermute | solution.py:375
  99.2 17.7 %collective-permute-start.21 = (bf16[256,512]{1,0:T(8,128)(2,1)S(1)}, bf16[256,512]{1,0:T(8,128)(2,1)S(1)}, u32[]{:S(2)}, u32[]{:S(2)}) collective-permute-start(bf16[256,512]{1,0:T(8,128)(2,1)S(1)} %get-tuple-element.103.refs_0_.refs_1_.block0), channel_id=1, source_target_pairs={{0,1},{1,2},{2,3},{3,0},{4,5},{5,6},{6,7},{7,4},{8,9},{9,10},{10,1... | collective-permute-start | bytes 786440 | tf_op jit(solution)/shard_map/ppermute | solution.py:370
  105.1 11.9 %collective-permute-start.22 = (bf16[256,512]{1,0:T(8,128)(2,1)S(1)}, bf16[256,512]{1,0:T(8,128)(2,1)S(1)}, u32[]{:S(2)}, u32[]{:S(2)}) collective-permute-start(bf16[256,512]{1,0:T(8,128)(2,1)S(1)} %get-tuple-element.103.refs_0_.refs_1_.block0), channel_id=1, source_target_pairs={{0,2},{1,3},{2,0},{3,1},{4,6},{5,7},{6,4},{7,5},{8,10},{9,11},{10,... | collective-permute-start | bytes 786440 | tf_op jit(solution)/shard_map/ppermute | solution.py:370
  106.8 10.1 %collective-permute-start.23 = (bf16[256,512]{1,0:T(8,128)(2,1)S(1)}, bf16[256,512]{1,0:T(8,128)(2,1)S(1)}, u32[]{:S(2)}, u32[]{:S(2)}) collective-permute-start(bf16[256,512]{1,0:T(8,128)(2,1)S(1)} %get-tuple-element.103.refs_0_.refs_1_.block0), channel_id=1, source_target_pairs={{0,3},{1,0},{2,1},{3,2},{4,7},{5,4},{6,5},{7,6},{8,11},{9,8},{10,9... | collective-permute-start | bytes 786440 | tf_op jit(solution)/shard_map/ppermute | solution.py:370
  108.8 8.1 %collective-permute-start.17 = (bf16[512,128]{1,0:T(8,128)(2,1)S(1)}, bf16[512,128]{1,0:T(8,128)(2,1)S(1)}, u32[]{:S(2)}, u32[]{:S(2)}) collective-permute-start(bf16[512,128]{1,0:T(8,128)(2,1)S(1)} %get-tuple-element.98), channel_id=1, source_target_pairs={{0,4},{1,5},{2,6},{3,7},{4,8},{5,9},{6,10},{7,11},{8,12},{9,13},{1... | collective-permute-start | bytes 393224 | tf_op jit(solution)/shard_map/ppermute | solution.py:375
  109.9 13.6 %collective-permute-start.31 = (bf16[256,512]{1,0:T(8,128)(2,1)S(1)}, bf16[256,512]{1,0:T(8,128)(2,1)S(1)}, u32[]{:S(2)}, u32[]{:S(2)}) collective-permute-start(bf16[256,512]{1,0:T(8,128)(2,1)S(1)} %get-tuple-element.111), channel_id=1, source_target_pairs={{0,16},{16,32},{32,48},{48,64},{64,80},{80,96},{96,112},{112,128},... | collective-permute-start | bytes 786440 | tf_op jit(solution)/shard_map/ppermute | solution.py:404
  124.1 30.7 %collective-permute-start.32 = (bf16[256,1024]{1,0:T(8,128)(2,1)S(1)}, bf16[256,1024]{1,0:T(8,128)(2,1)S(1)}, u32[]{:S(2)}, u32[]{:S(2)}) collective-permute-start(bf16[256,1024]{1,0:T(8,128)(2,1)S(1)} %shard_map.112.pair0), channel_id=1, source_target_pairs={{0,1},{1,2},{2,3},{3,0},{4,5},{5,6},{6,7},{7,4},{8,9},{9,10},{10,1... | collective-permute-start | bytes 1572872 | tf_op jit(solution)/shard_map/ppermute | solution.py:370
  124.5 30.4 %collective-permute-start.33 = (bf16[256,1024]{1,0:T(8,128)(2,1)S(1)}, bf16[256,1024]{1,0:T(8,128)(2,1)S(1)}, u32[]{:S(2)}, u32[]{:S(2)}) collective-permute-start(bf16[256,1024]{1,0:T(8,128)(2,1)S(1)} %shard_map.112.pair0), channel_id=1, source_target_pairs={{0,2},{1,3},{2,0},{3,1},{4,6},{5,7},{6,4},{7,5},{8,10},{9,11},{10,... | collective-permute-start | bytes 1572872 | tf_op jit(solution)/shard_map/ppermute | solution.py:370
  125.4 29.4 %collective-permute-start.34 = (bf16[256,1024]{1,0:T(8,128)(2,1)S(1)}, bf16[256,1024]{1,0:T(8,128)(2,1)S(1)}, u32[]{:S(2)}, u32[]{:S(2)}) collective-permute-start(bf16[256,1024]{1,0:T(8,128)(2,1)S(1)} %shard_map.112.pair0), channel_id=1, source_target_pairs={{0,3},{1,0},{2,1},{3,2},{4,7},{5,4},{6,5},{7,6},{8,11},{9,8},{10,9... | collective-permute-start | bytes 1572872 | tf_op jit(solution)/shard_map/ppermute | solution.py:370
  130.1 7.7 %collective-permute-start.27 = (bf16[512,128]{1,0:T(8,128)(2,1)S(1)}, bf16[512,128]{1,0:T(8,128)(2,1)S(1)}, u32[]{:S(2)}, u32[]{:S(2)}) collective-permute-start(bf16[512,128]{1,0:T(8,128)(2,1)S(1)} %get-tuple-element.109), channel_id=1, source_target_pairs={{0,12},{1,13},{2,14},{3,15},{4,0},{5,1},{6,2},{7,3},{8,4},{9,5},{1... | collective-permute-start | bytes 393224 | tf_op jit(solution)/shard_map/ppermute | solution.py:375
  145.1 11.1 %collective-permute-start.30 = (bf16[512,128]{1,0:T(8,128)(2,1)S(1)}, bf16[512,128]{1,0:T(8,128)(2,1)S(1)}, u32[]{:S(2)}, u32[]{:S(2)}) collective-permute-start(bf16[512,128]{1,0:T(8,128)(2,1)S(1)} %shard_map.110.solved), channel_id=1, source_target_pairs={{0,16},{16,32},{32,48},{48,64},{64,80},{80,96},{96,112},{112,128},... | collective-permute-start | bytes 393224 | tf_op jit(solution)/shard_map/ppermute | solution.py:404
  151.7 7.5 %collective-permute-start.35 = (bf16[512,128]{1,0:T(8,128)(2,1)S(1)}, bf16[512,128]{1,0:T(8,128)(2,1)S(1)}, u32[]{:S(2)}, u32[]{:S(2)}) collective-permute-start(bf16[512,128]{1,0:T(8,128)(2,1)S(1)} %shard_map.110.solved), channel_id=1, source_target_pairs={{16,0},{32,16},{48,32},{64,48},{80,64},{96,80},{112,96},{128,112},... | collective-permute-start | bytes 393224 | tf_op jit(solution)/shard_map/ppermute | solution.py:404
  (18 other events, 87.8 us)
Sparse Core Ops, SparseCore 0:
  11.2 28.6 all-gather.4
  41.7 33.8 all-gather.6

commit v6 on v5

--- a/solution.py
+++ b/solution.py
@@ -203,21 +203,16 @@
     put_pair(out, *wide_product(y, held, panels))
     out[:, pl.ds(512, 128)] = small_product(y, held, panels).astype(BF)
     put_pair(out_second, *wide_product(y, held, panels, 640))
-    out_second[pl.ds(256, 48), :] = jnp.zeros((48, 512), BF)
+    out_second[pl.ds(256, 16), :] = jnp.zeros((16, 512), BF)
 
 
 def even_kernel(s_ref, ca0, ca1, ca2, ca3, panel0, panel1, panel2, panel3, source,
-                ship, upper_new, source_part, a_rows, c_rows):
+                ship, ship_source, upper_new, source_part, a_rows, c_rows):
     y, x = s_ref[0], s_ref[1]
     panels = (panel0, panel1, panel2, panel3)
     stack_rows(x, [block.at[1] for block in (ca0, ca1, ca2, ca3)], a_rows)
     stack_rows(x, [block.at[0] for block in (ca0, ca1, ca2, ca3)], c_rows)
-    value = small_product(y, a_rows, panels)
-    lane = lanes_of(32)
-    for index in range(4):
-        low, high = value[index * 64 : index * 64 + 32], value[index * 64 + 32 : index * 64 + 64]
-        tile = jnp.where(lane < 64, low, pltpu.roll(high, 64, 1))
-        ship[pl.ds(256, 32), pl.ds(index * 128, 128)] = tile.astype(BF)
+    ship_source[...] = small_product(y, a_rows, panels).astype(BF)
     put_pair(ship, *wide_product(y, a_rows, panels))
     own = pltpu.roll(source[:, pl.ds(512, 128)].astype(F32), 64, 1)
     own = jnp.where(lanes_of(256) < 64, own, 0.0)
@@ -261,14 +256,8 @@
 
 
 def source_kernel(s_ref, g_ref, source_part, shipped, source_new, own, send, whole):
-    lane = lanes_of(32)
-    for index in range(4):
-        tile = shipped[pl.ds(256, 32), pl.ds(index * 128, 128)].astype(F32)
-        for half, moved in enumerate(halves(tile)):
-            rows = pl.ds(index * 64 + half * 32, 32)
-            value = source_part[rows, :] - jnp.where(lane < 64, moved, 0.0)
-            source_new[rows, :] = value.astype(BF)
-    source = source_new[...]
+    source = (source_part[...] - shipped[...].astype(F32)).astype(BF)
+    source_new[...] = source
     put_partial(g_ref, source, own, send, whole)
 
 
@@ -441,27 +430,26 @@
         0, scalars, *pieces, c_even, a_next,
     )
     g_columns = gathered_x(g_columns)
-    near = (g_rows, moved_x(couplings, 1), moved_x(couplings, 3))
-    panels, near = ring_gathered_y(scalars, panel, near)
-    g_rows = near[0]
-    ca_blocks = [couplings, near[1], moved_x(couplings, 2), near[2]]
+    panels, (g_rows,) = ring_gathered_y(scalars, panel, (g_rows,))
+    ca_blocks = [couplings] + [moved_x(couplings, by) for by in turns]
     first, second = call(
-        odd_kernel, [shape((256, 640)), shape((304, 512))], wide_flops,
+        odd_kernel, [shape((256, 640)), shape((272, 512))], wide_flops,
         scalars, g_rows, *panels,
         scratch=[pltpu.VMEM((512, 1024), BF), pltpu.VMEM((256, 1152), BF)],
     )
     firsts = gathered_y(first)
     second, g_columns, *ca_blocks = after((second, g_columns, *ca_blocks))
     seconds = gathered_y(second)
-    ship, upper_new, source_part, a_rows, c_rows = call(
+    ship, ship_source, upper_new, source_part, a_rows, c_rows = call(
         even_kernel,
-        [shape((288, 512)), shape((256, 512)), shape((256, 128), F32),
+        [shape((256, 512)), shape((256, 128)), shape((256, 512)), shape((256, 128), F32),
          shape((512, 1024)),
          shape((512, 1024))],
         2 * wide_flops,
         scalars, *ca_blocks, *firsts, panel,
     )
     shipped = along_cuts(ship, 1)
+    shipped_source = along_cuts(ship_source, 1)
     diagonal_new, ship_lower = call(
         diagonal_kernel, [shape((256, 512))] * 2, 2 * wide_flops,
         scalars, c_rows, a_rows, *seconds, diagonal, shipped,
@@ -472,7 +460,7 @@
     vector = pltpu.VMEM((1024, 128), BF)
     source, own, send = call(
         source_kernel, [shape((256, 128))] + packed_shapes, solve_flops,
-        scalars, g_columns, source_part, shipped, scratch=[whole],
+        scalars, g_columns, source_part, shipped_source, scratch=[whole],
     )
     got = gathered_y(send)[1:]
     lower_new = along_cuts(ship_lower, 1)

time: 174 us -> 178 us (1.023)
  waiting for transfers between devices: 51.1 us -> 57.3 us
  starting transfers between devices: 71.3 us -> 68.7 us
    ppermute x15, waiting for transfers between devices: 21.6 us -> 28.3 us  [moved_x(): return lax.ppermute(block, 'row', pairs)]
    ppermute x19, waiting for transfers between devices: 18 us -> 24.2 us  [moved_y(): return lax.ppermute(block, 'row', pairs)]
    all_gather x2, waiting for transfers between devices: 5 us -> 0.01 us  [gathered_x(): return lax.all_gather(block, 'row', axis_index_groups=groups)]
    ppermute x5 -> x6, starting transfers between devices: 23.3 us -> 28.1 us  [along_cuts(): return lax.ppermute(block, 'cuts', pairs)]
    ppermute x19, starting transfers between devices: 22.1 us -> 18.1 us  [moved_y(): return lax.ppermute(block, 'row', pairs)]
    ppermute x15, starting transfers between devices: 25.9 us -> 22.4 us  [moved_x(): return lax.ppermute(block, 'row', pairs)]
    ppermute x5 -> x6, waiting for transfers between devices: 6.54 us -> 4.64 us  [along_cuts(): return lax.ppermute(block, 'cuts', pairs)]
  transfers between devices with their start and end apart: 41 -> 42, of which waited for: 14 -> 15; matrix products, arithmetic and copies ran while one was open for 0% -> 0% of each run, Pallas kernels for 10% -> 10%
where the time goes in v6:
time: 178 us; the launch traced here: 177 us
  starting transfers between devices  68.7 us (39%)
  waiting for transfers between devices  57.3 us (32%)
  Pallas kernels  23.2 us (13%)
  between operations  14.3 us (8%)
  blocking collectives  9.62 us (5%)
  local copies, waits for them, and re-layouts  3.99 us (2%)
    ppermute x15, waiting for transfers between devices, moved_x(): return lax.ppermute(block, 'row', pairs)  28.3 us
    ppermute x6, starting transfers between devices, along_cuts(): return lax.ppermute(block, 'cuts', pairs)  28.1 us
    ppermute x19, waiting for transfers between devices, moved_y(): return lax.ppermute(block, 'row', pairs)  24.2 us
    pallas_call x15, Pallas kernels, call(): pl.pallas_call(kernel, out_shape=tuple(out_shapes), in_specs=[SMEM] + [an...  23.2 us
    ppermute x15, starting transfers between devices, moved_x(): return lax.ppermute(block, 'row', pairs)  22.4 us
    ppermute x19, starting transfers between devices, moved_y(): return lax.ppermute(block, 'row', pairs)  18.1 us
    all_to_all x1, blocking collectives, body(): lax.all_to_all(g_pieces, 'row', 0, 0, axis_index_groups=groups, tiled=True)  9.62 us
    ppermute x6, waiting for transfers between devices, along_cuts(): return lax.ppermute(block, 'cuts', pairs)  4.64 us
  transfers between devices with their start and end apart: 42, of which 15 were waited for; matrix products, arithmetic and copies ran while one was open for 0% of the time, Pallas kernels for 10%

profile of v6, /device:TPU:97, one launch (start us, length us, event | category | flops | bytes accessed | tf_op | source)
XLA Modules:
  0.0 177.3 jit_solution(5309388212863167784)
XLA Ops:
  8.1 2.9 %shard_map.101 = (bf16[64,1664]{1,0:T(8,128)(2,1)S(1)}, bf16[64,1664]{1,0:T(8,128)(2,1)S(1)}, bf16[64,1664]{1,0:T(8,128)(2,1)S(1)}, bf16[64,1664]{1,0:T(8,128)(2...) custom-call(s32[6]{0:T(128)S(1)} %pad_add_fusion.1.s_ref, ...), custom_call_target="tpu_custom_call" | custom-call | bytes 4063256 | tf_op jit(solution)/shard_map/pallas_call | solution.py:27
  11.1 2.6 %collective-permute-start = (bf16[2,64,1024]{2,1,0:T(8,128)(2,1)S(1)}, bf16[2,64,1024]{2,1,0:T(8,128)(2,1)S(1)}, u32[]{:S(2)}, u32[]{:S(2)}) collective-permute-start(bf16[2,64,1024]{2,1,0:T(8,128)(2,1)S(1)} %get-tuple-element.64), channel_id=1, source_target_pairs={{16,0},{32,16},{48,32},{64,48},{80,64},{96,80},{112,96},{128,112},... | collective-permute-start | bytes 786440 | tf_op jit(solution)/shard_map/ppermute | solution.py:393
  15.0 2.5 %collective-permute-start.2 = (bf16[64,1664]{1,0:T(8,128)(2,1)S(1)}, bf16[64,1664]{1,0:T(8,128)(2,1)S(1)}, u32[]{:S(2)}, u32[]{:S(2)}) collective-permute-start(bf16[64,1664]{1,0:T(8,128)(2,1)S(1)} %get-tuple-element.68), channel_id=1, source_target_pairs={{0,2},{1,3},{2,0},{3,1},{4,6},{5,7},{6,4},{7,5},{8,10},{9,11},{10,... | collective-permute-start | bytes 638984 | tf_op jit(solution)/shard_map/ppermute | solution.py:359
  18.6 9.6 %all_to_all.5 = bf16[4,2,64,256]{3,2,1,0:T(8,128)(2,1)} all-to-all(bf16[4,2,64,256]{3,2,1,0:T(8,128)(2,1)S(1)} %get-tuple-element.65), channel_id=1, replica_groups={{0,4,8,12},{1,5,9,13},{2,6,10,14},{3,7,11,15},{16,20,24,28},{17,21,25,2..., dimensions={0} | all-to-all | bytes 524288 | tf_op jit(solution)/shard_map/all_to_all | solution.py:423
  29.6 2.0 %collective-permute-start.4 = (bf16[256,1152]{1,0:T(8,128)(2,1)S(1)}, bf16[256,1152]{1,0:T(8,128)(2,1)S(1)}, u32[]{:S(2)}, u32[]{:S(2)}) collective-permute-start(bf16[256,1152]{1,0:T(8,128)(2,1)S(1)} %get-tuple-element.76.panel0.source), channel_id=1, source_target_pairs={{0,12},{1,13},{2,14},{3,15},{4,0},{5,1},{6,2},{7,3},{8,4},{9,5},{1... | collective-permute-start | bytes 1769480 | tf_op jit(solution)/shard_map/ppermute | solution.py:364
  31.6 2.2 %collective-permute-start.10 = (bf16[2,2,64,1024]{3,2,1,0:T(8,128)(2,1)S(1)}, bf16[2,2,64,1024]{3,2,1,0:T(8,128)(2,1)S(1)}, u32[]{:S(2)}, u32[]{:S(2)}) collective-permute-start(bf16[2,2,64,1024]{3,2,1,0:T(8,128)(2,1)S(1)} %get-tuple-element.87.ca0), channel_id=1, source_target_pairs={{0,3},{1,0},{2,1},{3,2},{4,7},{5,4},{6,5},{7,6},{8,11},{9,8},{10,9... | collective-permute-start | bytes 1572872 | tf_op jit(solution)/shard_map/ppermute | solution.py:359
  33.9 9.2 %collective-permute-done.4.other.panel1 = bf16[256,1152]{1,0:T(8,128)(2,1)S(1)} collective-permute-done((bf16[256,1152]{1,0:T(8,128)(2,1)S(1)}, bf16[256,1152]{1,0:T(8,128)(2,1)S(1)}, u32[]{:S(2)}, u32[]{:S(2)}) %collective-permute-start.4) | collective-permute-done | bytes 589856 | tf_op jit(solution)/shard_map/ppermute | solution.py:364
  43.1 3.1 %collective-permute-done.5.block.panel3 = bf16[256,1152]{1,0:T(8,128)(2,1)S(1)} collective-permute-done((bf16[256,1152]{1,0:T(8,128)(2,1)S(1)}, bf16[256,1152]{1,0:T(8,128)(2,1)S(1)}, u32[]{:S(2)}, u32[]{:S(2)}) %collective-permute-start.5) | collective-permute-done | bytes 589856 | tf_op jit(solution)/shard_map/ppermute | solution.py:364
  46.9 2.7 %collective-permute-start.7 = (bf16[128,1152]{1,0:T(8,128)(2,1)S(1)}, bf16[128,1152]{1,0:T(8,128)(2,1)S(1)}, u32[]{:S(2)}, u32[]{:S(2)}) collective-permute-start(bf16[128,1152]{1,0:T(8,128)(2,1)S(1)} %get-tuple-element.82), channel_id=1, source_target_pairs={{0,12},{1,13},{2,14},{3,15},{4,0},{5,1},{6,2},{7,3},{8,4},{9,5},{1... | collective-permute-start | bytes 884744 | tf_op jit(solution)/shard_map/ppermute | solution.py:364
  50.4 3.1 %collective-permute-start.9 = (bf16[2,2,64,1024]{3,2,1,0:T(8,128)(2,1)S(1)}, bf16[2,2,64,1024]{3,2,1,0:T(8,128)(2,1)S(1)}, u32[]{:S(2)}, u32[]{:S(2)}) collective-permute-start(bf16[2,2,64,1024]{3,2,1,0:T(8,128)(2,1)S(1)} %get-tuple-element.87.ca0), channel_id=1, source_target_pairs={{0,2},{1,3},{2,0},{3,1},{4,6},{5,7},{6,4},{7,5},{8,10},{9,11},{10,... | collective-permute-start | bytes 1572872 | tf_op jit(solution)/shard_map/ppermute | solution.py:359
  54.3 2.9 %shard_map.104 = (bf16[256,640]{1,0:T(8,128)(2,1)}, bf16[272,512]{1,0:T(8,128)(2,1)S(1)}) custom-call(s32[6]{0:T(128)S(1)} %pad_add_fusion.1.s_ref, bf16[4,2,64,1024]{3,2,1,0:T(8,128)(2,1)S(1)} %bitcast.12, bf16[256,1152]{1,0:T(8,128)(2,1)S(1)} %get-tuple-element.76.panel0.source, bf16[256,1152]{1,0:T(8,128)(2,1)S(1)} %collective-permute-done.4.other.panel1, ...), custom_call_target="tpu_custom_call" | custom-call | bytes 4014104 | tf_op jit(solution)/shard_map/pallas_call | solution.py:27
  58.0 2.4 %collective-permute-start.11 = (bf16[256,640]{1,0:T(8,128)(2,1)}, bf16[256,640]{1,0:T(8,128)(2,1)S(1)}, u32[]{:S(2)}, u32[]{:S(2)}) collective-permute-start(bf16[256,640]{1,0:T(8,128)(2,1)} %get-tuple-element.91.panel0), channel_id=1, source_target_pairs={{0,12},{1,13},{2,14},{3,15},{4,0},{5,1},{6,2},{7,3},{8,4},{9,5},{1... | collective-permute-start | bytes 983048 | tf_op jit(solution)/shard_map/ppermute | solution.py:364
  62.4 20.1 %collective-permute-done.9.ca2 = bf16[2,2,64,1024]{3,2,1,0:T(8,128)(2,1)S(1)} collective-permute-done((bf16[2,2,64,1024]{3,2,1,0:T(8,128)(2,1)S(1)}, bf16[2,2,64,1024]{3,2,1,0:T(8,128)(2,1)S(1)}, u32[]{:S(2)}, u32[]{:S(2)}) %collective-permute-start.9) | collective-permute-done | bytes 524320 | tf_op jit(solution)/shard_map/ppermute | solution.py:359
  85.8 2.9 %shard_map.105 = (bf16[256,512]{1,0:T(8,128)(2,1)S(1)}, bf16[256,128]{1,0:T(8,128)(2,1)S(1)}, bf16[256,512]{1,0:T(8,128)(2,1)S(1)}, f32[256,128]{1,0:T(8,128)S(1...) custom-call(s32[6]{0:T(128)S(1)} %pad_add_fusion.1.s_ref, ...), custom_call_target="tpu_custom_call" | custom-call | bytes 6815768 | tf_op jit(solution)/shard_map/pallas_call | solution.py:27
  88.7 9.4 %collective-permute-start.21 = (bf16[256,512]{1,0:T(8,128)(2,1)S(1)}, bf16[256,512]{1,0:T(8,128)(2,1)S(1)}, u32[]{:S(2)}, u32[]{:S(2)}) collective-permute-start(bf16[256,512]{1,0:T(8,128)(2,1)S(1)} %get-tuple-element.100), channel_id=1, source_target_pairs={{0,16},{16,32},{32,48},{48,64},{64,80},{80,96},{96,112},{112,128},... | collective-permute-start | bytes 786440 | tf_op jit(solution)/shard_map/ppermute | solution.py:393
  98.1 1.9 %collective-permute-start.14 = (bf16[256,128]{1,0:T(8,128)(2,1)S(1)}, bf16[256,128]{1,0:T(8,128)(2,1)S(1)}, u32[]{:S(2)}, u32[]{:S(2)}) collective-permute-start(bf16[256,128]{1,0:T(8,128)(2,1)S(1)} %get-tuple-element.93), channel_id=1, source_target_pairs={{0,16},{16,32},{32,48},{48,64},{64,80},{80,96},{96,112},{112,128},... | collective-permute-start | bytes 196616 | tf_op jit(solution)/shard_map/ppermute | solution.py:393
  100.0 2.1 %collective-permute-done.14.shipped = bf16[256,128]{1,0:T(8,128)(2,1)S(1)} collective-permute-done((bf16[256,128]{1,0:T(8,128)(2,1)S(1)}, bf16[256,128]{1,0:T(8,128)(2,1)S(1)}, u32[]{:S(2)}, u32[]{:S(2)}) %collective-permute-start.14) | collective-permute-done | bytes 65568 | tf_op jit(solution)/shard_map/ppermute | solution.py:393
  103.3 2.5 %collective-permute-start.15 = (bf16[512,128]{1,0:T(8,128)(2,1)S(1)}, bf16[512,128]{1,0:T(8,128)(2,1)S(1)}, u32[]{:S(2)}, u32[]{:S(2)}) collective-permute-start(bf16[512,128]{1,0:T(8,128)(2,1)S(1)} %get-tuple-element.95), channel_id=1, source_target_pairs={{0,12},{1,13},{2,14},{3,15},{4,0},{5,1},{6,2},{7,3},{8,4},{9,5},{1... | collective-permute-start | bytes 393224 | tf_op jit(solution)/shard_map/ppermute | solution.py:364
  109.3 2.6 %collective-permute-start.24 = (bf16[256,512]{1,0:T(8,128)(2,1)S(1)}, bf16[256,512]{1,0:T(8,128)(2,1)S(1)}, u32[]{:S(2)}, u32[]{:S(2)}) collective-permute-start(bf16[256,512]{1,0:T(8,128)(2,1)S(1)} %get-tuple-element.101.refs_0_.refs_1_.block0), channel_id=1, source_target_pairs={{0,3},{1,0},{2,1},{3,2},{4,7},{5,4},{6,5},{7,6},{8,11},{9,8},{10,9... | collective-permute-start | bytes 786440 | tf_op jit(solution)/shard_map/ppermute | solution.py:359
  112.7 6.9 %collective-permute-start.32 = (bf16[256,512]{1,0:T(8,128)(2,1)S(1)}, bf16[256,512]{1,0:T(8,128)(2,1)S(1)}, u32[]{:S(2)}, u32[]{:S(2)}) collective-permute-start(bf16[256,512]{1,0:T(8,128)(2,1)S(1)} %get-tuple-element.109), channel_id=1, source_target_pairs={{0,16},{16,32},{32,48},{48,64},{64,80},{80,96},{96,112},{112,128},... | collective-permute-start | bytes 786440 | tf_op jit(solution)/shard_map/ppermute | solution.py:393
  119.7 4.7 %collective-permute-done.22.refs_1_.refs_2_.block1 = bf16[256,512]{1,0:T(8,128)(2,1)S(1)} collective-permute-done((bf16[256,512]{1,0:T(8,128)(2,1)S(1)}, bf16[256,512]{1,0:T(8,128)(2,1)S(1)}, u32[]{:S(2)}, u32[]{:S(2)}) %collective-permute-start.22) | collective-permute-done | bytes 262176 | tf_op jit(solution)/shard_map/ppermute | solution.py:359
  124.7 1.8 %shard_map.108 = (bf16[512,128]{1,0:T(8,128)(2,1)S(1)}, f32[512,128]{1,0:T(8,128)S(1)}, bf16[512,128]{1,0:T(8,128)(2,1)S(1)}) custom-call(s32[6]{0:T(128)S(1)} %pad_add_fusion.1.s_ref, f32[512,128]{1,0:T(8,128)S(1)} %get-tuple-element.94.own, bf16[512,128]{1,0:T(8,128)(2,1)S(1)} %collective-permute-done.15.got1, ...), custom_call_target="tpu_custom_call" | custom-call | bytes 3342360 | tf_op jit(solution)/shard_map/pallas_call | solution.py:27
  126.7 2.1 %collective-permute-start.26 = (bf16[512,128]{1,0:T(8,128)(2,1)S(1)}, bf16[512,128]{1,0:T(8,128)(2,1)S(1)}, u32[]{:S(2)}, u32[]{:S(2)}) collective-permute-start(bf16[512,128]{1,0:T(8,128)(2,1)S(1)} %get-tuple-element.104), channel_id=1, source_target_pairs={{0,8},{1,9},{2,10},{3,11},{4,12},{5,13},{6,14},{7,15},{8,0},{9,1},... | collective-permute-start | bytes 393224 | tf_op jit(solution)/shard_map/ppermute | solution.py:364
  129.9 3.0 %collective-permute-start.34 = (bf16[256,1024]{1,0:T(8,128)(2,1)S(1)}, bf16[256,1024]{1,0:T(8,128)(2,1)S(1)}, u32[]{:S(2)}, u32[]{:S(2)}) collective-permute-start(bf16[256,1024]{1,0:T(8,128)(2,1)S(1)} %shard_map.112.pair0), channel_id=1, source_target_pairs={{0,2},{1,3},{2,0},{3,1},{4,6},{5,7},{6,4},{7,5},{8,10},{9,11},{10,... | collective-permute-start | bytes 1572872 | tf_op jit(solution)/shard_map/ppermute | solution.py:359
  133.0 2.6 %collective-permute-done.27.got3 = bf16[512,128]{1,0:T(8,128)(2,1)S(1)} collective-permute-done((bf16[512,128]{1,0:T(8,128)(2,1)S(1)}, bf16[512,128]{1,0:T(8,128)(2,1)S(1)}, u32[]{:S(2)}, u32[]{:S(2)}) %collective-permute-start.27) | collective-permute-done | bytes 131104 | tf_op jit(solution)/shard_map/ppermute | solution.py:364
  135.6 1.8 %shard_map.109 = (bf16[512,128]{1,0:T(8,128)(2,1)S(1)}, f32[512,128]{1,0:T(8,128)S(1)}, bf16[512,128]{1,0:T(8,128)(2,1)S(1)}) custom-call(s32[6]{0:T(128)S(1)} %pad_add_fusion.1.s_ref, f32[512,128]{1,0:T(8,128)S(1)} %get-tuple-element.103.own, bf16[512,128]{1,0:T(8,128)(2,1)S(1)} %collective-permute-done.25.got1, ...), custom_call_target="tpu_custom_call" | custom-call | bytes 3473432 | tf_op jit(solution)/shard_map/pallas_call | solution.py:27
  139.1 2.4 %collective-permute-done.28.got1 = bf16[512,128]{1,0:T(8,128)(2,1)S(1)} collective-permute-done((bf16[512,128]{1,0:T(8,128)(2,1)S(1)}, bf16[512,128]{1,0:T(8,128)(2,1)S(1)}, u32[]{:S(2)}, u32[]{:S(2)}) %collective-permute-start.28) | collective-permute-done | bytes 131104 | tf_op jit(solution)/shard_map/ppermute | solution.py:364
  143.3 4.2 %collective-permute-done.30.got3 = bf16[512,128]{1,0:T(8,128)(2,1)S(1)} collective-permute-done((bf16[512,128]{1,0:T(8,128)(2,1)S(1)}, bf16[512,128]{1,0:T(8,128)(2,1)S(1)}, u32[]{:S(2)}, u32[]{:S(2)}) %collective-permute-start.30) | collective-permute-done | bytes 131104 | tf_op jit(solution)/shard_map/ppermute | solution.py:364
  148.1 5.1 %collective-permute-start.31 = (bf16[512,128]{1,0:T(8,128)(2,1)S(1)}, bf16[512,128]{1,0:T(8,128)(2,1)S(1)}, u32[]{:S(2)}, u32[]{:S(2)}) collective-permute-start(bf16[512,128]{1,0:T(8,128)(2,1)S(1)} %shard_map.110.solved), channel_id=1, source_target_pairs={{0,16},{16,32},{32,48},{48,64},{64,80},{80,96},{96,112},{112,128},... | collective-permute-start | bytes 393224 | tf_op jit(solution)/shard_map/ppermute | solution.py:393
  153.2 2.2 %collective-permute-start.36 = (bf16[512,128]{1,0:T(8,128)(2,1)S(1)}, bf16[512,128]{1,0:T(8,128)(2,1)S(1)}, u32[]{:S(2)}, u32[]{:S(2)}) collective-permute-start(bf16[512,128]{1,0:T(8,128)(2,1)S(1)} %shard_map.110.solved), channel_id=1, source_target_pairs={{16,0},{32,16},{48,32},{64,48},{80,64},{96,80},{112,96},{128,112},... | collective-permute-start | bytes 393224 | tf_op jit(solution)/shard_map/ppermute | solution.py:393
  158.1 2.6 %collective-permute-done.36.above = bf16[512,128]{1,0:T(8,128)(2,1)S(1)} collective-permute-done((bf16[512,128]{1,0:T(8,128)(2,1)S(1)}, bf16[512,128]{1,0:T(8,128)(2,1)S(1)}, u32[]{:S(2)}, u32[]{:S(2)}) %collective-permute-start.36) | collective-permute-done | bytes 131104 | tf_op jit(solution)/shard_map/ppermute | solution.py:393
  162.1 2.7 %collective-permute-start.37 = (f32[64,128]{1,0:T(8,128)S(1)}, f32[64,128]{1,0:T(8,128)S(1)}, u32[]{:S(2)}, u32[]{:S(2)}) collective-permute-start(f32[64,128]{1,0:T(8,128)S(1)} %get-tuple-element.118), channel_id=1, source_target_pairs={{0,1},{1,2},{2,3},{3,0},{4,5},{5,6},{6,7},{7,4},{8,9},{9,10},{10,1... | collective-permute-start | bytes 98312 | tf_op jit(solution)/shard_map/ppermute | solution.py:359
  (91 shorter events, 34.2 us)
Async XLA Ops:
  7.2 39.1 %all-gather.5.cloned.1.call-start = ((), (), s32[]{:S(2)}) async-start(), calls=%async_computation.1 | async-start | bytes 1310720 | tf_op jit(solution)/shard_map/all_gather | solution.py:387
  11.1 72.2 %all-gather.7.cloned.1.call-start = ((), (), s32[]{:S(2)}) async-start(), calls=%async_computation.2 | async-start | bytes 1310720 | tf_op jit(solution)/shard_map/all_gather | solution.py:387
  11.1 17.1 %collective-permute-start = (bf16[2,64,1024]{2,1,0:T(8,128)(2,1)S(1)}, bf16[2,64,1024]{2,1,0:T(8,128)(2,1)S(1)}, u32[]{:S(2)}, u32[]{:S(2)}) collective-permute-start(bf16[2,64,1024]{2,1,0:T(8,128)(2,1)S(1)} %get-tuple-element.64), channel_id=1, source_target_pairs={{16,0},{32,16},{48,32},{64,48},{80,64},{96,80},{112,96},{128,112},... | collective-permute-start | bytes 786440 | tf_op jit(solution)/shard_map/ppermute | solution.py:393
  13.7 14.5 %collective-permute-start.1 = (bf16[64,1664]{1,0:T(8,128)(2,1)S(1)}, bf16[64,1664]{1,0:T(8,128)(2,1)S(1)}, u32[]{:S(2)}, u32[]{:S(2)}) collective-permute-start(bf16[64,1664]{1,0:T(8,128)(2,1)S(1)} %get-tuple-element.67), channel_id=1, source_target_pairs={{0,1},{1,2},{2,3},{3,0},{4,5},{5,6},{6,7},{7,4},{8,9},{9,10},{10,1... | collective-permute-start | bytes 638984 | tf_op jit(solution)/shard_map/ppermute | solution.py:359
  15.0 13.2 %collective-permute-start.2 = (bf16[64,1664]{1,0:T(8,128)(2,1)S(1)}, bf16[64,1664]{1,0:T(8,128)(2,1)S(1)}, u32[]{:S(2)}, u32[]{:S(2)}) collective-permute-start(bf16[64,1664]{1,0:T(8,128)(2,1)S(1)} %get-tuple-element.68), channel_id=1, source_target_pairs={{0,2},{1,3},{2,0},{3,1},{4,6},{5,7},{6,4},{7,5},{8,10},{9,11},{10,... | collective-permute-start | bytes 638984 | tf_op jit(solution)/shard_map/ppermute | solution.py:359
  17.4 10.8 %collective-permute-start.3 = (bf16[64,1664]{1,0:T(8,128)(2,1)S(1)}, bf16[64,1664]{1,0:T(8,128)(2,1)S(1)}, u32[]{:S(2)}, u32[]{:S(2)}) collective-permute-start(bf16[64,1664]{1,0:T(8,128)(2,1)S(1)} %get-tuple-element.69), channel_id=1, source_target_pairs={{0,3},{1,0},{2,1},{3,2},{4,7},{5,4},{6,5},{7,6},{8,11},{9,8},{10,9... | collective-permute-start | bytes 638984 | tf_op jit(solution)/shard_map/ppermute | solution.py:359
  29.6 13.5 %collective-permute-start.4 = (bf16[256,1152]{1,0:T(8,128)(2,1)S(1)}, bf16[256,1152]{1,0:T(8,128)(2,1)S(1)}, u32[]{:S(2)}, u32[]{:S(2)}) collective-permute-start(bf16[256,1152]{1,0:T(8,128)(2,1)S(1)} %get-tuple-element.76.panel0.source), channel_id=1, source_target_pairs={{0,12},{1,13},{2,14},{3,15},{4,0},{5,1},{6,2},{7,3},{8,4},{9,5},{1... | collective-permute-start | bytes 1769480 | tf_op jit(solution)/shard_map/ppermute | solution.py:364
  31.6 14.6 %collective-permute-start.5 = (bf16[256,1152]{1,0:T(8,128)(2,1)S(1)}, bf16[256,1152]{1,0:T(8,128)(2,1)S(1)}, u32[]{:S(2)}, u32[]{:S(2)}) collective-permute-start(bf16[256,1152]{1,0:T(8,128)(2,1)S(1)} %get-tuple-element.76.panel0.source), channel_id=1, source_target_pairs={{0,4},{1,5},{2,6},{3,7},{4,8},{5,9},{6,10},{7,11},{8,12},{9,13},{1... | collective-permute-start | bytes 1769480 | tf_op jit(solution)/shard_map/ppermute | solution.py:364
  31.6 28.7 %collective-permute-start.10 = (bf16[2,2,64,1024]{3,2,1,0:T(8,128)(2,1)S(1)}, bf16[2,2,64,1024]{3,2,1,0:T(8,128)(2,1)S(1)}, u32[]{:S(2)}, u32[]{:S(2)}) collective-permute-start(bf16[2,2,64,1024]{3,2,1,0:T(8,128)(2,1)S(1)} %get-tuple-element.87.ca0), channel_id=1, source_target_pairs={{0,3},{1,0},{2,1},{3,2},{4,7},{5,4},{6,5},{7,6},{8,11},{9,8},{10,9... | collective-permute-start | bytes 1572872 | tf_op jit(solution)/shard_map/ppermute | solution.py:359
  46.9 7.5 %collective-permute-start.6 = (bf16[128,1152]{1,0:T(8,128)(2,1)S(1)}, bf16[128,1152]{1,0:T(8,128)(2,1)S(1)}, u32[]{:S(2)}, u32[]{:S(2)}) collective-permute-start(bf16[128,1152]{1,0:T(8,128)(2,1)S(1)} %get-tuple-element.81), channel_id=1, source_target_pairs={{0,4},{1,5},{2,6},{3,7},{4,8},{5,9},{6,10},{7,11},{8,12},{9,13},{1... | collective-permute-start | bytes 884744 | tf_op jit(solution)/shard_map/ppermute | solution.py:364
  46.9 7.4 %collective-permute-start.7 = (bf16[128,1152]{1,0:T(8,128)(2,1)S(1)}, bf16[128,1152]{1,0:T(8,128)(2,1)S(1)}, u32[]{:S(2)}, u32[]{:S(2)}) collective-permute-start(bf16[128,1152]{1,0:T(8,128)(2,1)S(1)} %get-tuple-element.82), channel_id=1, source_target_pairs={{0,12},{1,13},{2,14},{3,15},{4,0},{5,1},{6,2},{7,3},{8,4},{9,5},{1... | collective-permute-start | bytes 884744 | tf_op jit(solution)/shard_map/ppermute | solution.py:364
  49.6 12.8 %collective-permute-start.8 = (bf16[2,2,64,1024]{3,2,1,0:T(8,128)(2,1)S(1)}, bf16[2,2,64,1024]{3,2,1,0:T(8,128)(2,1)S(1)}, u32[]{:S(2)}, u32[]{:S(2)}) collective-permute-start(bf16[2,2,64,1024]{3,2,1,0:T(8,128)(2,1)S(1)} %get-tuple-element.87.ca0), channel_id=1, source_target_pairs={{0,1},{1,2},{2,3},{3,0},{4,5},{5,6},{6,7},{7,4},{8,9},{9,10},{10,1... | collective-permute-start | bytes 1572872 | tf_op jit(solution)/shard_map/ppermute | solution.py:359
  50.4 32.1 %collective-permute-start.9 = (bf16[2,2,64,1024]{3,2,1,0:T(8,128)(2,1)S(1)}, bf16[2,2,64,1024]{3,2,1,0:T(8,128)(2,1)S(1)}, u32[]{:S(2)}, u32[]{:S(2)}) collective-permute-start(bf16[2,2,64,1024]{3,2,1,0:T(8,128)(2,1)S(1)} %get-tuple-element.87.ca0), channel_id=1, source_target_pairs={{0,2},{1,3},{2,0},{3,1},{4,6},{5,7},{6,4},{7,5},{8,10},{9,11},{10,... | collective-permute-start | bytes 1572872 | tf_op jit(solution)/shard_map/ppermute | solution.py:359
  58.0 26.3 %collective-permute-start.11 = (bf16[256,640]{1,0:T(8,128)(2,1)}, bf16[256,640]{1,0:T(8,128)(2,1)S(1)}, u32[]{:S(2)}, u32[]{:S(2)}) collective-permute-start(bf16[256,640]{1,0:T(8,128)(2,1)} %get-tuple-element.91.panel0), channel_id=1, source_target_pairs={{0,12},{1,13},{2,14},{3,15},{4,0},{5,1},{6,2},{7,3},{8,4},{9,5},{1... | collective-permute-start | bytes 983048 | tf_op jit(solution)/shard_map/ppermute | solution.py:364
  60.4 24.4 %collective-permute-start.12 = (bf16[256,640]{1,0:T(8,128)(2,1)}, bf16[256,640]{1,0:T(8,128)(2,1)S(1)}, u32[]{:S(2)}, u32[]{:S(2)}) collective-permute-start(bf16[256,640]{1,0:T(8,128)(2,1)} %get-tuple-element.91.panel0), channel_id=1, source_target_pairs={{0,8},{1,9},{2,10},{3,11},{4,12},{5,13},{6,14},{7,15},{8,0},{9,1},... | collective-permute-start | bytes 983048 | tf_op jit(solution)/shard_map/ppermute | solution.py:364
  60.4 24.4 %collective-permute-start.13 = (bf16[256,640]{1,0:T(8,128)(2,1)}, bf16[256,640]{1,0:T(8,128)(2,1)S(1)}, u32[]{:S(2)}, u32[]{:S(2)}) collective-permute-start(bf16[256,640]{1,0:T(8,128)(2,1)} %get-tuple-element.91.panel0), channel_id=1, source_target_pairs={{0,4},{1,5},{2,6},{3,7},{4,8},{5,9},{6,10},{7,11},{8,12},{9,13},{1... | collective-permute-start | bytes 983048 | tf_op jit(solution)/shard_map/ppermute | solution.py:364
  83.3 22.4 %collective-permute-start.18 = (bf16[272,512]{1,0:T(8,128)(2,1)}, bf16[272,512]{1,0:T(8,128)(2,1)S(1)}, u32[]{:S(2)}, u32[]{:S(2)}) collective-permute-start(bf16[272,512]{1,0:T(8,128)(2,1)} %copy-done.4), channel_id=1, source_target_pairs={{0,12},{1,13},{2,14},{3,15},{4,0},{5,1},{6,2},{7,3},{8,4},{9,5},{1... | collective-permute-start | bytes 835592 | tf_op jit(solution)/shard_map/ppermute | solution.py:364
  83.6 23.7 %collective-permute-start.19 = (bf16[272,512]{1,0:T(8,128)(2,1)}, bf16[272,512]{1,0:T(8,128)(2,1)S(1)}, u32[]{:S(2)}, u32[]{:S(2)}) collective-permute-start(bf16[272,512]{1,0:T(8,128)(2,1)} %copy-done.4), channel_id=1, source_target_pairs={{0,8},{1,9},{2,10},{3,11},{4,12},{5,13},{6,14},{7,15},{8,0},{9,1},... | collective-permute-start | bytes 835592 | tf_op jit(solution)/shard_map/ppermute | solution.py:364
  84.2 23.1 %collective-permute-start.20 = (bf16[272,512]{1,0:T(8,128)(2,1)}, bf16[272,512]{1,0:T(8,128)(2,1)S(1)}, u32[]{:S(2)}, u32[]{:S(2)}) collective-permute-start(bf16[272,512]{1,0:T(8,128)(2,1)} %copy-done.4), channel_id=1, source_target_pairs={{0,4},{1,5},{2,6},{3,7},{4,8},{5,9},{6,10},{7,11},{8,12},{9,13},{1... | collective-permute-start | bytes 835592 | tf_op jit(solution)/shard_map/ppermute | solution.py:364
  88.7 18.6 %collective-permute-start.21 = (bf16[256,512]{1,0:T(8,128)(2,1)S(1)}, bf16[256,512]{1,0:T(8,128)(2,1)S(1)}, u32[]{:S(2)}, u32[]{:S(2)}) collective-permute-start(bf16[256,512]{1,0:T(8,128)(2,1)S(1)} %get-tuple-element.100), channel_id=1, source_target_pairs={{0,16},{16,32},{32,48},{48,64},{64,80},{80,96},{96,112},{112,128},... | collective-permute-start | bytes 786440 | tf_op jit(solution)/shard_map/ppermute | solution.py:393
  103.3 8.6 %collective-permute-start.15 = (bf16[512,128]{1,0:T(8,128)(2,1)S(1)}, bf16[512,128]{1,0:T(8,128)(2,1)S(1)}, u32[]{:S(2)}, u32[]{:S(2)}) collective-permute-start(bf16[512,128]{1,0:T(8,128)(2,1)S(1)} %get-tuple-element.95), channel_id=1, source_target_pairs={{0,12},{1,13},{2,14},{3,15},{4,0},{5,1},{6,2},{7,3},{8,4},{9,5},{1... | collective-permute-start | bytes 393224 | tf_op jit(solution)/shard_map/ppermute | solution.py:364
  105.7 7.0 %collective-permute-start.16 = (bf16[512,128]{1,0:T(8,128)(2,1)S(1)}, bf16[512,128]{1,0:T(8,128)(2,1)S(1)}, u32[]{:S(2)}, u32[]{:S(2)}) collective-permute-start(bf16[512,128]{1,0:T(8,128)(2,1)S(1)} %get-tuple-element.95), channel_id=1, source_target_pairs={{0,8},{1,9},{2,10},{3,11},{4,12},{5,13},{6,14},{7,15},{8,0},{9,1},... | collective-permute-start | bytes 393224 | tf_op jit(solution)/shard_map/ppermute | solution.py:364
  109.1 15.2 %collective-permute-start.22 = (bf16[256,512]{1,0:T(8,128)(2,1)S(1)}, bf16[256,512]{1,0:T(8,128)(2,1)S(1)}, u32[]{:S(2)}, u32[]{:S(2)}) collective-permute-start(bf16[256,512]{1,0:T(8,128)(2,1)S(1)} %get-tuple-element.101.refs_0_.refs_1_.block0), channel_id=1, source_target_pairs={{0,1},{1,2},{2,3},{3,0},{4,5},{5,6},{6,7},{7,4},{8,9},{9,10},{10,1... | collective-permute-start | bytes 786440 | tf_op jit(solution)/shard_map/ppermute | solution.py:359
  109.2 15.1 %collective-permute-start.23 = (bf16[256,512]{1,0:T(8,128)(2,1)S(1)}, bf16[256,512]{1,0:T(8,128)(2,1)S(1)}, u32[]{:S(2)}, u32[]{:S(2)}) collective-permute-start(bf16[256,512]{1,0:T(8,128)(2,1)S(1)} %get-tuple-element.101.refs_0_.refs_1_.block0), channel_id=1, source_target_pairs={{0,2},{1,3},{2,0},{3,1},{4,6},{5,7},{6,4},{7,5},{8,10},{9,11},{10,... | collective-permute-start | bytes 786440 | tf_op jit(solution)/shard_map/ppermute | solution.py:359
  109.3 15.3 %collective-permute-start.24 = (bf16[256,512]{1,0:T(8,128)(2,1)S(1)}, bf16[256,512]{1,0:T(8,128)(2,1)S(1)}, u32[]{:S(2)}, u32[]{:S(2)}) collective-permute-start(bf16[256,512]{1,0:T(8,128)(2,1)S(1)} %get-tuple-element.101.refs_0_.refs_1_.block0), channel_id=1, source_target_pairs={{0,3},{1,0},{2,1},{3,2},{4,7},{5,4},{6,5},{7,6},{8,11},{9,8},{10,9... | collective-permute-start | bytes 786440 | tf_op jit(solution)/shard_map/ppermute | solution.py:359
  111.9 7.8 %collective-permute-start.17 = (bf16[512,128]{1,0:T(8,128)(2,1)S(1)}, bf16[512,128]{1,0:T(8,128)(2,1)S(1)}, u32[]{:S(2)}, u32[]{:S(2)}) collective-permute-start(bf16[512,128]{1,0:T(8,128)(2,1)S(1)} %get-tuple-element.95), channel_id=1, source_target_pairs={{0,4},{1,5},{2,6},{3,7},{4,8},{5,9},{6,10},{7,11},{8,12},{9,13},{1... | collective-permute-start | bytes 393224 | tf_op jit(solution)/shard_map/ppermute | solution.py:364
  112.7 16.1 %collective-permute-start.32 = (bf16[256,512]{1,0:T(8,128)(2,1)S(1)}, bf16[256,512]{1,0:T(8,128)(2,1)S(1)}, u32[]{:S(2)}, u32[]{:S(2)}) collective-permute-start(bf16[256,512]{1,0:T(8,128)(2,1)S(1)} %get-tuple-element.109), channel_id=1, source_target_pairs={{0,16},{16,32},{32,48},{48,64},{64,80},{80,96},{96,112},{112,128},... | collective-permute-start | bytes 786440 | tf_op jit(solution)/shard_map/ppermute | solution.py:393
  129.4 27.3 %collective-permute-start.33 = (bf16[256,1024]{1,0:T(8,128)(2,1)S(1)}, bf16[256,1024]{1,0:T(8,128)(2,1)S(1)}, u32[]{:S(2)}, u32[]{:S(2)}) collective-permute-start(bf16[256,1024]{1,0:T(8,128)(2,1)S(1)} %shard_map.112.pair0), channel_id=1, source_target_pairs={{0,1},{1,2},{2,3},{3,0},{4,5},{5,6},{6,7},{7,4},{8,9},{9,10},{10,1... | collective-permute-start | bytes 1572872 | tf_op jit(solution)/shard_map/ppermute | solution.py:359
  129.9 26.8 %collective-permute-start.34 = (bf16[256,1024]{1,0:T(8,128)(2,1)S(1)}, bf16[256,1024]{1,0:T(8,128)(2,1)S(1)}, u32[]{:S(2)}, u32[]{:S(2)}) collective-permute-start(bf16[256,1024]{1,0:T(8,128)(2,1)S(1)} %shard_map.112.pair0), channel_id=1, source_target_pairs={{0,2},{1,3},{2,0},{3,1},{4,6},{5,7},{6,4},{7,5},{8,10},{9,11},{10,... | collective-permute-start | bytes 1572872 | tf_op jit(solution)/shard_map/ppermute | solution.py:359
  133.0 23.7 %collective-permute-start.35 = (bf16[256,1024]{1,0:T(8,128)(2,1)S(1)}, bf16[256,1024]{1,0:T(8,128)(2,1)S(1)}, u32[]{:S(2)}, u32[]{:S(2)}) collective-permute-start(bf16[256,1024]{1,0:T(8,128)(2,1)S(1)} %shard_map.112.pair0), channel_id=1, source_target_pairs={{0,3},{1,0},{2,1},{3,2},{4,7},{5,4},{6,5},{7,6},{8,11},{9,8},{10,9... | collective-permute-start | bytes 1572872 | tf_op jit(solution)/shard_map/ppermute | solution.py:359
  148.1 10.0 %collective-permute-start.31 = (bf16[512,128]{1,0:T(8,128)(2,1)S(1)}, bf16[512,128]{1,0:T(8,128)(2,1)S(1)}, u32[]{:S(2)}, u32[]{:S(2)}) collective-permute-start(bf16[512,128]{1,0:T(8,128)(2,1)S(1)} %shard_map.110.solved), channel_id=1, source_target_pairs={{0,16},{16,32},{32,48},{48,64},{64,80},{80,96},{96,112},{112,128},... | collective-permute-start | bytes 393224 | tf_op jit(solution)/shard_map/ppermute | solution.py:393
  153.2 7.5 %collective-permute-start.36 = (bf16[512,128]{1,0:T(8,128)(2,1)S(1)}, bf16[512,128]{1,0:T(8,128)(2,1)S(1)}, u32[]{:S(2)}, u32[]{:S(2)}) collective-permute-start(bf16[512,128]{1,0:T(8,128)(2,1)S(1)} %shard_map.110.solved), channel_id=1, source_target_pairs={{16,0},{32,16},{48,32},{64,48},{80,64},{96,80},{112,96},{128,112},... | collective-permute-start | bytes 393224 | tf_op jit(solution)/shard_map/ppermute | solution.py:393
  (19 other events, 92.9 us)
Sparse Core Ops, SparseCore 0:
  11.2 28.8 all-gather.4
  41.9 34.3 all-gather.6

commit v7 on v5

--- a/solution.py
+++ b/solution.py
@@ -15,13 +15,15 @@
 SMEM = pl.BlockSpec(memory_space=pltpu.SMEM)
 
 
-def call(kernel, out_shapes, flops, *args, scratch=(), hbm=0, mib=MIB, hbm_out=False):
+def call(kernel, out_shapes, flops, *args, scratch=(), hbm=0, mib=MIB, hbm_out=False, pinned=()):
     moved = sum(a.size * a.dtype.itemsize for a in args) + sum(
         s.size * s.dtype.itemsize for s in out_shapes
     )
     anywhere = pl.BlockSpec(memory_space=pltpu.HBM)
     args = [
-        pltpu.with_memory_space_constraint(a, pltpu.HBM) if 0 < index <= hbm else a
+        pltpu.with_memory_space_constraint(a, pltpu.HBM) if 0 < index <= hbm
+        else pltpu.with_memory_space_constraint(a, pltpu.VMEM) if index in pinned
+        else a
         for index, a in enumerate(args)
     ]
     return pl.pallas_call(
@@ -385,12 +387,15 @@
 
 
 def ring_gathered_y(scalars, block, beside):
-    above, below, *beside = lax.optimization_barrier(
-        (moved_y(block, 3), moved_y(block, 1), *beside)
+    above, below, rows = lax.optimization_barrier(
+        (moved_y(block, 3), moved_y(block, 1), beside[0])
     )
     half = shape((128, block.shape[1]))
     low, high = call(split_kernel, [half, half], 0, scalars, below, above)
-    return (block, above, below, moved_y(low, 1), moved_y(high, 3)), beside
+    low, high, *couplings = lax.optimization_barrier(
+        (moved_y(low, 1), moved_y(high, 3), *beside[1:])
+    )
+    return (block, above, below, low, high), (rows, *couplings)
 
 
 def gathered_x(block):
@@ -459,12 +464,12 @@
          shape((512, 1024)),
          shape((512, 1024))],
         2 * wide_flops,
-        scalars, *ca_blocks, *firsts, panel,
+        scalars, *ca_blocks, *firsts, panel, pinned=(1, 2, 3, 4),
     )
     shipped = along_cuts(ship, 1)
     diagonal_new, ship_lower = call(
         diagonal_kernel, [shape((256, 512))] * 2, 2 * wide_flops,
-        scalars, c_rows, a_rows, *seconds, diagonal, shipped,
+        scalars, c_rows, a_rows, *seconds, diagonal, shipped, pinned=(3, 7),
     )
     diagonals = [diagonal_new] + [moved_x(diagonal_new, by) for by in turns]
     packed_shapes = [shape((512, 128), F32), shape((512, 128))]

time: 174 us -> 174 us (level)
  waiting for transfers between devices: 51.1 us -> 47.5 us
  starting transfers between devices: 71.3 us -> 73.9 us
    ppermute x15, waiting for transfers between devices: 21.6 us -> 4.07 us  [moved_x(): return lax.ppermute(block, 'row', pairs)]
    ppermute x19, waiting for transfers between devices: 18 us -> 26.5 us  [moved_y(): return lax.ppermute(block, 'row', pairs)]
    all_gather x2, waiting for transfers between devices: 5 us -> 10.3 us  [gathered_x(): return lax.all_gather(block, 'row', axis_index_groups=groups)]
    ppermute x5, starting transfers between devices: 23.3 us -> 27.2 us  [along_cuts(): return lax.ppermute(block, 'cuts', pairs)]
    ppermute x19, starting transfers between devices: 22.1 us -> 20.3 us  [moved_y(): return lax.ppermute(block, 'row', pairs)]
  transfers between devices with their start and end apart: 41 -> 41, of which waited for: 14 -> 16; matrix products, arithmetic and copies ran while one was open for 0% -> 0% of each run, Pallas kernels for 10% -> 10%
where the time goes in v7:
time: 174 us; the launch traced here: 173 us
  starting transfers between devices  73.9 us (42%)
  waiting for transfers between devices  47.5 us (27%)
  Pallas kernels  23.3 us (13%)
  between operations  14.3 us (8%)
  blocking collectives  9.62 us (6%)
  local copies, waits for them, and re-layouts  3.99 us (2%)
    ppermute x5, starting transfers between devices, along_cuts(): return lax.ppermute(block, 'cuts', pairs)  27.2 us
    ppermute x19, waiting for transfers between devices, moved_y(): return lax.ppermute(block, 'row', pairs)  26.5 us
    ppermute x15, starting transfers between devices, moved_x(): return lax.ppermute(block, 'row', pairs)  26.4 us
    pallas_call x15, Pallas kernels, call(): pl.pallas_call(kernel, out_shape=tuple(out_shapes), in_specs=[SMEM] + [an...  23.3 us
    ppermute x19, starting transfers between devices, moved_y(): return lax.ppermute(block, 'row', pairs)  20.3 us
    all_gather x2, waiting for transfers between devices, gathered_x(): return lax.all_gather(block, 'row', axis_index_groups=groups)  10.3 us
    all_to_all x1, blocking collectives, body(): lax.all_to_all(g_pieces, 'row', 0, 0, axis_index_groups=groups, tiled=True)  9.62 us
    ppermute x5, waiting for transfers between devices, along_cuts(): return lax.ppermute(block, 'cuts', pairs)  6.54 us
  transfers between devices with their start and end apart: 41, of which 16 were waited for; matrix products, arithmetic and copies ran while one was open for 0% of the time, Pallas kernels for 10%

profile of v7, /device:TPU:97, one launch (start us, length us, event | category | flops | bytes accessed | tf_op | source)
XLA Modules:
  0.0 172.7 jit_solution(13621448176414974258)
XLA Ops:
  8.1 2.9 %shard_map.101 = (bf16[64,1664]{1,0:T(8,128)(2,1)S(1)}, bf16[64,1664]{1,0:T(8,128)(2,1)S(1)}, bf16[64,1664]{1,0:T(8,128)(2,1)S(1)}, bf16[64,1664]{1,0:T(8,128)(2...) custom-call(s32[6]{0:T(128)S(1)} %pad_add_fusion.1.s_ref, ...), custom_call_target="tpu_custom_call" | custom-call | bytes 4063256 | tf_op jit(solution)/shard_map/pallas_call | solution.py:29
  11.1 2.6 %collective-permute-start = (bf16[2,64,1024]{2,1,0:T(8,128)(2,1)S(1)}, bf16[2,64,1024]{2,1,0:T(8,128)(2,1)S(1)}, u32[]{:S(2)}, u32[]{:S(2)}) collective-permute-start(bf16[2,64,1024]{2,1,0:T(8,128)(2,1)S(1)} %get-tuple-element.67), channel_id=1, source_target_pairs={{16,0},{32,16},{48,32},{64,48},{80,64},{96,80},{112,96},{128,112},... | collective-permute-start | bytes 786440 | tf_op jit(solution)/shard_map/ppermute | solution.py:409
  15.0 2.5 %collective-permute-start.2 = (bf16[64,1664]{1,0:T(8,128)(2,1)S(1)}, bf16[64,1664]{1,0:T(8,128)(2,1)S(1)}, u32[]{:S(2)}, u32[]{:S(2)}) collective-permute-start(bf16[64,1664]{1,0:T(8,128)(2,1)S(1)} %get-tuple-element.71), channel_id=1, source_target_pairs={{0,2},{1,3},{2,0},{3,1},{4,6},{5,7},{6,4},{7,5},{8,10},{9,11},{10,... | collective-permute-start | bytes 638984 | tf_op jit(solution)/shard_map/ppermute | solution.py:372
  18.6 9.6 %all_to_all.5 = bf16[4,2,64,256]{3,2,1,0:T(8,128)(2,1)} all-to-all(bf16[4,2,64,256]{3,2,1,0:T(8,128)(2,1)S(1)} %get-tuple-element.68), channel_id=1, replica_groups={{0,4,8,12},{1,5,9,13},{2,6,10,14},{3,7,11,15},{16,20,24,28},{17,21,25,2..., dimensions={0} | all-to-all | bytes 524288 | tf_op jit(solution)/shard_map/all_to_all | solution.py:439
  29.6 2.0 %collective-permute-start.4 = (bf16[256,1152]{1,0:T(8,128)(2,1)S(1)}, bf16[256,1152]{1,0:T(8,128)(2,1)S(1)}, u32[]{:S(2)}, u32[]{:S(2)}) collective-permute-start(bf16[256,1152]{1,0:T(8,128)(2,1)S(1)} %get-tuple-element.79.panel0.source), channel_id=1, source_target_pairs={{0,12},{1,13},{2,14},{3,15},{4,0},{5,1},{6,2},{7,3},{8,4},{9,5},{1... | collective-permute-start | bytes 1769480 | tf_op jit(solution)/shard_map/ppermute | solution.py:377
  32.3 2.0 %collective-permute-start.9 = (bf16[2,2,64,1024]{3,2,1,0:T(8,128)(2,1)S(1)}, bf16[2,2,64,1024]{3,2,1,0:T(8,128)(2,1)S(1)}, u32[]{:S(2)}, u32[]{:S(2)}) collective-permute-start(bf16[2,2,64,1024]{3,2,1,0:T(8,128)(2,1)S(1)} %get-tuple-element.94.ca0), channel_id=1, source_target_pairs={{0,3},{1,0},{2,1},{3,2},{4,7},{5,4},{6,5},{7,6},{8,11},{9,8},{10,9... | collective-permute-start | bytes 1572872 | tf_op jit(solution)/shard_map/ppermute | solution.py:372
  34.3 8.8 %collective-permute-done.4.other.panel1 = bf16[256,1152]{1,0:T(8,128)(2,1)S(1)} collective-permute-done((bf16[256,1152]{1,0:T(8,128)(2,1)S(1)}, bf16[256,1152]{1,0:T(8,128)(2,1)S(1)}, u32[]{:S(2)}, u32[]{:S(2)}) %collective-permute-start.4) | collective-permute-done | bytes 589856 | tf_op jit(solution)/shard_map/ppermute | solution.py:377
  43.1 3.1 %collective-permute-done.5.block.panel3 = bf16[256,1152]{1,0:T(8,128)(2,1)S(1)} collective-permute-done((bf16[256,1152]{1,0:T(8,128)(2,1)S(1)}, bf16[256,1152]{1,0:T(8,128)(2,1)S(1)}, u32[]{:S(2)}, u32[]{:S(2)}) %collective-permute-start.5) | collective-permute-done | bytes 589856 | tf_op jit(solution)/shard_map/ppermute | solution.py:377
  46.9 2.7 %collective-permute-start.7 = (bf16[128,1152]{1,0:T(8,128)(2,1)S(1)}, bf16[128,1152]{1,0:T(8,128)(2,1)S(1)}, u32[]{:S(2)}, u32[]{:S(2)}) collective-permute-start(bf16[128,1152]{1,0:T(8,128)(2,1)S(1)} %get-tuple-element.85), channel_id=1, source_target_pairs={{0,12},{1,13},{2,14},{3,15},{4,0},{5,1},{6,2},{7,3},{8,4},{9,5},{1... | collective-permute-start | bytes 884744 | tf_op jit(solution)/shard_map/ppermute | solution.py:377
  49.6 2.0 %collective-permute-start.10 = (bf16[2,2,64,1024]{3,2,1,0:T(8,128)(2,1)S(1)}, bf16[2,2,64,1024]{3,2,1,0:T(8,128)(2,1)S(1)}, u32[]{:S(2)}, u32[]{:S(2)}) collective-permute-start(bf16[2,2,64,1024]{3,2,1,0:T(8,128)(2,1)S(1)} %get-tuple-element.94.ca0), channel_id=1, source_target_pairs={{0,2},{1,3},{2,0},{3,1},{4,6},{5,7},{6,4},{7,5},{8,10},{9,11},{10,... | collective-permute-start | bytes 1572872 | tf_op jit(solution)/shard_map/ppermute | solution.py:372
  51.6 2.7 %collective-permute-done.6.low = bf16[128,1152]{1,0:T(8,128)(2,1)S(1)} collective-permute-done((bf16[128,1152]{1,0:T(8,128)(2,1)S(1)}, bf16[128,1152]{1,0:T(8,128)(2,1)S(1)}, u32[]{:S(2)}, u32[]{:S(2)}) %collective-permute-start.6) | collective-permute-done | bytes 294944 | tf_op jit(solution)/shard_map/ppermute | solution.py:377
  54.3 3.0 %shard_map.104 = (bf16[256,640]{1,0:T(8,128)(2,1)}, bf16[304,512]{1,0:T(8,128)(2,1)S(1)}) custom-call(s32[6]{0:T(128)S(1)} %pad_add_fusion.1.s_ref, bf16[4,2,64,1024]{3,2,1,0:T(8,128)(2,1)S(1)} %bitcast.12, bf16[256,1152]{1,0:T(8,128)(2,1)S(1)} %get-tuple-element.79.panel0.source, bf16[256,1152]{1,0:T(8,128)(2,1)S(1)} %collective-permute-done.4.other.panel1, ...), custom_call_target="tpu_custom_call" | custom-call | bytes 4046872 | tf_op jit(solution)/shard_map/pallas_call | solution.py:29
  58.0 2.4 %collective-permute-start.11 = (bf16[256,640]{1,0:T(8,128)(2,1)}, bf16[256,640]{1,0:T(8,128)(2,1)S(1)}, u32[]{:S(2)}, u32[]{:S(2)}) collective-permute-start(bf16[256,640]{1,0:T(8,128)(2,1)} %get-tuple-element.98.panel0), channel_id=1, source_target_pairs={{0,12},{1,13},{2,14},{3,15},{4,0},{5,1},{6,2},{7,3},{8,4},{9,5},{1... | collective-permute-start | bytes 983048 | tf_op jit(solution)/shard_map/ppermute | solution.py:377
  63.5 10.3 %all-gather.7.cloned.1.call-done = bf16[16,2,64,256]{3,2,1,0:T(8,128)(2,1)} async-done(((bf16[4,2,64,256]{3,2,1,0:T(8,128)(2,1)}), bf16[16,2,64,256]{3,2,1,0:T(8,128)(2,1)}) %all-gather.7.cloned.1.call-update) | async-done | bytes 1048592 | tf_op jit(solution)/shard_map/all_gather | solution.py:403
  75.3 2.5 %collective-permute-done.13.panel3 = bf16[256,640]{1,0:T(8,128)(2,1)S(1)} collective-permute-done((bf16[256,640]{1,0:T(8,128)(2,1)}, bf16[256,640]{1,0:T(8,128)(2,1)S(1)}, u32[]{:S(2)}, u32[]{:S(2)}) %collective-permute-start.13) | collective-permute-done | bytes 327712 | tf_op jit(solution)/shard_map/ppermute | solution.py:377
  78.8 2.9 %shard_map.105 = (bf16[288,512]{1,0:T(8,128)(2,1)S(1)}, bf16[256,512]{1,0:T(8,128)(2,1)S(1)}, f32[256,128]{1,0:T(8,128)S(1)}, bf16[512,1024]{1,0:T(8,128)(2,1)S(1)}, bf16[512,1024]{1,0:T(8,128)(2,1)S(1)}) custom-call(s32[6]{0:T(128)S(1)} %pad_add_fusion.1.s_ref, bf16[2,2,64,1024]{3,2,1,0:T(8,128)(2,1)S(1)} %get-tuple-element.94.ca0, ...), custom_call_target="tpu_custom_call" | custom-call | bytes 6783000 | tf_op jit(solution)/shard_map/pallas_call | solution.py:29
  81.7 5.9 %collective-permute-start.14 = (bf16[288,512]{1,0:T(8,128)(2,1)S(1)}, bf16[288,512]{1,0:T(8,128)(2,1)S(1)}, u32[]{:S(2)}, u32[]{:S(2)}) collective-permute-start(bf16[288,512]{1,0:T(8,128)(2,1)S(1)} %get-tuple-element.100), channel_id=1, source_target_pairs={{0,16},{16,32},{32,48},{48,64},{64,80},{80,96},{96,112},{112,128},... | collective-permute-start | bytes 884744 | tf_op jit(solution)/shard_map/ppermute | solution.py:409
  87.5 3.6 %collective-permute-done.14.shipped = bf16[288,512]{1,0:T(8,128)(2,1)S(1)} collective-permute-done((bf16[288,512]{1,0:T(8,128)(2,1)S(1)}, bf16[288,512]{1,0:T(8,128)(2,1)S(1)}, u32[]{:S(2)}, u32[]{:S(2)}) %collective-permute-start.14) | collective-permute-done | bytes 294944 | tf_op jit(solution)/shard_map/ppermute | solution.py:409
  97.0 8.7 %collective-permute-start.22 = (bf16[256,512]{1,0:T(8,128)(2,1)S(1)}, bf16[256,512]{1,0:T(8,128)(2,1)S(1)}, u32[]{:S(2)}, u32[]{:S(2)}) collective-permute-start(bf16[256,512]{1,0:T(8,128)(2,1)S(1)} %get-tuple-element.107.refs_0_.refs_1_.block0), channel_id=1, source_target_pairs={{0,2},{1,3},{2,0},{3,1},{4,6},{5,7},{6,4},{7,5},{8,10},{9,11},{10,... | collective-permute-start | bytes 786440 | tf_op jit(solution)/shard_map/ppermute | solution.py:372
  107.0 6.7 %collective-permute-start.31 = (bf16[256,512]{1,0:T(8,128)(2,1)S(1)}, bf16[256,512]{1,0:T(8,128)(2,1)S(1)}, u32[]{:S(2)}, u32[]{:S(2)}) collective-permute-start(bf16[256,512]{1,0:T(8,128)(2,1)S(1)} %get-tuple-element.115), channel_id=1, source_target_pairs={{0,16},{16,32},{32,48},{48,64},{64,80},{80,96},{96,112},{112,128},... | collective-permute-start | bytes 786440 | tf_op jit(solution)/shard_map/ppermute | solution.py:409
  113.9 1.8 %shard_map.108 = (bf16[512,128]{1,0:T(8,128)(2,1)S(1)}, f32[512,128]{1,0:T(8,128)S(1)}, bf16[512,128]{1,0:T(8,128)(2,1)S(1)}) custom-call(s32[6]{0:T(128)S(1)} %pad_add_fusion.1.s_ref, f32[512,128]{1,0:T(8,128)S(1)} %get-tuple-element.101.own, bf16[512,128]{1,0:T(8,128)(2,1)S(1)} %collective-permute-done.15.got1, ...), custom_call_target="tpu_custom_call" | custom-call | bytes 3342360 | tf_op jit(solution)/shard_map/pallas_call | solution.py:29
  115.7 3.0 %collective-permute-start.24 = (bf16[512,128]{1,0:T(8,128)(2,1)S(1)}, bf16[512,128]{1,0:T(8,128)(2,1)S(1)}, u32[]{:S(2)}, u32[]{:S(2)}) collective-permute-start(bf16[512,128]{1,0:T(8,128)(2,1)S(1)} %get-tuple-element.110), channel_id=1, source_target_pairs={{0,12},{1,13},{2,14},{3,15},{4,0},{5,1},{6,2},{7,3},{8,4},{9,5},{1... | collective-permute-start | bytes 393224 | tf_op jit(solution)/shard_map/ppermute | solution.py:377
  121.0 2.0 %collective-permute-start.32 = (bf16[256,1024]{1,0:T(8,128)(2,1)S(1)}, bf16[256,1024]{1,0:T(8,128)(2,1)S(1)}, u32[]{:S(2)}, u32[]{:S(2)}) collective-permute-start(bf16[256,1024]{1,0:T(8,128)(2,1)S(1)} %shard_map.112.pair0), channel_id=1, source_target_pairs={{0,1},{1,2},{2,3},{3,0},{4,5},{5,6},{6,7},{7,4},{8,9},{9,10},{10,1... | collective-permute-start | bytes 1572872 | tf_op jit(solution)/shard_map/ppermute | solution.py:372
  123.3 2.2 %collective-permute-start.34 = (bf16[256,1024]{1,0:T(8,128)(2,1)S(1)}, bf16[256,1024]{1,0:T(8,128)(2,1)S(1)}, u32[]{:S(2)}, u32[]{:S(2)}) collective-permute-start(bf16[256,1024]{1,0:T(8,128)(2,1)S(1)} %shard_map.112.pair0), channel_id=1, source_target_pairs={{0,3},{1,0},{2,1},{3,2},{4,7},{5,4},{6,5},{7,6},{8,11},{9,8},{10,9... | collective-permute-start | bytes 1572872 | tf_op jit(solution)/shard_map/ppermute | solution.py:372
  125.7 1.8 %shard_map.109 = (bf16[512,128]{1,0:T(8,128)(2,1)S(1)}, f32[512,128]{1,0:T(8,128)S(1)}, bf16[512,128]{1,0:T(8,128)(2,1)S(1)}) custom-call(s32[6]{0:T(128)S(1)} %pad_add_fusion.1.s_ref, f32[512,128]{1,0:T(8,128)S(1)} %get-tuple-element.109.own, bf16[512,128]{1,0:T(8,128)(2,1)S(1)} %collective-permute-done.24.got1, ...), custom_call_target="tpu_custom_call" | custom-call | bytes 3473432 | tf_op jit(solution)/shard_map/pallas_call | solution.py:29
  127.5 3.1 %collective-permute-start.27 = (bf16[512,128]{1,0:T(8,128)(2,1)S(1)}, bf16[512,128]{1,0:T(8,128)(2,1)S(1)}, u32[]{:S(2)}, u32[]{:S(2)}) collective-permute-start(bf16[512,128]{1,0:T(8,128)(2,1)S(1)} %get-tuple-element.113), channel_id=1, source_target_pairs={{0,12},{1,13},{2,14},{3,15},{4,0},{5,1},{6,2},{7,3},{8,4},{9,5},{1... | collective-permute-start | bytes 393224 | tf_op jit(solution)/shard_map/ppermute | solution.py:377
  130.7 3.4 %collective-permute-done.27.got1 = bf16[512,128]{1,0:T(8,128)(2,1)S(1)} collective-permute-done((bf16[512,128]{1,0:T(8,128)(2,1)S(1)}, bf16[512,128]{1,0:T(8,128)(2,1)S(1)}, u32[]{:S(2)}, u32[]{:S(2)}) %collective-permute-start.27) | collective-permute-done | bytes 131104 | tf_op jit(solution)/shard_map/ppermute | solution.py:377
  134.1 2.1 %collective-permute-done.28.got2 = bf16[512,128]{1,0:T(8,128)(2,1)S(1)} collective-permute-done((bf16[512,128]{1,0:T(8,128)(2,1)S(1)}, bf16[512,128]{1,0:T(8,128)(2,1)S(1)}, u32[]{:S(2)}, u32[]{:S(2)}) %collective-permute-start.28) | collective-permute-done | bytes 131104 | tf_op jit(solution)/shard_map/ppermute | solution.py:377
  136.3 3.6 %collective-permute-done.29.got3 = bf16[512,128]{1,0:T(8,128)(2,1)S(1)} collective-permute-done((bf16[512,128]{1,0:T(8,128)(2,1)S(1)}, bf16[512,128]{1,0:T(8,128)(2,1)S(1)}, u32[]{:S(2)}, u32[]{:S(2)}) %collective-permute-start.29) | collective-permute-done | bytes 131104 | tf_op jit(solution)/shard_map/ppermute | solution.py:377
  140.5 10.1 %collective-permute-start.30 = (bf16[512,128]{1,0:T(8,128)(2,1)S(1)}, bf16[512,128]{1,0:T(8,128)(2,1)S(1)}, u32[]{:S(2)}, u32[]{:S(2)}) collective-permute-start(bf16[512,128]{1,0:T(8,128)(2,1)S(1)} %shard_map.110.solved), channel_id=1, source_target_pairs={{0,16},{16,32},{32,48},{48,64},{64,80},{80,96},{96,112},{112,128},... | collective-permute-start | bytes 393224 | tf_op jit(solution)/shard_map/ppermute | solution.py:409
  150.6 1.9 %collective-permute-start.35 = (bf16[512,128]{1,0:T(8,128)(2,1)S(1)}, bf16[512,128]{1,0:T(8,128)(2,1)S(1)}, u32[]{:S(2)}, u32[]{:S(2)}) collective-permute-start(bf16[512,128]{1,0:T(8,128)(2,1)S(1)} %shard_map.110.solved), channel_id=1, source_target_pairs={{16,0},{32,16},{48,32},{64,48},{80,64},{96,80},{112,96},{128,112},... | collective-permute-start | bytes 393224 | tf_op jit(solution)/shard_map/ppermute | solution.py:409
  155.2 2.9 %collective-permute-done.35.above = bf16[512,128]{1,0:T(8,128)(2,1)S(1)} collective-permute-done((bf16[512,128]{1,0:T(8,128)(2,1)S(1)}, bf16[512,128]{1,0:T(8,128)(2,1)S(1)}, u32[]{:S(2)}, u32[]{:S(2)}) %collective-permute-start.35) | collective-permute-done | bytes 131104 | tf_op jit(solution)/shard_map/ppermute | solution.py:409
  (89 shorter events, 33.7 us)
Async XLA Ops:
  7.2 39.1 %all-gather.5.cloned.1.call-start = ((), (), s32[]{:S(2)}) async-start(), calls=%async_computation.1 | async-start | bytes 1310720 | tf_op jit(solution)/shard_map/all_gather | solution.py:403
  11.1 62.7 %all-gather.7.cloned.1.call-start = ((), (), s32[]{:S(2)}) async-start(), calls=%async_computation.2 | async-start | bytes 1310720 | tf_op jit(solution)/shard_map/all_gather | solution.py:403
  11.1 17.1 %collective-permute-start = (bf16[2,64,1024]{2,1,0:T(8,128)(2,1)S(1)}, bf16[2,64,1024]{2,1,0:T(8,128)(2,1)S(1)}, u32[]{:S(2)}, u32[]{:S(2)}) collective-permute-start(bf16[2,64,1024]{2,1,0:T(8,128)(2,1)S(1)} %get-tuple-element.67), channel_id=1, source_target_pairs={{16,0},{32,16},{48,32},{64,48},{80,64},{96,80},{112,96},{128,112},... | collective-permute-start | bytes 786440 | tf_op jit(solution)/shard_map/ppermute | solution.py:409
  13.7 14.5 %collective-permute-start.1 = (bf16[64,1664]{1,0:T(8,128)(2,1)S(1)}, bf16[64,1664]{1,0:T(8,128)(2,1)S(1)}, u32[]{:S(2)}, u32[]{:S(2)}) collective-permute-start(bf16[64,1664]{1,0:T(8,128)(2,1)S(1)} %get-tuple-element.70), channel_id=1, source_target_pairs={{0,1},{1,2},{2,3},{3,0},{4,5},{5,6},{6,7},{7,4},{8,9},{9,10},{10,1... | collective-permute-start | bytes 638984 | tf_op jit(solution)/shard_map/ppermute | solution.py:372
  15.0 13.2 %collective-permute-start.2 = (bf16[64,1664]{1,0:T(8,128)(2,1)S(1)}, bf16[64,1664]{1,0:T(8,128)(2,1)S(1)}, u32[]{:S(2)}, u32[]{:S(2)}) collective-permute-start(bf16[64,1664]{1,0:T(8,128)(2,1)S(1)} %get-tuple-element.71), channel_id=1, source_target_pairs={{0,2},{1,3},{2,0},{3,1},{4,6},{5,7},{6,4},{7,5},{8,10},{9,11},{10,... | collective-permute-start | bytes 638984 | tf_op jit(solution)/shard_map/ppermute | solution.py:372
  17.4 10.8 %collective-permute-start.3 = (bf16[64,1664]{1,0:T(8,128)(2,1)S(1)}, bf16[64,1664]{1,0:T(8,128)(2,1)S(1)}, u32[]{:S(2)}, u32[]{:S(2)}) collective-permute-start(bf16[64,1664]{1,0:T(8,128)(2,1)S(1)} %get-tuple-element.72), channel_id=1, source_target_pairs={{0,3},{1,0},{2,1},{3,2},{4,7},{5,4},{6,5},{7,6},{8,11},{9,8},{10,9... | collective-permute-start | bytes 638984 | tf_op jit(solution)/shard_map/ppermute | solution.py:372
  29.6 13.5 %collective-permute-start.4 = (bf16[256,1152]{1,0:T(8,128)(2,1)S(1)}, bf16[256,1152]{1,0:T(8,128)(2,1)S(1)}, u32[]{:S(2)}, u32[]{:S(2)}) collective-permute-start(bf16[256,1152]{1,0:T(8,128)(2,1)S(1)} %get-tuple-element.79.panel0.source), channel_id=1, source_target_pairs={{0,12},{1,13},{2,14},{3,15},{4,0},{5,1},{6,2},{7,3},{8,4},{9,5},{1... | collective-permute-start | bytes 1769480 | tf_op jit(solution)/shard_map/ppermute | solution.py:377
  31.6 14.6 %collective-permute-start.5 = (bf16[256,1152]{1,0:T(8,128)(2,1)S(1)}, bf16[256,1152]{1,0:T(8,128)(2,1)S(1)}, u32[]{:S(2)}, u32[]{:S(2)}) collective-permute-start(bf16[256,1152]{1,0:T(8,128)(2,1)S(1)} %get-tuple-element.79.panel0.source), channel_id=1, source_target_pairs={{0,4},{1,5},{2,6},{3,7},{4,8},{5,9},{6,10},{7,11},{8,12},{9,13},{1... | collective-permute-start | bytes 1769480 | tf_op jit(solution)/shard_map/ppermute | solution.py:377
  31.6 19.9 %collective-permute-start.8 = (bf16[2,2,64,1024]{3,2,1,0:T(8,128)(2,1)S(1)}, bf16[2,2,64,1024]{3,2,1,0:T(8,128)(2,1)S(1)}, u32[]{:S(2)}, u32[]{:S(2)}) collective-permute-start(bf16[2,2,64,1024]{3,2,1,0:T(8,128)(2,1)S(1)} %get-tuple-element.94.ca0), channel_id=1, source_target_pairs={{0,1},{1,2},{2,3},{3,0},{4,5},{5,6},{6,7},{7,4},{8,9},{9,10},{10,1... | collective-permute-start | bytes 1572872 | tf_op jit(solution)/shard_map/ppermute | solution.py:372
  32.3 19.3 %collective-permute-start.9 = (bf16[2,2,64,1024]{3,2,1,0:T(8,128)(2,1)S(1)}, bf16[2,2,64,1024]{3,2,1,0:T(8,128)(2,1)S(1)}, u32[]{:S(2)}, u32[]{:S(2)}) collective-permute-start(bf16[2,2,64,1024]{3,2,1,0:T(8,128)(2,1)S(1)} %get-tuple-element.94.ca0), channel_id=1, source_target_pairs={{0,3},{1,0},{2,1},{3,2},{4,7},{5,4},{6,5},{7,6},{8,11},{9,8},{10,9... | collective-permute-start | bytes 1572872 | tf_op jit(solution)/shard_map/ppermute | solution.py:372
  46.9 7.5 %collective-permute-start.6 = (bf16[128,1152]{1,0:T(8,128)(2,1)S(1)}, bf16[128,1152]{1,0:T(8,128)(2,1)S(1)}, u32[]{:S(2)}, u32[]{:S(2)}) collective-permute-start(bf16[128,1152]{1,0:T(8,128)(2,1)S(1)} %get-tuple-element.84), channel_id=1, source_target_pairs={{0,4},{1,5},{2,6},{3,7},{4,8},{5,9},{6,10},{7,11},{8,12},{9,13},{1... | collective-permute-start | bytes 884744 | tf_op jit(solution)/shard_map/ppermute | solution.py:377
  49.6 13.1 %collective-permute-start.10 = (bf16[2,2,64,1024]{3,2,1,0:T(8,128)(2,1)S(1)}, bf16[2,2,64,1024]{3,2,1,0:T(8,128)(2,1)S(1)}, u32[]{:S(2)}, u32[]{:S(2)}) collective-permute-start(bf16[2,2,64,1024]{3,2,1,0:T(8,128)(2,1)S(1)} %get-tuple-element.94.ca0), channel_id=1, source_target_pairs={{0,2},{1,3},{2,0},{3,1},{4,6},{5,7},{6,4},{7,5},{8,10},{9,11},{10,... | collective-permute-start | bytes 1572872 | tf_op jit(solution)/shard_map/ppermute | solution.py:372
  58.0 16.6 %collective-permute-start.11 = (bf16[256,640]{1,0:T(8,128)(2,1)}, bf16[256,640]{1,0:T(8,128)(2,1)S(1)}, u32[]{:S(2)}, u32[]{:S(2)}) collective-permute-start(bf16[256,640]{1,0:T(8,128)(2,1)} %get-tuple-element.98.panel0), channel_id=1, source_target_pairs={{0,12},{1,13},{2,14},{3,15},{4,0},{5,1},{6,2},{7,3},{8,4},{9,5},{1... | collective-permute-start | bytes 983048 | tf_op jit(solution)/shard_map/ppermute | solution.py:377
  60.4 14.9 %collective-permute-start.12 = (bf16[256,640]{1,0:T(8,128)(2,1)}, bf16[256,640]{1,0:T(8,128)(2,1)S(1)}, u32[]{:S(2)}, u32[]{:S(2)}) collective-permute-start(bf16[256,640]{1,0:T(8,128)(2,1)} %get-tuple-element.98.panel0), channel_id=1, source_target_pairs={{0,8},{1,9},{2,10},{3,11},{4,12},{5,13},{6,14},{7,15},{8,0},{9,1},... | collective-permute-start | bytes 983048 | tf_op jit(solution)/shard_map/ppermute | solution.py:377
  60.4 17.3 %collective-permute-start.13 = (bf16[256,640]{1,0:T(8,128)(2,1)}, bf16[256,640]{1,0:T(8,128)(2,1)S(1)}, u32[]{:S(2)}, u32[]{:S(2)}) collective-permute-start(bf16[256,640]{1,0:T(8,128)(2,1)} %get-tuple-element.98.panel0), channel_id=1, source_target_pairs={{0,4},{1,5},{2,6},{3,7},{4,8},{5,9},{6,10},{7,11},{8,12},{9,13},{1... | collective-permute-start | bytes 983048 | tf_op jit(solution)/shard_map/ppermute | solution.py:377
  73.8 20.5 %collective-permute-start.18 = (bf16[304,512]{1,0:T(8,128)(2,1)}, bf16[304,512]{1,0:T(8,128)(2,1)S(1)}, u32[]{:S(2)}, u32[]{:S(2)}) collective-permute-start(bf16[304,512]{1,0:T(8,128)(2,1)} %copy-done.4), channel_id=1, source_target_pairs={{0,12},{1,13},{2,14},{3,15},{4,0},{5,1},{6,2},{7,3},{8,4},{9,5},{1... | collective-permute-start | bytes 933896 | tf_op jit(solution)/shard_map/ppermute | solution.py:377
  74.1 20.2 %collective-permute-start.19 = (bf16[304,512]{1,0:T(8,128)(2,1)}, bf16[304,512]{1,0:T(8,128)(2,1)S(1)}, u32[]{:S(2)}, u32[]{:S(2)}) collective-permute-start(bf16[304,512]{1,0:T(8,128)(2,1)} %copy-done.4), channel_id=1, source_target_pairs={{0,8},{1,9},{2,10},{3,11},{4,12},{5,13},{6,14},{7,15},{8,0},{9,1},... | collective-permute-start | bytes 933896 | tf_op jit(solution)/shard_map/ppermute | solution.py:377
  74.6 19.7 %collective-permute-start.20 = (bf16[304,512]{1,0:T(8,128)(2,1)}, bf16[304,512]{1,0:T(8,128)(2,1)S(1)}, u32[]{:S(2)}, u32[]{:S(2)}) collective-permute-start(bf16[304,512]{1,0:T(8,128)(2,1)} %copy-done.4), channel_id=1, source_target_pairs={{0,4},{1,5},{2,6},{3,7},{4,8},{5,9},{6,10},{7,11},{8,12},{9,13},{1... | collective-permute-start | bytes 933896 | tf_op jit(solution)/shard_map/ppermute | solution.py:377
  81.7 9.5 %collective-permute-start.14 = (bf16[288,512]{1,0:T(8,128)(2,1)S(1)}, bf16[288,512]{1,0:T(8,128)(2,1)S(1)}, u32[]{:S(2)}, u32[]{:S(2)}) collective-permute-start(bf16[288,512]{1,0:T(8,128)(2,1)S(1)} %get-tuple-element.100), channel_id=1, source_target_pairs={{0,16},{16,32},{32,48},{48,64},{64,80},{80,96},{96,112},{112,128},... | collective-permute-start | bytes 884744 | tf_op jit(solution)/shard_map/ppermute | solution.py:409
  92.4 13.3 %collective-permute-start.15 = (bf16[512,128]{1,0:T(8,128)(2,1)S(1)}, bf16[512,128]{1,0:T(8,128)(2,1)S(1)}, u32[]{:S(2)}, u32[]{:S(2)}) collective-permute-start(bf16[512,128]{1,0:T(8,128)(2,1)S(1)} %get-tuple-element.102), channel_id=1, source_target_pairs={{0,12},{1,13},{2,14},{3,15},{4,0},{5,1},{6,2},{7,3},{8,4},{9,5},{1... | collective-permute-start | bytes 393224 | tf_op jit(solution)/shard_map/ppermute | solution.py:377
  93.1 13.9 %collective-permute-start.16 = (bf16[512,128]{1,0:T(8,128)(2,1)S(1)}, bf16[512,128]{1,0:T(8,128)(2,1)S(1)}, u32[]{:S(2)}, u32[]{:S(2)}) collective-permute-start(bf16[512,128]{1,0:T(8,128)(2,1)S(1)} %get-tuple-element.102), channel_id=1, source_target_pairs={{0,8},{1,9},{2,10},{3,11},{4,12},{5,13},{6,14},{7,15},{8,0},{9,1},... | collective-permute-start | bytes 393224 | tf_op jit(solution)/shard_map/ppermute | solution.py:377
  96.1 17.6 %collective-permute-start.21 = (bf16[256,512]{1,0:T(8,128)(2,1)S(1)}, bf16[256,512]{1,0:T(8,128)(2,1)S(1)}, u32[]{:S(2)}, u32[]{:S(2)}) collective-permute-start(bf16[256,512]{1,0:T(8,128)(2,1)S(1)} %get-tuple-element.107.refs_0_.refs_1_.block0), channel_id=1, source_target_pairs={{0,1},{1,2},{2,3},{3,0},{4,5},{5,6},{6,7},{7,4},{8,9},{9,10},{10,1... | collective-permute-start | bytes 786440 | tf_op jit(solution)/shard_map/ppermute | solution.py:372
  97.0 16.8 %collective-permute-start.22 = (bf16[256,512]{1,0:T(8,128)(2,1)S(1)}, bf16[256,512]{1,0:T(8,128)(2,1)S(1)}, u32[]{:S(2)}, u32[]{:S(2)}) collective-permute-start(bf16[256,512]{1,0:T(8,128)(2,1)S(1)} %get-tuple-element.107.refs_0_.refs_1_.block0), channel_id=1, source_target_pairs={{0,2},{1,3},{2,0},{3,1},{4,6},{5,7},{6,4},{7,5},{8,10},{9,11},{10,... | collective-permute-start | bytes 786440 | tf_op jit(solution)/shard_map/ppermute | solution.py:372
  105.7 8.2 %collective-permute-start.23 = (bf16[256,512]{1,0:T(8,128)(2,1)S(1)}, bf16[256,512]{1,0:T(8,128)(2,1)S(1)}, u32[]{:S(2)}, u32[]{:S(2)}) collective-permute-start(bf16[256,512]{1,0:T(8,128)(2,1)S(1)} %get-tuple-element.107.refs_0_.refs_1_.block0), channel_id=1, source_target_pairs={{0,3},{1,0},{2,1},{3,2},{4,7},{5,4},{6,5},{7,6},{8,11},{9,8},{10,9... | collective-permute-start | bytes 786440 | tf_op jit(solution)/shard_map/ppermute | solution.py:372
  105.7 8.1 %collective-permute-start.17 = (bf16[512,128]{1,0:T(8,128)(2,1)S(1)}, bf16[512,128]{1,0:T(8,128)(2,1)S(1)}, u32[]{:S(2)}, u32[]{:S(2)}) collective-permute-start(bf16[512,128]{1,0:T(8,128)(2,1)S(1)} %get-tuple-element.102), channel_id=1, source_target_pairs={{0,4},{1,5},{2,6},{3,7},{4,8},{5,9},{6,10},{7,11},{8,12},{9,13},{1... | collective-permute-start | bytes 393224 | tf_op jit(solution)/shard_map/ppermute | solution.py:377
  107.0 13.4 %collective-permute-start.31 = (bf16[256,512]{1,0:T(8,128)(2,1)S(1)}, bf16[256,512]{1,0:T(8,128)(2,1)S(1)}, u32[]{:S(2)}, u32[]{:S(2)}) collective-permute-start(bf16[256,512]{1,0:T(8,128)(2,1)S(1)} %get-tuple-element.115), channel_id=1, source_target_pairs={{0,16},{16,32},{32,48},{48,64},{64,80},{80,96},{96,112},{112,128},... | collective-permute-start | bytes 786440 | tf_op jit(solution)/shard_map/ppermute | solution.py:409
  115.7 7.6 %collective-permute-start.24 = (bf16[512,128]{1,0:T(8,128)(2,1)S(1)}, bf16[512,128]{1,0:T(8,128)(2,1)S(1)}, u32[]{:S(2)}, u32[]{:S(2)}) collective-permute-start(bf16[512,128]{1,0:T(8,128)(2,1)S(1)} %get-tuple-element.110), channel_id=1, source_target_pairs={{0,12},{1,13},{2,14},{3,15},{4,0},{5,1},{6,2},{7,3},{8,4},{9,5},{1... | collective-permute-start | bytes 393224 | tf_op jit(solution)/shard_map/ppermute | solution.py:377
  121.0 32.8 %collective-permute-start.32 = (bf16[256,1024]{1,0:T(8,128)(2,1)S(1)}, bf16[256,1024]{1,0:T(8,128)(2,1)S(1)}, u32[]{:S(2)}, u32[]{:S(2)}) collective-permute-start(bf16[256,1024]{1,0:T(8,128)(2,1)S(1)} %shard_map.112.pair0), channel_id=1, source_target_pairs={{0,1},{1,2},{2,3},{3,0},{4,5},{5,6},{6,7},{7,4},{8,9},{9,10},{10,1... | collective-permute-start | bytes 1572872 | tf_op jit(solution)/shard_map/ppermute | solution.py:372
  123.0 30.8 %collective-permute-start.33 = (bf16[256,1024]{1,0:T(8,128)(2,1)S(1)}, bf16[256,1024]{1,0:T(8,128)(2,1)S(1)}, u32[]{:S(2)}, u32[]{:S(2)}) collective-permute-start(bf16[256,1024]{1,0:T(8,128)(2,1)S(1)} %shard_map.112.pair0), channel_id=1, source_target_pairs={{0,2},{1,3},{2,0},{3,1},{4,6},{5,7},{6,4},{7,5},{8,10},{9,11},{10,... | collective-permute-start | bytes 1572872 | tf_op jit(solution)/shard_map/ppermute | solution.py:372
  123.3 30.5 %collective-permute-start.34 = (bf16[256,1024]{1,0:T(8,128)(2,1)S(1)}, bf16[256,1024]{1,0:T(8,128)(2,1)S(1)}, u32[]{:S(2)}, u32[]{:S(2)}) collective-permute-start(bf16[256,1024]{1,0:T(8,128)(2,1)S(1)} %shard_map.112.pair0), channel_id=1, source_target_pairs={{0,3},{1,0},{2,1},{3,2},{4,7},{5,4},{6,5},{7,6},{8,11},{9,8},{10,9... | collective-permute-start | bytes 1572872 | tf_op jit(solution)/shard_map/ppermute | solution.py:372
  140.5 14.7 %collective-permute-start.30 = (bf16[512,128]{1,0:T(8,128)(2,1)S(1)}, bf16[512,128]{1,0:T(8,128)(2,1)S(1)}, u32[]{:S(2)}, u32[]{:S(2)}) collective-permute-start(bf16[512,128]{1,0:T(8,128)(2,1)S(1)} %shard_map.110.solved), channel_id=1, source_target_pairs={{0,16},{16,32},{32,48},{48,64},{64,80},{80,96},{96,112},{112,128},... | collective-permute-start | bytes 393224 | tf_op jit(solution)/shard_map/ppermute | solution.py:409
  150.6 7.5 %collective-permute-start.35 = (bf16[512,128]{1,0:T(8,128)(2,1)S(1)}, bf16[512,128]{1,0:T(8,128)(2,1)S(1)}, u32[]{:S(2)}, u32[]{:S(2)}) collective-permute-start(bf16[512,128]{1,0:T(8,128)(2,1)S(1)} %shard_map.110.solved), channel_id=1, source_target_pairs={{16,0},{32,16},{48,32},{64,48},{80,64},{96,80},{112,96},{128,112},... | collective-permute-start | bytes 393224 | tf_op jit(solution)/shard_map/ppermute | solution.py:409
  (18 other events, 86.0 us)
Sparse Core Ops, SparseCore 0:
  11.2 28.6 all-gather.4
  41.7 32.0 all-gather.6

commit v8 on v7

--- a/solution.py
+++ b/solution.py
@@ -196,24 +196,29 @@
     out[pl.ds(0, 256), pl.ds(256, 256)] = imag.astype(out.dtype)
 
 
-def odd_kernel(s_ref, g_ref, panel0, panel1, panel3, low, high, out, out_second, held, panel2):
-    y, x = s_ref[0], s_ref[1]
+def take_odd(s_ref, g_ref, panel0, panel1, panel3, low, high, held, panel2):
     panel2[pl.ds(0, 128), :] = low[...]
     panel2[pl.ds(128, 128), :] = high[...]
-    panels = (panel0, panel1, panel2, panel3)
     held[...] = g_ref[...].reshape(512, 1024)
-    put_pair(out, *wide_product(y, held, panels))
-    out[:, pl.ds(512, 128)] = small_product(y, held, panels).astype(BF)
-    put_pair(out_second, *wide_product(y, held, panels, 640))
-    out_second[pl.ds(256, 48), :] = jnp.zeros((48, 512), BF)
-
-
-def even_kernel(s_ref, ca0, ca1, ca2, ca3, panel0, panel1, panel2, panel3, source,
-                ship, upper_new, source_part, a_rows, c_rows):
+    return s_ref[0], held, (panel0, panel1, panel2, panel3)
+
+
+def odd_kernel(s_ref, g_ref, panel0, panel1, panel3, low, high, out, held, panel2):
+    taken = take_odd(s_ref, g_ref, panel0, panel1, panel3, low, high, held, panel2)
+    put_pair(out, *wide_product(*taken))
+    out[:, pl.ds(512, 128)] = small_product(*taken).astype(BF)
+
+
+def odd_second_kernel(s_ref, g_ref, panel0, panel1, panel3, low, high, out, held, panel2):
+    taken = take_odd(s_ref, g_ref, panel0, panel1, panel3, low, high, held, panel2)
+    put_pair(out, *wide_product(*taken, 640))
+    out[pl.ds(256, 48), :] = jnp.zeros((48, 512), BF)
+
+
+def even_kernel(s_ref, ca0, ca1, ca2, ca3, panel0, panel1, panel2, panel3, ship, a_rows):
     y, x = s_ref[0], s_ref[1]
     panels = (panel0, panel1, panel2, panel3)
     stack_rows(x, [block.at[1] for block in (ca0, ca1, ca2, ca3)], a_rows)
-    stack_rows(x, [block.at[0] for block in (ca0, ca1, ca2, ca3)], c_rows)
     value = small_product(y, a_rows, panels)
     lane = lanes_of(32)
     for index in range(4):
@@ -221,6 +226,13 @@
         tile = jnp.where(lane < 64, low, pltpu.roll(high, 64, 1))
         ship[pl.ds(256, 32), pl.ds(index * 128, 128)] = tile.astype(BF)
     put_pair(ship, *wide_product(y, a_rows, panels))
+
+
+def upper_kernel(s_ref, ca0, ca1, ca2, ca3, panel0, panel1, panel2, panel3, source,
+                 upper_new, source_part, c_rows):
+    y, x = s_ref[0], s_ref[1]
+    panels = (panel0, panel1, panel2, panel3)
+    stack_rows(x, [block.at[0] for block in (ca0, ca1, ca2, ca3)], c_rows)
     own = pltpu.roll(source[:, pl.ds(512, 128)].astype(F32), 64, 1)
     own = jnp.where(lanes_of(256) < 64, own, 0.0)
     source_part[...] = own - small_product(y, c_rows, panels)
@@ -228,12 +240,15 @@
     put_pair(upper_new, -real, -imag)
 
 
-def diagonal_kernel(s_ref, c_rows, a_rows, panel0, panel1, panel2, panel3, diagonal, shipped,
-                    out, lower):
+def diagonal_kernel(s_ref, c_rows, panel0, panel1, panel2, panel3, diagonal, shipped,
+                    out):
     real, imag = wide_product(s_ref[0], c_rows, (panel0, panel1, panel2, panel3))
     real = diagonal[:, pl.ds(0, 256)].astype(F32) - real - shipped[pl.ds(0, 256), pl.ds(0, 256)].astype(F32)
     imag = diagonal[:, pl.ds(256, 256)].astype(F32) - imag - shipped[pl.ds(0, 256), pl.ds(256, 256)].astype(F32)
     put_pair(out, real, imag)
+
+
+def lower_kernel(s_ref, a_rows, panel0, panel1, panel2, panel3, lower):
     real, imag = wide_product(s_ref[0], a_rows, (panel0, panel1, panel2, panel3))
     put_pair(lower, -real, -imag)
 
@@ -450,26 +465,34 @@
     panels, near = ring_gathered_y(scalars, panel, near)
     g_rows = near[0]
     ca_blocks = [couplings, near[1], moved_x(couplings, 2), near[2]]
-    first, second = call(
-        odd_kernel, [shape((256, 640)), shape((304, 512))], wide_flops,
-        scalars, g_rows, *panels,
-        scratch=[pltpu.VMEM((512, 1024), BF), pltpu.VMEM((256, 1152), BF)],
+    taken = [pltpu.VMEM((512, 1024), BF), pltpu.VMEM((256, 1152), BF)]
+    (first,) = call(
+        odd_kernel, [shape((256, 640))], wide_flops, scalars, g_rows, *panels, scratch=taken
+    )
+    (second,) = call(
+        odd_second_kernel, [shape((304, 512))], wide_flops,
+        scalars, g_rows, *panels, scratch=taken,
     )
     firsts = gathered_y(first)
     second, g_columns, *ca_blocks = after((second, g_columns, *ca_blocks))
     seconds = gathered_y(second)
-    ship, upper_new, source_part, a_rows, c_rows = call(
-        even_kernel,
-        [shape((288, 512)), shape((256, 512)), shape((256, 128), F32),
-         shape((512, 1024)),
-         shape((512, 1024))],
-        2 * wide_flops,
-        scalars, *ca_blocks, *firsts, panel, pinned=(1, 2, 3, 4),
+    ship, a_rows = call(
+        even_kernel, [shape((288, 512)), shape((512, 1024))], wide_flops,
+        scalars, *ca_blocks, *firsts,
+    )
+    upper_new, source_part, c_rows = call(
+        upper_kernel,
+        [shape((256, 512)), shape((256, 128), F32), shape((512, 1024))],
+        wide_flops,
+        scalars, *ca_blocks, *firsts, panel,
     )
     shipped = along_cuts(ship, 1)
-    diagonal_new, ship_lower = call(
-        diagonal_kernel, [shape((256, 512))] * 2, 2 * wide_flops,
-        scalars, c_rows, a_rows, *seconds, diagonal, shipped, pinned=(3, 7),
+    (diagonal_new,) = call(
+        diagonal_kernel, [shape((256, 512))], wide_flops,
+        scalars, c_rows, *seconds, diagonal, shipped,
+    )
+    (ship_lower,) = call(
+        lower_kernel, [shape((256, 512))], wide_flops, scalars, a_rows, *seconds
     )
     diagonals = [diagonal_new] + [moved_x(diagonal_new, by) for by in turns]
     packed_shapes = [shape((512, 128), F32), shape((512, 128))]

time: 174 us -> 167 us (0.960)
  starting transfers between devices: 73.9 us -> 65.7 us
  waiting for transfers between devices: 47.5 us -> 43.9 us
  Pallas kernels: 23.3 us -> 25.7 us
  local copies, waits for them, and re-layouts: 3.99 us -> 6.13 us
    ppermute x5, waiting for transfers between devices: 6.54 us -> 2.16 us  [along_cuts(): return lax.ppermute(block, 'cuts', pairs)]
    ppermute x15, starting transfers between devices: 26.4 us -> 22.5 us  [moved_x(): return lax.ppermute(block, 'row', pairs)]
    ppermute x5, starting transfers between devices: 27.2 us -> 23.5 us  [along_cuts(): return lax.ppermute(block, 'cuts', pairs)]
    ppermute x15, waiting for transfers between devices: 4.07 us -> 6.71 us  [moved_x(): return lax.ppermute(block, 'row', pairs)]
    pallas_call x15 -> x18, Pallas kernels: 23.3 us -> 25.7 us  [call(): pl.pallas_call(kernel, out_shape=tuple(out_shapes), in_specs=[SMEM] + [an...]
    unnamed x18 -> x20, local copies, waits for them, and re-layouts: 3.92 us -> 6.05 us
    ppermute x19, waiting for transfers between devices: 26.5 us -> 24.7 us  [moved_y(): return lax.ppermute(block, 'row', pairs)]
  transfers between devices with their start and end apart: 41 -> 41, of which waited for: 16 -> 14; matrix products, arithmetic and copies ran while one was open for 0% -> 0% of each run, Pallas kernels for 10% -> 12%
where the time goes in v8:
time: 167 us; the launch traced here: 165 us
  starting transfers between devices  65.7 us (39%)
  waiting for transfers between devices  43.9 us (26%)
  Pallas kernels  25.7 us (15%)
  between operations  14.3 us (9%)
  blocking collectives  9.62 us (6%)
  local copies, waits for them, and re-layouts  6.13 us (4%)
    pallas_call x18, Pallas kernels, call(): pl.pallas_call(kernel, out_shape=tuple(out_shapes), in_specs=[SMEM] + [an...  25.7 us
    ppermute x19, waiting for transfers between devices, moved_y(): return lax.ppermute(block, 'row', pairs)  24.7 us
    ppermute x5, starting transfers between devices, along_cuts(): return lax.ppermute(block, 'cuts', pairs)  23.5 us
    ppermute x15, starting transfers between devices, moved_x(): return lax.ppermute(block, 'row', pairs)  22.5 us
    ppermute x19, starting transfers between devices, moved_y(): return lax.ppermute(block, 'row', pairs)  19.7 us
    all_gather x2, waiting for transfers between devices, gathered_x(): return lax.all_gather(block, 'row', axis_index_groups=groups)  10.3 us
    all_to_all x1, blocking collectives, body(): lax.all_to_all(g_pieces, 'row', 0, 0, axis_index_groups=groups, tiled=True)  9.62 us
    ppermute x15, waiting for transfers between devices, moved_x(): return lax.ppermute(block, 'row', pairs)  6.71 us
  transfers between devices with their start and end apart: 41, of which 14 were waited for; matrix products, arithmetic and copies ran while one was open for 0% of the time, Pallas kernels for 12%

profile of v8, /device:TPU:97, one launch (start us, length us, event | category | flops | bytes accessed | tf_op | source)
XLA Modules:
  0.0 165.5 jit_solution(13435589494350422096)
XLA Ops:
  8.1 2.9 %shard_map.101 = (bf16[64,1664]{1,0:T(8,128)(2,1)S(1)}, bf16[64,1664]{1,0:T(8,128)(2,1)S(1)}, bf16[64,1664]{1,0:T(8,128)(2,1)S(1)}, bf16[64,1664]{1,0:T(8,128)(2...) custom-call(s32[6]{0:T(128)S(1)} %pad_add_fusion.1.s_ref, ...), custom_call_target="tpu_custom_call" | custom-call | bytes 4063256 | tf_op jit(solution)/shard_map/pallas_call | solution.py:29
  11.1 2.6 %collective-permute-start = (bf16[2,64,1024]{2,1,0:T(8,128)(2,1)S(1)}, bf16[2,64,1024]{2,1,0:T(8,128)(2,1)S(1)}, u32[]{:S(2)}, u32[]{:S(2)}) collective-permute-start(bf16[2,64,1024]{2,1,0:T(8,128)(2,1)S(1)} %get-tuple-element.63), channel_id=1, source_target_pairs={{16,0},{32,16},{48,32},{64,48},{80,64},{96,80},{112,96},{128,112},... | collective-permute-start | bytes 786440 | tf_op jit(solution)/shard_map/ppermute | solution.py:424
  15.0 2.5 %collective-permute-start.2 = (bf16[64,1664]{1,0:T(8,128)(2,1)S(1)}, bf16[64,1664]{1,0:T(8,128)(2,1)S(1)}, u32[]{:S(2)}, u32[]{:S(2)}) collective-permute-start(bf16[64,1664]{1,0:T(8,128)(2,1)S(1)} %get-tuple-element.67), channel_id=1, source_target_pairs={{0,2},{1,3},{2,0},{3,1},{4,6},{5,7},{6,4},{7,5},{8,10},{9,11},{10,... | collective-permute-start | bytes 638984 | tf_op jit(solution)/shard_map/ppermute | solution.py:387
  18.6 9.6 %all_to_all.5 = bf16[4,2,64,256]{3,2,1,0:T(8,128)(2,1)} all-to-all(bf16[4,2,64,256]{3,2,1,0:T(8,128)(2,1)S(1)} %get-tuple-element.64), channel_id=1, replica_groups={{0,4,8,12},{1,5,9,13},{2,6,10,14},{3,7,11,15},{16,20,24,28},{17,21,25,2..., dimensions={0} | all-to-all | bytes 524288 | tf_op jit(solution)/shard_map/all_to_all | solution.py:454
  29.6 2.0 %collective-permute-start.4 = (bf16[256,1152]{1,0:T(8,128)(2,1)S(1)}, bf16[256,1152]{1,0:T(8,128)(2,1)S(1)}, u32[]{:S(2)}, u32[]{:S(2)}) collective-permute-start(bf16[256,1152]{1,0:T(8,128)(2,1)S(1)} %get-tuple-element.75.panel0.source), channel_id=1, source_target_pairs={{0,12},{1,13},{2,14},{3,15},{4,0},{5,1},{6,2},{7,3},{8,4},{9,5},{1... | collective-permute-start | bytes 1769480 | tf_op jit(solution)/shard_map/ppermute | solution.py:392
  32.3 2.0 %collective-permute-start.9 = (bf16[2,2,64,1024]{3,2,1,0:T(8,128)(2,1)S(1)}, bf16[2,2,64,1024]{3,2,1,0:T(8,128)(2,1)S(1)}, u32[]{:S(2)}, u32[]{:S(2)}) collective-permute-start(bf16[2,2,64,1024]{3,2,1,0:T(8,128)(2,1)S(1)} %get-tuple-element.89.ca0), channel_id=1, source_target_pairs={{0,3},{1,0},{2,1},{3,2},{4,7},{5,4},{6,5},{7,6},{8,11},{9,8},{10,9... | collective-permute-start | bytes 1572872 | tf_op jit(solution)/shard_map/ppermute | solution.py:387
  34.3 8.8 %collective-permute-done.4.other.panel1 = bf16[256,1152]{1,0:T(8,128)(2,1)S(1)} collective-permute-done((bf16[256,1152]{1,0:T(8,128)(2,1)S(1)}, bf16[256,1152]{1,0:T(8,128)(2,1)S(1)}, u32[]{:S(2)}, u32[]{:S(2)}) %collective-permute-start.4) | collective-permute-done | bytes 589856 | tf_op jit(solution)/shard_map/ppermute | solution.py:392
  43.1 3.1 %collective-permute-done.5.block.panel3 = bf16[256,1152]{1,0:T(8,128)(2,1)S(1)} collective-permute-done((bf16[256,1152]{1,0:T(8,128)(2,1)S(1)}, bf16[256,1152]{1,0:T(8,128)(2,1)S(1)}, u32[]{:S(2)}, u32[]{:S(2)}) %collective-permute-start.5) | collective-permute-done | bytes 589856 | tf_op jit(solution)/shard_map/ppermute | solution.py:392
  46.9 2.7 %collective-permute-start.7 = (bf16[128,1152]{1,0:T(8,128)(2,1)S(1)}, bf16[128,1152]{1,0:T(8,128)(2,1)S(1)}, u32[]{:S(2)}, u32[]{:S(2)}) collective-permute-start(bf16[128,1152]{1,0:T(8,128)(2,1)S(1)} %get-tuple-element.81), channel_id=1, source_target_pairs={{0,12},{1,13},{2,14},{3,15},{4,0},{5,1},{6,2},{7,3},{8,4},{9,5},{1... | collective-permute-start | bytes 884744 | tf_op jit(solution)/shard_map/ppermute | solution.py:392
  49.6 2.0 %collective-permute-start.10 = (bf16[2,2,64,1024]{3,2,1,0:T(8,128)(2,1)S(1)}, bf16[2,2,64,1024]{3,2,1,0:T(8,128)(2,1)S(1)}, u32[]{:S(2)}, u32[]{:S(2)}) collective-permute-start(bf16[2,2,64,1024]{3,2,1,0:T(8,128)(2,1)S(1)} %get-tuple-element.89.ca0), channel_id=1, source_target_pairs={{0,2},{1,3},{2,0},{3,1},{4,6},{5,7},{6,4},{7,5},{8,10},{9,11},{10,... | collective-permute-start | bytes 1572872 | tf_op jit(solution)/shard_map/ppermute | solution.py:387
  52.4 1.9 %collective-permute-done.6.low = bf16[128,1152]{1,0:T(8,128)(2,1)S(1)} collective-permute-done((bf16[128,1152]{1,0:T(8,128)(2,1)S(1)}, bf16[128,1152]{1,0:T(8,128)(2,1)S(1)}, u32[]{:S(2)}, u32[]{:S(2)}) %collective-permute-start.6) | collective-permute-done | bytes 294944 | tf_op jit(solution)/shard_map/ppermute | solution.py:392
  56.0 2.5 %collective-permute-start.11 = (bf16[256,640]{1,0:T(8,128)(2,1)S(1)}, bf16[256,640]{1,0:T(8,128)(2,1)}, u32[]{:S(2)}, u32[]{:S(2)}) collective-permute-start(bf16[256,640]{1,0:T(8,128)(2,1)S(1)} %shard_map.105.panel0), channel_id=1, source_target_pairs={{0,12},{1,13},{2,14},{3,15},{4,0},{5,1},{6,2},{7,3},{8,4},{9,5},{1... | collective-permute-start | bytes 983048 | tf_op jit(solution)/shard_map/ppermute | solution.py:392
  60.5 2.2 %collective-permute-done.10.ca2 = bf16[2,2,64,1024]{3,2,1,0:T(8,128)(2,1)S(1)} collective-permute-done((bf16[2,2,64,1024]{3,2,1,0:T(8,128)(2,1)S(1)}, bf16[2,2,64,1024]{3,2,1,0:T(8,128)(2,1)S(1)}, u32[]{:S(2)}, u32[]{:S(2)}) %collective-permute-start.10) | collective-permute-done | bytes 524320 | tf_op jit(solution)/shard_map/ppermute | solution.py:387
  63.5 10.3 %all-gather.7.cloned.1.call-done = bf16[16,2,64,256]{3,2,1,0:T(8,128)(2,1)} async-done(((bf16[4,2,64,256]{3,2,1,0:T(8,128)(2,1)}), bf16[16,2,64,256]{3,2,1,0:T(8,128)(2,1)}) %all-gather.7.cloned.1.call-update) | async-done | bytes 1048592 | tf_op jit(solution)/shard_map/all_gather | solution.py:418
  77.8 2.2 %shard_map.107 = (bf16[288,512]{1,0:T(8,128)(2,1)S(1)}, bf16[512,1024]{1,0:T(8,128)(2,1)S(1)}) custom-call(s32[6]{0:T(128)S(1)} %pad_add_fusion.1.s_ref, bf16[2,2,64,1024]{3,2,1,0:T(8,128)(2,1)S(1)} %get-tuple-element.89.ca0, bf16[2,2,64,1024]{3,2,1,0:T(8,128)(2,1)S(1)} %collective-permute-done.8.ca1, bf16[2,2,64,1024]{3,2,1,0:T(8,128)(2,1)S(1)} %copy-done.6, ...), custom_call_target="tpu_custom_call" | custom-call | bytes 4751384 | tf_op jit(solution)/shard_map/pallas_call | solution.py:29
  80.0 6.0 %collective-permute-start.14 = (bf16[288,512]{1,0:T(8,128)(2,1)S(1)}, bf16[288,512]{1,0:T(8,128)(2,1)S(1)}, u32[]{:S(2)}, u32[]{:S(2)}) collective-permute-start(bf16[288,512]{1,0:T(8,128)(2,1)S(1)} %get-tuple-element.94), channel_id=1, source_target_pairs={{0,16},{16,32},{32,48},{48,64},{64,80},{80,96},{96,112},{112,128},... | collective-permute-start | bytes 884744 | tf_op jit(solution)/shard_map/ppermute | solution.py:424
  87.1 2.2 %shard_map.106 = (bf16[256,512]{1,0:T(8,128)(2,1)S(1)}, f32[256,128]{1,0:T(8,128)S(1)}, bf16[512,1024]{1,0:T(8,128)(2,1)S(1)}) custom-call(s32[6]{0:T(128)S(1)} %pad_add_fusion.1.s_ref, bf16[2,2,64,1024]{3,2,1,0:T(8,128)(2,1)S(1)} %get-tuple-element.89.ca0, bf16[2,2,64,1024]{3,2,1,0:T(8,128)(2,1)S(1)} %collective-permute-done.8.ca1, ...), custom_call_target="tpu_custom_call" | custom-call | bytes 5439512 | tf_op jit(solution)/shard_map/pallas_call | solution.py:29
  90.9 2.7 %collective-permute-start.15 = (bf16[512,128]{1,0:T(8,128)(2,1)S(1)}, bf16[512,128]{1,0:T(8,128)(2,1)S(1)}, u32[]{:S(2)}, u32[]{:S(2)}) collective-permute-start(bf16[512,128]{1,0:T(8,128)(2,1)S(1)} %get-tuple-element.96), channel_id=1, source_target_pairs={{0,12},{1,13},{2,14},{3,15},{4,0},{5,1},{6,2},{7,3},{8,4},{9,5},{1... | collective-permute-start | bytes 393224 | tf_op jit(solution)/shard_map/ppermute | solution.py:392
  96.7 4.0 %collective-permute-start.22 = (bf16[256,512]{1,0:T(8,128)(2,1)S(1)}, bf16[256,512]{1,0:T(8,128)(2,1)S(1)}, u32[]{:S(2)}, u32[]{:S(2)}) collective-permute-start(bf16[256,512]{1,0:T(8,128)(2,1)S(1)} %shard_map.109.refs_0_.refs_1_.block0), channel_id=1, source_target_pairs={{0,2},{1,3},{2,0},{3,1},{4,6},{5,7},{6,4},{7,5},{8,10},{9,11},{10,... | collective-permute-start | bytes 786440 | tf_op jit(solution)/shard_map/ppermute | solution.py:387
  102.7 7.0 %collective-permute-start.31 = (bf16[256,512]{1,0:T(8,128)(2,1)S(1)}, bf16[256,512]{1,0:T(8,128)(2,1)S(1)}, u32[]{:S(2)}, u32[]{:S(2)}) collective-permute-start(bf16[256,512]{1,0:T(8,128)(2,1)S(1)} %shard_map.114), channel_id=1, source_target_pairs={{0,16},{16,32},{32,48},{48,64},{64,80},{80,96},{96,112},{112,128},... | collective-permute-start | bytes 786440 | tf_op jit(solution)/shard_map/ppermute | solution.py:424
  109.7 2.9 %collective-permute-done.22.refs_2_.refs_3_.block2 = bf16[256,512]{1,0:T(8,128)(2,1)S(1)} collective-permute-done((bf16[256,512]{1,0:T(8,128)(2,1)S(1)}, bf16[256,512]{1,0:T(8,128)(2,1)S(1)}, u32[]{:S(2)}, u32[]{:S(2)}) %collective-permute-start.22) | collective-permute-done | bytes 262176 | tf_op jit(solution)/shard_map/ppermute | solution.py:387
  115.6 2.1 %collective-permute-start.25 = (bf16[512,128]{1,0:T(8,128)(2,1)S(1)}, bf16[512,128]{1,0:T(8,128)(2,1)S(1)}, u32[]{:S(2)}, u32[]{:S(2)}) collective-permute-start(bf16[512,128]{1,0:T(8,128)(2,1)S(1)} %get-tuple-element.102), channel_id=1, source_target_pairs={{0,8},{1,9},{2,10},{3,11},{4,12},{5,13},{6,14},{7,15},{8,0},{9,1},... | collective-permute-start | bytes 393224 | tf_op jit(solution)/shard_map/ppermute | solution.py:392
  118.9 2.5 %collective-permute-start.33 = (bf16[256,1024]{1,0:T(8,128)(2,1)S(1)}, bf16[256,1024]{1,0:T(8,128)(2,1)S(1)}, u32[]{:S(2)}, u32[]{:S(2)}) collective-permute-start(bf16[256,1024]{1,0:T(8,128)(2,1)S(1)} %shard_map.115.pair0), channel_id=1, source_target_pairs={{0,2},{1,3},{2,0},{3,1},{4,6},{5,7},{6,4},{7,5},{8,10},{9,11},{10,... | collective-permute-start | bytes 1572872 | tf_op jit(solution)/shard_map/ppermute | solution.py:387
  121.6 3.1 %collective-permute-done.26.got3 = bf16[512,128]{1,0:T(8,128)(2,1)S(1)} collective-permute-done((bf16[512,128]{1,0:T(8,128)(2,1)S(1)}, bf16[512,128]{1,0:T(8,128)(2,1)S(1)}, u32[]{:S(2)}, u32[]{:S(2)}) %collective-permute-start.26) | collective-permute-done | bytes 131104 | tf_op jit(solution)/shard_map/ppermute | solution.py:392
  124.7 1.8 %shard_map.111 = (bf16[512,128]{1,0:T(8,128)(2,1)S(1)}, f32[512,128]{1,0:T(8,128)S(1)}, bf16[512,128]{1,0:T(8,128)(2,1)S(1)}) custom-call(s32[6]{0:T(128)S(1)} %pad_add_fusion.1.s_ref, f32[512,128]{1,0:T(8,128)S(1)} %get-tuple-element.101.own, bf16[512,128]{1,0:T(8,128)(2,1)S(1)} %collective-permute-done.24.got1, ...), custom_call_target="tpu_custom_call" | custom-call | bytes 3473432 | tf_op jit(solution)/shard_map/pallas_call | solution.py:29
  126.6 2.0 %collective-permute-start.28 = (bf16[512,128]{1,0:T(8,128)(2,1)S(1)}, bf16[512,128]{1,0:T(8,128)(2,1)S(1)}, u32[]{:S(2)}, u32[]{:S(2)}) collective-permute-start(bf16[512,128]{1,0:T(8,128)(2,1)S(1)} %get-tuple-element.105), channel_id=1, source_target_pairs={{0,8},{1,9},{2,10},{3,11},{4,12},{5,13},{6,14},{7,15},{8,0},{9,1},... | collective-permute-start | bytes 393224 | tf_op jit(solution)/shard_map/ppermute | solution.py:392
  128.6 2.1 %collective-permute-done.27.got1 = bf16[512,128]{1,0:T(8,128)(2,1)S(1)} collective-permute-done((bf16[512,128]{1,0:T(8,128)(2,1)S(1)}, bf16[512,128]{1,0:T(8,128)(2,1)S(1)}, u32[]{:S(2)}, u32[]{:S(2)}) %collective-permute-start.27) | collective-permute-done | bytes 131104 | tf_op jit(solution)/shard_map/ppermute | solution.py:392
  132.0 4.0 %collective-permute-done.29.got3 = bf16[512,128]{1,0:T(8,128)(2,1)S(1)} collective-permute-done((bf16[512,128]{1,0:T(8,128)(2,1)S(1)}, bf16[512,128]{1,0:T(8,128)(2,1)S(1)}, u32[]{:S(2)}, u32[]{:S(2)}) %collective-permute-start.29) | collective-permute-done | bytes 131104 | tf_op jit(solution)/shard_map/ppermute | solution.py:392
  136.7 4.9 %collective-permute-start.30 = (bf16[512,128]{1,0:T(8,128)(2,1)S(1)}, bf16[512,128]{1,0:T(8,128)(2,1)S(1)}, u32[]{:S(2)}, u32[]{:S(2)}) collective-permute-start(bf16[512,128]{1,0:T(8,128)(2,1)S(1)} %shard_map.112.solved), channel_id=1, source_target_pairs={{0,16},{16,32},{32,48},{48,64},{64,80},{80,96},{96,112},{112,128},... | collective-permute-start | bytes 393224 | tf_op jit(solution)/shard_map/ppermute | solution.py:424
  141.5 3.0 %collective-permute-start.35 = (bf16[512,128]{1,0:T(8,128)(2,1)S(1)}, bf16[512,128]{1,0:T(8,128)(2,1)S(1)}, u32[]{:S(2)}, u32[]{:S(2)}) collective-permute-start(bf16[512,128]{1,0:T(8,128)(2,1)S(1)} %shard_map.112.solved), channel_id=1, source_target_pairs={{16,0},{32,16},{48,32},{64,48},{80,64},{96,80},{112,96},{128,112},... | collective-permute-start | bytes 393224 | tf_op jit(solution)/shard_map/ppermute | solution.py:424
  150.5 2.5 %collective-permute-start.36 = (f32[64,128]{1,0:T(8,128)S(1)}, f32[64,128]{1,0:T(8,128)S(1)}, u32[]{:S(2)}, u32[]{:S(2)}) collective-permute-start(f32[64,128]{1,0:T(8,128)S(1)} %get-tuple-element.116), channel_id=1, source_target_pairs={{0,1},{1,2},{2,3},{3,0},{4,5},{5,6},{6,7},{7,4},{8,9},{9,10},{10,1... | collective-permute-start | bytes 98312 | tf_op jit(solution)/shard_map/ppermute | solution.py:387
  153.7 2.0 %collective-permute-start.38 = (f32[64,128]{1,0:T(8,128)S(1)}, f32[64,128]{1,0:T(8,128)S(1)}, u32[]{:S(2)}, u32[]{:S(2)}) collective-permute-start(f32[64,128]{1,0:T(8,128)S(1)} %get-tuple-element.118), channel_id=1, source_target_pairs={{0,3},{1,0},{2,1},{3,2},{4,7},{5,4},{6,5},{7,6},{8,11},{9,8},{10,9... | collective-permute-start | bytes 98312 | tf_op jit(solution)/shard_map/ppermute | solution.py:387
  (94 shorter events, 39.0 us)
Async XLA Ops:
  7.2 39.1 %all-gather.5.cloned.1.call-start = ((), (), s32[]{:S(2)}) async-start(), calls=%async_computation.1 | async-start | bytes 1310720 | tf_op jit(solution)/shard_map/all_gather | solution.py:418
  11.1 62.7 %all-gather.7.cloned.1.call-start = ((), (), s32[]{:S(2)}) async-start(), calls=%async_computation.2 | async-start | bytes 1310720 | tf_op jit(solution)/shard_map/all_gather | solution.py:418
  11.1 17.1 %collective-permute-start = (bf16[2,64,1024]{2,1,0:T(8,128)(2,1)S(1)}, bf16[2,64,1024]{2,1,0:T(8,128)(2,1)S(1)}, u32[]{:S(2)}, u32[]{:S(2)}) collective-permute-start(bf16[2,64,1024]{2,1,0:T(8,128)(2,1)S(1)} %get-tuple-element.63), channel_id=1, source_target_pairs={{16,0},{32,16},{48,32},{64,48},{80,64},{96,80},{112,96},{128,112},... | collective-permute-start | bytes 786440 | tf_op jit(solution)/shard_map/ppermute | solution.py:424
  13.7 14.5 %collective-permute-start.1 = (bf16[64,1664]{1,0:T(8,128)(2,1)S(1)}, bf16[64,1664]{1,0:T(8,128)(2,1)S(1)}, u32[]{:S(2)}, u32[]{:S(2)}) collective-permute-start(bf16[64,1664]{1,0:T(8,128)(2,1)S(1)} %get-tuple-element.66), channel_id=1, source_target_pairs={{0,1},{1,2},{2,3},{3,0},{4,5},{5,6},{6,7},{7,4},{8,9},{9,10},{10,1... | collective-permute-start | bytes 638984 | tf_op jit(solution)/shard_map/ppermute | solution.py:387
  15.0 13.2 %collective-permute-start.2 = (bf16[64,1664]{1,0:T(8,128)(2,1)S(1)}, bf16[64,1664]{1,0:T(8,128)(2,1)S(1)}, u32[]{:S(2)}, u32[]{:S(2)}) collective-permute-start(bf16[64,1664]{1,0:T(8,128)(2,1)S(1)} %get-tuple-element.67), channel_id=1, source_target_pairs={{0,2},{1,3},{2,0},{3,1},{4,6},{5,7},{6,4},{7,5},{8,10},{9,11},{10,... | collective-permute-start | bytes 638984 | tf_op jit(solution)/shard_map/ppermute | solution.py:387
  17.4 10.8 %collective-permute-start.3 = (bf16[64,1664]{1,0:T(8,128)(2,1)S(1)}, bf16[64,1664]{1,0:T(8,128)(2,1)S(1)}, u32[]{:S(2)}, u32[]{:S(2)}) collective-permute-start(bf16[64,1664]{1,0:T(8,128)(2,1)S(1)} %get-tuple-element.68), channel_id=1, source_target_pairs={{0,3},{1,0},{2,1},{3,2},{4,7},{5,4},{6,5},{7,6},{8,11},{9,8},{10,9... | collective-permute-start | bytes 638984 | tf_op jit(solution)/shard_map/ppermute | solution.py:387
  29.6 13.5 %collective-permute-start.4 = (bf16[256,1152]{1,0:T(8,128)(2,1)S(1)}, bf16[256,1152]{1,0:T(8,128)(2,1)S(1)}, u32[]{:S(2)}, u32[]{:S(2)}) collective-permute-start(bf16[256,1152]{1,0:T(8,128)(2,1)S(1)} %get-tuple-element.75.panel0.source), channel_id=1, source_target_pairs={{0,12},{1,13},{2,14},{3,15},{4,0},{5,1},{6,2},{7,3},{8,4},{9,5},{1... | collective-permute-start | bytes 1769480 | tf_op jit(solution)/shard_map/ppermute | solution.py:392
  31.6 14.6 %collective-permute-start.5 = (bf16[256,1152]{1,0:T(8,128)(2,1)S(1)}, bf16[256,1152]{1,0:T(8,128)(2,1)S(1)}, u32[]{:S(2)}, u32[]{:S(2)}) collective-permute-start(bf16[256,1152]{1,0:T(8,128)(2,1)S(1)} %get-tuple-element.75.panel0.source), channel_id=1, source_target_pairs={{0,4},{1,5},{2,6},{3,7},{4,8},{5,9},{6,10},{7,11},{8,12},{9,13},{1... | collective-permute-start | bytes 1769480 | tf_op jit(solution)/shard_map/ppermute | solution.py:392
  31.6 19.9 %collective-permute-start.8 = (bf16[2,2,64,1024]{3,2,1,0:T(8,128)(2,1)S(1)}, bf16[2,2,64,1024]{3,2,1,0:T(8,128)(2,1)S(1)}, u32[]{:S(2)}, u32[]{:S(2)}) collective-permute-start(bf16[2,2,64,1024]{3,2,1,0:T(8,128)(2,1)S(1)} %get-tuple-element.89.ca0), channel_id=1, source_target_pairs={{0,1},{1,2},{2,3},{3,0},{4,5},{5,6},{6,7},{7,4},{8,9},{9,10},{10,1... | collective-permute-start | bytes 1572872 | tf_op jit(solution)/shard_map/ppermute | solution.py:387
  32.3 19.3 %collective-permute-start.9 = (bf16[2,2,64,1024]{3,2,1,0:T(8,128)(2,1)S(1)}, bf16[2,2,64,1024]{3,2,1,0:T(8,128)(2,1)S(1)}, u32[]{:S(2)}, u32[]{:S(2)}) collective-permute-start(bf16[2,2,64,1024]{3,2,1,0:T(8,128)(2,1)S(1)} %get-tuple-element.89.ca0), channel_id=1, source_target_pairs={{0,3},{1,0},{2,1},{3,2},{4,7},{5,4},{6,5},{7,6},{8,11},{9,8},{10,9... | collective-permute-start | bytes 1572872 | tf_op jit(solution)/shard_map/ppermute | solution.py:387
  46.8 7.5 %collective-permute-start.6 = (bf16[128,1152]{1,0:T(8,128)(2,1)S(1)}, bf16[128,1152]{1,0:T(8,128)(2,1)S(1)}, u32[]{:S(2)}, u32[]{:S(2)}) collective-permute-start(bf16[128,1152]{1,0:T(8,128)(2,1)S(1)} %get-tuple-element.80), channel_id=1, source_target_pairs={{0,4},{1,5},{2,6},{3,7},{4,8},{5,9},{6,10},{7,11},{8,12},{9,13},{1... | collective-permute-start | bytes 884744 | tf_op jit(solution)/shard_map/ppermute | solution.py:392
  46.9 7.4 %collective-permute-start.7 = (bf16[128,1152]{1,0:T(8,128)(2,1)S(1)}, bf16[128,1152]{1,0:T(8,128)(2,1)S(1)}, u32[]{:S(2)}, u32[]{:S(2)}) collective-permute-start(bf16[128,1152]{1,0:T(8,128)(2,1)S(1)} %get-tuple-element.81), channel_id=1, source_target_pairs={{0,12},{1,13},{2,14},{3,15},{4,0},{5,1},{6,2},{7,3},{8,4},{9,5},{1... | collective-permute-start | bytes 884744 | tf_op jit(solution)/shard_map/ppermute | solution.py:392
  49.6 13.1 %collective-permute-start.10 = (bf16[2,2,64,1024]{3,2,1,0:T(8,128)(2,1)S(1)}, bf16[2,2,64,1024]{3,2,1,0:T(8,128)(2,1)S(1)}, u32[]{:S(2)}, u32[]{:S(2)}) collective-permute-start(bf16[2,2,64,1024]{3,2,1,0:T(8,128)(2,1)S(1)} %get-tuple-element.89.ca0), channel_id=1, source_target_pairs={{0,2},{1,3},{2,0},{3,1},{4,6},{5,7},{6,4},{7,5},{8,10},{9,11},{10,... | collective-permute-start | bytes 1572872 | tf_op jit(solution)/shard_map/ppermute | solution.py:387
  56.0 18.6 %collective-permute-start.11 = (bf16[256,640]{1,0:T(8,128)(2,1)S(1)}, bf16[256,640]{1,0:T(8,128)(2,1)}, u32[]{:S(2)}, u32[]{:S(2)}) collective-permute-start(bf16[256,640]{1,0:T(8,128)(2,1)S(1)} %shard_map.105.panel0), channel_id=1, source_target_pairs={{0,12},{1,13},{2,14},{3,15},{4,0},{5,1},{6,2},{7,3},{8,4},{9,5},{1... | collective-permute-start | bytes 983048 | tf_op jit(solution)/shard_map/ppermute | solution.py:392
  58.5 16.8 %collective-permute-start.12 = (bf16[256,640]{1,0:T(8,128)(2,1)S(1)}, bf16[256,640]{1,0:T(8,128)(2,1)}, u32[]{:S(2)}, u32[]{:S(2)}) collective-permute-start(bf16[256,640]{1,0:T(8,128)(2,1)S(1)} %shard_map.105.panel0), channel_id=1, source_target_pairs={{0,8},{1,9},{2,10},{3,11},{4,12},{5,13},{6,14},{7,15},{8,0},{9,1},... | collective-permute-start | bytes 983048 | tf_op jit(solution)/shard_map/ppermute | solution.py:392
  58.5 17.2 %collective-permute-start.13 = (bf16[256,640]{1,0:T(8,128)(2,1)S(1)}, bf16[256,640]{1,0:T(8,128)(2,1)}, u32[]{:S(2)}, u32[]{:S(2)}) collective-permute-start(bf16[256,640]{1,0:T(8,128)(2,1)S(1)} %shard_map.105.panel0), channel_id=1, source_target_pairs={{0,4},{1,5},{2,6},{3,7},{4,8},{5,9},{6,10},{7,11},{8,12},{9,13},{1... | collective-permute-start | bytes 983048 | tf_op jit(solution)/shard_map/ppermute | solution.py:392
  73.8 21.0 %collective-permute-start.18 = (bf16[304,512]{1,0:T(8,128)(2,1)S(1)}, bf16[304,512]{1,0:T(8,128)(2,1)S(1)}, u32[]{:S(2)}, u32[]{:S(2)}) collective-permute-start(bf16[304,512]{1,0:T(8,128)(2,1)S(1)} %shard_map.104.panel0), channel_id=1, source_target_pairs={{0,12},{1,13},{2,14},{3,15},{4,0},{5,1},{6,2},{7,3},{8,4},{9,5},{1... | collective-permute-start | bytes 933896 | tf_op jit(solution)/shard_map/ppermute | solution.py:392
  74.2 20.6 %collective-permute-start.19 = (bf16[304,512]{1,0:T(8,128)(2,1)S(1)}, bf16[304,512]{1,0:T(8,128)(2,1)S(1)}, u32[]{:S(2)}, u32[]{:S(2)}) collective-permute-start(bf16[304,512]{1,0:T(8,128)(2,1)S(1)} %shard_map.104.panel0), channel_id=1, source_target_pairs={{0,8},{1,9},{2,10},{3,11},{4,12},{5,13},{6,14},{7,15},{8,0},{9,1},... | collective-permute-start | bytes 933896 | tf_op jit(solution)/shard_map/ppermute | solution.py:392
  74.6 20.2 %collective-permute-start.20 = (bf16[304,512]{1,0:T(8,128)(2,1)S(1)}, bf16[304,512]{1,0:T(8,128)(2,1)S(1)}, u32[]{:S(2)}, u32[]{:S(2)}) collective-permute-start(bf16[304,512]{1,0:T(8,128)(2,1)S(1)} %shard_map.104.panel0), channel_id=1, source_target_pairs={{0,4},{1,5},{2,6},{3,7},{4,8},{5,9},{6,10},{7,11},{8,12},{9,13},{1... | collective-permute-start | bytes 933896 | tf_op jit(solution)/shard_map/ppermute | solution.py:392
  80.0 9.7 %collective-permute-start.14 = (bf16[288,512]{1,0:T(8,128)(2,1)S(1)}, bf16[288,512]{1,0:T(8,128)(2,1)S(1)}, u32[]{:S(2)}, u32[]{:S(2)}) collective-permute-start(bf16[288,512]{1,0:T(8,128)(2,1)S(1)} %get-tuple-element.94), channel_id=1, source_target_pairs={{0,16},{16,32},{32,48},{48,64},{64,80},{80,96},{96,112},{112,128},... | collective-permute-start | bytes 884744 | tf_op jit(solution)/shard_map/ppermute | solution.py:424
  90.9 9.7 %collective-permute-start.15 = (bf16[512,128]{1,0:T(8,128)(2,1)S(1)}, bf16[512,128]{1,0:T(8,128)(2,1)S(1)}, u32[]{:S(2)}, u32[]{:S(2)}) collective-permute-start(bf16[512,128]{1,0:T(8,128)(2,1)S(1)} %get-tuple-element.96), channel_id=1, source_target_pairs={{0,12},{1,13},{2,14},{3,15},{4,0},{5,1},{6,2},{7,3},{8,4},{9,5},{1... | collective-permute-start | bytes 393224 | tf_op jit(solution)/shard_map/ppermute | solution.py:392
  93.6 9.0 %collective-permute-start.16 = (bf16[512,128]{1,0:T(8,128)(2,1)S(1)}, bf16[512,128]{1,0:T(8,128)(2,1)S(1)}, u32[]{:S(2)}, u32[]{:S(2)}) collective-permute-start(bf16[512,128]{1,0:T(8,128)(2,1)S(1)} %get-tuple-element.96), channel_id=1, source_target_pairs={{0,8},{1,9},{2,10},{3,11},{4,12},{5,13},{6,14},{7,15},{8,0},{9,1},... | collective-permute-start | bytes 393224 | tf_op jit(solution)/shard_map/ppermute | solution.py:392
  96.1 13.6 %collective-permute-start.21 = (bf16[256,512]{1,0:T(8,128)(2,1)S(1)}, bf16[256,512]{1,0:T(8,128)(2,1)S(1)}, u32[]{:S(2)}, u32[]{:S(2)}) collective-permute-start(bf16[256,512]{1,0:T(8,128)(2,1)S(1)} %shard_map.109.refs_0_.refs_1_.block0), channel_id=1, source_target_pairs={{0,1},{1,2},{2,3},{3,0},{4,5},{5,6},{6,7},{7,4},{8,9},{9,10},{10,1... | collective-permute-start | bytes 786440 | tf_op jit(solution)/shard_map/ppermute | solution.py:387
  96.7 15.9 %collective-permute-start.22 = (bf16[256,512]{1,0:T(8,128)(2,1)S(1)}, bf16[256,512]{1,0:T(8,128)(2,1)S(1)}, u32[]{:S(2)}, u32[]{:S(2)}) collective-permute-start(bf16[256,512]{1,0:T(8,128)(2,1)S(1)} %shard_map.109.refs_0_.refs_1_.block0), channel_id=1, source_target_pairs={{0,2},{1,3},{2,0},{3,1},{4,6},{5,7},{6,4},{7,5},{8,10},{9,11},{10,... | collective-permute-start | bytes 786440 | tf_op jit(solution)/shard_map/ppermute | solution.py:387
  100.7 11.9 %collective-permute-start.23 = (bf16[256,512]{1,0:T(8,128)(2,1)S(1)}, bf16[256,512]{1,0:T(8,128)(2,1)S(1)}, u32[]{:S(2)}, u32[]{:S(2)}) collective-permute-start(bf16[256,512]{1,0:T(8,128)(2,1)S(1)} %shard_map.109.refs_0_.refs_1_.block0), channel_id=1, source_target_pairs={{0,3},{1,0},{2,1},{3,2},{4,7},{5,4},{6,5},{7,6},{8,11},{9,8},{10,9... | collective-permute-start | bytes 786440 | tf_op jit(solution)/shard_map/ppermute | solution.py:387
  100.7 9.0 %collective-permute-start.17 = (bf16[512,128]{1,0:T(8,128)(2,1)S(1)}, bf16[512,128]{1,0:T(8,128)(2,1)S(1)}, u32[]{:S(2)}, u32[]{:S(2)}) collective-permute-start(bf16[512,128]{1,0:T(8,128)(2,1)S(1)} %get-tuple-element.96), channel_id=1, source_target_pairs={{0,4},{1,5},{2,6},{3,7},{4,8},{5,9},{6,10},{7,11},{8,12},{9,13},{1... | collective-permute-start | bytes 393224 | tf_op jit(solution)/shard_map/ppermute | solution.py:392
  102.7 15.1 %collective-permute-start.31 = (bf16[256,512]{1,0:T(8,128)(2,1)S(1)}, bf16[256,512]{1,0:T(8,128)(2,1)S(1)}, u32[]{:S(2)}, u32[]{:S(2)}) collective-permute-start(bf16[256,512]{1,0:T(8,128)(2,1)S(1)} %shard_map.114), channel_id=1, source_target_pairs={{0,16},{16,32},{32,48},{48,64},{64,80},{80,96},{96,112},{112,128},... | collective-permute-start | bytes 786440 | tf_op jit(solution)/shard_map/ppermute | solution.py:424
  118.3 27.6 %collective-permute-start.32 = (bf16[256,1024]{1,0:T(8,128)(2,1)S(1)}, bf16[256,1024]{1,0:T(8,128)(2,1)S(1)}, u32[]{:S(2)}, u32[]{:S(2)}) collective-permute-start(bf16[256,1024]{1,0:T(8,128)(2,1)S(1)} %shard_map.115.pair0), channel_id=1, source_target_pairs={{0,1},{1,2},{2,3},{3,0},{4,5},{5,6},{6,7},{7,4},{8,9},{9,10},{10,1... | collective-permute-start | bytes 1572872 | tf_op jit(solution)/shard_map/ppermute | solution.py:387
  118.9 27.0 %collective-permute-start.33 = (bf16[256,1024]{1,0:T(8,128)(2,1)S(1)}, bf16[256,1024]{1,0:T(8,128)(2,1)S(1)}, u32[]{:S(2)}, u32[]{:S(2)}) collective-permute-start(bf16[256,1024]{1,0:T(8,128)(2,1)S(1)} %shard_map.115.pair0), channel_id=1, source_target_pairs={{0,2},{1,3},{2,0},{3,1},{4,6},{5,7},{6,4},{7,5},{8,10},{9,11},{10,... | collective-permute-start | bytes 1572872 | tf_op jit(solution)/shard_map/ppermute | solution.py:387
  121.4 24.5 %collective-permute-start.34 = (bf16[256,1024]{1,0:T(8,128)(2,1)S(1)}, bf16[256,1024]{1,0:T(8,128)(2,1)S(1)}, u32[]{:S(2)}, u32[]{:S(2)}) collective-permute-start(bf16[256,1024]{1,0:T(8,128)(2,1)S(1)} %shard_map.115.pair0), channel_id=1, source_target_pairs={{0,3},{1,0},{2,1},{3,2},{4,7},{5,4},{6,5},{7,6},{8,11},{9,8},{10,9... | collective-permute-start | bytes 1572872 | tf_op jit(solution)/shard_map/ppermute | solution.py:387
  136.7 10.6 %collective-permute-start.30 = (bf16[512,128]{1,0:T(8,128)(2,1)S(1)}, bf16[512,128]{1,0:T(8,128)(2,1)S(1)}, u32[]{:S(2)}, u32[]{:S(2)}) collective-permute-start(bf16[512,128]{1,0:T(8,128)(2,1)S(1)} %shard_map.112.solved), channel_id=1, source_target_pairs={{0,16},{16,32},{32,48},{48,64},{64,80},{80,96},{96,112},{112,128},... | collective-permute-start | bytes 393224 | tf_op jit(solution)/shard_map/ppermute | solution.py:424
  141.5 7.5 %collective-permute-start.35 = (bf16[512,128]{1,0:T(8,128)(2,1)S(1)}, bf16[512,128]{1,0:T(8,128)(2,1)S(1)}, u32[]{:S(2)}, u32[]{:S(2)}) collective-permute-start(bf16[512,128]{1,0:T(8,128)(2,1)S(1)} %shard_map.112.solved), channel_id=1, source_target_pairs={{16,0},{32,16},{48,32},{64,48},{80,64},{96,80},{112,96},{128,112},... | collective-permute-start | bytes 393224 | tf_op jit(solution)/shard_map/ppermute | solution.py:424
  (19 other events, 76.9 us)
Sparse Core Ops, SparseCore 0:
  11.2 28.6 all-gather.4
  41.7 32.0 all-gather.6

commit v9 on v8

--- a/solution.py
+++ b/solution.py
@@ -11,7 +11,7 @@
 BF = jnp.bfloat16
 F32 = jnp.float32
 VMEM = pl.BlockSpec(memory_space=pltpu.VMEM)
-MIB = 12
+MIB = 8
 SMEM = pl.BlockSpec(memory_space=pltpu.SMEM)
 
 

time: 167 us -> 167 us (level)
  no operation moved by 1% of the time
where the time goes in v9:
time: 167 us; the launch traced here: 165 us
  starting transfers between devices  65.7 us (39%)
  waiting for transfers between devices  43.9 us (26%)
  Pallas kernels  25.7 us (15%)
  between operations  14.3 us (9%)
  blocking collectives  9.62 us (6%)
  local copies, waits for them, and re-layouts  6.13 us (4%)
    pallas_call x18, Pallas kernels, call(): pl.pallas_call(kernel, out_shape=tuple(out_shapes), in_specs=[SMEM] + [an...  25.7 us
    ppermute x19, waiting for transfers between devices, moved_y(): return lax.ppermute(block, 'row', pairs)  24.7 us
    ppermute x5, starting transfers between devices, along_cuts(): return lax.ppermute(block, 'cuts', pairs)  23.5 us
    ppermute x15, starting transfers between devices, moved_x(): return lax.ppermute(block, 'row', pairs)  22.5 us
    ppermute x19, starting transfers between devices, moved_y(): return lax.ppermute(block, 'row', pairs)  19.7 us
    all_gather x2, waiting for transfers between devices, gathered_x(): return lax.all_gather(block, 'row', axis_index_groups=groups)  10.3 us
    all_to_all x1, blocking collectives, body(): lax.all_to_all(g_pieces, 'row', 0, 0, axis_index_groups=groups, tiled=True)  9.62 us
    ppermute x15, waiting for transfers between devices, moved_x(): return lax.ppermute(block, 'row', pairs)  6.71 us
  transfers between devices with their start and end apart: 41, of which 14 were waited for; matrix products, arithmetic and copies ran while one was open for 0% of the time, Pallas kernels for 12%

profile of v9, /device:TPU:97, one launch (start us, length us, event | category | flops | bytes accessed | tf_op | source)
XLA Modules:
  0.0 165.5 jit_solution(15607656150563693107)
XLA Ops:
  8.1 2.9 %shard_map.101 = (bf16[64,1664]{1,0:T(8,128)(2,1)S(1)}, bf16[64,1664]{1,0:T(8,128)(2,1)S(1)}, bf16[64,1664]{1,0:T(8,128)(2,1)S(1)}, bf16[64,1664]{1,0:T(8,128)(2...) custom-call(s32[6]{0:T(128)S(1)} %pad_add_fusion.1.s_ref, ...), custom_call_target="tpu_custom_call" | custom-call | bytes 4063256 | tf_op jit(solution)/shard_map/pallas_call | solution.py:29
  11.1 2.6 %collective-permute-start = (bf16[2,64,1024]{2,1,0:T(8,128)(2,1)S(1)}, bf16[2,64,1024]{2,1,0:T(8,128)(2,1)S(1)}, u32[]{:S(2)}, u32[]{:S(2)}) collective-permute-start(bf16[2,64,1024]{2,1,0:T(8,128)(2,1)S(1)} %get-tuple-element.63), channel_id=1, source_target_pairs={{16,0},{32,16},{48,32},{64,48},{80,64},{96,80},{112,96},{128,112},... | collective-permute-start | bytes 786440 | tf_op jit(solution)/shard_map/ppermute | solution.py:424
  15.0 2.5 %collective-permute-start.2 = (bf16[64,1664]{1,0:T(8,128)(2,1)S(1)}, bf16[64,1664]{1,0:T(8,128)(2,1)S(1)}, u32[]{:S(2)}, u32[]{:S(2)}) collective-permute-start(bf16[64,1664]{1,0:T(8,128)(2,1)S(1)} %get-tuple-element.67), channel_id=1, source_target_pairs={{0,2},{1,3},{2,0},{3,1},{4,6},{5,7},{6,4},{7,5},{8,10},{9,11},{10,... | collective-permute-start | bytes 638984 | tf_op jit(solution)/shard_map/ppermute | solution.py:387
  18.6 9.6 %all_to_all.5 = bf16[4,2,64,256]{3,2,1,0:T(8,128)(2,1)} all-to-all(bf16[4,2,64,256]{3,2,1,0:T(8,128)(2,1)S(1)} %get-tuple-element.64), channel_id=1, replica_groups={{0,4,8,12},{1,5,9,13},{2,6,10,14},{3,7,11,15},{16,20,24,28},{17,21,25,2..., dimensions={0} | all-to-all | bytes 524288 | tf_op jit(solution)/shard_map/all_to_all | solution.py:454
  29.6 2.0 %collective-permute-start.4 = (bf16[256,1152]{1,0:T(8,128)(2,1)S(1)}, bf16[256,1152]{1,0:T(8,128)(2,1)S(1)}, u32[]{:S(2)}, u32[]{:S(2)}) collective-permute-start(bf16[256,1152]{1,0:T(8,128)(2,1)S(1)} %get-tuple-element.75.panel0.source), channel_id=1, source_target_pairs={{0,12},{1,13},{2,14},{3,15},{4,0},{5,1},{6,2},{7,3},{8,4},{9,5},{1... | collective-permute-start | bytes 1769480 | tf_op jit(solution)/shard_map/ppermute | solution.py:392
  32.3 2.0 %collective-permute-start.9 = (bf16[2,2,64,1024]{3,2,1,0:T(8,128)(2,1)S(1)}, bf16[2,2,64,1024]{3,2,1,0:T(8,128)(2,1)S(1)}, u32[]{:S(2)}, u32[]{:S(2)}) collective-permute-start(bf16[2,2,64,1024]{3,2,1,0:T(8,128)(2,1)S(1)} %get-tuple-element.89.ca0), channel_id=1, source_target_pairs={{0,3},{1,0},{2,1},{3,2},{4,7},{5,4},{6,5},{7,6},{8,11},{9,8},{10,9... | collective-permute-start | bytes 1572872 | tf_op jit(solution)/shard_map/ppermute | solution.py:387
  34.3 8.8 %collective-permute-done.4.other.panel1 = bf16[256,1152]{1,0:T(8,128)(2,1)S(1)} collective-permute-done((bf16[256,1152]{1,0:T(8,128)(2,1)S(1)}, bf16[256,1152]{1,0:T(8,128)(2,1)S(1)}, u32[]{:S(2)}, u32[]{:S(2)}) %collective-permute-start.4) | collective-permute-done | bytes 589856 | tf_op jit(solution)/shard_map/ppermute | solution.py:392
  43.1 3.1 %collective-permute-done.5.block.panel3 = bf16[256,1152]{1,0:T(8,128)(2,1)S(1)} collective-permute-done((bf16[256,1152]{1,0:T(8,128)(2,1)S(1)}, bf16[256,1152]{1,0:T(8,128)(2,1)S(1)}, u32[]{:S(2)}, u32[]{:S(2)}) %collective-permute-start.5) | collective-permute-done | bytes 589856 | tf_op jit(solution)/shard_map/ppermute | solution.py:392
  46.9 2.7 %collective-permute-start.7 = (bf16[128,1152]{1,0:T(8,128)(2,1)S(1)}, bf16[128,1152]{1,0:T(8,128)(2,1)S(1)}, u32[]{:S(2)}, u32[]{:S(2)}) collective-permute-start(bf16[128,1152]{1,0:T(8,128)(2,1)S(1)} %get-tuple-element.81), channel_id=1, source_target_pairs={{0,12},{1,13},{2,14},{3,15},{4,0},{5,1},{6,2},{7,3},{8,4},{9,5},{1... | collective-permute-start | bytes 884744 | tf_op jit(solution)/shard_map/ppermute | solution.py:392
  49.6 2.0 %collective-permute-start.10 = (bf16[2,2,64,1024]{3,2,1,0:T(8,128)(2,1)S(1)}, bf16[2,2,64,1024]{3,2,1,0:T(8,128)(2,1)S(1)}, u32[]{:S(2)}, u32[]{:S(2)}) collective-permute-start(bf16[2,2,64,1024]{3,2,1,0:T(8,128)(2,1)S(1)} %get-tuple-element.89.ca0), channel_id=1, source_target_pairs={{0,2},{1,3},{2,0},{3,1},{4,6},{5,7},{6,4},{7,5},{8,10},{9,11},{10,... | collective-permute-start | bytes 1572872 | tf_op jit(solution)/shard_map/ppermute | solution.py:387
  52.4 1.9 %collective-permute-done.6.low = bf16[128,1152]{1,0:T(8,128)(2,1)S(1)} collective-permute-done((bf16[128,1152]{1,0:T(8,128)(2,1)S(1)}, bf16[128,1152]{1,0:T(8,128)(2,1)S(1)}, u32[]{:S(2)}, u32[]{:S(2)}) %collective-permute-start.6) | collective-permute-done | bytes 294944 | tf_op jit(solution)/shard_map/ppermute | solution.py:392
  56.0 2.5 %collective-permute-start.11 = (bf16[256,640]{1,0:T(8,128)(2,1)S(1)}, bf16[256,640]{1,0:T(8,128)(2,1)}, u32[]{:S(2)}, u32[]{:S(2)}) collective-permute-start(bf16[256,640]{1,0:T(8,128)(2,1)S(1)} %shard_map.105.panel0), channel_id=1, source_target_pairs={{0,12},{1,13},{2,14},{3,15},{4,0},{5,1},{6,2},{7,3},{8,4},{9,5},{1... | collective-permute-start | bytes 983048 | tf_op jit(solution)/shard_map/ppermute | solution.py:392
  60.5 2.2 %collective-permute-done.10.ca2 = bf16[2,2,64,1024]{3,2,1,0:T(8,128)(2,1)S(1)} collective-permute-done((bf16[2,2,64,1024]{3,2,1,0:T(8,128)(2,1)S(1)}, bf16[2,2,64,1024]{3,2,1,0:T(8,128)(2,1)S(1)}, u32[]{:S(2)}, u32[]{:S(2)}) %collective-permute-start.10) | collective-permute-done | bytes 524320 | tf_op jit(solution)/shard_map/ppermute | solution.py:387
  63.5 10.3 %all-gather.7.cloned.1.call-done = bf16[16,2,64,256]{3,2,1,0:T(8,128)(2,1)} async-done(((bf16[4,2,64,256]{3,2,1,0:T(8,128)(2,1)}), bf16[16,2,64,256]{3,2,1,0:T(8,128)(2,1)}) %all-gather.7.cloned.1.call-update) | async-done | bytes 1048592 | tf_op jit(solution)/shard_map/all_gather | solution.py:418
  77.8 2.2 %shard_map.107 = (bf16[288,512]{1,0:T(8,128)(2,1)S(1)}, bf16[512,1024]{1,0:T(8,128)(2,1)S(1)}) custom-call(s32[6]{0:T(128)S(1)} %pad_add_fusion.1.s_ref, bf16[2,2,64,1024]{3,2,1,0:T(8,128)(2,1)S(1)} %get-tuple-element.89.ca0, bf16[2,2,64,1024]{3,2,1,0:T(8,128)(2,1)S(1)} %collective-permute-done.8.ca1, bf16[2,2,64,1024]{3,2,1,0:T(8,128)(2,1)S(1)} %copy-done.6, ...), custom_call_target="tpu_custom_call" | custom-call | bytes 4751384 | tf_op jit(solution)/shard_map/pallas_call | solution.py:29
  80.0 6.0 %collective-permute-start.14 = (bf16[288,512]{1,0:T(8,128)(2,1)S(1)}, bf16[288,512]{1,0:T(8,128)(2,1)S(1)}, u32[]{:S(2)}, u32[]{:S(2)}) collective-permute-start(bf16[288,512]{1,0:T(8,128)(2,1)S(1)} %get-tuple-element.94), channel_id=1, source_target_pairs={{0,16},{16,32},{32,48},{48,64},{64,80},{80,96},{96,112},{112,128},... | collective-permute-start | bytes 884744 | tf_op jit(solution)/shard_map/ppermute | solution.py:424
  87.1 2.2 %shard_map.106 = (bf16[256,512]{1,0:T(8,128)(2,1)S(1)}, f32[256,128]{1,0:T(8,128)S(1)}, bf16[512,1024]{1,0:T(8,128)(2,1)S(1)}) custom-call(s32[6]{0:T(128)S(1)} %pad_add_fusion.1.s_ref, bf16[2,2,64,1024]{3,2,1,0:T(8,128)(2,1)S(1)} %get-tuple-element.89.ca0, bf16[2,2,64,1024]{3,2,1,0:T(8,128)(2,1)S(1)} %collective-permute-done.8.ca1, ...), custom_call_target="tpu_custom_call" | custom-call | bytes 5439512 | tf_op jit(solution)/shard_map/pallas_call | solution.py:29
  90.9 2.7 %collective-permute-start.15 = (bf16[512,128]{1,0:T(8,128)(2,1)S(1)}, bf16[512,128]{1,0:T(8,128)(2,1)S(1)}, u32[]{:S(2)}, u32[]{:S(2)}) collective-permute-start(bf16[512,128]{1,0:T(8,128)(2,1)S(1)} %get-tuple-element.96), channel_id=1, source_target_pairs={{0,12},{1,13},{2,14},{3,15},{4,0},{5,1},{6,2},{7,3},{8,4},{9,5},{1... | collective-permute-start | bytes 393224 | tf_op jit(solution)/shard_map/ppermute | solution.py:392
  96.7 4.0 %collective-permute-start.22 = (bf16[256,512]{1,0:T(8,128)(2,1)S(1)}, bf16[256,512]{1,0:T(8,128)(2,1)S(1)}, u32[]{:S(2)}, u32[]{:S(2)}) collective-permute-start(bf16[256,512]{1,0:T(8,128)(2,1)S(1)} %shard_map.109.refs_0_.refs_1_.block0), channel_id=1, source_target_pairs={{0,2},{1,3},{2,0},{3,1},{4,6},{5,7},{6,4},{7,5},{8,10},{9,11},{10,... | collective-permute-start | bytes 786440 | tf_op jit(solution)/shard_map/ppermute | solution.py:387
  102.7 7.0 %collective-permute-start.31 = (bf16[256,512]{1,0:T(8,128)(2,1)S(1)}, bf16[256,512]{1,0:T(8,128)(2,1)S(1)}, u32[]{:S(2)}, u32[]{:S(2)}) collective-permute-start(bf16[256,512]{1,0:T(8,128)(2,1)S(1)} %shard_map.114), channel_id=1, source_target_pairs={{0,16},{16,32},{32,48},{48,64},{64,80},{80,96},{96,112},{112,128},... | collective-permute-start | bytes 786440 | tf_op jit(solution)/shard_map/ppermute | solution.py:424
  109.7 2.9 %collective-permute-done.22.refs_2_.refs_3_.block2 = bf16[256,512]{1,0:T(8,128)(2,1)S(1)} collective-permute-done((bf16[256,512]{1,0:T(8,128)(2,1)S(1)}, bf16[256,512]{1,0:T(8,128)(2,1)S(1)}, u32[]{:S(2)}, u32[]{:S(2)}) %collective-permute-start.22) | collective-permute-done | bytes 262176 | tf_op jit(solution)/shard_map/ppermute | solution.py:387
  115.6 2.1 %collective-permute-start.25 = (bf16[512,128]{1,0:T(8,128)(2,1)S(1)}, bf16[512,128]{1,0:T(8,128)(2,1)S(1)}, u32[]{:S(2)}, u32[]{:S(2)}) collective-permute-start(bf16[512,128]{1,0:T(8,128)(2,1)S(1)} %get-tuple-element.102), channel_id=1, source_target_pairs={{0,8},{1,9},{2,10},{3,11},{4,12},{5,13},{6,14},{7,15},{8,0},{9,1},... | collective-permute-start | bytes 393224 | tf_op jit(solution)/shard_map/ppermute | solution.py:392
  118.9 2.5 %collective-permute-start.33 = (bf16[256,1024]{1,0:T(8,128)(2,1)S(1)}, bf16[256,1024]{1,0:T(8,128)(2,1)S(1)}, u32[]{:S(2)}, u32[]{:S(2)}) collective-permute-start(bf16[256,1024]{1,0:T(8,128)(2,1)S(1)} %shard_map.115.pair0), channel_id=1, source_target_pairs={{0,2},{1,3},{2,0},{3,1},{4,6},{5,7},{6,4},{7,5},{8,10},{9,11},{10,... | collective-permute-start | bytes 1572872 | tf_op jit(solution)/shard_map/ppermute | solution.py:387
  121.6 3.1 %collective-permute-done.26.got3 = bf16[512,128]{1,0:T(8,128)(2,1)S(1)} collective-permute-done((bf16[512,128]{1,0:T(8,128)(2,1)S(1)}, bf16[512,128]{1,0:T(8,128)(2,1)S(1)}, u32[]{:S(2)}, u32[]{:S(2)}) %collective-permute-start.26) | collective-permute-done | bytes 131104 | tf_op jit(solution)/shard_map/ppermute | solution.py:392
  124.7 1.8 %shard_map.111 = (bf16[512,128]{1,0:T(8,128)(2,1)S(1)}, f32[512,128]{1,0:T(8,128)S(1)}, bf16[512,128]{1,0:T(8,128)(2,1)S(1)}) custom-call(s32[6]{0:T(128)S(1)} %pad_add_fusion.1.s_ref, f32[512,128]{1,0:T(8,128)S(1)} %get-tuple-element.101.own, bf16[512,128]{1,0:T(8,128)(2,1)S(1)} %collective-permute-done.24.got1, ...), custom_call_target="tpu_custom_call" | custom-call | bytes 3473432 | tf_op jit(solution)/shard_map/pallas_call | solution.py:29
  126.6 2.0 %collective-permute-start.28 = (bf16[512,128]{1,0:T(8,128)(2,1)S(1)}, bf16[512,128]{1,0:T(8,128)(2,1)S(1)}, u32[]{:S(2)}, u32[]{:S(2)}) collective-permute-start(bf16[512,128]{1,0:T(8,128)(2,1)S(1)} %get-tuple-element.105), channel_id=1, source_target_pairs={{0,8},{1,9},{2,10},{3,11},{4,12},{5,13},{6,14},{7,15},{8,0},{9,1},... | collective-permute-start | bytes 393224 | tf_op jit(solution)/shard_map/ppermute | solution.py:392
  128.6 2.1 %collective-permute-done.27.got1 = bf16[512,128]{1,0:T(8,128)(2,1)S(1)} collective-permute-done((bf16[512,128]{1,0:T(8,128)(2,1)S(1)}, bf16[512,128]{1,0:T(8,128)(2,1)S(1)}, u32[]{:S(2)}, u32[]{:S(2)}) %collective-permute-start.27) | collective-permute-done | bytes 131104 | tf_op jit(solution)/shard_map/ppermute | solution.py:392
  132.0 4.0 %collective-permute-done.29.got3 = bf16[512,128]{1,0:T(8,128)(2,1)S(1)} collective-permute-done((bf16[512,128]{1,0:T(8,128)(2,1)S(1)}, bf16[512,128]{1,0:T(8,128)(2,1)S(1)}, u32[]{:S(2)}, u32[]{:S(2)}) %collective-permute-start.29) | collective-permute-done | bytes 131104 | tf_op jit(solution)/shard_map/ppermute | solution.py:392
  136.7 4.9 %collective-permute-start.30 = (bf16[512,128]{1,0:T(8,128)(2,1)S(1)}, bf16[512,128]{1,0:T(8,128)(2,1)S(1)}, u32[]{:S(2)}, u32[]{:S(2)}) collective-permute-start(bf16[512,128]{1,0:T(8,128)(2,1)S(1)} %shard_map.112.solved), channel_id=1, source_target_pairs={{0,16},{16,32},{32,48},{48,64},{64,80},{80,96},{96,112},{112,128},... | collective-permute-start | bytes 393224 | tf_op jit(solution)/shard_map/ppermute | solution.py:424
  141.5 3.0 %collective-permute-start.35 = (bf16[512,128]{1,0:T(8,128)(2,1)S(1)}, bf16[512,128]{1,0:T(8,128)(2,1)S(1)}, u32[]{:S(2)}, u32[]{:S(2)}) collective-permute-start(bf16[512,128]{1,0:T(8,128)(2,1)S(1)} %shard_map.112.solved), channel_id=1, source_target_pairs={{16,0},{32,16},{48,32},{64,48},{80,64},{96,80},{112,96},{128,112},... | collective-permute-start | bytes 393224 | tf_op jit(solution)/shard_map/ppermute | solution.py:424
  150.5 2.5 %collective-permute-start.36 = (f32[64,128]{1,0:T(8,128)S(1)}, f32[64,128]{1,0:T(8,128)S(1)}, u32[]{:S(2)}, u32[]{:S(2)}) collective-permute-start(f32[64,128]{1,0:T(8,128)S(1)} %get-tuple-element.116), channel_id=1, source_target_pairs={{0,1},{1,2},{2,3},{3,0},{4,5},{5,6},{6,7},{7,4},{8,9},{9,10},{10,1... | collective-permute-start | bytes 98312 | tf_op jit(solution)/shard_map/ppermute | solution.py:387
  153.7 2.0 %collective-permute-start.38 = (f32[64,128]{1,0:T(8,128)S(1)}, f32[64,128]{1,0:T(8,128)S(1)}, u32[]{:S(2)}, u32[]{:S(2)}) collective-permute-start(f32[64,128]{1,0:T(8,128)S(1)} %get-tuple-element.118), channel_id=1, source_target_pairs={{0,3},{1,0},{2,1},{3,2},{4,7},{5,4},{6,5},{7,6},{8,11},{9,8},{10,9... | collective-permute-start | bytes 98312 | tf_op jit(solution)/shard_map/ppermute | solution.py:387
  (94 shorter events, 39.0 us)
Async XLA Ops:
  7.2 39.1 %all-gather.5.cloned.1.call-start = ((), (), s32[]{:S(2)}) async-start(), calls=%async_computation.1 | async-start | bytes 1310720 | tf_op jit(solution)/shard_map/all_gather | solution.py:418
  11.1 62.7 %all-gather.7.cloned.1.call-start = ((), (), s32[]{:S(2)}) async-start(), calls=%async_computation.2 | async-start | bytes 1310720 | tf_op jit(solution)/shard_map/all_gather | solution.py:418
  11.1 17.1 %collective-permute-start = (bf16[2,64,1024]{2,1,0:T(8,128)(2,1)S(1)}, bf16[2,64,1024]{2,1,0:T(8,128)(2,1)S(1)}, u32[]{:S(2)}, u32[]{:S(2)}) collective-permute-start(bf16[2,64,1024]{2,1,0:T(8,128)(2,1)S(1)} %get-tuple-element.63), channel_id=1, source_target_pairs={{16,0},{32,16},{48,32},{64,48},{80,64},{96,80},{112,96},{128,112},... | collective-permute-start | bytes 786440 | tf_op jit(solution)/shard_map/ppermute | solution.py:424
  13.7 14.5 %collective-permute-start.1 = (bf16[64,1664]{1,0:T(8,128)(2,1)S(1)}, bf16[64,1664]{1,0:T(8,128)(2,1)S(1)}, u32[]{:S(2)}, u32[]{:S(2)}) collective-permute-start(bf16[64,1664]{1,0:T(8,128)(2,1)S(1)} %get-tuple-element.66), channel_id=1, source_target_pairs={{0,1},{1,2},{2,3},{3,0},{4,5},{5,6},{6,7},{7,4},{8,9},{9,10},{10,1... | collective-permute-start | bytes 638984 | tf_op jit(solution)/shard_map/ppermute | solution.py:387
  15.0 13.2 %collective-permute-start.2 = (bf16[64,1664]{1,0:T(8,128)(2,1)S(1)}, bf16[64,1664]{1,0:T(8,128)(2,1)S(1)}, u32[]{:S(2)}, u32[]{:S(2)}) collective-permute-start(bf16[64,1664]{1,0:T(8,128)(2,1)S(1)} %get-tuple-element.67), channel_id=1, source_target_pairs={{0,2},{1,3},{2,0},{3,1},{4,6},{5,7},{6,4},{7,5},{8,10},{9,11},{10,... | collective-permute-start | bytes 638984 | tf_op jit(solution)/shard_map/ppermute | solution.py:387
  17.4 10.8 %collective-permute-start.3 = (bf16[64,1664]{1,0:T(8,128)(2,1)S(1)}, bf16[64,1664]{1,0:T(8,128)(2,1)S(1)}, u32[]{:S(2)}, u32[]{:S(2)}) collective-permute-start(bf16[64,1664]{1,0:T(8,128)(2,1)S(1)} %get-tuple-element.68), channel_id=1, source_target_pairs={{0,3},{1,0},{2,1},{3,2},{4,7},{5,4},{6,5},{7,6},{8,11},{9,8},{10,9... | collective-permute-start | bytes 638984 | tf_op jit(solution)/shard_map/ppermute | solution.py:387
  29.6 13.5 %collective-permute-start.4 = (bf16[256,1152]{1,0:T(8,128)(2,1)S(1)}, bf16[256,1152]{1,0:T(8,128)(2,1)S(1)}, u32[]{:S(2)}, u32[]{:S(2)}) collective-permute-start(bf16[256,1152]{1,0:T(8,128)(2,1)S(1)} %get-tuple-element.75.panel0.source), channel_id=1, source_target_pairs={{0,12},{1,13},{2,14},{3,15},{4,0},{5,1},{6,2},{7,3},{8,4},{9,5},{1... | collective-permute-start | bytes 1769480 | tf_op jit(solution)/shard_map/ppermute | solution.py:392
  31.6 14.6 %collective-permute-start.5 = (bf16[256,1152]{1,0:T(8,128)(2,1)S(1)}, bf16[256,1152]{1,0:T(8,128)(2,1)S(1)}, u32[]{:S(2)}, u32[]{:S(2)}) collective-permute-start(bf16[256,1152]{1,0:T(8,128)(2,1)S(1)} %get-tuple-element.75.panel0.source), channel_id=1, source_target_pairs={{0,4},{1,5},{2,6},{3,7},{4,8},{5,9},{6,10},{7,11},{8,12},{9,13},{1... | collective-permute-start | bytes 1769480 | tf_op jit(solution)/shard_map/ppermute | solution.py:392
  31.6 19.9 %collective-permute-start.8 = (bf16[2,2,64,1024]{3,2,1,0:T(8,128)(2,1)S(1)}, bf16[2,2,64,1024]{3,2,1,0:T(8,128)(2,1)S(1)}, u32[]{:S(2)}, u32[]{:S(2)}) collective-permute-start(bf16[2,2,64,1024]{3,2,1,0:T(8,128)(2,1)S(1)} %get-tuple-element.89.ca0), channel_id=1, source_target_pairs={{0,1},{1,2},{2,3},{3,0},{4,5},{5,6},{6,7},{7,4},{8,9},{9,10},{10,1... | collective-permute-start | bytes 1572872 | tf_op jit(solution)/shard_map/ppermute | solution.py:387
  32.3 19.3 %collective-permute-start.9 = (bf16[2,2,64,1024]{3,2,1,0:T(8,128)(2,1)S(1)}, bf16[2,2,64,1024]{3,2,1,0:T(8,128)(2,1)S(1)}, u32[]{:S(2)}, u32[]{:S(2)}) collective-permute-start(bf16[2,2,64,1024]{3,2,1,0:T(8,128)(2,1)S(1)} %get-tuple-element.89.ca0), channel_id=1, source_target_pairs={{0,3},{1,0},{2,1},{3,2},{4,7},{5,4},{6,5},{7,6},{8,11},{9,8},{10,9... | collective-permute-start | bytes 1572872 | tf_op jit(solution)/shard_map/ppermute | solution.py:387
  46.8 7.5 %collective-permute-start.6 = (bf16[128,1152]{1,0:T(8,128)(2,1)S(1)}, bf16[128,1152]{1,0:T(8,128)(2,1)S(1)}, u32[]{:S(2)}, u32[]{:S(2)}) collective-permute-start(bf16[128,1152]{1,0:T(8,128)(2,1)S(1)} %get-tuple-element.80), channel_id=1, source_target_pairs={{0,4},{1,5},{2,6},{3,7},{4,8},{5,9},{6,10},{7,11},{8,12},{9,13},{1... | collective-permute-start | bytes 884744 | tf_op jit(solution)/shard_map/ppermute | solution.py:392
  46.9 7.4 %collective-permute-start.7 = (bf16[128,1152]{1,0:T(8,128)(2,1)S(1)}, bf16[128,1152]{1,0:T(8,128)(2,1)S(1)}, u32[]{:S(2)}, u32[]{:S(2)}) collective-permute-start(bf16[128,1152]{1,0:T(8,128)(2,1)S(1)} %get-tuple-element.81), channel_id=1, source_target_pairs={{0,12},{1,13},{2,14},{3,15},{4,0},{5,1},{6,2},{7,3},{8,4},{9,5},{1... | collective-permute-start | bytes 884744 | tf_op jit(solution)/shard_map/ppermute | solution.py:392
  49.6 13.1 %collective-permute-start.10 = (bf16[2,2,64,1024]{3,2,1,0:T(8,128)(2,1)S(1)}, bf16[2,2,64,1024]{3,2,1,0:T(8,128)(2,1)S(1)}, u32[]{:S(2)}, u32[]{:S(2)}) collective-permute-start(bf16[2,2,64,1024]{3,2,1,0:T(8,128)(2,1)S(1)} %get-tuple-element.89.ca0), channel_id=1, source_target_pairs={{0,2},{1,3},{2,0},{3,1},{4,6},{5,7},{6,4},{7,5},{8,10},{9,11},{10,... | collective-permute-start | bytes 1572872 | tf_op jit(solution)/shard_map/ppermute | solution.py:387
  56.0 18.6 %collective-permute-start.11 = (bf16[256,640]{1,0:T(8,128)(2,1)S(1)}, bf16[256,640]{1,0:T(8,128)(2,1)}, u32[]{:S(2)}, u32[]{:S(2)}) collective-permute-start(bf16[256,640]{1,0:T(8,128)(2,1)S(1)} %shard_map.105.panel0), channel_id=1, source_target_pairs={{0,12},{1,13},{2,14},{3,15},{4,0},{5,1},{6,2},{7,3},{8,4},{9,5},{1... | collective-permute-start | bytes 983048 | tf_op jit(solution)/shard_map/ppermute | solution.py:392
  58.5 16.8 %collective-permute-start.12 = (bf16[256,640]{1,0:T(8,128)(2,1)S(1)}, bf16[256,640]{1,0:T(8,128)(2,1)}, u32[]{:S(2)}, u32[]{:S(2)}) collective-permute-start(bf16[256,640]{1,0:T(8,128)(2,1)S(1)} %shard_map.105.panel0), channel_id=1, source_target_pairs={{0,8},{1,9},{2,10},{3,11},{4,12},{5,13},{6,14},{7,15},{8,0},{9,1},... | collective-permute-start | bytes 983048 | tf_op jit(solution)/shard_map/ppermute | solution.py:392
  58.5 17.2 %collective-permute-start.13 = (bf16[256,640]{1,0:T(8,128)(2,1)S(1)}, bf16[256,640]{1,0:T(8,128)(2,1)}, u32[]{:S(2)}, u32[]{:S(2)}) collective-permute-start(bf16[256,640]{1,0:T(8,128)(2,1)S(1)} %shard_map.105.panel0), channel_id=1, source_target_pairs={{0,4},{1,5},{2,6},{3,7},{4,8},{5,9},{6,10},{7,11},{8,12},{9,13},{1... | collective-permute-start | bytes 983048 | tf_op jit(solution)/shard_map/ppermute | solution.py:392
  73.8 21.0 %collective-permute-start.18 = (bf16[304,512]{1,0:T(8,128)(2,1)S(1)}, bf16[304,512]{1,0:T(8,128)(2,1)S(1)}, u32[]{:S(2)}, u32[]{:S(2)}) collective-permute-start(bf16[304,512]{1,0:T(8,128)(2,1)S(1)} %shard_map.104.panel0), channel_id=1, source_target_pairs={{0,12},{1,13},{2,14},{3,15},{4,0},{5,1},{6,2},{7,3},{8,4},{9,5},{1... | collective-permute-start | bytes 933896 | tf_op jit(solution)/shard_map/ppermute | solution.py:392
  74.2 20.6 %collective-permute-start.19 = (bf16[304,512]{1,0:T(8,128)(2,1)S(1)}, bf16[304,512]{1,0:T(8,128)(2,1)S(1)}, u32[]{:S(2)}, u32[]{:S(2)}) collective-permute-start(bf16[304,512]{1,0:T(8,128)(2,1)S(1)} %shard_map.104.panel0), channel_id=1, source_target_pairs={{0,8},{1,9},{2,10},{3,11},{4,12},{5,13},{6,14},{7,15},{8,0},{9,1},... | collective-permute-start | bytes 933896 | tf_op jit(solution)/shard_map/ppermute | solution.py:392
  74.6 20.2 %collective-permute-start.20 = (bf16[304,512]{1,0:T(8,128)(2,1)S(1)}, bf16[304,512]{1,0:T(8,128)(2,1)S(1)}, u32[]{:S(2)}, u32[]{:S(2)}) collective-permute-start(bf16[304,512]{1,0:T(8,128)(2,1)S(1)} %shard_map.104.panel0), channel_id=1, source_target_pairs={{0,4},{1,5},{2,6},{3,7},{4,8},{5,9},{6,10},{7,11},{8,12},{9,13},{1... | collective-permute-start | bytes 933896 | tf_op jit(solution)/shard_map/ppermute | solution.py:392
  80.0 9.7 %collective-permute-start.14 = (bf16[288,512]{1,0:T(8,128)(2,1)S(1)}, bf16[288,512]{1,0:T(8,128)(2,1)S(1)}, u32[]{:S(2)}, u32[]{:S(2)}) collective-permute-start(bf16[288,512]{1,0:T(8,128)(2,1)S(1)} %get-tuple-element.94), channel_id=1, source_target_pairs={{0,16},{16,32},{32,48},{48,64},{64,80},{80,96},{96,112},{112,128},... | collective-permute-start | bytes 884744 | tf_op jit(solution)/shard_map/ppermute | solution.py:424
  90.9 9.7 %collective-permute-start.15 = (bf16[512,128]{1,0:T(8,128)(2,1)S(1)}, bf16[512,128]{1,0:T(8,128)(2,1)S(1)}, u32[]{:S(2)}, u32[]{:S(2)}) collective-permute-start(bf16[512,128]{1,0:T(8,128)(2,1)S(1)} %get-tuple-element.96), channel_id=1, source_target_pairs={{0,12},{1,13},{2,14},{3,15},{4,0},{5,1},{6,2},{7,3},{8,4},{9,5},{1... | collective-permute-start | bytes 393224 | tf_op jit(solution)/shard_map/ppermute | solution.py:392
  93.6 9.0 %collective-permute-start.16 = (bf16[512,128]{1,0:T(8,128)(2,1)S(1)}, bf16[512,128]{1,0:T(8,128)(2,1)S(1)}, u32[]{:S(2)}, u32[]{:S(2)}) collective-permute-start(bf16[512,128]{1,0:T(8,128)(2,1)S(1)} %get-tuple-element.96), channel_id=1, source_target_pairs={{0,8},{1,9},{2,10},{3,11},{4,12},{5,13},{6,14},{7,15},{8,0},{9,1},... | collective-permute-start | bytes 393224 | tf_op jit(solution)/shard_map/ppermute | solution.py:392
  96.1 13.6 %collective-permute-start.21 = (bf16[256,512]{1,0:T(8,128)(2,1)S(1)}, bf16[256,512]{1,0:T(8,128)(2,1)S(1)}, u32[]{:S(2)}, u32[]{:S(2)}) collective-permute-start(bf16[256,512]{1,0:T(8,128)(2,1)S(1)} %shard_map.109.refs_0_.refs_1_.block0), channel_id=1, source_target_pairs={{0,1},{1,2},{2,3},{3,0},{4,5},{5,6},{6,7},{7,4},{8,9},{9,10},{10,1... | collective-permute-start | bytes 786440 | tf_op jit(solution)/shard_map/ppermute | solution.py:387
  96.7 15.9 %collective-permute-start.22 = (bf16[256,512]{1,0:T(8,128)(2,1)S(1)}, bf16[256,512]{1,0:T(8,128)(2,1)S(1)}, u32[]{:S(2)}, u32[]{:S(2)}) collective-permute-start(bf16[256,512]{1,0:T(8,128)(2,1)S(1)} %shard_map.109.refs_0_.refs_1_.block0), channel_id=1, source_target_pairs={{0,2},{1,3},{2,0},{3,1},{4,6},{5,7},{6,4},{7,5},{8,10},{9,11},{10,... | collective-permute-start | bytes 786440 | tf_op jit(solution)/shard_map/ppermute | solution.py:387
  100.7 11.9 %collective-permute-start.23 = (bf16[256,512]{1,0:T(8,128)(2,1)S(1)}, bf16[256,512]{1,0:T(8,128)(2,1)S(1)}, u32[]{:S(2)}, u32[]{:S(2)}) collective-permute-start(bf16[256,512]{1,0:T(8,128)(2,1)S(1)} %shard_map.109.refs_0_.refs_1_.block0), channel_id=1, source_target_pairs={{0,3},{1,0},{2,1},{3,2},{4,7},{5,4},{6,5},{7,6},{8,11},{9,8},{10,9... | collective-permute-start | bytes 786440 | tf_op jit(solution)/shard_map/ppermute | solution.py:387
  100.7 9.0 %collective-permute-start.17 = (bf16[512,128]{1,0:T(8,128)(2,1)S(1)}, bf16[512,128]{1,0:T(8,128)(2,1)S(1)}, u32[]{:S(2)}, u32[]{:S(2)}) collective-permute-start(bf16[512,128]{1,0:T(8,128)(2,1)S(1)} %get-tuple-element.96), channel_id=1, source_target_pairs={{0,4},{1,5},{2,6},{3,7},{4,8},{5,9},{6,10},{7,11},{8,12},{9,13},{1... | collective-permute-start | bytes 393224 | tf_op jit(solution)/shard_map/ppermute | solution.py:392
  102.7 15.1 %collective-permute-start.31 = (bf16[256,512]{1,0:T(8,128)(2,1)S(1)}, bf16[256,512]{1,0:T(8,128)(2,1)S(1)}, u32[]{:S(2)}, u32[]{:S(2)}) collective-permute-start(bf16[256,512]{1,0:T(8,128)(2,1)S(1)} %shard_map.114), channel_id=1, source_target_pairs={{0,16},{16,32},{32,48},{48,64},{64,80},{80,96},{96,112},{112,128},... | collective-permute-start | bytes 786440 | tf_op jit(solution)/shard_map/ppermute | solution.py:424
  118.3 27.6 %collective-permute-start.32 = (bf16[256,1024]{1,0:T(8,128)(2,1)S(1)}, bf16[256,1024]{1,0:T(8,128)(2,1)S(1)}, u32[]{:S(2)}, u32[]{:S(2)}) collective-permute-start(bf16[256,1024]{1,0:T(8,128)(2,1)S(1)} %shard_map.115.pair0), channel_id=1, source_target_pairs={{0,1},{1,2},{2,3},{3,0},{4,5},{5,6},{6,7},{7,4},{8,9},{9,10},{10,1... | collective-permute-start | bytes 1572872 | tf_op jit(solution)/shard_map/ppermute | solution.py:387
  118.9 27.0 %collective-permute-start.33 = (bf16[256,1024]{1,0:T(8,128)(2,1)S(1)}, bf16[256,1024]{1,0:T(8,128)(2,1)S(1)}, u32[]{:S(2)}, u32[]{:S(2)}) collective-permute-start(bf16[256,1024]{1,0:T(8,128)(2,1)S(1)} %shard_map.115.pair0), channel_id=1, source_target_pairs={{0,2},{1,3},{2,0},{3,1},{4,6},{5,7},{6,4},{7,5},{8,10},{9,11},{10,... | collective-permute-start | bytes 1572872 | tf_op jit(solution)/shard_map/ppermute | solution.py:387
  121.4 24.5 %collective-permute-start.34 = (bf16[256,1024]{1,0:T(8,128)(2,1)S(1)}, bf16[256,1024]{1,0:T(8,128)(2,1)S(1)}, u32[]{:S(2)}, u32[]{:S(2)}) collective-permute-start(bf16[256,1024]{1,0:T(8,128)(2,1)S(1)} %shard_map.115.pair0), channel_id=1, source_target_pairs={{0,3},{1,0},{2,1},{3,2},{4,7},{5,4},{6,5},{7,6},{8,11},{9,8},{10,9... | collective-permute-start | bytes 1572872 | tf_op jit(solution)/shard_map/ppermute | solution.py:387
  136.7 10.6 %collective-permute-start.30 = (bf16[512,128]{1,0:T(8,128)(2,1)S(1)}, bf16[512,128]{1,0:T(8,128)(2,1)S(1)}, u32[]{:S(2)}, u32[]{:S(2)}) collective-permute-start(bf16[512,128]{1,0:T(8,128)(2,1)S(1)} %shard_map.112.solved), channel_id=1, source_target_pairs={{0,16},{16,32},{32,48},{48,64},{64,80},{80,96},{96,112},{112,128},... | collective-permute-start | bytes 393224 | tf_op jit(solution)/shard_map/ppermute | solution.py:424
  141.5 7.5 %collective-permute-start.35 = (bf16[512,128]{1,0:T(8,128)(2,1)S(1)}, bf16[512,128]{1,0:T(8,128)(2,1)S(1)}, u32[]{:S(2)}, u32[]{:S(2)}) collective-permute-start(bf16[512,128]{1,0:T(8,128)(2,1)S(1)} %shard_map.112.solved), channel_id=1, source_target_pairs={{16,0},{32,16},{48,32},{64,48},{80,64},{96,80},{112,96},{128,112},... | collective-permute-start | bytes 393224 | tf_op jit(solution)/shard_map/ppermute | solution.py:424
  (19 other events, 76.9 us)
Sparse Core Ops, SparseCore 0:
  11.2 28.6 all-gather.4
  41.7 32.0 all-gather.6
